TPU v7x, 32 devices: a whole 2x2x4 slice. The times are simulated.
32 devices in a mesh: rows: 4 (over y, x), seq: 8 (over z, core).
Axes of the slice: x: 2, y: 2, z: 4, core: 2. Of those that a mesh axis runs over, the one named last changes fastest.
Arguments:
- tokens: bfloat16 [8, 1024, 2048], P('rows', 'seq'), may hold values from -6 to 6
- kv_cache: bfloat16 [8, 1024, 2, 512], P('rows', 'seq'), may hold values from -6 to 6
- lengths: int32 [8], P('rows'), may hold values from 1 to 1024, as said below
- norm_gains: float32 [2, 2048], replicated, may hold values from 0.5 to 1.5
- query_weight: bfloat16 [2048, 2048], P('seq'), may hold values from -0.125 to 0.125
- output_weight: bfloat16 [2048, 2048], P('seq'), may hold values from -1 to 1
- ffn_in_weight: bfloat16 [8192, 2, 2048], P('seq'), may hold values from -0.125 to 0.125
- down_weight: bfloat16 [8192, 2048], P('seq'), may hold values from -0.0625 to 0.0625
- cotangent: bfloat16 [8, 1024, 2048], P('rows', 'seq'), may hold values from -6 to 6
Outputs:
- layer_out: bfloat16 [8, 1024, 2048], P('rows', 'seq')
- input_grad: float32 [8, 1024, 2048], P('rows', 'seq')
- cache_grad: float32 [8, 1024, 2, 512], P('rows', 'seq')
- gain_grad: float32 [2, 2048], replicated
- query_weight_grad: float32 [2048, 2048], P('seq')
- output_weight_grad: float32 [2048, 2048], P('seq')
- ffn_in_grad: float32 [8192, 2, 2048], P('seq')
- down_grad: float32 [8192, 2048], P('seq')
Inputs may be any that keep to these rules, and one draw needn't show every extreme that they name: `lengths`: in every aligned group of 2 rows at least one row has length 1024; the others are heavy-tailed.
All inputs are finite; a program needn't handle non-finite values.
Results may differ from a plain program's by a relative error of at most 0.024.
Values may be sent and summed in bfloat16 or wider, within the bound.
No kernel may reach another device: no remote copies, remote signals or barrier semaphores. Data moves between devices by JAX's collectives and lax.ppermute only.
A program may use at most 384 MiB of HBM per device.

v0:
```python
import jax
import jax.numpy as jnp
from jax import lax
from jax.sharding import PartitionSpec as P

HEADS = 16
HEAD = 128
KV = 4
GROUP = 4


EPS = 1e-05
NEG = -1e30


def dot_trans(left, right):
    return lax.dot_general(
        left, right, (((1,), (1,)), ((), ())), preferred_element_type=jnp.float32
    )


def norm_back(grad_normed, scaled, inverse, gain):
    inner = grad_normed * gain
    return inverse * (inner - scaled * jnp.mean(inner * scaled, axis=-1, keepdims=True))


def swiglu_back(gate_up, grad_hidden):
    gate = gate_up[:, 0]
    upper = gate_up[:, 1]
    sigma = jax.nn.sigmoid(gate)
    grad_gate = grad_hidden * upper * sigma * (1.0 + gate * (1.0 - sigma))
    grad_up = grad_hidden * gate * sigma
    return jnp.stack([grad_gate, grad_up], axis=1).astype(jnp.bfloat16)


def local(
    tokens,
    kv_cache,
    lengths,
    norm_gains,
    query_weight,
    output_weight,
    ffn_in_weight,
    down_weight,
    cotangent,
):
    rows_here, seg_len, width = tokens.shape
    seq_count = lax.axis_size("seq")
    tok_count = rows_here * seg_len
    full_len = seg_len * seq_count
    feat_count = HEADS * HEAD
    scale = HEAD ** (-0.5)
    query_pos = lax.axis_index("seq") * seg_len + jnp.arange(seg_len, dtype=jnp.int32)
    limit = jnp.minimum(query_pos[None, :], lengths[:, None] - 1)
    live_rows = (query_pos[None, :] < lengths[:, None]).astype(jnp.float32).reshape(tok_count, 1)
    query_limit = jnp.broadcast_to(limit[:, None, :], (rows_here, GROUP, seg_len)).reshape(
        rows_here, GROUP * seg_len
    )
    inputs = tokens.astype(jnp.float32).reshape(tok_count, width)
    gain_one = norm_gains[0]
    gain_two = norm_gains[1]
    inverse_one = lax.rsqrt(jnp.mean(inputs * inputs, axis=-1, keepdims=True) + EPS)
    normed_one = (inputs * inverse_one * gain_one).astype(jnp.bfloat16)
    query_all, output_all = (
        lax.all_gather(query_weight, "seq", axis=0, tiled=True),
        lax.all_gather(output_weight, "seq", axis=0, tiled=True),
    )
    query_low = dot_trans(normed_one, query_all).astype(jnp.bfloat16)
    query_heads = query_low.reshape(rows_here, seg_len, KV, GROUP, HEAD).transpose(0, 2, 3, 1, 4)
    query_heads = query_heads.reshape(rows_here, KV, GROUP * seg_len, HEAD)
    start_best = jnp.full((rows_here, KV, GROUP * seg_len), NEG, jnp.float32)
    start_total = jnp.zeros((rows_here, KV, GROUP * seg_len), jnp.float32)
    start_accum = jnp.zeros((rows_here, KV, GROUP * seg_len, HEAD), jnp.float32)
    piece = lax.all_gather(kv_cache, "seq", axis=1, tiled=True)
    count = piece.shape[1]
    key_pos = jnp.arange(count, dtype=jnp.int32)
    keys = piece[:, :, 0].reshape(rows_here, count, KV, HEAD)
    values = piece[:, :, 1].reshape(rows_here, count, KV, HEAD)

    def one_row(item):
        query_row, key_row, value_row, limit_row, best_row, total_row, accum_row = item
        scores = (
            jnp.einsum("kqd,rkd->kqr", query_row, key_row, preferred_element_type=jnp.float32)
            * scale
        )
        scores = jnp.where(key_pos[None, None, :] <= limit_row[None, :, None], scores, NEG)
        best_new = jnp.maximum(best_row, jnp.max(scores, axis=-1))
        factor = jnp.exp(best_row - best_new)
        weights = jnp.exp(scores - best_new[..., None])
        total_new = total_row * factor + jnp.sum(weights, axis=-1)
        accum_new = accum_row * factor[..., None] + jnp.einsum(
            "kqr,rkd->kqd",
            weights.astype(jnp.bfloat16),
            value_row,
            preferred_element_type=jnp.float32,
        )
        return (best_new, total_new, accum_new)

    best, total, accum = lax.map(
        one_row, (query_heads, keys, values, query_limit, start_best, start_total, start_accum)
    )
    mixed_heads = accum / total[..., None]
    log_total = best + jnp.log(total)
    mixed_low = mixed_heads.reshape(rows_here, KV, GROUP, seg_len, HEAD).transpose(0, 3, 1, 2, 4)
    mixed_low = mixed_low.reshape(tok_count, feat_count).astype(jnp.bfloat16)
    middle = inputs + jnp.dot(mixed_low, output_all, preferred_element_type=jnp.float32)
    inverse_two = lax.rsqrt(jnp.mean(middle * middle, axis=-1, keepdims=True) + EPS)
    normed_two = (middle * inverse_two * gain_two).astype(jnp.bfloat16)
    grad_out = cotangent.astype(jnp.float32).reshape(tok_count, width) * live_rows
    grad_low = grad_out.astype(jnp.bfloat16)
    normed_group = lax.all_gather(normed_two, "seq", axis=0, tiled=True)
    kept = jnp.einsum(
        "td,nkd->tkn", normed_group, ffn_in_weight, preferred_element_type=jnp.float32
    )
    hidden_group = (jax.nn.silu(kept[:, 0]) * kept[:, 1]).astype(jnp.bfloat16)
    ffn_out = lax.psum_scatter(
        jnp.dot(hidden_group, down_weight, preferred_element_type=jnp.float32).astype(jnp.bfloat16),
        "seq",
        scatter_dimension=0,
        tiled=True,
    ).astype(jnp.float32)
    grad_group = lax.all_gather(grad_low, "seq", axis=0, tiled=True)
    grad_gate_up = swiglu_back(kept, dot_trans(grad_group, down_weight))
    grad_normed_two = lax.psum_scatter(
        jnp.einsum(
            "tkn,nkd->td", grad_gate_up, ffn_in_weight, preferred_element_type=jnp.float32
        ).astype(jnp.bfloat16),
        "seq",
        scatter_dimension=0,
        tiled=True,
    ).astype(jnp.float32)
    in_grad = jnp.einsum(
        "tkn,td->nkd", grad_gate_up, normed_group, preferred_element_type=jnp.float32
    )
    down_part = jnp.einsum(
        "tn,td->nd", hidden_group, grad_group, preferred_element_type=jnp.float32
    )
    layer_out = (
        (live_rows * (middle + ffn_out)).astype(jnp.bfloat16).reshape(rows_here, seg_len, width)
    )
    scaled_two = middle * inverse_two
    gain_two_grad = jnp.sum(grad_normed_two * scaled_two, axis=0)
    grad_middle = grad_out + norm_back(grad_normed_two, scaled_two, inverse_two, gain_two)
    grad_branch = grad_middle.astype(jnp.bfloat16)
    grad_mixed = dot_trans(grad_branch, output_all).astype(jnp.bfloat16)
    grad_heads = grad_mixed.reshape(rows_here, seg_len, KV, GROUP, HEAD).transpose(0, 2, 3, 1, 4)
    grad_heads = grad_heads.reshape(rows_here, KV, GROUP * seg_len, HEAD)
    delta = jnp.sum(grad_heads.astype(jnp.float32) * mixed_heads, axis=-1)
    cache_full = lax.all_gather(kv_cache, "seq", axis=1, tiled=True)
    key_all = jnp.arange(full_len, dtype=jnp.int32)

    def row_back(item):
        query_row, grad_row, delta_row, lse_row, limit_row, cache_row = item
        keys = cache_row[:, 0].reshape(full_len, KV, HEAD)
        values = cache_row[:, 1].reshape(full_len, KV, HEAD)
        scores = (
            jnp.einsum("kqd,rkd->kqr", query_row, keys, preferred_element_type=jnp.float32) * scale
        )
        valid = key_all[None, None, :] <= limit_row[None, :, None]
        probs = jnp.where(valid, jnp.exp(scores - lse_row[..., None]), 0.0)
        grad_probs = jnp.einsum(
            "kqd,rkd->kqr", grad_row, values, preferred_element_type=jnp.float32
        )
        grad_scores = (probs * (grad_probs - delta_row[..., None])).astype(jnp.bfloat16)
        grad_query = (
            jnp.einsum("kqr,rkd->kqd", grad_scores, keys, preferred_element_type=jnp.float32)
            * scale
        )
        grad_keys = (
            jnp.einsum("kqr,kqd->rkd", grad_scores, query_row, preferred_element_type=jnp.float32)
            * scale
        )
        grad_values = jnp.einsum(
            "kqr,kqd->rkd", probs.astype(jnp.bfloat16), grad_row, preferred_element_type=jnp.float32
        )
        return (
            grad_query,
            jnp.stack(
                [grad_keys.reshape(full_len, KV * HEAD), grad_values.reshape(full_len, KV * HEAD)],
                axis=1,
            ),
        )

    grad_query_heads, cache_terms = lax.map(
        row_back, (query_heads, grad_heads, delta, log_total, query_limit, cache_full)
    )
    cache_grad = lax.psum_scatter(
        cache_terms.astype(jnp.bfloat16), "seq", scatter_dimension=1, tiled=True
    ).astype(jnp.float32)
    grad_query = grad_query_heads.reshape(rows_here, KV, GROUP, seg_len, HEAD).transpose(
        0, 3, 1, 2, 4
    )
    grad_query = grad_query.reshape(tok_count, feat_count).astype(jnp.bfloat16)
    grad_normed_one = jnp.dot(grad_query, query_all, preferred_element_type=jnp.float32)
    query_grad_rows = jnp.einsum(
        "tn,td->nd", grad_query, normed_one, preferred_element_type=jnp.float32
    )
    output_grad_rows = jnp.einsum(
        "tn,td->nd", mixed_low, grad_branch, preferred_element_type=jnp.float32
    )
    attn_grad = lax.psum_scatter(
        jnp.stack([query_grad_rows, output_grad_rows], axis=1).astype(jnp.bfloat16),
        "seq",
        scatter_dimension=0,
        tiled=True,
    ).astype(jnp.float32)
    scaled_one = inputs * inverse_one
    gain_one_grad = jnp.sum(grad_normed_one * scaled_one, axis=0)
    input_grad = grad_middle + norm_back(grad_normed_one, scaled_one, inverse_one, gain_one)
    gain_grad = lax.psum(jnp.stack([gain_one_grad, gain_two_grad]), ("rows", "seq"))
    query_grad, output_grad, ffn_in_grad, down_grad = (
        lax.psum(attn_grad[:, 0].astype(jnp.bfloat16), "rows").astype(jnp.float32),
        lax.psum(attn_grad[:, 1].astype(jnp.bfloat16), "rows").astype(jnp.float32),
        lax.psum(in_grad.astype(jnp.bfloat16), "rows").astype(jnp.float32),
        lax.psum(down_part.astype(jnp.bfloat16), "rows").astype(jnp.float32),
    )
    return (
        layer_out,
        input_grad.reshape(rows_here, seg_len, width),
        cache_grad,
        gain_grad,
        query_grad,
        output_grad,
        ffn_in_grad,
        down_grad,
    )


def solution(mesh):
    in_specs = (
        P("rows", "seq", None),
        P("rows", "seq", None, None),
        P("rows"),
        P(),
        P("seq", None),
        P("seq", None),
        P("seq", None, None),
        P("seq", None),
        P("rows", "seq", None),
    )
    out_specs = (
        P("rows", "seq", None),
        P("rows", "seq", None),
        P("rows", "seq", None, None),
        P(),
        P("seq", None),
        P("seq", None),
        P("seq", None, None),
        P("seq", None),
    )
    return jax.shard_map(local, mesh=mesh, in_specs=in_specs, out_specs=out_specs, check_vma=False)
```

profile of v0, /device:TPU:0, one launch (start us, length us, event | category | flops | bytes accessed | tf_op | source)
XLA Modules:
  0.0 1240.6 jit_solution(16044014437185275343)
XLA Ops:
  13.9 46.9 %all-gather.8.cloned.1.call-done = bf16[2,1024,2,512]{1,3,0,2:T(8,128)(2,1)} async-done(((bf16[2,128,2,512]{1,3,0,2:T(8,128)(2,1)}), bf16[2,1024,2,512]{1,3,0,2:T(8,128)(2,1)}) %all-gather.8.cloned.1.call-update) | async-done | bytes 4194320 | tf_op jit(solution)/shard_map/all_gather | solution.py:74
  64.9 77.7 %all-gather.6.cloned.1.call-done = bf16[2048,2048]{1,0:T(8,128)(2,1)} async-done(((bf16[256,2048]{1,0:T(8,128)(2,1)}), bf16[2048,2048]{1,0:T(8,128)(2,1)}) %all-gather.6.cloned.1.call-update) | async-done | bytes 8388624 | tf_op jit(solution)/shard_map/all_gather | solution.py:65
  142.6 7.1 convolution_convert_fusion.3
  155.1 18.7 %while.30 = (s32[]{:T(128)}, f32[2,4,512]{2,1,0:T(4,128)S(1)}, f32[2,4,512]{2,1,0:T(4,128)S(1)}, f32[2,4,512,128]{3,2,1,0:T(8,128)}, s32[2,512]{1,0:T(2,128)S(1)...) while((s32[]{:T(128)}, f32[2,4,512]{2,1,0:T(4,128)S(1)}, ...), condition=%wide.region_4.5_spmd.clone.clone, body=%wide.region_1.4_spmd.clone.sunk.clone | while | flops 1097607168 | bytes 56205496 | solution.py:99
  178.3 46.6 %all-gather.10.cloned.1.call-done = bf16[2048,2048]{1,0:T(8,128)(2,1)} async-done(((bf16[256,2048]{1,0:T(8,128)(2,1)}), bf16[2048,2048]{1,0:T(8,128)(2,1)}) %all-gather.10.cloned.1.call-update) | async-done | bytes 8388624 | tf_op jit(solution)/shard_map/all_gather | solution.py:66
  235.0 78.1 %all-gather.12.cloned.1.call-done = bf16[2048,2048]{1,0:T(8,128)(2,1)} async-done(((bf16[256,2048]{1,0:T(8,128)(2,1)}), bf16[2048,2048]{1,0:T(8,128)(2,1)}) %all-gather.12.cloned.1.call-update) | async-done | bytes 8388624 | tf_op jit(solution)/shard_map/all_gather | solution.py:111
  313.1 25.0 %fusion.63 = f32[2048,2,1024]{2,0,1:T(8,128)} fusion(bf16[1024,2,2048]{2,1,0:T(2,128)(2,1)} %param.19, bf16[2048,2048]{1,0:T(8,128)(2,1)} %all-gather.12.cloned.1.call-done), kind=kOutput, calls=%fused_computation.86 | convolution fusion | flops 17179869184 | bytes 33554432 | tf_op jit(solution)/shard_map/td,nkd->tkn/dot_general | solution.py:112
  338.1 57.6 %all-gather.14.cloned.1.call-done = bf16[2048,2048]{1,0:T(8,128)(2,1)} async-done(((bf16[256,2048]{1,0:T(8,128)(2,1)}), bf16[2048,2048]{1,0:T(8,128)(2,1)}) %all-gather.14.cloned.1.call-update) | async-done | bytes 8388624 | tf_op jit(solution)/shard_map/all_gather | solution.py:122
  395.7 23.0 %fusion.71 = (bf16[2048,1,1024]{2,0,1:T(8,128)(2,1)}, bf16[2048,1,1024]{2,0,1:T(8,128)(2,1)}, bf16[2048,1024]{1,0:T(8,128)(2,1)}) fusion(f32[2048,2,1024]{2,0,1:T(8,128)} %fusion.63, bf16[2048,2048]{1,0:T(8,128)(2,1)} %all-gather.14.cloned.1.call-done, bf16[1024,2048]{1,0:T(8,128)(2,1)} %param.20), kind=kOutput, calls=%fused_computation.89 | convolution fusion | flops 8623489024 | bytes 41943040 | tf_op jit(solution)/shard_map/dot_general | solution.py:17
  418.7 24.7 %bitcast_convert_fusion = bf16[2048,2048]{1,0:T(8,128)(2,1)} fusion(bf16[1024,2,2048]{2,1,0:T(2,128)(2,1)} %param.19, bf16[2048,1,1024]{2,0,1:T(8,128)(2,1)} %get-tuple-element.272, bf16[2048,1,1024]{2,0,1:T(8,128)(2,1)} %get-tuple-element.271), kind=kOutput, calls=%fused_computation.68 | convolution fusion | flops 17188257792 | bytes 25165824 | tf_op jit(solution)/shard_map/tkn,nkd->td/dot_general | solution.py:125
  443.5 13.9 %convolution_convert_fusion = bf16[2048,2048]{1,0:T(8,128)(2,1)} fusion(bf16[2048,1024]{1,0:T(8,128)(2,1)} %get-tuple-element.273, bf16[1024,2048]{1,0:T(8,128)(2,1)} %param.20), kind=kOutput, calls=%fused_computation.83 | convolution fusion | flops 8594128896 | bytes 16777216 | tf_op jit(solution)/shard_map/dot_general | solution.py:117
  460.2 71.6 %reduce-scatter.10.cloned.1.call-done = bf16[256,2048]{1,0:T(8,128)(2,1)} async-done(((bf16[2048,2048]{1,0:T(8,128)(2,1)}), bf16[256,2048]{1,0:T(8,128)(2,1)}) %reduce-scatter.10.cloned.1.call-update) | async-done | bytes 1048592 | tf_op jit(solution)/shard_map/reduce_scatter | solution.py:124
  534.4 88.3 %reduce-scatter.8.cloned.1.call-done = bf16[256,2048]{1,0:T(8,128)(2,1)} async-done(((bf16[2048,2048]{1,0:T(8,128)(2,1)}), bf16[256,2048]{1,0:T(8,128)(2,1)}) %reduce-scatter.8.cloned.1.call-update) | async-done | bytes 1048592 | tf_op jit(solution)/shard_map/reduce_scatter | solution.py:116
  639.4 46.5 %while.31 = (s32[]{:T(128)}, bf16[2,4,512,128]{3,2,1,0:T(8,128)(2,1)}, bf16[2,1024,2,512]{3,2,1,0:T(2,128)(2,1)}, s32[2,512]{1,0:T(2,128)S(1)}, bf16[2,4,512,128...) while((s32[]{:T(128)}, ...), condition=%wide.region_11.12_spmd.clone.clone, body=%wide.region_10.11_spmd.clone.sunk.clone | while | flops 2708209664 | bytes 77134016 | solution.py:184
  691.7 10.5 pad_maximum_fusion
  702.2 7.1 copy.97
  709.3 7.9 reshape.284
  717.3 14.3 %convolution_convert_fusion.1 = bf16[1024,2048]{1,0:T(8,128)(2,1)} fusion(bf16[2048,1024]{1,0:T(8,128)(2,1)} %get-tuple-element.273, bf16[2048,2048]{1,0:T(8,128)(2,1)} %all-gather.14.cloned.1.call-done), kind=kOutput, calls=%fused_computation.90 | convolution fusion | flops 8592031744 | bytes 16777216 | tf_op jit(solution)/shard_map/tn,td->nd/dot_general | solution.py:135
  731.6 21.9 %convert_bitcast_fusion = bf16[1024,2,2048]{0,2,1:T(8,128)(2,1)} fusion(bf16[2048,1,1024]{2,0,1:T(8,128)(2,1)S(1)} %copy-done.25, bf16[2048,1,1024]{2,0,1:T(8,128)(2,1)S(1)} %copy-done.24, bf16[2048,2048]{1,0:T(8,128)(2,1)} %all-gather.12.cloned.1.call-done), kind=kOutput, calls=%fused_computation.76 | convolution fusion | flops 17200840704 | bytes 25165824 | tf_op jit(solution)/shard_map/tkn,td->nkd/dot_general | solution.py:132
  753.5 115.4 %reduce-scatter.12.cloned.1.call-done = bf16[256,2,2048]{2,0,1:T(8,128)(2,1)} async-done(((bf16[2048,2,2048]{2,0,1:T(8,128)(2,1)}), bf16[256,2,2048]{2,0,1:T(8,128)(2,1)}) %reduce-scatter.12.cloned.1.call-update) | async-done | bytes 2097168 | tf_op jit(solution)/shard_map/reduce_scatter | solution.py:201
  873.4 8.1 multiply_reduce_fusion
  881.4 39.8 %psum.35 = f32[2,2048]{1,0:T(2,128)} all-reduce(f32[2,2048]{1,0:T(2,128)S(1)} %pad_maximum_fusion.6), channel_id=1, replica_groups=mesh['rows'=4,'seq'=8] {'rows','seq'}, use_global_device_ids=true, to_apply=%region_16.17 | all-reduce | flops 4096 | bytes 32768 | tf_op jit(solution)/shard_map/psum | solution.py:210
  927.5 271.5 %all-reduce.3.cloned.1.call-done = (bf16[1024,2,2048]{0,2,1:T(8,128)(2,1)}, bf16[256,2048]{1,0:T(8,128)(2,1)}, bf16[256,2048]{1,0:T(8,128)(2,1)}, bf16[1024,2048]{1,0:T(8,128)(2,1)}) async-done(((bf16[1024,2,2048]{0,2,1:T(8,128)(2,1)}, bf16[256,2048]{1,0:T(8,128)(2,1)}, bf16[256,2048]{1,0:T(8,128)(2,1)}, bf16[1024,2048]{1,0:T(8,128)(2,1)}), (bf16[1024,2,2048]{0,2,1:T(8,128)(2,1)}, ...) | async-done | bytes 14680080 | tf_op jit(solution)/shard_map/psum | solution.py:214
  1204.6 22.3 %copy.63 = f32[1024,2,2048]{2,1,0:T(2,128)} copy(bf16[1024,2,2048]{0,2,1:T(8,128)(2,1)} %get-tuple-element.257) | data formatting | bytes 25165824
  (176 shorter events, 146.2 us)
Async XLA Ops:
  7.2 4.5 copy-start.2
  7.2 5.4 copy-start.19
  7.2 53.5 %all-gather.8.cloned.1.call-start = ((), (), s32[]{:S(2)}) async-start(), calls=%async_computation.5 | async-start | bytes 4718592 | tf_op jit(solution)/shard_map/all_gather | solution.py:74
  9.3 133.3 %all-gather.6.cloned.1.call-start = ((), (), s32[]{:S(2)}) async-start(), calls=%async_computation.4 | async-start | bytes 9437184 | tf_op jit(solution)/shard_map/all_gather | solution.py:65
  10.1 214.8 %all-gather.10.cloned.1.call-start = ((), (), s32[]{:S(2)}) async-start(), calls=%async_computation.6 | async-start | bytes 9437184 | tf_op jit(solution)/shard_map/all_gather | solution.py:66
  10.8 302.2 %all-gather.12.cloned.1.call-start = ((), (), s32[]{:S(2)}) async-start(), calls=%async_computation.7 | async-start | bytes 9437184 | tf_op jit(solution)/shard_map/all_gather | solution.py:111
  12.5 52.4 %copy-start.20 = (f32[256]{0:T(256)}, f32[256]{0:T(256)S(1)}, u32[]{:S(2)}) copy-start(f32[256]{0:T(256)S(1)} %get-tuple-element.283) | copy-start | bytes 3076
  12.6 52.4 %copy-start.15 = (f32[1,2048]{1,0:T(1,128)}, f32[1,2048]{1,0:T(1,128)S(1)}, u32[]{:S(2)}) copy-start(f32[1,2048]{1,0:T(1,128)S(1)} %get-tuple-element.281) | copy-start | bytes 24580
  173.9 57.2 %copy-start.13 = (s32[2,512]{1,0:T(2,128)}, s32[2,512]{1,0:T(2,128)S(1)}, u32[]{:S(2)}) copy-start(s32[2,512]{1,0:T(2,128)S(1)} %get-tuple-element.560) | copy-start | bytes 12292
  232.3 163.4 %all-gather.14.cloned.1.call-start = ((), (), s32[]{:S(2)}) async-start(), calls=%async_computation.9 | async-start | bytes 9437184 | tf_op jit(solution)/shard_map/all_gather | solution.py:122
  234.9 296.9 %reduce-scatter.10.cloned.1.call-start = ((), (), s32[]{:S(2)}) async-start(), calls=%async_computation.10 | async-start | bytes 9437184 | tf_op jit(solution)/shard_map/reduce_scatter | solution.py:124
  443.5 179.2 %reduce-scatter.8.cloned.1.call-start = ((), (), s32[]{:S(2)}) async-start(), calls=%async_computation.8 | async-start | bytes 9437184 | tf_op jit(solution)/shard_map/reduce_scatter | solution.py:116
  457.5 411.5 %reduce-scatter.12.cloned.1.call-start = ((), (), s32[]{:S(2)}) async-start(), calls=%async_computation.11 | async-start | bytes 18874368 | tf_op jit(solution)/shard_map/reduce_scatter | solution.py:201
  534.4 92.1 %copy-start.7 = (bf16[256,2048]{1,0:T(8,128)(2,1)S(1)}, bf16[256,2048]{1,0:T(8,128)(2,1)}, u32[]{:S(2)}) copy-start(bf16[256,2048]{1,0:T(8,128)(2,1)} %convert_element_type.140) | copy-start | bytes 3145732
  622.6 9.7 slice-start
  626.5 5.8 copy-start
  626.5 5.8 slice-start.1
  634.7 4.7 copy-start.14
  702.2 222.5 %reduce-scatter.14.cloned.1.call-start = ((), (), s32[]{:S(2)}) async-start(), calls=%async_computation.12 | async-start | bytes 4718592
  717.2 481.8 %all-reduce.3.cloned.1.call-start = ((), (), s32[]{:S(2)}) async-start(), calls=%async_computation.13 | async-start | bytes 29360128 | tf_op jit(solution)/shard_map/psum | solution.py:214
  717.3 14.3 %copy-start.24 = (bf16[2048,1,1024]{2,0,1:T(8,128)(2,1)S(1)}, bf16[2048,1,1024]{2,0,1:T(8,128)(2,1)}, u32[]{:S(2)}) copy-start(bf16[2048,1,1024]{2,0,1:T(8,128)(2,1)} %get-tuple-element.271) | copy-start | bytes 12582916
  717.3 14.3 %copy-start.25 = (bf16[2048,1,1024]{2,0,1:T(8,128)(2,1)S(1)}, bf16[2048,1,1024]{2,0,1:T(8,128)(2,1)}, u32[]{:S(2)}) copy-start(bf16[2048,1,1024]{2,0,1:T(8,128)(2,1)} %get-tuple-element.272) | copy-start | bytes 12582916
  873.3 8.1 copy-start.18
  873.3 47.9 %copy-start.1 = (f32[256,2048]{1,0:T(8,128)S(1)}, f32[256,2048]{1,0:T(8,128)}, u32[]{:S(2)}) copy-start(f32[256,2048]{1,0:T(8,128)} %copy-done) | copy-start | bytes 6291460
  (19 other events, 41.7 us)
Sparse Core Ops, SparseCore 0:
  10.2 50.4 all-gather.7
  62.3 80.2 all-gather.5
  144.2 80.5 all-gather.9
  232.4 80.5 all-gather.11
  315.1 80.5 all-gather.13
  443.6 88.1 reduce-scatter.9
  534.6 87.9 reduce-scatter.7
  702.3 166.6 reduce-scatter.11
  871.2 49.3 reduce-scatter.13
  925.0 273.9 all-reduce.2
where the time goes:
time: 1250 us; the launch traced here: 1240 us
  waiting for transfers between devices  855 us (68%)
  matrix products  189 us (15%)
  local copies, waits for them, and re-layouts  85.6 us (7%)
  other arithmetic  55.7 us (4%)
  blocking collectives  39.8 us (3%)
  between operations  14.6 us (1%)
    psum x1, waiting for transfers between devices, local(): lax.psum(in_grad.astype(jnp.bfloat16), 'rows').astype(jnp.float32)  272 us
    reduce_scatter x1, waiting for transfers between devices, local(): lax.psum_scatter(jnp.stack([query_grad_rows, output_grad_rows], axis=1).a...  115 us
    reduce_scatter x1, waiting for transfers between devices, local(): lax.psum_scatter(jnp.dot(hidden_group, down_weight, preferred_element_typ...  88.3 us
    all_gather x1, waiting for transfers between devices, local(): normed_group = lax.all_gather(normed_two, 'seq', axis=0, tiled=True)  78.1 us
    all_gather x1, waiting for transfers between devices, local(): lax.all_gather(query_weight, 'seq', axis=0, tiled=True)  77.7 us
    reduce_scatter x1, waiting for transfers between devices, local(): lax.psum_scatter(jnp.einsum('tkn,nkd->td', grad_gate_up, ffn_in_weight, p...  71.6 us
    all_gather x1, waiting for transfers between devices, local(): grad_group = lax.all_gather(grad_low, 'seq', axis=0, tiled=True)  57.6 us
    all_gather x1, waiting for transfers between devices, local(): piece = lax.all_gather(kv_cache, 'seq', axis=1, tiled=True)  46.9 us
  transfers between devices with their start and end apart: 10, of which 9 were waited for; matrix products, arithmetic and copies ran while one was open for 12% of the time, Pallas kernels for 0%

commit v1 on v0

v1 whole, which is shorter than its diff:
```python
import jax
import jax.numpy as jnp
from jax import lax
from jax.sharding import PartitionSpec as P

HEADS = 16
HEAD = 128
KV = 4
GROUP = 4
EPS = 1e-05
NEG = -1e30
F32 = jnp.float32
BF16 = jnp.bfloat16


def dot(left, right, dims):
    return lax.dot_general(left, right, (dims, ((), ())), preferred_element_type=F32)


def tie(value, dep):
    if dep is None:
        return value
    return lax.optimization_barrier((value, dep))[0]


def norm_back(grad_normed, scaled, inverse, gain):
    inner = grad_normed * gain
    return inverse * (inner - scaled * jnp.mean(inner * scaled, axis=-1, keepdims=True))


def swap_core(value, seq):
    return lax.ppermute(value, "seq", [(s, s ^ 1) for s in range(seq)])


def ring(value, chips):
    pairs = [(2 * z + c, 2 * ((z + 1) % chips) + c) for z in range(chips) for c in range(2)]
    return lax.ppermute(value, "seq", pairs)


def swap_row(value, rows, mask):
    return lax.ppermute(value, "rows", [(r, r ^ mask) for r in range(rows)])


def ring_gather(own, chips, dep=None):
    got = [tie(own, dep)]
    for _ in range(1, chips):
        got.append(ring(got[-1], chips))
    return [own] + got[:0:-1], got[-2]


def ring_scatter(parts, chips, dep=None):
    moving = ring(tie(parts[chips - 1], dep), chips)
    for j in range(chips - 2, -1, -1):
        total = moving.astype(F32) + parts[j].astype(F32)
        if j:
            moving = ring(total.astype(BF16), chips)
    return total


def xor_order(value, at):
    shape = value.shape
    value = value.reshape(2, 2, *shape[1:])
    value = jnp.where(at % 2 == 1, value[:, ::-1], value)
    return jnp.where(at // 2 == 1, value[::-1], value).reshape(shape)


def own_order(value, chips, place, core):
    count = value.shape[0]
    value = value.reshape(count, chips, 2, -1)
    value = jnp.where(core == 0, value, value[:, :, ::-1])
    value = jnp.concatenate([value, value], axis=1)
    value = lax.dynamic_slice_in_dim(value, place, chips, axis=1)
    return value.transpose(0, 2, 1, 3).reshape(count, -1)


def index_order(value, chips, place, core):
    count = value.shape[0]
    value = value.reshape(count, 2, chips, -1).transpose(0, 2, 1, 3)
    value = jnp.concatenate([value, value], axis=1)
    value = lax.dynamic_slice_in_dim(value, (chips - place) % chips, chips, axis=1)
    value = jnp.where(core == 0, value, value[:, :, ::-1])
    return value.reshape(count, -1)


class Weight:
    def __init__(self, shard, chips, rows, row_at, order, dep=None):
        seq = 2 * chips
        self.chips, self.row_at, self.order = chips, row_at, order
        depth, width = shard.shape
        self.depth = depth
        self.split = rows == 4 and depth % 32 == 0 and width % 512 == 0
        if not self.split:
            self.whole = lax.all_gather(shard, "seq", axis=0, tiled=True)
            self.token = dep
            return
        part = width // rows
        half = depth // 2
        mine = lax.dynamic_slice_in_dim(shard, row_at * part, part, axis=1)
        slots, self.token = ring_gather(mine, chips, dep=dep)
        first = jnp.stack([v[:half] for v in slots[1:]])
        second = jnp.stack([v[half:] for v in slots[1:]])
        first_x = swap_row(first, rows, 1)
        second_y = swap_row(second, rows, 2)
        first_pair = swap_row(jnp.stack([first, first_x]), rows, 2)
        second_pair = swap_row(jnp.stack([second, second_y]), rows, 1)
        parts = jnp.stack(
            [
                jnp.stack([first, first_x, first_pair[0], first_pair[1]]),
                jnp.stack([second, second_pair[0], second_y, second_pair[1]]),
            ],
            axis=2,
        )
        parts = parts.reshape(rows, (chips - 1) * depth, part)
        self.far = [parts, swap_core(parts, seq)]
        self.near = [shard, swap_core(shard, seq)]

    def features(self, value):
        if not self.split:
            return own_order(dot(value, self.whole, ((1,), (1,))), *self.order)
        count = value.shape[0]
        blocks = value.reshape(count, 4, -1).transpose(1, 0, 2)
        blocks = xor_order(blocks, self.row_at)
        out = []
        for near, far in zip(self.near, self.far, strict=True):
            out.append(dot(value, near, ((1,), (1,))))
            term = jnp.einsum("ktc,kfc->ktf", blocks, far, preferred_element_type=F32)
            out.append(jnp.sum(term, axis=0))
        return jnp.concatenate(out, axis=1)

    def back(self, value):
        if not self.split:
            return dot(index_order(value, *self.order), self.whole, ((1,), (0,)))
        count = value.shape[0]
        half = value.shape[1] // 2
        near_sum = far_sum = 0.0
        for i in range(2):
            part = value[:, i * half : (i + 1) * half]
            near_sum += dot(part[:, : self.depth], self.near[i], ((1,), (0,)))
            far_sum += jnp.einsum(
                "tf,kfc->ktc", part[:, self.depth :], self.far[i], preferred_element_type=F32
            )
        far_sum = xor_order(far_sum, self.row_at).transpose(1, 0, 2).reshape(count, -1)
        return near_sum + far_sum


def gather_tokens(own, chips, dep=None):
    slots, token = ring_gather(own, chips, dep=dep)
    block = jnp.concatenate(slots, axis=0)
    return jnp.concatenate([block, swap_core(block, 2 * chips)], axis=0), token


def scatter_tokens(part, chips, dep=None):
    half = part.shape[0] // 2
    block = part[:half].astype(F32) + swap_core(part[half:], 2 * chips).astype(F32)
    block = block.astype(BF16)
    size = half // chips
    return ring_scatter([block[j * size : (j + 1) * size] for j in range(chips)], chips, dep=dep)


def sum_rows(value, rows):
    if rows != 4:
        return lax.psum(value.astype(BF16), "rows").astype(F32)
    half = value.shape[0] // 2
    first, second = value[:half].astype(BF16), value[half:].astype(BF16)

    def pair(item, mask):
        return item.astype(F32) + swap_row(item, rows, mask).astype(F32)

    first, second = pair(first, 1).astype(BF16), pair(second, 2).astype(BF16)
    return jnp.concatenate([pair(first, 2), pair(second, 1)], axis=0)


def sum_all(value, rows, seq):
    mask = 1
    while mask < seq:
        value = value + lax.ppermute(value, "seq", [(s, s ^ mask) for s in range(seq)])
        mask *= 2
    mask = 1
    while mask < rows:
        value = value + swap_row(value, rows, mask)
        mask *= 2
    return value


def local(
    tokens,
    kv_cache,
    lengths,
    norm_gains,
    query_weight,
    output_weight,
    ffn_in_weight,
    down_weight,
    cotangent,
):
    rows_here, seg_len, width = tokens.shape
    seq = lax.axis_size("seq")
    rows = lax.axis_size("rows")
    chips = seq // 2
    seq_at = lax.axis_index("seq")
    row_at = lax.axis_index("rows")
    place, core = seq_at // 2, seq_at % 2
    full_len = seg_len * seq
    units = down_weight.shape[0]
    scale = HEAD ** (-0.5)
    gain_one, gain_two = norm_gains[0], norm_gains[1]
    positions = jnp.arange(seg_len, dtype=jnp.int32)
    query_pos = seq_at * seg_len + positions
    chip_order = (place + jnp.arange(chips, dtype=jnp.int32)) % chips
    core_order = jnp.stack([core, 1 - core])
    key_pos = (
        (chip_order[None, :, None] * 2 + core_order[:, None, None]) * seg_len
        + positions[None, None, :]
    ).reshape(full_len)

    order = (chips, place, core)
    query_proj = Weight(query_weight, chips, rows, row_at, order)
    output_proj = Weight(output_weight, chips, rows, row_at, order, dep=query_proj.token)
    token = output_proj.token
    cache_own = jnp.stack([kv_cache[:, :, 0], kv_cache[:, :, 1]])
    cache_slots, token = ring_gather(cache_own, chips, dep=token)
    cache_block = jnp.stack(cache_slots)
    cache_all = jnp.stack([cache_block, swap_core(cache_block, seq)])

    live = [
        (query_pos < lengths[r]).astype(F32).reshape(seg_len, 1) for r in range(rows_here)
    ]
    grad_out = [cotangent[r].astype(F32) * live[r] for r in range(rows_here)]
    grad_group = [None] * rows_here
    grad_group[0], token = gather_tokens(grad_out[0].astype(BF16), chips, dep=token)

    inputs = [tokens[r].astype(F32) for r in range(rows_here)]
    inverse_one = [
        lax.rsqrt(jnp.mean(v * v, axis=-1, keepdims=True) + EPS) for v in inputs
    ]
    normed_one = [
        (v * i * gain_one).astype(BF16) for v, i in zip(inputs, inverse_one, strict=True)
    ]
    gate_up_weight = jnp.concatenate([ffn_in_weight[:, 0], ffn_in_weight[:, 1]], axis=0)
    normed_all = jnp.concatenate(normed_one, axis=0)
    query = index_order(query_proj.features(normed_all).astype(BF16), *order)

    def to_heads(value):
        value = value.reshape(seg_len, KV, GROUP, HEAD).transpose(1, 2, 0, 3)
        return value.reshape(KV, GROUP * seg_len, HEAD)

    def from_heads(value):
        value = value.reshape(KV, GROUP, seg_len, HEAD).transpose(2, 0, 1, 3)
        return value.reshape(seg_len, HEADS * HEAD)

    query_heads, keys, values, valid = [], [], [], []
    mixed_heads, lse, mixed_low, middle, inverse_two, normed_two = [], [], [], [], [], []
    for r in range(rows_here):
        query_heads.append(to_heads(query[r * seg_len : (r + 1) * seg_len]))
        keys.append(cache_all[:, :, 0, r].reshape(full_len, KV, HEAD))
        values.append(cache_all[:, :, 1, r].reshape(full_len, KV, HEAD))
        limit = jnp.minimum(query_pos, lengths[r] - 1)
        limit = jnp.broadcast_to(limit[None], (GROUP, seg_len)).reshape(GROUP * seg_len)
        valid.append((key_pos[None, :] <= limit[:, None])[None])
        scores = (
            jnp.einsum("kqd,rkd->kqr", query_heads[r], keys[r], preferred_element_type=F32)
            * scale
        )
        scores = jnp.where(valid[r], scores, NEG)
        best = jnp.max(scores, axis=-1)
        weights = jnp.exp(scores - best[..., None])
        total = jnp.sum(weights, axis=-1)
        accum = jnp.einsum(
            "kqr,rkd->kqd", weights.astype(BF16), values[r], preferred_element_type=F32
        )
        mixed_heads.append(accum / total[..., None])
        lse.append(best + jnp.log(total))
        mixed_low.append(own_order(from_heads(mixed_heads[r]).astype(BF16), *order))
        middle.append(inputs[r] + output_proj.back(mixed_low[r]))
        inverse_two.append(
            lax.rsqrt(jnp.mean(middle[r] * middle[r], axis=-1, keepdims=True) + EPS)
        )
        normed_two.append((middle[r] * inverse_two[r] * gain_two).astype(BF16))

    normed_group, hidden, grad_gate_up, ffn_part, grad_part = [], [], [], [], []
    for r in range(rows_here):
        group, token = gather_tokens(normed_two[r], chips, dep=token)
        normed_group.append(group)
        if r > 0:
            grad_group[r], token = gather_tokens(
                grad_out[r].astype(BF16), chips, dep=token
            )
    for r in range(rows_here):
        kept = dot(normed_group[r], gate_up_weight, ((1,), (1,)))
        gate, upper = kept[:, :units], kept[:, units:]
        sigma = jax.nn.sigmoid(gate)
        grad_hidden = dot(grad_group[r], down_weight, ((1,), (1,)))
        hidden.append((gate * sigma * upper).astype(BF16))
        grad_gate = grad_hidden * upper * sigma * (1.0 + gate * (1.0 - sigma))
        grad_up = grad_hidden * gate * sigma
        grad_gate_up.append(jnp.concatenate([grad_gate, grad_up], axis=1).astype(BF16))
        grad_part.append(dot(grad_gate_up[r], gate_up_weight, ((1,), (0,))).astype(BF16))
        ffn_part.append(dot(hidden[r], down_weight, ((1,), (0,))).astype(BF16))

    down_part = sum(
        dot(hidden[r], grad_group[r], ((0,), (0,))) for r in range(rows_here)
    ).astype(BF16)
    in_part = sum(
        dot(grad_gate_up[r], normed_group[r], ((0,), (0,))) for r in range(rows_here)
    ).astype(BF16)
    down_grad, in_grad = lax.psum((down_part, in_part), "rows")

    grad_middle, gain_two_terms, grad_branch = [], [], []
    query_terms, cache_terms = [], []
    for r in range(rows_here):
        grad_normed_two = scatter_tokens(grad_part[r], chips)
        scaled_two = middle[r] * inverse_two[r]
        gain_two_terms.append(jnp.sum(grad_normed_two * scaled_two, axis=0))
        grad_middle.append(
            grad_out[r] + norm_back(grad_normed_two, scaled_two, inverse_two[r], gain_two)
        )
        grad_branch.append(grad_middle[r].astype(BF16))
        grad_mixed = output_proj.features(grad_branch[r]).astype(BF16)
        grad_heads = to_heads(index_order(grad_mixed, *order))
        delta = jnp.sum(grad_heads.astype(F32) * mixed_heads[r], axis=-1)
        scores = (
            jnp.einsum("kqd,rkd->kqr", query_heads[r], keys[r], preferred_element_type=F32)
            * scale
        )
        probs = jnp.where(valid[r], jnp.exp(scores - lse[r][..., None]), 0.0)
        grad_probs = jnp.einsum(
            "kqd,rkd->kqr", grad_heads, values[r], preferred_element_type=F32
        )
        grad_scores = (probs * (grad_probs - delta[..., None])).astype(BF16)
        grad_query = (
            jnp.einsum("kqr,rkd->kqd", grad_scores, keys[r], preferred_element_type=F32)
            * scale
        )
        grad_keys = (
            jnp.einsum("kqr,kqd->rkd", grad_scores, query_heads[r], preferred_element_type=F32)
            * scale
        )
        grad_values = jnp.einsum(
            "kqr,kqd->rkd", probs.astype(BF16), grad_heads, preferred_element_type=F32
        )
        query_terms.append(own_order(from_heads(grad_query).astype(BF16), *order))
        cache_terms.append(
            jnp.stack([grad_keys, grad_values]).astype(BF16).reshape(2, 2, chips, seg_len, KV * HEAD)
        )

    layer_out = []
    for r in range(rows_here):
        ffn_out = scatter_tokens(ffn_part[r], chips)
        layer_out.append((live[r] * (middle[r] + ffn_out)).astype(BF16))

    branch_all = jnp.concatenate(grad_branch, axis=0)
    query_term = jnp.concatenate(query_terms, axis=0)
    output_part = dot(
        jnp.concatenate(mixed_low, axis=0), branch_all, ((0,), (0,))
    ).astype(BF16)
    output_grad = sum_rows(scatter_tokens(output_part, chips), rows)

    cache_part = jnp.stack(cache_terms, axis=3)
    cache_sum = cache_part[:, 0].astype(F32) + swap_core(cache_part[:, 1], seq).astype(F32)
    cache_sum = cache_sum.astype(BF16)
    cache_grad = ring_scatter([cache_sum[:, j] for j in range(chips)], chips)
    cache_grad = jnp.stack([cache_grad[0], cache_grad[1]], axis=2)

    query_part = dot(query_term, normed_all, ((0,), (0,))).astype(BF16)
    query_grad = sum_rows(scatter_tokens(query_part, chips), rows)
    grad_normed_one = query_proj.back(query_term)
    gain_one_terms, input_grad = [], []
    for r in range(rows_here):
        grad_r = grad_normed_one[r * seg_len : (r + 1) * seg_len]
        scaled_one = inputs[r] * inverse_one[r]
        gain_one_terms.append(jnp.sum(grad_r * scaled_one, axis=0))
        input_grad.append(
            grad_middle[r] + norm_back(grad_r, scaled_one, inverse_one[r], gain_one)
        )
    gain_grad = sum_all(jnp.stack([sum(gain_one_terms), sum(gain_two_terms)]), rows, seq)
    return (
        jnp.stack(layer_out),
        jnp.stack(input_grad),
        cache_grad,
        gain_grad,
        query_grad,
        output_grad,
        jnp.stack([in_grad[:units], in_grad[units:]], axis=1).astype(F32),
        down_grad.astype(F32),
    )


def solution(mesh):
    in_specs = (
        P("rows", "seq", None),
        P("rows", "seq", None, None),
        P("rows"),
        P(),
        P("seq", None),
        P("seq", None),
        P("seq", None, None),
        P("seq", None),
        P("rows", "seq", None),
    )
    out_specs = (
        P("rows", "seq", None),
        P("rows", "seq", None),
        P("rows", "seq", None, None),
        P(),
        P("seq", None),
        P("seq", None),
        P("seq", None, None),
        P("seq", None),
    )
    return jax.shard_map(local, mesh=mesh, in_specs=in_specs, out_specs=out_specs, check_vma=False)
```

time: 1250 us -> 1120 us (0.90)
  waiting for transfers between devices: 855 us -> 400 us
  local copies, waits for them, and re-layouts: 85.6 us -> 247 us
  other arithmetic: 55.7 us -> 136 us
  starting transfers between devices: 0.58 us -> 57.9 us
  matrix products: 189 us -> 244 us
  blocking collectives: 39.8 us -> 0 us
    ppermute x0 -> x79, waiting for transfers between devices: none -> 400 us  [the longest x42 359 us: ring(): return lax.ppermute(value, 'seq', pairs)]
    all_gather x5 -> x0, waiting for transfers between devices: 307 us -> none  [the longest x1 78.1 us: local(): normed_group = lax.all_gather(normed_two, 'seq', axis=0, tiled=True)]
    reduce_scatter x3 -> x0, waiting for transfers between devices: 275 us -> none  [the longest x1 115 us: local(): lax.psum_scatter(jnp.stack([query_grad_rows, output_grad_rows], axis=1).a...]
    psum x1, waiting for transfers between devices: 272 us -> 0.01 us  [local(): down_grad, in_grad = lax.psum((down_part, in_part), 'rows')]
    another operation x0 -> x23, local copies, waits for them, and re-layouts: none -> 61.2 us  [the longest x8 36 us: local(): jnp.stack([grad_keys, grad_values]).astype(BF16)]
    ppermute x0 -> x79, starting transfers between devices: none -> 57.9 us  [the longest x42 31.9 us: ring(): return lax.ppermute(value, 'seq', pairs)]
    dot_general x26 -> x50, matrix products: 189 us -> 244 us  [the longest x26 172 us: dot(): lax.dot_general(left, right, (dims, ((), ())), preferred_element_type=F32)]
    psum x1 -> x0, blocking collectives: 39.8 us -> none  [local(): lax.psum(jnp.stack([gain_one_grad, gain_two_grad]), ('rows', 'seq'))]
  transfers between devices with their start and end apart: 10 -> 80, of which waited for: 9 -> 40; matrix products, arithmetic and copies ran while one was open for 12% -> 51% of each run, Pallas kernels for 0% -> 0%
where the time goes in v1:
time: 1120 us; the launch traced here: 1100 us
  waiting for transfers between devices  400 us (36%)
  local copies, waits for them, and re-layouts  247 us (22%)
  matrix products  244 us (22%)
  other arithmetic  136 us (12%)
  starting transfers between devices  57.9 us (5%)
  between operations  18.1 us (2%)
    ppermute x42, waiting for transfers between devices, ring(): return lax.ppermute(value, 'seq', pairs)  359 us
    dot_general x26, matrix products, dot(): lax.dot_general(left, right, (dims, ((), ())), preferred_element_type=F32)  172 us
    unnamed x249, local copies, waits for them, and re-layouts  67.6 us
    ppermute x18, waiting for transfers between devices, swap_row(): return lax.ppermute(value, 'rows', [(r, r ^ mask) for r in range(rows)])  37.4 us
    another operation x8, local copies, waits for them, and re-layouts, local(): jnp.stack([grad_keys, grad_values]).astype(BF16)  36 us
    ppermute x42, starting transfers between devices, ring(): return lax.ppermute(value, 'seq', pairs)  31.9 us
  transfers between devices with their start and end apart: 80, of which 40 were waited for; matrix products, arithmetic and copies ran while one was open for 51% of the time, Pallas kernels for 0%

profile of v1, /device:TPU:0, one launch (start us, length us, event | category | flops | bytes accessed | tf_op | source)
XLA Modules:
  0.0 1103.8 jit_solution(2114747145134113091)
XLA Ops:
  67.7 13.7 %collective-permute-done.11 = bf16[2,2,128,512]{3,2,1,0:T(8,128)(2,1)S(1)} collective-permute-done((bf16[2,2,128,512]{3,2,1,0:T(8,128)(2,1)S(1)}, bf16[2,2,128,512]{3,2,1,0:T(8,128)(2,1)S(1)}, u32[]{:S(2)}, u32[]{:S(2)}) %collective-permute-start.11) | collective-permute-done | bytes 524320 | tf_op jit(solution)/shard_map/ppermute | solution.py:37
  118.3 11.2 %collective-permute-done.20 = bf16[2,3,128,512]{3,2,1,0:T(8,128)(2,1)} collective-permute-done((bf16[2,3,128,512]{3,2,1,0:T(8,128)(2,1)}, bf16[2,3,128,512]{3,2,1,0:T(8,128)(2,1)}, u32[]{:S(2)}, u32[]{:S(2)}) %collective-permute-start.20) | collective-permute-done | bytes 786464 | tf_op jit(solution)/shard_map/ppermute | solution.py:41
  197.4 10.8 fusion.2
  254.1 12.3 %collective-permute-done.24 = bf16[128,2048]{1,0:T(8,128)(2,1)} collective-permute-done((bf16[128,2048]{1,0:T(8,128)(2,1)S(1)}, bf16[128,2048]{1,0:T(8,128)(2,1)}, u32[]{:S(2)}, u32[]{:S(2)}) %collective-permute-start.24) | collective-permute-done | bytes 524320 | tf_op jit(solution)/shard_map/ppermute | solution.py:37
  266.4 16.8 %fusion.152 = (bf16[1024,1,2048]{2,1,0:T(2,128)(2,1)S(1)}, bf16[1024,1,2048]{2,1,0:T(2,128)(2,1)S(1)}) fusion(bf16[1024,2,2048]{2,1,0:T(2,128)(2,1)} %param.15), kind=kLoop, calls=%fused_computation.398 | loop fusion | bytes 16777216 | tf_op jit(solution)/shard_map/slice | solution.py:239
  307.2 11.2 %collective-permute-done.26 = bf16[128,2048]{1,0:T(8,128)(2,1)S(1)} collective-permute-done((bf16[128,2048]{1,0:T(8,128)(2,1)}, bf16[128,2048]{1,0:T(8,128)(2,1)S(1)}, u32[]{:S(2)}, u32[]{:S(2)}) %collective-permute-start.26) | collective-permute-done | bytes 524320 | tf_op jit(solution)/shard_map/ppermute | solution.py:37
  330.2 14.0 %collective-permute-done.34 = bf16[128,2048]{1,0:T(8,128)(2,1)S(1)} collective-permute-done((bf16[128,2048]{1,0:T(8,128)(2,1)S(1)}, bf16[128,2048]{1,0:T(8,128)(2,1)S(1)}, u32[]{:S(2)}, u32[]{:S(2)}) %collective-permute-start.34) | collective-permute-done | bytes 524320 | tf_op jit(solution)/shard_map/ppermute | solution.py:37
  367.0 13.4 %fusion.144 = f32[1024,2048]{1,0:T(8,128)} fusion(bf16[1024,2048]{1,0:T(8,128)(2,1)} %copy-done.84, bf16[1024,2048]{1,0:T(8,128)(2,1)S(1)} %bitcast.393, bf16[1024,2048]{1,0:T(8,128)(2,1)S(1)} %bitcast.397), kind=kOutput, calls=%fused_computation.394 | convolution fusion | flops 8606711808 | bytes 20971520 | tf_op jit(solution)/shard_map/dot_general | solution.py:17
  391.0 12.2 %convolution_convert_fusion.3 = bf16[1024,2048]{1,0:T(8,128)(2,1)S(1)} fusion(bf16[1024,1024]{1,0:T(8,128)(2,1)} %get-tuple-element.61, bf16[1024,1024]{1,0:T(8,128)(2,1)S(1)} %get-tuple-element.60, bf16[1024,2048]{1,0:T(8,128)(2,1)S(1)} %bitcast.394, bf16[1024,2048]{1,0:T(8,128)(2,1)S(1)} %bitcast.398), kind=kOutput, calls=%fused_computation.64 | convolution fusion | flops 8617197568 | bytes 16777216 | tf_op jit(solution)/shard_map/dot_general | solution.py:17
  421.8 12.7 %fusion.143 = f32[1024,2048]{1,0:T(8,128)} fusion(bf16[1024,2048]{1,0:T(8,128)(2,1)} %constant_dynamic-update-slice_fusion.5, bf16[1024,2048]{1,0:T(8,128)(2,1)S(1)} %bitcast.395, bf16[1024,2048]{1,0:T(8,128)(2,1)S(1)} %bitcast.399), kind=kOutput, calls=%fused_computation.393 | convolution fusion | flops 8606711808 | bytes 20971520 | tf_op jit(solution)/shard_map/dot_general | solution.py:17
  446.8 11.3 %multiply_convert_fusion.3 = (bf16[1024,1024]{1,0:T(8,128)(2,1)}, bf16[1024,1024]{1,0:T(8,128)(2,1)}, bf16[1024,1024]{1,0:T(8,128)(2,1)S(1)}) fusion(f32[1024,2048]{1,0:T(8,128)} %fusion.143, bf16[1024,2048]{1,0:T(8,128)(2,1)} %constant_dynamic-update-slice_fusion.15, bf16[1024,2048]{1,0:T(8,128)(2,1)S(1)} %copy-done.104), kind=kOutput, calls=%fused_computation.41 | convolution fusion | flops 4311744512 | bytes 23068672 | tf_op jit(solution)/shard_map/dot_general | solution.py:17
  458.1 10.8 convolution_convert_fusion.2
  468.9 17.0 %fusion.26 = f32[2048,2048]{1,0:T(8,128)} fusion(bf16[1024,2048]{1,0:T(8,128)(2,1)} %constant_dynamic-update-slice_fusion.5, bf16[1024,1024]{1,0:T(8,128)(2,1)} %get-tuple-element.63, bf16[1024,1024]{1,0:T(8,128)(2,1)} %get-tuple-element.62), kind=kOutput, calls=%fused_computation.73 | convolution fusion | flops 8598323200 | bytes 25165824 | tf_op jit(solution)/shard_map/dot_general | solution.py:17
  505.8 16.3 %add_convert_fusion = bf16[2048,2048]{1,0:T(8,128)(2,1)} fusion(f32[2048,2048]{1,0:T(8,128)} %fusion.26, bf16[1024,2048]{1,0:T(8,128)(2,1)S(1)} %copy-done.85, bf16[1024,1024]{1,0:T(8,128)(2,1)} %get-tuple-element.61, bf16[1024,1024]{1,0:T(8,128)(2,1)} %copy-done.107), kind=kOutput, calls=%fused_computation | convolution fusion | flops 8606711808 | bytes 33554432 | tf_op jit(solution)/shard_map/dot_general | solution.py:17
  522.0 11.8 %add_convert_fusion.1 = bf16[1024,2048]{1,0:T(8,128)(2,1)} fusion(f32[1024,2048]{1,0:T(8,128)} %fusion.163, bf16[1024,1024]{1,0:T(8,128)(2,1)} %copy-done.106, bf16[1024,2048]{1,0:T(8,128)(2,1)} %constant_dynamic-update-slice_fusion.10), kind=kOutput, calls=%fused_computation.3 | convolution fusion | flops 4299161600 | bytes 18874368 | tf_op jit(solution)/shard_map/dot_general | solution.py:17
  546.6 26.5 %collective-permute-done.51 = bf16[128,2048]{1,0:T(8,128)(2,1)S(1)} collective-permute-done((bf16[128,2048]{1,0:T(8,128)(2,1)S(1)}, bf16[128,2048]{1,0:T(8,128)(2,1)S(1)}, u32[]{:S(2)}, u32[]{:S(2)}) %collective-permute-start.51) | collective-permute-done | bytes 524320 | tf_op jit(solution)/shard_map/ppermute | solution.py:37
  599.1 19.0 %collective-permute-done.38 = bf16[128,2048]{1,0:T(8,128)(2,1)S(1)} collective-permute-done((bf16[128,2048]{1,0:T(8,128)(2,1)S(1)}, bf16[128,2048]{1,0:T(8,128)(2,1)S(1)}, u32[]{:S(2)}, u32[]{:S(2)}) %collective-permute-start.38) | collective-permute-done | bytes 524320 | tf_op jit(solution)/shard_map/ppermute | solution.py:37
  856.2 15.6 %collective-permute-done.64 = bf16[256,2048]{1,0:T(8,128)(2,1)S(1)} collective-permute-done((bf16[256,2048]{1,0:T(8,128)(2,1)}, bf16[256,2048]{1,0:T(8,128)(2,1)S(1)}, u32[]{:S(2)}, u32[]{:S(2)}) %collective-permute-start.64) | collective-permute-done | bytes 1048608 | tf_op jit(solution)/shard_map/ppermute | solution.py:37
  872.3 33.2 %collective-permute-done.55 = bf16[2,2,128,512]{3,0,2,1:T(2,128)(2,1)S(1)} collective-permute-done((bf16[2,2,128,512]{3,0,2,1:T(2,128)(2,1)S(1)}, bf16[2,2,128,512]{3,0,2,1:T(2,128)(2,1)S(1)}, u32[]{:S(2)}, u32[]{:S(2)}) %collective-permute-start.55) | collective-permute-done | bytes 524320 | tf_op jit(solution)/shard_map/ppermute | solution.py:37
  907.3 31.9 %collective-permute-done.56 = bf16[2,2,128,512]{3,0,2,1:T(2,128)(2,1)S(1)} collective-permute-done((bf16[2,2,128,512]{3,0,2,1:T(2,128)(2,1)S(1)}, bf16[2,2,128,512]{3,0,2,1:T(2,128)(2,1)S(1)}, u32[]{:S(2)}, u32[]{:S(2)}) %collective-permute-start.56) | collective-permute-done | bytes 524320 | tf_op jit(solution)/shard_map/ppermute | solution.py:37
  941.0 31.9 %collective-permute-done.57 = bf16[2,2,128,512]{3,0,2,1:T(2,128)(2,1)S(1)} collective-permute-done((bf16[2,2,128,512]{3,0,2,1:T(2,128)(2,1)S(1)}, bf16[2,2,128,512]{3,0,2,1:T(2,128)(2,1)S(1)}, u32[]{:S(2)}, u32[]{:S(2)}) %collective-permute-start.57) | collective-permute-done | bytes 524320 | tf_op jit(solution)/shard_map/ppermute | solution.py:37
  975.0 20.4 %collective-permute-done.66 = bf16[256,2048]{1,0:T(8,128)(2,1)S(1)} collective-permute-done((bf16[256,2048]{1,0:T(8,128)(2,1)S(1)}, bf16[256,2048]{1,0:T(8,128)(2,1)S(1)}, u32[]{:S(2)}, u32[]{:S(2)}) %collective-permute-start.66) | collective-permute-done | bytes 1048608 | tf_op jit(solution)/shard_map/ppermute | solution.py:37
  998.1 15.6 %collective-permute-done.74 = bf16[256,2048]{1,0:T(8,128)(2,1)S(1)} collective-permute-done((bf16[256,2048]{1,0:T(8,128)(2,1)S(1)}, bf16[256,2048]{1,0:T(8,128)(2,1)S(1)}, u32[]{:S(2)}, u32[]{:S(2)}) %collective-permute-start.74) | collective-permute-done | bytes 1048608 | tf_op jit(solution)/shard_map/ppermute | solution.py:37
  1063.3 28.7 %copy.115 = f32[1024,2,2048]{2,1,0:T(2,128)} copy(f32[1024,2,2048]{2,0,1:T(8,128)} %maximum_convert_fusion) | data formatting | bytes 33554432
  (657 shorter events, 667.2 us)
Async XLA Ops:
  7.2 1041.8 %all-reduce.3.cloned.1.call-start = ((), (), s32[]{:S(2)}) async-start(), calls=%async_computation | async-start | bytes 25165824 | tf_op jit(solution)/shard_map/psum | solution.py:306
  7.2 104.8 %collective-permute-start.7 = (bf16[256,2048]{1,0:T(8,128)(2,1)}, bf16[256,2048]{1,0:T(8,128)(2,1)}, u32[]{:S(2)}, u32[]{:S(2)}) collective-permute-start(bf16[256,2048]{1,0:T(8,128)(2,1)} %param.13), channel_id=1, source_target_pairs={{0,1},{1,0},{2,3},{3,2},{4,5},{5,4},{6,7},{7,6},{8,9},{9,8},{10,11... | collective-permute-start | bytes 3145736 | tf_op jit(solution)/shard_map/ppermute | solution.py:32
  86.3 72.0 %collective-permute-start.8 = (bf16[4,768,512]{2,1,0:T(8,128)(2,1)}, bf16[4,768,512]{2,1,0:T(8,128)(2,1)}, u32[]{:S(2)}, u32[]{:S(2)}) collective-permute-start(bf16[4,768,512]{2,1,0:T(8,128)(2,1)} %bitcast.22), channel_id=1, source_target_pairs={{0,1},{1,0},{2,3},{3,2},{4,5},{5,4},{6,7},{7,6},{8,9},{9,8},{10,11... | collective-permute-start | bytes 9437192 | tf_op jit(solution)/shard_map/ppermute | solution.py:32
  107.1 38.9 %collective-permute-start.14 = (bf16[4,2,2,128,512]{4,3,2,1,0:T(8,128)(2,1)}, bf16[4,2,2,128,512]{4,3,2,1,0:T(8,128)(2,1)}, u32[]{:S(2)}, u32[]{:S(2)}) collective-permute-start(bf16[4,2,2,128,512]{4,3,2,1,0:T(8,128)(2,1)} %get-tuple-element.76), channel_id=1, source_target_pairs={{0,1},{1,0},{2,3},{3,2},{4,5},{5,4},{6,7},{7,6},{8,9},{9,8},{10,11... | collective-permute-start | bytes 6291464 | tf_op jit(solution)/shard_map/ppermute | solution.py:32
  129.5 105.8 %collective-permute-start.15 = (bf16[256,2048]{1,0:T(8,128)(2,1)}, bf16[256,2048]{1,0:T(8,128)(2,1)}, u32[]{:S(2)}, u32[]{:S(2)}) collective-permute-start(bf16[256,2048]{1,0:T(8,128)(2,1)} %param.14), channel_id=1, source_target_pairs={{0,1},{1,0},{2,3},{3,2},{4,5},{5,4},{6,7},{7,6},{8,9},{9,8},{10,11... | collective-permute-start | bytes 3145736 | tf_op jit(solution)/shard_map/ppermute | solution.py:32
  144.0 82.0 %collective-permute-start.21 = (bf16[4,768,512]{1,2,0:T(8,128)(2,1)S(1)}, bf16[4,768,512]{1,2,0:T(8,128)(2,1)}, u32[]{:S(2)}, u32[]{:S(2)}) collective-permute-start(bf16[4,768,512]{1,2,0:T(8,128)(2,1)S(1)} %reshape.492), channel_id=1, source_target_pairs={{0,1},{1,0},{2,3},{3,2},{4,5},{5,4},{6,7},{7,6},{8,9},{9,8},{10,11... | collective-permute-start | bytes 9437192 | tf_op jit(solution)/shard_map/ppermute | solution.py:32
  145.9 105.1 %collective-permute-start.40 = (bf16[128,2048]{1,0:T(8,128)(2,1)}, bf16[128,2048]{1,0:T(8,128)(2,1)}, u32[]{:S(2)}, u32[]{:S(2)}) collective-permute-start(bf16[128,2048]{1,0:T(8,128)(2,1)} %collective-permute-done.23), channel_id=1, source_target_pairs={{0,2},{1,3},{2,4},{3,5},{4,6},{5,7},{6,0},{7,1},{8,10},{9,11},{10,... | collective-permute-start | bytes 1572872 | tf_op jit(solution)/shard_map/ppermute | solution.py:37
  254.1 66.4 %collective-permute-start.41 = (bf16[512,2048]{1,0:T(8,128)(2,1)}, bf16[512,2048]{1,0:T(8,128)(2,1)}, u32[]{:S(2)}, u32[]{:S(2)}) collective-permute-start(bf16[512,2048]{1,0:T(8,128)(2,1)} %pad_maximum_fusion.12), channel_id=1, source_target_pairs={{0,1},{1,0},{2,3},{3,2},{4,5},{5,4},{6,7},{7,6},{8,9},{9,8},{10,11... | collective-permute-start | bytes 6291464 | tf_op jit(solution)/shard_map/ppermute | solution.py:32
  319.8 45.1 %collective-permute-start.27 = (bf16[512,2048]{1,0:T(8,128)(2,1)S(1)}, bf16[512,2048]{1,0:T(8,128)(2,1)S(1)}, u32[]{:S(2)}, u32[]{:S(2)}) collective-permute-start(bf16[512,2048]{1,0:T(8,128)(2,1)S(1)} %pad_maximum_fusion.10), channel_id=1, source_target_pairs={{0,1},{1,0},{2,3},{3,2},{4,5},{5,4},{6,7},{7,6},{8,9},{9,8},{10,11... | collective-permute-start | bytes 6291464 | tf_op jit(solution)/shard_map/ppermute | solution.py:32
  345.6 73.0 %collective-permute-start.35 = (bf16[512,2048]{1,0:T(8,128)(2,1)}, bf16[512,2048]{1,0:T(8,128)(2,1)}, u32[]{:S(2)}, u32[]{:S(2)}) collective-permute-start(bf16[512,2048]{1,0:T(8,128)(2,1)} %pad_maximum_fusion.11), channel_id=1, source_target_pairs={{0,1},{1,0},{2,3},{3,2},{4,5},{5,4},{6,7},{7,6},{8,9},{9,8},{10,11... | collective-permute-start | bytes 6291464 | tf_op jit(solution)/shard_map/ppermute | solution.py:32
  364.9 49.2 %collective-permute-start.48 = (bf16[128,2048]{1,0:T(8,128)(2,1)S(1)}, bf16[128,2048]{1,0:T(8,128)(2,1)S(1)}, u32[]{:S(2)}, u32[]{:S(2)}) collective-permute-start(bf16[128,2048]{1,0:T(8,128)(2,1)S(1)} %collective-permute-done.47), channel_id=1, source_target_pairs={{0,2},{1,3},{2,4},{3,5},{4,6},{5,7},{6,0},{7,1},{8,10},{9,11},{10,... | collective-permute-start | bytes 1572872 | tf_op jit(solution)/shard_map/ppermute | solution.py:37
  438.4 95.5 %collective-permute-start.43 = (bf16[128,2048]{1,0:T(8,128)(2,1)}, bf16[128,2048]{1,0:T(8,128)(2,1)S(1)}, u32[]{:S(2)}, u32[]{:S(2)}) collective-permute-start(bf16[128,2048]{1,0:T(8,128)(2,1)} %slice.490), channel_id=1, source_target_pairs={{0,2},{1,3},{2,4},{3,5},{4,6},{5,7},{6,0},{7,1},{8,10},{9,11},{10,... | collective-permute-start | bytes 1572872 | tf_op jit(solution)/shard_map/ppermute | solution.py:37
  442.9 95.4 %collective-permute-start.29 = (bf16[128,2048]{1,0:T(8,128)(2,1)}, bf16[128,2048]{1,0:T(8,128)(2,1)S(1)}, u32[]{:S(2)}, u32[]{:S(2)}) collective-permute-start(bf16[128,2048]{1,0:T(8,128)(2,1)} %slice.469), channel_id=1, source_target_pairs={{0,2},{1,3},{2,4},{3,5},{4,6},{5,7},{6,0},{7,1},{8,10},{9,11},{10,... | collective-permute-start | bytes 1572872 | tf_op jit(solution)/shard_map/ppermute | solution.py:37
  504.3 39.9 %collective-permute-start.36 = (bf16[512,2048]{1,0:T(8,128)(2,1)}, bf16[512,2048]{1,0:T(8,128)(2,1)}, u32[]{:S(2)}, u32[]{:S(2)}) collective-permute-start(bf16[512,2048]{1,0:T(8,128)(2,1)} %slice.483), channel_id=1, source_target_pairs={{0,1},{1,0},{2,3},{3,2},{4,5},{5,4},{6,7},{7,6},{8,9},{9,8},{10,11... | collective-permute-start | bytes 6291464 | tf_op jit(solution)/shard_map/ppermute | solution.py:32
  534.0 41.9 %collective-permute-start.44 = (bf16[128,2048]{1,0:T(8,128)(2,1)S(1)}, bf16[128,2048]{1,0:T(8,128)(2,1)S(1)}, u32[]{:S(2)}, u32[]{:S(2)}) collective-permute-start(bf16[128,2048]{1,0:T(8,128)(2,1)S(1)} %add_convert_fusion.21), channel_id=1, source_target_pairs={{0,2},{1,3},{2,4},{3,5},{4,6},{5,7},{6,0},{7,1},{8,10},{9,11},{10,... | collective-permute-start | bytes 1572872 | tf_op jit(solution)/shard_map/ppermute | solution.py:37
  539.5 58.8 %collective-permute-start.30 = (bf16[128,2048]{1,0:T(8,128)(2,1)S(1)}, bf16[128,2048]{1,0:T(8,128)(2,1)S(1)}, u32[]{:S(2)}, u32[]{:S(2)}) collective-permute-start(bf16[128,2048]{1,0:T(8,128)(2,1)S(1)} %add_convert_fusion.25), channel_id=1, source_target_pairs={{0,2},{1,3},{2,4},{3,5},{4,6},{5,7},{6,0},{7,1},{8,10},{9,11},{10,... | collective-permute-start | bytes 1572872 | tf_op jit(solution)/shard_map/ppermute | solution.py:37
  576.0 44.9 %collective-permute-start.45 = (bf16[128,2048]{1,0:T(8,128)(2,1)S(1)}, bf16[128,2048]{1,0:T(8,128)(2,1)S(1)}, u32[]{:S(2)}, u32[]{:S(2)}) collective-permute-start(bf16[128,2048]{1,0:T(8,128)(2,1)S(1)} %add_convert_fusion.20), channel_id=1, source_target_pairs={{0,2},{1,3},{2,4},{3,5},{4,6},{5,7},{6,0},{7,1},{8,10},{9,11},{10,... | collective-permute-start | bytes 1572872 | tf_op jit(solution)/shard_map/ppermute | solution.py:37
  598.5 42.1 %collective-permute-start.31 = (bf16[128,2048]{1,0:T(8,128)(2,1)S(1)}, bf16[128,2048]{1,0:T(8,128)(2,1)S(1)}, u32[]{:S(2)}, u32[]{:S(2)}) collective-permute-start(bf16[128,2048]{1,0:T(8,128)(2,1)S(1)} %add_convert_fusion.24), channel_id=1, source_target_pairs={{0,2},{1,3},{2,4},{3,5},{4,6},{5,7},{6,0},{7,1},{8,10},{9,11},{10,... | collective-permute-start | bytes 1572872 | tf_op jit(solution)/shard_map/ppermute | solution.py:37
  849.2 57.0 %collective-permute-start.72 = (bf16[256,2048]{1,0:T(8,128)(2,1)S(1)}, bf16[256,2048]{1,0:T(8,128)(2,1)S(1)}, u32[]{:S(2)}, u32[]{:S(2)}) collective-permute-start(bf16[256,2048]{1,0:T(8,128)(2,1)S(1)} %slice.524), channel_id=1, source_target_pairs={{0,2},{1,3},{2,4},{3,5},{4,6},{5,7},{6,0},{7,1},{8,10},{9,11},{10,... | collective-permute-start | bytes 3145736 | tf_op jit(solution)/shard_map/ppermute | solution.py:37
  854.9 50.6 %collective-permute-start.55 = (bf16[2,2,128,512]{3,0,2,1:T(2,128)(2,1)S(1)}, bf16[2,2,128,512]{3,0,2,1:T(2,128)(2,1)S(1)}, u32[]{:S(2)}, u32[]{:S(2)}) collective-permute-start(bf16[2,2,128,512]{3,0,2,1:T(2,128)(2,1)S(1)} %slice_bitcast_fusion.9), channel_id=1, source_target_pairs={{0,2},{1,3},{2,4},{3,5},{4,6},{5,7},{6,0},{7,1},{8,10},{9,11},{10,... | collective-permute-start | bytes 1572872 | tf_op jit(solution)/shard_map/ppermute | solution.py:37
  872.2 67.6 %collective-permute-start.65 = (bf16[256,2048]{1,0:T(8,128)(2,1)S(1)}, bf16[256,2048]{1,0:T(8,128)(2,1)S(1)}, u32[]{:S(2)}, u32[]{:S(2)}) collective-permute-start(bf16[256,2048]{1,0:T(8,128)(2,1)S(1)} %add_convert_fusion.13), channel_id=1, source_target_pairs={{0,2},{1,3},{2,4},{3,5},{4,6},{5,7},{6,0},{7,1},{8,10},{9,11},{10,... | collective-permute-start | bytes 3145736 | tf_op jit(solution)/shard_map/ppermute | solution.py:37
  906.5 66.9 %collective-permute-start.73 = (bf16[256,2048]{1,0:T(8,128)(2,1)S(1)}, bf16[256,2048]{1,0:T(8,128)(2,1)S(1)}, u32[]{:S(2)}, u32[]{:S(2)}) collective-permute-start(bf16[256,2048]{1,0:T(8,128)(2,1)S(1)} %add_convert_fusion.10), channel_id=1, source_target_pairs={{0,2},{1,3},{2,4},{3,5},{4,6},{5,7},{6,0},{7,1},{8,10},{9,11},{10,... | collective-permute-start | bytes 3145736 | tf_op jit(solution)/shard_map/ppermute | solution.py:37
  940.3 55.2 %collective-permute-start.66 = (bf16[256,2048]{1,0:T(8,128)(2,1)S(1)}, bf16[256,2048]{1,0:T(8,128)(2,1)S(1)}, u32[]{:S(2)}, u32[]{:S(2)}) collective-permute-start(bf16[256,2048]{1,0:T(8,128)(2,1)S(1)} %add_convert_fusion.12), channel_id=1, source_target_pairs={{0,2},{1,3},{2,4},{3,5},{4,6},{5,7},{6,0},{7,1},{8,10},{9,11},{10,... | collective-permute-start | bytes 3145736 | tf_op jit(solution)/shard_map/ppermute | solution.py:37
  973.9 39.8 %collective-permute-start.74 = (bf16[256,2048]{1,0:T(8,128)(2,1)S(1)}, bf16[256,2048]{1,0:T(8,128)(2,1)S(1)}, u32[]{:S(2)}, u32[]{:S(2)}) collective-permute-start(bf16[256,2048]{1,0:T(8,128)(2,1)S(1)} %add_convert_fusion.9), channel_id=1, source_target_pairs={{0,2},{1,3},{2,4},{3,5},{4,6},{5,7},{6,0},{7,1},{8,10},{9,11},{10,... | collective-permute-start | bytes 3145736 | tf_op jit(solution)/shard_map/ppermute | solution.py:37
  (170 other events, 3052.0 us)
Sparse Core Ops, SparseCore 0:
  534.0 241.2 all-reduce.2

commit v2 on v0

--- a/solution.py
+++ b/solution.py
@@ -1,6 +1,8 @@
 import jax
 import jax.numpy as jnp
 from jax import lax
+from jax.experimental import pallas as pl
+from jax.experimental.pallas import tpu as pltpu
 from jax.sharding import PartitionSpec as P
 
 HEADS = 16
@@ -31,6 +33,56 @@
     grad_gate = grad_hidden * upper * sigma * (1.0 + gate * (1.0 - sigma))
     grad_up = grad_hidden * gate * sigma
     return jnp.stack([grad_gate, grad_up], axis=1).astype(jnp.bfloat16)
+
+
+def widen_pairs(part):
+    units, width = part.shape[0] // 2, part.shape[1]
+    block = min(units, 128)
+
+    def kernel(gate_ref, up_ref, out_ref):
+        out_ref[:, 0] = gate_ref[...].astype(jnp.float32)
+        out_ref[:, 1] = up_ref[...].astype(jnp.float32)
+
+    steps = units // block
+    return pl.pallas_call(
+        kernel,
+        out_shape=jax.ShapeDtypeStruct((units, 2, width), jnp.float32),
+        grid=(steps,),
+        in_specs=[
+            pl.BlockSpec((block, width), lambda i: (i, 0)),
+            pl.BlockSpec((block, width), lambda i: (i + steps, 0)),
+        ],
+        out_specs=pl.BlockSpec((block, 2, width), lambda i: (i, 0, 0)),
+        compiler_params=pltpu.CompilerParams(vmem_limit_bytes=32 * 2**20),
+        cost_estimate=pl.CostEstimate(
+            flops=0, bytes_accessed=12 * units * width, transcendentals=0
+        ),
+    )(part, part)
+
+
+def sum_rows(value, rows):
+    if rows != 4:
+        return lax.psum(value.astype(BF16), "rows").astype(jnp.float32)
+    half = value.shape[0] // 2
+    first, second = value[:half].astype(BF16), value[half:].astype(BF16)
+
+    def pair(item, mask):
+        return item.astype(jnp.float32) + swap_row(item, rows, mask).astype(jnp.float32)
+
+    first, second = pair(first, 1).astype(BF16), pair(second, 2).astype(BF16)
+    return jnp.concatenate([pair(first, 2), pair(second, 1)], axis=0)
+
+
+def sum_all(value, rows, seq):
+    mask = 1
+    while mask < seq:
+        value = value + lax.ppermute(value, "seq", [(s, s ^ mask) for s in range(seq)])
+        mask *= 2
+    mask = 1
+    while mask < rows:
+        value = value + swap_row(value, rows, mask)
+        mask *= 2
+    return value
 
 
 def local(
@@ -211,7 +263,7 @@
     query_grad, output_grad, ffn_in_grad, down_grad = (
         lax.psum(attn_grad[:, 0].astype(jnp.bfloat16), "rows").astype(jnp.float32),
         lax.psum(attn_grad[:, 1].astype(jnp.bfloat16), "rows").astype(jnp.float32),
-        lax.psum(in_grad.astype(jnp.bfloat16), "rows").astype(jnp.float32),
+        widen_pairs(lax.psum(in_grad.astype(jnp.bfloat16).transpose(1, 0, 2).reshape(-1, width), "rows")),
         lax.psum(down_part.astype(jnp.bfloat16), "rows").astype(jnp.float32),
     )
     return (

time: 1250 us -> 1230 us (0.984)
  local copies, waits for them, and re-layouts: 85.6 us -> 66.7 us
    unnamed x53 -> x56, local copies, waits for them, and re-layouts: 42 us -> 23.1 us
  transfers between devices with their start and end apart: 10 -> 10, of which waited for: 9 -> 9; matrix products, arithmetic and copies ran while one was open for 12% -> 13% of each run, Pallas kernels for 0% -> 0%
where the time goes in v2:
time: 1230 us
  waiting for transfers between devices  855 us (70%)
  matrix products  188 us (15%)
  local copies, waits for them, and re-layouts  66.7 us (5%)
  other arithmetic  53.5 us (4%)
  blocking collectives  39.9 us (3%)
  between operations  14.6 us (1%)
    psum x1, waiting for transfers between devices, local(): lax.psum(attn_grad[:, 0].astype(jnp.bfloat16), 'rows').astype(jnp.float32)  271 us
    reduce_scatter x1, waiting for transfers between devices, local(): lax.psum_scatter(jnp.stack([query_grad_rows, output_grad_rows], axis=1).a...  116 us
    reduce_scatter x1, waiting for transfers between devices, local(): lax.psum_scatter(jnp.dot(hidden_group, down_weight, preferred_element_typ...  88.2 us
    all_gather x1, waiting for transfers between devices, local(): normed_group = lax.all_gather(normed_two, 'seq', axis=0, tiled=True)  78.1 us
    all_gather x1, waiting for transfers between devices, local(): lax.all_gather(query_weight, 'seq', axis=0, tiled=True)  77.7 us
    reduce_scatter x1, waiting for transfers between devices, local(): lax.psum_scatter(jnp.einsum('tkn,nkd->td', grad_gate_up, ffn_in_weight, p...  71.6 us
    all_gather x1, waiting for transfers between devices, local(): grad_group = lax.all_gather(grad_low, 'seq', axis=0, tiled=True)  57.6 us
    all_gather x1, waiting for transfers between devices, local(): piece = lax.all_gather(kv_cache, 'seq', axis=1, tiled=True)  46.9 us
  transfers between devices with their start and end apart: 10, of which 9 were waited for; matrix products, arithmetic and copies ran while one was open for 13% of the time, Pallas kernels for 0%

profile of v2, /device:TPU:0, one launch (start us, length us, event | category | flops | bytes accessed | tf_op | source)
XLA Modules:
  0.0 1227.2 jit_solution(156758834397526337)
XLA Ops:
  13.9 46.9 %all-gather.8.cloned.1.call-done = bf16[2,1024,2,512]{1,3,0,2:T(8,128)(2,1)} async-done(((bf16[2,128,2,512]{1,3,0,2:T(8,128)(2,1)}), bf16[2,1024,2,512]{1,3,0,2:T(8,128)(2,1)}) %all-gather.8.cloned.1.call-update) | async-done | bytes 4194320 | tf_op jit(solution)/shard_map/all_gather | solution.py:126
  64.9 77.7 %all-gather.6.cloned.1.call-done = bf16[2048,2048]{1,0:T(8,128)(2,1)} async-done(((bf16[256,2048]{1,0:T(8,128)(2,1)}), bf16[2048,2048]{1,0:T(8,128)(2,1)}) %all-gather.6.cloned.1.call-update) | async-done | bytes 8388624 | tf_op jit(solution)/shard_map/all_gather | solution.py:117
  142.6 7.1 convolution_convert_fusion.3
  155.1 18.7 %while.30 = (s32[]{:T(128)}, f32[2,4,512]{2,1,0:T(4,128)S(1)}, f32[2,4,512]{2,1,0:T(4,128)S(1)}, f32[2,4,512,128]{3,2,1,0:T(8,128)}, s32[2,512]{1,0:T(2,128)S(1)...) while((s32[]{:T(128)}, f32[2,4,512]{2,1,0:T(4,128)S(1)}, ...), condition=%wide.region_4.5_spmd.clone.clone, body=%wide.region_1.4_spmd.clone.sunk.clone | while | flops 1097607168 | bytes 56205496 | solution.py:151
  178.3 46.6 %all-gather.10.cloned.1.call-done = bf16[2048,2048]{1,0:T(8,128)(2,1)} async-done(((bf16[256,2048]{1,0:T(8,128)(2,1)}), bf16[2048,2048]{1,0:T(8,128)(2,1)}) %all-gather.10.cloned.1.call-update) | async-done | bytes 8388624 | tf_op jit(solution)/shard_map/all_gather | solution.py:118
  235.0 78.1 %all-gather.12.cloned.1.call-done = bf16[2048,2048]{1,0:T(8,128)(2,1)} async-done(((bf16[256,2048]{1,0:T(8,128)(2,1)}), bf16[2048,2048]{1,0:T(8,128)(2,1)}) %all-gather.12.cloned.1.call-update) | async-done | bytes 8388624 | tf_op jit(solution)/shard_map/all_gather | solution.py:163
  313.1 25.0 %fusion.63 = f32[2048,2,1024]{2,0,1:T(8,128)} fusion(bf16[1024,2,2048]{2,1,0:T(2,128)(2,1)} %param.19, bf16[2048,2048]{1,0:T(8,128)(2,1)} %all-gather.12.cloned.1.call-done), kind=kOutput, calls=%fused_computation.85 | convolution fusion | flops 17179869184 | bytes 33554432 | tf_op jit(solution)/shard_map/td,nkd->tkn/dot_general | solution.py:164
  338.1 57.6 %all-gather.14.cloned.1.call-done = bf16[2048,2048]{1,0:T(8,128)(2,1)} async-done(((bf16[256,2048]{1,0:T(8,128)(2,1)}), bf16[2048,2048]{1,0:T(8,128)(2,1)}) %all-gather.14.cloned.1.call-update) | async-done | bytes 8388624 | tf_op jit(solution)/shard_map/all_gather | solution.py:174
  395.7 23.0 %fusion.72 = (bf16[2048,1,1024]{2,0,1:T(8,128)(2,1)}, bf16[2048,1,1024]{2,0,1:T(8,128)(2,1)}, bf16[2048,1024]{1,0:T(8,128)(2,1)}) fusion(f32[2048,2,1024]{2,0,1:T(8,128)} %fusion.63, bf16[2048,2048]{1,0:T(8,128)(2,1)} %all-gather.14.cloned.1.call-done, bf16[1024,2048]{1,0:T(8,128)(2,1)} %param.20), kind=kOutput, calls=%fused_computation.89 | convolution fusion | flops 8623489024 | bytes 41943040 | tf_op jit(solution)/shard_map/dot_general | solution.py:19
  418.7 24.7 %bitcast_convert_fusion = bf16[2048,2048]{1,0:T(8,128)(2,1)} fusion(bf16[1024,2,2048]{2,1,0:T(2,128)(2,1)} %param.19, bf16[2048,1,1024]{2,0,1:T(8,128)(2,1)} %get-tuple-element.248, bf16[2048,1,1024]{2,0,1:T(8,128)(2,1)} %get-tuple-element.247), kind=kOutput, calls=%fused_computation.68 | convolution fusion | flops 17188257792 | bytes 25165824 | tf_op jit(solution)/shard_map/tkn,nkd->td/dot_general | solution.py:177
  443.5 13.9 %convolution_convert_fusion = bf16[2048,2048]{1,0:T(8,128)(2,1)} fusion(bf16[2048,1024]{1,0:T(8,128)(2,1)} %get-tuple-element.249, bf16[1024,2048]{1,0:T(8,128)(2,1)} %param.20), kind=kOutput, calls=%fused_computation.82 | convolution fusion | flops 8594128896 | bytes 16777216 | tf_op jit(solution)/shard_map/dot_general | solution.py:169
  460.1 71.6 %reduce-scatter.10.cloned.1.call-done = bf16[256,2048]{1,0:T(8,128)(2,1)} async-done(((bf16[2048,2048]{1,0:T(8,128)(2,1)}), bf16[256,2048]{1,0:T(8,128)(2,1)}) %reduce-scatter.10.cloned.1.call-update) | async-done | bytes 1048592 | tf_op jit(solution)/shard_map/reduce_scatter | solution.py:176
  534.4 88.2 %reduce-scatter.8.cloned.1.call-done = bf16[256,2048]{1,0:T(8,128)(2,1)} async-done(((bf16[2048,2048]{1,0:T(8,128)(2,1)}), bf16[256,2048]{1,0:T(8,128)(2,1)}) %reduce-scatter.8.cloned.1.call-update) | async-done | bytes 1048592 | tf_op jit(solution)/shard_map/reduce_scatter | solution.py:168
  639.3 46.5 %while.31 = (s32[]{:T(128)}, bf16[2,4,512,128]{3,2,1,0:T(8,128)(2,1)}, bf16[2,1024,2,512]{3,2,1,0:T(2,128)(2,1)}, s32[2,512]{1,0:T(2,128)S(1)}, bf16[2,4,512,128...) while((s32[]{:T(128)}, ...), condition=%wide.region_11.12_spmd.clone.clone, body=%wide.region_10.11_spmd.clone.sunk.clone | while | flops 2708209664 | bytes 77134016 | solution.py:236
  691.6 10.5 pad_maximum_fusion
  702.2 7.1 copy.93
  709.3 7.9 reshape.287
  717.3 14.3 %convolution_convert_fusion.1 = bf16[1024,2048]{1,0:T(8,128)(2,1)} fusion(bf16[2048,1024]{1,0:T(8,128)(2,1)} %get-tuple-element.249, bf16[2048,2048]{1,0:T(8,128)(2,1)} %all-gather.14.cloned.1.call-done), kind=kOutput, calls=%fused_computation.90 | convolution fusion | flops 8592031744 | bytes 16777216 | tf_op jit(solution)/shard_map/tn,td->nd/dot_general | solution.py:187
  731.5 21.7 %fusion.68 = bf16[2,1024,2048]{2,1,0:T(8,128)(2,1)} fusion(bf16[2048,2048]{1,0:T(8,128)(2,1)} %all-gather.12.cloned.1.call-done, bf16[2048,1,1024]{2,0,1:T(8,128)(2,1)S(1)} %copy-done.27, bf16[2048,1,1024]{2,0,1:T(8,128)(2,1)S(1)} %copy-done.26), kind=kOutput, calls=%fused_computation.86 | convolution fusion | flops 17188257792 | bytes 25165824 | tf_op jit(solution)/shard_map/tkn,td->nkd/dot_general | solution.py:184
  753.2 115.7 %reduce-scatter.12.cloned.1.call-done = bf16[256,2,2048]{2,0,1:T(8,128)(2,1)} async-done(((bf16[2048,2,2048]{2,0,1:T(8,128)(2,1)}), bf16[256,2,2048]{2,0,1:T(8,128)(2,1)}) %reduce-scatter.12.cloned.1.call-update) | async-done | bytes 2097168 | tf_op jit(solution)/shard_map/reduce_scatter | solution.py:253
  873.3 8.1 multiply_reduce_fusion
  881.4 39.9 %psum.35 = f32[2,2048]{1,0:T(2,128)} all-reduce(f32[2,2048]{1,0:T(2,128)S(1)} %pad_maximum_fusion.6), channel_id=1, replica_groups=mesh['rows'=4,'seq'=8] {'rows','seq'}, use_global_device_ids=true, to_apply=%region_16.17 | all-reduce | flops 4096 | bytes 32768 | tf_op jit(solution)/shard_map/psum | solution.py:262
  927.5 271.5 %all-reduce.3.cloned.1.call-done = (bf16[256,2048]{1,0:T(8,128)(2,1)}, bf16[256,2048]{1,0:T(8,128)(2,1)}, bf16[2048,2048]{1,0:T(8,128)(2,1)}, bf16[1024,2048]{1,0:T(8,128)(2,1)}) async-done(((bf16[256,2048]{1,0:T(8,128)(2,1)}, bf16[256,2048]{1,0:T(8,128)(2,1)}, bf16[2048,2048]{1,0:T(8,128)(2,1)}, bf16[1024,2048]{1,0:T(8,128)(2,1)}), (bf16[256,2048]{1,0:T(8,128)(2,1)}, bf16[256,2048]{1,0:T(8,128)(2,1)}, ...) | async-done | bytes 14680080 | tf_op jit(solution)/shard_map/psum | solution.py:264
  1207.9 7.7 shard_map.152
  (180 shorter events, 147.5 us)
Async XLA Ops:
  7.2 5.4 copy-start.21
  7.2 53.5 %all-gather.8.cloned.1.call-start = ((), (), s32[]{:S(2)}) async-start(), calls=%async_computation.5 | async-start | bytes 4718592 | tf_op jit(solution)/shard_map/all_gather | solution.py:126
  9.3 133.3 %all-gather.6.cloned.1.call-start = ((), (), s32[]{:S(2)}) async-start(), calls=%async_computation.4 | async-start | bytes 9437184 | tf_op jit(solution)/shard_map/all_gather | solution.py:117
  10.1 214.8 %all-gather.10.cloned.1.call-start = ((), (), s32[]{:S(2)}) async-start(), calls=%async_computation.6 | async-start | bytes 9437184 | tf_op jit(solution)/shard_map/all_gather | solution.py:118
  10.8 302.2 %all-gather.12.cloned.1.call-start = ((), (), s32[]{:S(2)}) async-start(), calls=%async_computation.7 | async-start | bytes 9437184 | tf_op jit(solution)/shard_map/all_gather | solution.py:163
  12.5 52.4 %copy-start.22 = (f32[256]{0:T(256)}, f32[256]{0:T(256)S(1)}, u32[]{:S(2)}) copy-start(f32[256]{0:T(256)S(1)} %get-tuple-element.259) | copy-start | bytes 3076
  12.6 52.4 %copy-start.17 = (f32[1,2048]{1,0:T(1,128)}, f32[1,2048]{1,0:T(1,128)S(1)}, u32[]{:S(2)}) copy-start(f32[1,2048]{1,0:T(1,128)S(1)} %get-tuple-element.257) | copy-start | bytes 24580
  173.9 57.2 %copy-start.15 = (s32[2,512]{1,0:T(2,128)}, s32[2,512]{1,0:T(2,128)S(1)}, u32[]{:S(2)}) copy-start(s32[2,512]{1,0:T(2,128)S(1)} %get-tuple-element.536) | copy-start | bytes 12292
  232.3 163.4 %all-gather.14.cloned.1.call-start = ((), (), s32[]{:S(2)}) async-start(), calls=%async_computation.9 | async-start | bytes 9437184 | tf_op jit(solution)/shard_map/all_gather | solution.py:174
  234.9 296.9 %reduce-scatter.10.cloned.1.call-start = ((), (), s32[]{:S(2)}) async-start(), calls=%async_computation.10 | async-start | bytes 9437184 | tf_op jit(solution)/shard_map/reduce_scatter | solution.py:176
  443.5 179.1 %reduce-scatter.8.cloned.1.call-start = ((), (), s32[]{:S(2)}) async-start(), calls=%async_computation.8 | async-start | bytes 9437184 | tf_op jit(solution)/shard_map/reduce_scatter | solution.py:168
  457.5 411.4 %reduce-scatter.12.cloned.1.call-start = ((), (), s32[]{:S(2)}) async-start(), calls=%async_computation.11 | async-start | bytes 18874368 | tf_op jit(solution)/shard_map/reduce_scatter | solution.py:253
  534.4 92.1 %copy-start.8 = (bf16[256,2048]{1,0:T(8,128)(2,1)S(1)}, bf16[256,2048]{1,0:T(8,128)(2,1)}, u32[]{:S(2)}) copy-start(bf16[256,2048]{1,0:T(8,128)(2,1)} %convert_element_type.135) | copy-start | bytes 3145732
  622.6 9.7 slice-start
  626.5 5.8 copy-start.1
  626.5 5.8 slice-start.1
  634.7 4.7 copy-start.16
  702.2 222.6 %reduce-scatter.14.cloned.1.call-start = ((), (), s32[]{:S(2)}) async-start(), calls=%async_computation.12 | async-start | bytes 4718592
  717.2 481.8 %all-reduce.3.cloned.1.call-start = ((), (), s32[]{:S(2)}) async-start(), calls=%async_computation.13 | async-start | bytes 29360128 | tf_op jit(solution)/shard_map/psum | solution.py:264
  717.2 14.3 %copy-start.26 = (bf16[2048,1,1024]{2,0,1:T(8,128)(2,1)S(1)}, bf16[2048,1,1024]{2,0,1:T(8,128)(2,1)}, u32[]{:S(2)}) copy-start(bf16[2048,1,1024]{2,0,1:T(8,128)(2,1)} %get-tuple-element.247) | copy-start | bytes 12582916
  717.2 14.3 %copy-start.27 = (bf16[2048,1,1024]{2,0,1:T(8,128)(2,1)S(1)}, bf16[2048,1,1024]{2,0,1:T(8,128)(2,1)}, u32[]{:S(2)}) copy-start(bf16[2048,1,1024]{2,0,1:T(8,128)(2,1)} %get-tuple-element.248) | copy-start | bytes 12582916
  873.3 8.1 copy-start.20
  873.3 48.0 %copy-start.2 = (f32[256,2048]{1,0:T(8,128)S(1)}, f32[256,2048]{1,0:T(8,128)}, u32[]{:S(2)}) copy-start(f32[256,2048]{1,0:T(8,128)} %copy-done.1) | copy-start | bytes 6291460
  1207.9 7.7 copy-start.10
  (21 other events, 49.6 us)
Sparse Core Ops, SparseCore 0:
  10.2 50.4 all-gather.7
  62.3 80.2 all-gather.5
  144.2 80.5 all-gather.9
  232.4 80.5 all-gather.11
  315.1 80.5 all-gather.13
  443.6 88.1 reduce-scatter.9
  534.6 87.9 reduce-scatter.7
  702.3 166.5 reduce-scatter.11
  871.2 49.4 reduce-scatter.13
  925.0 273.9 all-reduce.2

commit v3 on v1

v3 whole, which is shorter than its diff:
```python
import jax
import jax.numpy as jnp
from jax import lax
from jax.sharding import PartitionSpec as P

HEADS = 16
HEAD = 128
KV = 4
GROUP = 4
EPS = 1e-05
NEG = -1e30
F32 = jnp.float32
BF16 = jnp.bfloat16


def dot(left, right, dims):
    return lax.dot_general(left, right, (dims, ((), ())), preferred_element_type=F32)


def tie(value, dep):
    if dep is None:
        return value
    return lax.optimization_barrier((value, dep))[0]


def norm_back(grad_normed, scaled, inverse, gain):
    inner = grad_normed * gain
    return inverse * (inner - scaled * jnp.mean(inner * scaled, axis=-1, keepdims=True))


def swap_core(value, seq):
    return lax.ppermute(value, "seq", [(s, s ^ 1) for s in range(seq)])


def ring(value, chips):
    pairs = [(2 * z + c, 2 * ((z + 1) % chips) + c) for z in range(chips) for c in range(2)]
    return lax.ppermute(value, "seq", pairs)


def swap_row(value, rows, mask):
    return lax.ppermute(value, "rows", [(r, r ^ mask) for r in range(rows)])


def ring_gather(own, chips, dep=None):
    got = [tie(own, dep)]
    for _ in range(1, chips):
        got.append(ring(got[-1], chips))
    return [own] + got[:0:-1], got[-2]


def ring_scatter(parts, chips):
    sent = parts[chips - 1]
    for j in range(chips - 2, -1, -1):
        yield sent
        total = ring(sent, chips).astype(F32) + parts[j].astype(F32)
        sent = total.astype(BF16)
    return total


class Lane:
    def __init__(self):
        self.waiting, self.results, self.sent = [], {}, None

    def add(self, name, steps):
        self.waiting.append((name, steps))

    def step(self):
        if self.waiting:
            name, steps = self.waiting[0]
            try:
                sent = next(steps)
                self.sent = sent
                return sent
            except StopIteration as end:
                self.results[name] = end.value
                self.waiting.pop(0)
                return self.step()
        return None

    def result(self, name):
        while name not in self.results:
            self.step()
        return self.results[name]


def beside(value, *lanes):
    for lane in lanes:
        value = tie(value, lane.step())
    return value


def xor_order(value, at):
    shape = value.shape
    value = value.reshape(2, 2, *shape[1:])
    value = jnp.where(at % 2 == 1, value[:, ::-1], value)
    return jnp.where(at // 2 == 1, value[::-1], value).reshape(shape)


def own_order(value, chips, place, core):
    count = value.shape[0]
    value = value.reshape(count, chips, 2, -1)
    value = jnp.where(core == 0, value, value[:, :, ::-1])
    value = jnp.concatenate([value, value], axis=1)
    value = lax.dynamic_slice_in_dim(value, place, chips, axis=1)
    return value.transpose(0, 2, 1, 3).reshape(count, -1)


def index_order(value, chips, place, core):
    count = value.shape[0]
    value = value.reshape(count, 2, chips, -1).transpose(0, 2, 1, 3)
    value = jnp.concatenate([value, value], axis=1)
    value = lax.dynamic_slice_in_dim(value, (chips - place) % chips, chips, axis=1)
    value = jnp.where(core == 0, value, value[:, :, ::-1])
    return value.reshape(count, -1)


class Weight:
    def __init__(self, shard, chips, rows, row_at, order, dep=None):
        seq = 2 * chips
        self.chips, self.row_at, self.order = chips, row_at, order
        depth, width = shard.shape
        self.depth = depth
        self.split = rows == 4 and depth % 32 == 0 and width % 512 == 0
        if not self.split:
            self.whole = lax.all_gather(shard, "seq", axis=0, tiled=True)
            self.token = dep
            return
        part = width // rows
        half = depth // 2
        mine = lax.dynamic_slice_in_dim(shard, row_at * part, part, axis=1)
        slots, self.token = ring_gather(mine, chips, dep=dep)
        first = jnp.stack([v[:half] for v in slots[1:]])
        second = jnp.stack([v[half:] for v in slots[1:]])
        first_x = swap_row(first, rows, 1)
        second_y = swap_row(second, rows, 2)
        first_pair = swap_row(jnp.stack([first, first_x]), rows, 2)
        second_pair = swap_row(jnp.stack([second, second_y]), rows, 1)
        parts = jnp.stack(
            [
                jnp.stack([first, first_x, first_pair[0], first_pair[1]]),
                jnp.stack([second, second_pair[0], second_y, second_pair[1]]),
            ],
            axis=2,
        )
        parts = parts.reshape(rows, (chips - 1) * depth, part)
        self.far = [parts, swap_core(parts, seq)]
        self.near = [shard, swap_core(shard, seq)]

    def features(self, value):
        if not self.split:
            out = own_order(dot(value, self.whole, ((1,), (1,))), *self.order)
            half = out.shape[1] // 2
            return [out[:, :half].astype(BF16), out[:, half:].astype(BF16)]
        count = value.shape[0]
        blocks = value.reshape(count, 4, -1).transpose(1, 0, 2)
        blocks = xor_order(blocks, self.row_at)
        out = []
        for near, far in zip(self.near, self.far, strict=True):
            term = jnp.einsum("ktc,kfc->ktf", blocks, far, preferred_element_type=F32)
            term = jnp.sum(term, axis=0).astype(BF16)
            out.append(jnp.concatenate([dot(value, near, ((1,), (1,))).astype(BF16), term], axis=1))
        return out

    def back(self, halves):
        if not self.split:
            value = jnp.concatenate(halves, axis=1)
            return dot(index_order(value, *self.order), self.whole, ((1,), (0,)))
        count = halves[0].shape[0]
        near_sum = far_sum = 0.0
        for part, near, far in zip(halves, self.near, self.far, strict=True):
            near_sum += dot(part[:, : self.depth], near, ((1,), (0,)))
            far_sum += jnp.einsum(
                "tf,kfc->ktc", part[:, self.depth :], far, preferred_element_type=F32
            )
        far_sum = xor_order(far_sum, self.row_at).transpose(1, 0, 2).reshape(count, -1)
        return near_sum + far_sum


def scatter_halves(own, sib, got_at, chips):
    got = swap_core(sib, 2 * chips)
    parts = [own(j).astype(F32) + got_at(got, j).astype(F32) for j in range(chips)]
    return (yield from ring_scatter([p.astype(BF16) for p in parts], chips))


def block_of(value, j, chips):
    size = value.shape[0] // chips
    return value[j * size : (j + 1) * size]


def scatter_tokens(part, chips, place, core):
    size = part.shape[0] // (2 * chips)

    def block(j, at):
        start = (2 * ((place + j) % chips) + at) * size
        return lax.dynamic_slice_in_dim(part, start, size, axis=0)

    sib = jnp.concatenate([block(j, 1 - core) for j in range(chips)], axis=0)
    return scatter_halves(
        lambda j: block(j, core), sib, lambda got, j: block_of(got, j, chips), chips
    )


def sum_rows(value, rows):
    if rows != 4:
        return lax.psum(value.astype(BF16), "rows").astype(F32)
    half = value.shape[0] // 2
    first, second = value[:half].astype(BF16), value[half:].astype(BF16)

    def pair(item, mask):
        return item.astype(F32) + swap_row(item, rows, mask).astype(F32)

    first, second = pair(first, 1).astype(BF16), pair(second, 2).astype(BF16)
    return jnp.concatenate([pair(first, 2), pair(second, 1)], axis=0)


def sum_all(value, rows, seq):
    mask = 1
    while mask < seq:
        value = value + lax.ppermute(value, "seq", [(s, s ^ mask) for s in range(seq)])
        mask *= 2
    mask = 1
    while mask < rows:
        value = value + swap_row(value, rows, mask)
        mask *= 2
    return value


def local(
    tokens,
    kv_cache,
    lengths,
    norm_gains,
    query_weight,
    output_weight,
    ffn_in_weight,
    down_weight,
    cotangent,
):
    rows_here, seg_len, width = tokens.shape
    seq = lax.axis_size("seq")
    rows = lax.axis_size("rows")
    chips = seq // 2
    seq_at = lax.axis_index("seq")
    row_at = lax.axis_index("rows")
    place, core = seq_at // 2, seq_at % 2
    order = (chips, place, core)
    gain_one, gain_two = norm_gains[0], norm_gains[1]
    query_pos = seq_at * seg_len + jnp.arange(seg_len, dtype=jnp.int32)
    chip_range = jnp.arange(chips, dtype=jnp.int32)
    ring_at = (place + chip_range) % chips
    starts = jnp.concatenate([2 * ring_at + core, 2 * ring_at + 1 - core]) * seg_len

    live = [
        (query_pos < lengths[r]).astype(F32).reshape(seg_len, 1) for r in range(rows_here)
    ]
    grad_out = [cotangent[r].astype(F32) * live[r] for r in range(rows_here)]
    grad_group = [
        lax.all_gather(g.astype(BF16), "seq", axis=0, tiled=True) for g in grad_out
    ]

    query_proj = Weight(query_weight, chips, rows, row_at, order)
    cache_own = kv_cache.reshape(rows_here, seg_len, 2, KV, HEAD).transpose(2, 0, 3, 1, 4)
    cache_slots, token = ring_gather(cache_own, chips, dep=query_proj.token)
    cache_block = jnp.concatenate(cache_slots, axis=3)
    cache_all = jnp.concatenate([cache_block, swap_core(cache_block, seq)], axis=3)
    output_proj = Weight(output_weight, chips, rows, row_at, order, dep=token)
    per = chips // KV

    def to_slots(value):
        value = jnp.repeat(value, per, axis=2) if per > 1 else value
        value = jnp.concatenate([value, value], axis=2)
        return lax.dynamic_slice_in_dim(value, place, chips, axis=2)

    def from_slots(value):
        value = jnp.concatenate([value, value], axis=2)
        value = lax.dynamic_slice_in_dim(value, (chips - place) % chips, chips, axis=2)
        if per > 1:
            shape = value.shape
            value = value.reshape(*shape[:2], KV, per, *shape[3:]).astype(F32).sum(axis=3)
        return value.astype(BF16)

    def to_heads(halves):
        value = jnp.stack([h.reshape(rows_here, seg_len, chips, -1, HEAD) for h in halves])
        value = value.transpose(1, 3, 0, 4, 2, 5)
        return value.reshape(rows_here, chips, -1, HEAD)

    def from_heads(value):
        value = value.reshape(rows_here, chips, 2, -1, seg_len, HEAD).transpose(2, 0, 4, 1, 3, 5)
        value = value.reshape(2, rows_here * seg_len, -1)
        return [value[0], value[1]]

    def heads_dot(spec, left, right):
        return jnp.einsum(spec, left, right, preferred_element_type=F32)

    key_pos = (starts[:, None] + jnp.arange(seg_len, dtype=jnp.int32)).reshape(-1)
    limit = jnp.minimum(query_pos[None], lengths[:, None] - 1)
    limit = jnp.tile(limit, (1, HEADS // chips))
    valid = (key_pos[None, None] <= limit[:, :, None])[:, None]
    scale = HEAD ** (-0.5)

    inputs = tokens.astype(F32).reshape(rows_here * seg_len, width)
    inverse_one = lax.rsqrt(jnp.mean(inputs * inputs, axis=-1, keepdims=True) + EPS)
    normed_one = (inputs * inverse_one * gain_one).astype(BF16)
    query = tie(query_proj.features(normed_one), grad_group)
    cache_slot = to_slots(cache_all)
    keys, values = cache_slot[0], cache_slot[1]
    query_heads = to_heads(query)
    scores = heads_dot("rjqd,rjkd->rjqk", query_heads, keys) * scale
    scores = jnp.where(valid, scores, NEG)
    best = jnp.max(scores, axis=-1, keepdims=True)
    weights = jnp.exp(scores - best)
    total = jnp.sum(weights, axis=-1, keepdims=True)
    mixed_heads = heads_dot("rjqk,rjkd->rjqd", weights.astype(BF16), values) / total
    lse = best + jnp.log(total)
    mixed = from_heads(mixed_heads.astype(BF16))
    middle_all = inputs + output_proj.back(mixed)
    inverse_all = lax.rsqrt(jnp.mean(middle_all * middle_all, axis=-1, keepdims=True) + EPS)
    normed_all = (middle_all * inverse_all * gain_two).astype(BF16)

    def split(value):
        return [value[r * seg_len : (r + 1) * seg_len] for r in range(rows_here)]

    middle, inverse_two, normed_two = split(middle_all), split(inverse_all), split(normed_all)
    normed_group = [lax.all_gather(n, "seq", axis=0, tiled=True) for n in normed_two]

    main, fill = Lane(), Lane()
    hidden, grad_gate, grad_up = [], [], []
    for r in range(rows_here):
        kept = jnp.einsum(
            "td,nkd->tkn", beside(normed_group[r], main), ffn_in_weight, preferred_element_type=F32
        )
        gate, upper = kept[:, 0], kept[:, 1]
        sigma = jax.nn.sigmoid(gate)
        grad_hidden = dot(beside(grad_group[r], main), down_weight, ((1,), (1,)))
        hidden.append((gate * sigma * upper).astype(BF16))
        grad_gate.append(
            (grad_hidden * upper * sigma * (1.0 + gate * (1.0 - sigma))).astype(BF16)
        )
        grad_up.append((grad_hidden * gate * sigma).astype(BF16))
        pair = beside(jnp.stack([grad_gate[r], grad_up[r]], axis=1), main)
        part = jnp.einsum("tkn,nkd->td", pair, ffn_in_weight, preferred_element_type=F32)
        main.add(("grad", r), scatter_tokens(part.astype(BF16), chips, place, core))
        part = dot(hidden[r], down_weight, ((1,), (0,))).astype(BF16)
        fill.add(("ffn", r), scatter_tokens(part, chips, place, core))

    def over_tokens(left, right):
        return sum(
            dot(a, b, ((0,), (0,))) for a, b in zip(left, right, strict=True)
        ).astype(BF16)

    down_part = over_tokens(hidden, grad_group)
    gate_part = over_tokens(grad_gate, normed_group)
    up_part = over_tokens(grad_up, normed_group)
    gate_grad, up_grad = lax.psum((gate_part, up_part), "rows")

    grad_middle, gain_two_grad = [], 0.0
    for r in range(rows_here):
        grad_normed_two = main.result(("grad", r))
        scaled_two = middle[r] * inverse_two[r]
        gain_two_grad += jnp.sum(grad_normed_two * scaled_two, axis=0)
        grad_middle.append(
            grad_out[r] + norm_back(grad_normed_two, scaled_two, inverse_two[r], gain_two)
        )
    grad_middle = jnp.concatenate(grad_middle, axis=0)
    grad_branch = beside(grad_middle.astype(BF16), fill)
    output_part = [dot(half, grad_branch, ((0,), (0,))).astype(BF16) for half in mixed]

    def scatter_rows(parts):
        def take(value, j):
            return block_of(value, j, chips)

        return scatter_halves(lambda j: take(parts[0], j), parts[1], take, chips)

    main.add("output", scatter_rows(output_part))
    grad_heads = to_heads(output_proj.features(beside(grad_branch, main, fill)))
    grad_heads = beside(grad_heads, main, fill)
    delta = jnp.sum(grad_heads.astype(F32) * mixed_heads, axis=-1, keepdims=True)
    scores = heads_dot("rjqd,rjkd->rjqk", query_heads, keys) * scale
    probs = jnp.where(valid, jnp.exp(scores - lse), 0.0)
    grad_probs = heads_dot("rjqd,rjkd->rjqk", grad_heads, values)
    grad_scores = (probs * (grad_probs - delta)).astype(BF16)
    query_term = from_heads(
        (heads_dot("rjqk,rjkd->rjqd", grad_scores, keys) * scale).astype(BF16)
    )
    grad_keys = heads_dot("rjqk,rjqd->rjkd", grad_scores, query_heads) * scale
    grad_values = heads_dot("rjqk,rjqd->rjkd", probs.astype(BF16), grad_heads)
    cache_part = from_slots(jnp.stack([grad_keys.astype(BF16), grad_values.astype(BF16)]))
    half_len = cache_part.shape[3] // 2

    def positions_of(value, j):
        return value[:, :, :, j * seg_len : (j + 1) * seg_len]

    main.step()
    fill.step()
    fill.add(
        "cache",
        scatter_halves(
            lambda j: positions_of(cache_part, j), cache_part[:, :, :, half_len:], positions_of, chips
        ),
    )
    query_part = [dot(half, normed_one, ((0,), (0,))).astype(BF16) for half in query_term]
    main.add("query", scatter_rows(query_part))

    grad_normed_one = query_proj.back(query_term)
    scaled_one = inputs * inverse_one
    gain_one_grad = jnp.sum(grad_normed_one * scaled_one, axis=0)
    input_grad = grad_middle + norm_back(grad_normed_one, scaled_one, inverse_one, gain_one)
    gain_grad = sum_all(jnp.stack([gain_one_grad, gain_two_grad]), rows, seq)

    output_grad = sum_rows(main.result("output"), rows)
    layer_out = [
        (live[r] * (middle[r] + fill.result(("ffn", r)))).astype(BF16) for r in range(rows_here)
    ]
    cache_grad = fill.result("cache")
    cache_grad = cache_grad.transpose(1, 3, 0, 2, 4).reshape(rows_here, seg_len, 2, KV * HEAD)
    query_grad = sum_rows(main.result("query"), rows)
    down_grad = sum_rows(down_part, rows)
    gate_grad, up_grad = lax.optimization_barrier((gate_grad, up_grad, query_grad))[:2]
    in_grad = jnp.stack([gate_grad, up_grad], axis=1)
    return (
        jnp.stack(layer_out),
        input_grad.reshape(rows_here, seg_len, width),
        cache_grad,
        gain_grad,
        query_grad,
        output_grad,
        in_grad.astype(F32),
        down_grad,
    )


def solution(mesh):
    in_specs = (
        P("rows", "seq", None),
        P("rows", "seq", None, None),
        P("rows"),
        P(),
        P("seq", None),
        P("seq", None),
        P("seq", None, None),
        P("seq", None),
        P("rows", "seq", None),
    )
    out_specs = (
        P("rows", "seq", None),
        P("rows", "seq", None),
        P("rows", "seq", None, None),
        P(),
        P("seq", None),
        P("seq", None),
        P("seq", None, None),
        P("seq", None),
    )
    return jax.shard_map(local, mesh=mesh, in_specs=in_specs, out_specs=out_specs, check_vma=False)
```

time: 1120 us -> 948 us (0.85)
  local copies, waits for them, and re-layouts: 247 us -> 116 us
  matrix products: 244 us -> 228 us
  waiting for transfers between devices: 400 us -> 384 us
  starting transfers between devices: 57.9 us -> 72.2 us
  other arithmetic: 136 us -> 122 us
    ppermute x42 -> x30, waiting for transfers between devices: 359 us -> 245 us  [ring(): return lax.ppermute(value, 'seq', pairs)]
    dot_general x26 -> x22, matrix products: 172 us -> 102 us  [dot(): lax.dot_general(left, right, (dims, ((), ())), preferred_element_type=F32)]
    dot_general x18 -> x14, matrix products: 58.6 us -> 114 us  [the longest x6 44.1 us: heads_dot(): return jnp.einsum(spec, left, right, preferred_element_type=F32)]
    ppermute x18 -> x22, waiting for transfers between devices: 37.4 us -> 91.7 us  [swap_row(): return lax.ppermute(value, 'rows', [(r, r ^ mask) for r in range(rows)])]
    all_gather x0 -> x4, waiting for transfers between devices: none -> 45.7 us  [the longest x2 45.7 us: local(): lax.all_gather(n, 'seq', axis=0, tiled=True)]
    another operation x15 -> x6, local copies, waits for them, and re-layouts: 50.7 us -> 6.13 us  [to_heads(): jnp.stack([h.reshape(rows_here, seg_len, chips, -1, HEAD) for h in halves])]
    slice x15 -> x9, local copies, waits for them, and re-layouts: 38.2 us -> 4.21 us  [the longest x6 2.36 us: from_heads(): return [value[0], value[1]]]
    another operation x11 -> x5, other arithmetic: 20.6 us -> 4.01 us  [the longest x1 9.64 us: local(): cache_part = jnp.stack(cache_terms, axis=3)]
  transfers between devices with their start and end apart: 80 -> 72, of which waited for: 40 -> 34; matrix products, arithmetic and copies ran while one was open for 51% -> 43% of each run, Pallas kernels for 0% -> 0%
where the time goes in v3:
time: 948 us; the launch traced here: 938 us
  waiting for transfers between devices  384 us (41%)
  matrix products  228 us (24%)
  other arithmetic  122 us (13%)
  local copies, waits for them, and re-layouts  116 us (12%)
  starting transfers between devices  72.2 us (8%)
  between operations  16.2 us (2%)
    ppermute x30, waiting for transfers between devices, ring(): return lax.ppermute(value, 'seq', pairs)  245 us
    dot_general x22, matrix products, dot(): lax.dot_general(left, right, (dims, ((), ())), preferred_element_type=F32)  102 us
    ppermute x22, waiting for transfers between devices, swap_row(): return lax.ppermute(value, 'rows', [(r, r ^ mask) for r in range(rows)])  91.7 us
    unnamed x179, local copies, waits for them, and re-layouts  52.7 us
    all_gather x2, waiting for transfers between devices, local(): lax.all_gather(n, 'seq', axis=0, tiled=True)  45.7 us
    dot_general x6, matrix products, heads_dot(): return jnp.einsum(spec, left, right, preferred_element_type=F32)  44.1 us
    ppermute x22, starting transfers between devices, swap_row(): return lax.ppermute(value, 'rows', [(r, r ^ mask) for r in range(rows)])  33.7 us
    dot_general x2, matrix products, local(): jnp.einsum('td,nkd->tkn', beside(normed_group[r], main), ffn_in_weight, p...  33 us
  transfers between devices with their start and end apart: 72, of which 34 were waited for; matrix products, arithmetic and copies ran while one was open for 43% of the time, Pallas kernels for 0%

profile of v3, /device:TPU:0, one launch (start us, length us, event | category | flops | bytes accessed | tf_op | source)
XLA Modules:
  0.0 937.7 jit_solution(4158049222670336674)
XLA Ops:
  31.9 12.5 %collective-permute-done.1 = bf16[256,512]{1,0:T(8,128)(2,1)S(1)} collective-permute-done((bf16[256,512]{1,0:T(8,128)(2,1)}, bf16[256,512]{1,0:T(8,128)(2,1)S(1)}, u32[]{:S(2)}, u32[]{:S(2)}) %collective-permute-start.1) | collective-permute-done | bytes 262176 | tf_op jit(solution)/shard_map/ppermute | solution.py:37
  52.7 10.9 %collective-permute-done.2 = bf16[256,512]{1,0:T(8,128)(2,1)S(1)} collective-permute-done((bf16[256,512]{1,0:T(8,128)(2,1)S(1)}, bf16[256,512]{1,0:T(8,128)(2,1)S(1)}, u32[]{:S(2)}, u32[]{:S(2)}) %collective-permute-start.2) | collective-permute-done | bytes 262176 | tf_op jit(solution)/shard_map/ppermute | solution.py:37
  67.9 15.9 %collective-permute-done.9 = bf16[2,2,4,128,128]{4,3,2,1,0:T(8,128)(2,1)} collective-permute-done((bf16[2,2,4,128,128]{4,3,2,1,0:T(8,128)(2,1)}, bf16[2,2,4,128,128]{4,3,2,1,0:T(8,128)(2,1)}, u32[]{:S(2)}, u32[]{:S(2)}) %collective-permute-start.9) | collective-permute-done | bytes 524320 | tf_op jit(solution)/shard_map/ppermute | solution.py:37
  92.5 11.9 %collective-permute-done.10 = bf16[2,2,4,128,128]{4,3,2,1,0:T(8,128)(2,1)} collective-permute-done((bf16[2,2,4,128,128]{4,3,2,1,0:T(8,128)(2,1)}, bf16[2,2,4,128,128]{4,3,2,1,0:T(8,128)(2,1)}, u32[]{:S(2)}, u32[]{:S(2)}) %collective-permute-start.10) | collective-permute-done | bytes 524320 | tf_op jit(solution)/shard_map/ppermute | solution.py:37
  109.1 10.3 %collective-permute-done.14 = bf16[256,512]{1,0:T(8,128)(2,1)S(1)} collective-permute-done((bf16[256,512]{1,0:T(8,128)(2,1)S(1)}, bf16[256,512]{1,0:T(8,128)(2,1)S(1)}, u32[]{:S(2)}, u32[]{:S(2)}) %collective-permute-start.14) | collective-permute-done | bytes 262176 | tf_op jit(solution)/shard_map/ppermute | solution.py:37
  129.8 26.0 %collective-permute-done.15 = bf16[256,512]{1,0:T(8,128)(2,1)S(1)} collective-permute-done((bf16[256,512]{1,0:T(8,128)(2,1)S(1)}, bf16[256,512]{1,0:T(8,128)(2,1)S(1)}, u32[]{:S(2)}, u32[]{:S(2)}) %collective-permute-start.15) | collective-permute-done | bytes 262176 | tf_op jit(solution)/shard_map/ppermute | solution.py:37
  271.7 45.7 %all-gather.9.cloned.1.call-done = bf16[1024,2048]{1,0:T(8,128)(2,1)} async-done(((bf16[128,2048]{1,0:T(8,128)(2,1)}), bf16[1024,2048]{1,0:T(8,128)(2,1)}) %all-gather.9.cloned.1.call-update) | async-done | bytes 4194320 | tf_op jit(solution)/shard_map/all_gather | solution.py:324
  317.4 16.4 %fusion.35 = f32[1024,2,1024]{2,0,1:T(8,128)} fusion(bf16[1024,2,2048]{2,1,0:T(2,128)(2,1)} %param.15, bf16[1024,2048]{1,0:T(8,128)(2,1)} %all-gather.9.cloned.1.call-done), kind=kOutput, calls=%fused_computation.68 | convolution fusion | flops 8589934592 | bytes 20971520 | tf_op jit(solution)/shard_map/td,nkd->tkn/dot_general | solution.py:329
  333.8 10.5 %multiply_convert_fusion.6 = (bf16[1024,1024]{1,0:T(8,128)(2,1)}, bf16[1024,1024]{1,0:T(8,128)(2,1)}, bf16[1024,1024]{1,0:T(8,128)(2,1)}) fusion(f32[1024,2,1024]{2,0,1:T(8,128)} %fusion.35, bf16[1024,2048]{1,0:T(8,128)(2,1)S(1)} %copy-done.72, bf16[1024,2048]{1,0:T(8,128)(2,1)S(1)} %copy-done.69), kind=kOutput, calls=%fused_computation.59 | convolution fusion | flops 4311744512 | bytes 23068672 | tf_op jit(solution)/shard_map/dot_general | solution.py:17
  344.3 13.1 %bitcast_convert_fusion.1 = bf16[1024,2048]{1,0:T(8,128)(2,1)S(1)} fusion(bf16[1024,2,2048]{2,1,0:T(2,128)(2,1)S(1)} %bitcast.348, bf16[1024,1,1024]{2,0,1:T(8,128)(2,1)} %bitcast.349, bf16[1024,1,1024]{2,0,1:T(8,128)(2,1)} %bitcast.350), kind=kOutput, calls=%fused_computation.17 | convolution fusion | flops 8594128896 | bytes 16777216 | tf_op jit(solution)/shard_map/tkn,nkd->td/dot_general | solution.py:341
  394.4 16.6 %fusion.40 = f32[1024,2,1024]{2,0,1:T(8,128)} fusion(bf16[1024,2,2048]{2,1,0:T(2,128)(2,1)} %param.15, bf16[1024,2048]{1,0:T(8,128)(2,1)} %all-gather.11.cloned.1.call-done), kind=kOutput, calls=%fused_computation.69 | convolution fusion | flops 8589934592 | bytes 20971520 | tf_op jit(solution)/shard_map/td,nkd->tkn/dot_general | solution.py:329
  432.7 11.7 %bitcast_convert_fusion = bf16[1024,2048]{1,0:T(8,128)(2,1)S(1)} fusion(bf16[1024,2,1024]{2,0,1:T(8,128)(2,1)S(1)} %pad_maximum_fusion.1, bf16[1024,2,2048]{2,1,0:T(2,128)(2,1)} %param.15), kind=kOutput, calls=%fused_computation.16 | convolution fusion | flops 8592031744 | bytes 16777216 | tf_op jit(solution)/shard_map/tkn,nkd->td/dot_general | solution.py:341
  476.8 10.1 %collective-permute-done.35 = bf16[128,2048]{1,0:T(8,128)(2,1)S(1)} collective-permute-done((bf16[128,2048]{1,0:T(8,128)(2,1)S(1)}, bf16[128,2048]{1,0:T(8,128)(2,1)S(1)}, u32[]{:S(2)}, u32[]{:S(2)}) %collective-permute-start.35) | collective-permute-done | bytes 524320 | tf_op jit(solution)/shard_map/ppermute | solution.py:37
  499.2 10.1 %collective-permute-done.36 = bf16[128,2048]{1,0:T(8,128)(2,1)S(1)} collective-permute-done((bf16[128,2048]{1,0:T(8,128)(2,1)S(1)}, bf16[128,2048]{1,0:T(8,128)(2,1)S(1)}, u32[]{:S(2)}, u32[]{:S(2)}) %collective-permute-start.36) | collective-permute-done | bytes 524320 | tf_op jit(solution)/shard_map/ppermute | solution.py:37
  520.6 11.2 %collective-permute-done.30 = bf16[128,2048]{1,0:T(8,128)(2,1)S(1)} collective-permute-done((bf16[128,2048]{1,0:T(8,128)(2,1)S(1)}, bf16[128,2048]{1,0:T(8,128)(2,1)S(1)}, u32[]{:S(2)}, u32[]{:S(2)}) %collective-permute-start.30) | collective-permute-done | bytes 524320 | tf_op jit(solution)/shard_map/ppermute | solution.py:37
  531.8 10.7 %collective-permute-done.37 = bf16[128,2048]{1,0:T(8,128)(2,1)S(1)} collective-permute-done((bf16[128,2048]{1,0:T(8,128)(2,1)S(1)}, bf16[128,2048]{1,0:T(8,128)(2,1)S(1)}, u32[]{:S(2)}, u32[]{:S(2)}) %collective-permute-start.37) | collective-permute-done | bytes 524320 | tf_op jit(solution)/shard_map/ppermute | solution.py:37
  575.8 60.3 %collective-permute-done.66 = bf16[512,2048]{1,0:T(8,128)(2,1)} collective-permute-done((bf16[512,2048]{1,0:T(8,128)(2,1)}, bf16[512,2048]{1,0:T(8,128)(2,1)}, u32[]{:S(2)}, u32[]{:S(2)}) %collective-permute-start.66) | collective-permute-done | bytes 2097184 | tf_op jit(solution)/shard_map/ppermute | solution.py:41
  677.4 11.8 %multiply_convert_fusion = bf16[2,4,512,1024]{3,2,1,0:T(8,128)(2,1)} fusion(f32[2,4,512,1024]{3,2,1,0:T(8,128)} %copy-done, f32[2,4,512]{2,1,0:T(4,128)S(1)} %multiply_reduce_fusion.2, f32[2,4,512]{2,1,0:T(4,128)S(1)} %bitcast.345, pred[2,512,1024]{2,1,0:T(8,128)(4,1)S(1)} %copy-done.12, bf16[2,4,512,128]{3,2,1,0:T(8,128)(2,1)S(1)} %bitcast.309, ...), kind=kOutput, calls=%fused_computation | convolution fusion | flops 1098907648 | bytes 29392896 | tf_op jit(solution)/shard_map/rjqd,rjkd->rjqk/dot_general | solution.py:293
  756.2 15.8 %collective-permute-done.50 = bf16[256,2048]{1,0:T(8,128)(2,1)S(1)} collective-permute-done((bf16[256,2048]{1,0:T(8,128)(2,1)S(1)}, bf16[256,2048]{1,0:T(8,128)(2,1)S(1)}, u32[]{:S(2)}, u32[]{:S(2)}) %collective-permute-start.50) | collective-permute-done | bytes 1048608 | tf_op jit(solution)/shard_map/ppermute | solution.py:37
  774.0 20.5 %collective-permute-done.58 = bf16[256,2048]{1,0:T(8,128)(2,1)S(1)} collective-permute-done((bf16[256,2048]{1,0:T(8,128)(2,1)S(1)}, bf16[256,2048]{1,0:T(8,128)(2,1)S(1)}, u32[]{:S(2)}, u32[]{:S(2)}) %collective-permute-start.58) | collective-permute-done | bytes 1048608 | tf_op jit(solution)/shard_map/ppermute | solution.py:37
  806.5 21.8 %collective-permute-done.51 = bf16[256,2048]{1,0:T(8,128)(2,1)S(1)} collective-permute-done((bf16[256,2048]{1,0:T(8,128)(2,1)S(1)}, bf16[256,2048]{1,0:T(8,128)(2,1)S(1)}, u32[]{:S(2)}, u32[]{:S(2)}) %collective-permute-start.51) | collective-permute-done | bytes 1048608 | tf_op jit(solution)/shard_map/ppermute | solution.py:37
  839.9 22.0 %collective-permute-done.52 = bf16[256,2048]{1,0:T(8,128)(2,1)S(1)} collective-permute-done((bf16[256,2048]{1,0:T(8,128)(2,1)S(1)}, bf16[256,2048]{1,0:T(8,128)(2,1)S(1)}, u32[]{:S(2)}, u32[]{:S(2)}) %collective-permute-start.52) | collective-permute-done | bytes 1048608 | tf_op jit(solution)/shard_map/ppermute | solution.py:37
  891.8 10.4 %maximum_convert_fusion = f32[1024,2,2048]{2,0,1:T(8,128)} fusion(bf16[1024,1,2048]{2,0,1:T(8,128)(2,1)} %bitcast.316, bf16[1024,1,2048]{2,0,1:T(8,128)(2,1)} %bitcast.315), kind=kLoop, calls=%fused_computation.14 | loop fusion | flops 8388608 | bytes 25165824 | tf_op jit(solution)/shard_map/convert_element_type | solution.py:427
  902.2 28.6 %copy.82 = f32[1024,2,2048]{2,1,0:T(2,128)} copy(f32[1024,2,2048]{2,0,1:T(8,128)} %maximum_convert_fusion) | data formatting | bytes 33554432
  (510 shorter events, 486.8 us)
Async XLA Ops:
  7.2 219.6 %all-gather.7.cloned.1.call-start = ((), (), s32[]{:S(2)}) async-start(), calls=%async_computation.1 | async-start | bytes 4718592 | tf_op jit(solution)/shard_map/all_gather | solution.py:258
  12.4 214.5 %all-gather.5.cloned.1.call-start = ((), (), s32[]{:S(2)}) async-start(), calls=%async_computation | async-start | bytes 4718592 | tf_op jit(solution)/shard_map/all_gather | solution.py:258
  12.4 154.4 %collective-permute-start.7 = (bf16[256,2048]{1,0:T(8,128)(2,1)}, bf16[256,2048]{1,0:T(8,128)(2,1)}, u32[]{:S(2)}, u32[]{:S(2)}) collective-permute-start(bf16[256,2048]{1,0:T(8,128)(2,1)} %param.13), channel_id=1, source_target_pairs={{0,1},{1,0},{2,3},{3,2},{4,5},{5,4},{6,7},{7,6},{8,9},{9,8},{10,11... | collective-permute-start | bytes 3145736 | tf_op jit(solution)/shard_map/ppermute | solution.py:32
  16.6 247.6 %collective-permute-start.13 = (bf16[256,2048]{1,0:T(8,128)(2,1)}, bf16[256,2048]{1,0:T(8,128)(2,1)}, u32[]{:S(2)}, u32[]{:S(2)}) collective-permute-start(bf16[256,2048]{1,0:T(8,128)(2,1)} %param.14), channel_id=1, source_target_pairs={{0,1},{1,0},{2,3},{3,2},{4,5},{5,4},{6,7},{7,6},{8,9},{9,8},{10,11... | collective-permute-start | bytes 3145736 | tf_op jit(solution)/shard_map/ppermute | solution.py:32
  16.8 300.6 %all-gather.9.cloned.1.call-start = ((), (), s32[]{:S(2)}) async-start(), calls=%async_computation.2 | async-start | bytes 4718592 | tf_op jit(solution)/shard_map/all_gather | solution.py:324
  66.4 38.0 %collective-permute-start.3 = (bf16[3,128,512]{2,1,0:T(8,128)(2,1)}, bf16[3,128,512]{2,1,0:T(8,128)(2,1)}, u32[]{:S(2)}, u32[]{:S(2)}) collective-permute-start(bf16[3,128,512]{2,1,0:T(8,128)(2,1)} %get-tuple-element.114), channel_id=1, source_target_pairs={{0,8},{8,0},{16,24},{24,16},{1,9},{9,1},{17,25},{25,17},{2,10},{10... | collective-permute-start | bytes 1179656 | tf_op jit(solution)/shard_map/ppermute | solution.py:41
  129.8 94.0 %collective-permute-start.8 = (bf16[4,768,512]{2,1,0:T(8,128)(2,1)}, bf16[4,768,512]{2,1,0:T(8,128)(2,1)}, u32[]{:S(2)}, u32[]{:S(2)}) collective-permute-start(bf16[4,768,512]{2,1,0:T(8,128)(2,1)} %bitcast.20), channel_id=1, source_target_pairs={{0,1},{1,0},{2,3},{3,2},{4,5},{5,4},{6,7},{7,6},{8,9},{9,8},{10,11... | collective-permute-start | bytes 9437192 | tf_op jit(solution)/shard_map/ppermute | solution.py:32
  159.3 56.5 %collective-permute-start.12 = (bf16[2,2,4,512,128]{4,3,2,1,0:T(8,128)(2,1)}, bf16[2,2,4,512,128]{4,3,2,1,0:T(8,128)(2,1)}, u32[]{:S(2)}, u32[]{:S(2)}) collective-permute-start(bf16[2,2,4,512,128]{4,3,2,1,0:T(8,128)(2,1)} %pad_maximum_fusion.4), channel_id=1, source_target_pairs={{0,1},{1,0},{2,3},{3,2},{4,5},{5,4},{6,7},{7,6},{8,9},{9,8},{10,11... | collective-permute-start | bytes 6291464 | tf_op jit(solution)/shard_map/ppermute | solution.py:32
  215.9 39.0 %collective-permute-start.21 = (bf16[4,768,512]{1,2,0:T(8,128)(2,1)}, bf16[4,768,512]{1,2,0:T(8,128)(2,1)}, u32[]{:S(2)}, u32[]{:S(2)}) collective-permute-start(bf16[4,768,512]{1,2,0:T(8,128)(2,1)} %reshape.290), channel_id=1, source_target_pairs={{0,1},{1,0},{2,3},{3,2},{4,5},{5,4},{6,7},{7,6},{8,9},{9,8},{10,11... | collective-permute-start | bytes 9437192 | tf_op jit(solution)/shard_map/ppermute | solution.py:32
  268.9 121.8 %all-gather.11.cloned.1.call-start = ((), (), s32[]{:S(2)}) async-start(), calls=%async_computation.3 | async-start | bytes 4718592 | tf_op jit(solution)/shard_map/all_gather | solution.py:324
  271.6 620.2 %all-reduce.3.cloned.1.call-start = ((), (), s32[]{:S(2)}) async-start(), calls=%async_computation.4 | async-start | bytes 16777216 | tf_op jit(solution)/shard_map/psum | solution.py:354
  393.3 52.1 %collective-permute-start.23 = (bf16[128,2048]{1,0:T(8,128)(2,1)}, bf16[128,2048]{1,0:T(8,128)(2,1)}, u32[]{:S(2)}, u32[]{:S(2)}) collective-permute-start(bf16[128,2048]{1,0:T(8,128)(2,1)} %add_convert_fusion.52), channel_id=1, source_target_pairs={{0,2},{1,3},{2,4},{3,5},{4,6},{5,7},{6,0},{7,1},{8,10},{9,11},{10,... | collective-permute-start | bytes 1572872 | tf_op jit(solution)/shard_map/ppermute | solution.py:37
  447.8 102.8 %collective-permute-start.24 = (bf16[128,2048]{1,0:T(8,128)(2,1)}, bf16[128,2048]{1,0:T(8,128)(2,1)S(1)}, u32[]{:S(2)}, u32[]{:S(2)}) collective-permute-start(bf16[128,2048]{1,0:T(8,128)(2,1)} %add_convert_fusion.50), channel_id=1, source_target_pairs={{0,2},{1,3},{2,4},{3,5},{4,6},{5,7},{6,0},{7,1},{8,10},{9,11},{10,... | collective-permute-start | bytes 1572872 | tf_op jit(solution)/shard_map/ppermute | solution.py:37
  463.9 47.1 %collective-permute-start.63 = (bf16[512,2048]{1,0:T(8,128)(2,1)}, bf16[512,2048]{1,0:T(8,128)(2,1)S(1)}, u32[]{:S(2)}, u32[]{:S(2)}) collective-permute-start(bf16[512,2048]{1,0:T(8,128)(2,1)} %get-tuple-element.72), channel_id=1, source_target_pairs={{0,8},{8,0},{16,24},{24,16},{1,9},{9,1},{17,25},{25,17},{2,10},{10... | collective-permute-start | bytes 6291464 | tf_op jit(solution)/shard_map/ppermute | solution.py:41
  465.4 46.9 %collective-permute-start.65 = (bf16[512,2048]{1,0:T(8,128)(2,1)}, bf16[512,2048]{1,0:T(8,128)(2,1)}, u32[]{:S(2)}, u32[]{:S(2)}) collective-permute-start(bf16[512,2048]{1,0:T(8,128)(2,1)} %get-tuple-element.73), channel_id=1, source_target_pairs={{0,16},{8,24},{16,0},{24,8},{1,17},{9,25},{17,1},{25,9},{2,18},{10... | collective-permute-start | bytes 6291464 | tf_op jit(solution)/shard_map/ppermute | solution.py:41
  518.2 54.5 %collective-permute-start.64 = (bf16[512,2048]{1,0:T(8,128)(2,1)}, bf16[512,2048]{1,0:T(8,128)(2,1)}, u32[]{:S(2)}, u32[]{:S(2)}) collective-permute-start(bf16[512,2048]{1,0:T(8,128)(2,1)} %get-tuple-element.70), channel_id=1, source_target_pairs={{0,16},{8,24},{16,0},{24,8},{1,17},{9,25},{17,1},{25,9},{2,18},{10... | collective-permute-start | bytes 6291464 | tf_op jit(solution)/shard_map/ppermute | solution.py:41
  550.6 93.9 %collective-permute-start.38 = (bf16[1024,2048]{1,0:T(8,128)(2,1)}, bf16[1024,2048]{1,0:T(8,128)(2,1)}, u32[]{:S(2)}, u32[]{:S(2)}) collective-permute-start(bf16[1024,2048]{1,0:T(8,128)(2,1)} %convolution_convert_fusion.2), channel_id=1, source_target_pairs={{0,1},{1,0},{2,3},{3,2},{4,5},{5,4},{6,7},{7,6},{8,9},{9,8},{10,11... | collective-permute-start | bytes 12582920 | tf_op jit(solution)/shard_map/ppermute | solution.py:32
  554.7 81.4 %collective-permute-start.66 = (bf16[512,2048]{1,0:T(8,128)(2,1)}, bf16[512,2048]{1,0:T(8,128)(2,1)}, u32[]{:S(2)}, u32[]{:S(2)}) collective-permute-start(bf16[512,2048]{1,0:T(8,128)(2,1)} %get-tuple-element.71), channel_id=1, source_target_pairs={{0,8},{8,0},{16,24},{24,16},{1,9},{9,1},{17,25},{25,17},{2,10},{10... | collective-permute-start | bytes 6291464 | tf_op jit(solution)/shard_map/ppermute | solution.py:41
  676.5 69.6 %collective-permute-start.57 = (bf16[256,2048]{1,0:T(8,128)(2,1)}, bf16[256,2048]{1,0:T(8,128)(2,1)}, u32[]{:S(2)}, u32[]{:S(2)}) collective-permute-start(bf16[256,2048]{1,0:T(8,128)(2,1)} %add_convert_fusion.16), channel_id=1, source_target_pairs={{0,2},{1,3},{2,4},{3,5},{4,6},{5,7},{6,0},{7,1},{8,10},{9,11},{10,... | collective-permute-start | bytes 3145736 | tf_op jit(solution)/shard_map/ppermute | solution.py:37
  748.3 46.2 %collective-permute-start.58 = (bf16[256,2048]{1,0:T(8,128)(2,1)S(1)}, bf16[256,2048]{1,0:T(8,128)(2,1)S(1)}, u32[]{:S(2)}, u32[]{:S(2)}) collective-permute-start(bf16[256,2048]{1,0:T(8,128)(2,1)S(1)} %add_convert_fusion.7), channel_id=1, source_target_pairs={{0,2},{1,3},{2,4},{3,5},{4,6},{5,7},{6,0},{7,1},{8,10},{9,11},{10,... | collective-permute-start | bytes 3145736 | tf_op jit(solution)/shard_map/ppermute | solution.py:37
  753.9 78.2 %collective-permute-start.48 = (f32[2,2048]{1,0:T(2,128)S(1)}, f32[2,2048]{1,0:T(2,128)S(1)}, u32[]{:S(2)}, u32[]{:S(2)}) collective-permute-start(f32[2,2048]{1,0:T(2,128)S(1)} %add.677), channel_id=1, source_target_pairs={{0,16},{8,24},{16,0},{24,8},{1,17},{9,25},{17,1},{25,9},{2,18},{10... | collective-permute-start | bytes 49160 | tf_op jit(solution)/shard_map/ppermute | solution.py:41
  755.6 50.2 %collective-permute-start.41 = (bf16[2,2,4,128,128]{3,4,2,1,0:T(8,128)(2,1)S(1)}, bf16[2,2,4,128,128]{3,4,2,1,0:T(8,128)(2,1)S(1)}, u32[]{:S(2)}, u32[]{:S(2)}) collective-permute-start(bf16[2,2,4,128,128]{3,4,2,1,0:T(8,128)(2,1)S(1)} %add_convert_fusion.28), channel_id=1, source_target_pairs={{0,2},{1,3},{2,4},{3,5},{4,6},{5,7},{6,0},{7,1},{8,10},{9,11},{10,... | collective-permute-start | bytes 1572872 | tf_op jit(solution)/shard_map/ppermute | solution.py:37
  773.8 54.4 %collective-permute-start.51 = (bf16[256,2048]{1,0:T(8,128)(2,1)S(1)}, bf16[256,2048]{1,0:T(8,128)(2,1)S(1)}, u32[]{:S(2)}, u32[]{:S(2)}) collective-permute-start(bf16[256,2048]{1,0:T(8,128)(2,1)S(1)} %add_convert_fusion.13), channel_id=1, source_target_pairs={{0,2},{1,3},{2,4},{3,5},{4,6},{5,7},{6,0},{7,1},{8,10},{9,11},{10,... | collective-permute-start | bytes 3145736 | tf_op jit(solution)/shard_map/ppermute | solution.py:37
  839.7 41.4 %collective-permute-start.43 = (bf16[2,2,4,128,128]{3,4,2,1,0:T(8,128)(2,1)S(1)}, bf16[2,2,4,128,128]{3,4,2,1,0:T(8,128)(2,1)S(1)}, u32[]{:S(2)}, u32[]{:S(2)}) collective-permute-start(bf16[2,2,4,128,128]{3,4,2,1,0:T(8,128)(2,1)S(1)} %add_convert_fusion.24), channel_id=1, source_target_pairs={{0,2},{1,3},{2,4},{3,5},{4,6},{5,7},{6,0},{7,1},{8,10},{9,11},{10,... | collective-permute-start | bytes 1572872 | tf_op jit(solution)/shard_map/ppermute | solution.py:37
  (132 other events, 2726.4 us)
Sparse Core Ops, SparseCore 0:
  12.5 69.9 all-gather.6
  84.1 71.1 all-gather.4
  269.0 48.2 all-gather.8
  318.8 45.8 all-gather.10
  562.5 205.5 all-reduce.2

commit v4 on v3

--- a/solution.py
+++ b/solution.py
@@ -115,12 +115,13 @@
 
 
 class Weight:
-    def __init__(self, shard, chips, rows, row_at, order, dep=None):
+    def __init__(self, shard, chips, rows, row_at, order, dep=None, beside=None):
         seq = 2 * chips
         self.chips, self.row_at, self.order = chips, row_at, order
         depth, width = shard.shape
         self.depth = depth
         self.split = rows == 4 and depth % 32 == 0 and width % 512 == 0
+        self.beside = beside
         if not self.split:
             self.whole = lax.all_gather(shard, "seq", axis=0, tiled=True)
             self.token = dep
@@ -130,6 +131,9 @@
         mine = lax.dynamic_slice_in_dim(shard, row_at * part, part, axis=1)
         slots, self.token = ring_gather(mine, chips, dep=dep)
         first = jnp.stack([v[:half] for v in slots[1:]])
+        self.beside = beside
+        if beside is not None:
+            first, self.beside = lax.optimization_barrier((first, beside))
         second = jnp.stack([v[half:] for v in slots[1:]])
         first_x = swap_row(first, rows, 1)
         second_y = swap_row(second, rows, 2)
@@ -254,16 +258,17 @@
         (query_pos < lengths[r]).astype(F32).reshape(seg_len, 1) for r in range(rows_here)
     ]
     grad_out = [cotangent[r].astype(F32) * live[r] for r in range(rows_here)]
-    grad_group = [
-        lax.all_gather(g.astype(BF16), "seq", axis=0, tiled=True) for g in grad_out
-    ]
-
-    query_proj = Weight(query_weight, chips, rows, row_at, order)
+    gate_up_weight = jnp.concatenate([ffn_in_weight[:, 0], ffn_in_weight[:, 1]], axis=0)
+    query_proj = Weight(query_weight, chips, rows, row_at, order, beside=gate_up_weight)
+    gate_up_weight = query_proj.beside
     cache_own = kv_cache.reshape(rows_here, seg_len, 2, KV, HEAD).transpose(2, 0, 3, 1, 4)
     cache_slots, token = ring_gather(cache_own, chips, dep=query_proj.token)
     cache_block = jnp.concatenate(cache_slots, axis=3)
     cache_all = jnp.concatenate([cache_block, swap_core(cache_block, seq)], axis=3)
     output_proj = Weight(output_weight, chips, rows, row_at, order, dep=token)
+    grad_group = [
+        lax.all_gather(g.astype(BF16), "seq", axis=0, tiled=True) for g in grad_out
+    ]
     per = chips // KV
 
     def to_slots(value):
@@ -301,7 +306,8 @@
     inputs = tokens.astype(F32).reshape(rows_here * seg_len, width)
     inverse_one = lax.rsqrt(jnp.mean(inputs * inputs, axis=-1, keepdims=True) + EPS)
     normed_one = (inputs * inverse_one * gain_one).astype(BF16)
-    query = tie(query_proj.features(normed_one), grad_group)
+    query = query_proj.features(normed_one)
+    query, grad_group[0] = lax.optimization_barrier((query, grad_group[0]))
     cache_slot = to_slots(cache_all)
     keys, values = cache_slot[0], cache_slot[1]
     query_heads = to_heads(query)
@@ -313,6 +319,7 @@
     mixed_heads = heads_dot("rjqk,rjkd->rjqd", weights.astype(BF16), values) / total
     lse = best + jnp.log(total)
     mixed = from_heads(mixed_heads.astype(BF16))
+    mixed, grad_group[1:] = lax.optimization_barrier((mixed, grad_group[1:]))
     middle_all = inputs + output_proj.back(mixed)
     inverse_all = lax.rsqrt(jnp.mean(middle_all * middle_all, axis=-1, keepdims=True) + EPS)
     normed_all = (middle_all * inverse_all * gain_two).astype(BF16)
@@ -324,43 +331,48 @@
     normed_group = [lax.all_gather(n, "seq", axis=0, tiled=True) for n in normed_two]
 
     main, fill = Lane(), Lane()
-    hidden, grad_gate, grad_up = [], [], []
+    units = down_weight.shape[0]
+    hidden, grad_gate_up, grad_part, ffn_part = [], [], [], []
     for r in range(rows_here):
-        kept = jnp.einsum(
-            "td,nkd->tkn", beside(normed_group[r], main), ffn_in_weight, preferred_element_type=F32
-        )
-        gate, upper = kept[:, 0], kept[:, 1]
+        kept = dot(beside(normed_group[r], main), gate_up_weight, ((1,), (1,)))
+        gate, upper = kept[:, :units], kept[:, units:]
         sigma = jax.nn.sigmoid(gate)
         grad_hidden = dot(beside(grad_group[r], main), down_weight, ((1,), (1,)))
         hidden.append((gate * sigma * upper).astype(BF16))
-        grad_gate.append(
-            (grad_hidden * upper * sigma * (1.0 + gate * (1.0 - sigma))).astype(BF16)
-        )
-        grad_up.append((grad_hidden * gate * sigma).astype(BF16))
-        pair = beside(jnp.stack([grad_gate[r], grad_up[r]], axis=1), main)
-        part = jnp.einsum("tkn,nkd->td", pair, ffn_in_weight, preferred_element_type=F32)
-        main.add(("grad", r), scatter_tokens(part.astype(BF16), chips, place, core))
-        part = dot(hidden[r], down_weight, ((1,), (0,))).astype(BF16)
-        fill.add(("ffn", r), scatter_tokens(part, chips, place, core))
-
-    def over_tokens(left, right):
-        return sum(
-            dot(a, b, ((0,), (0,))) for a, b in zip(left, right, strict=True)
-        ).astype(BF16)
-
-    down_part = over_tokens(hidden, grad_group)
-    gate_part = over_tokens(grad_gate, normed_group)
-    up_part = over_tokens(grad_up, normed_group)
-    gate_grad, up_grad = lax.psum((gate_part, up_part), "rows")
+        grad_gate = grad_hidden * upper * sigma * (1.0 + gate * (1.0 - sigma))
+        grad_up = grad_hidden * gate * sigma
+        grad_gate_up.append(jnp.concatenate([grad_gate, grad_up], axis=1).astype(BF16))
+        part = dot(beside(grad_gate_up[r], main), gate_up_weight, ((1,), (0,))).astype(BF16)
+        grad_part.append(part)
+        ffn_part.append(dot(hidden[r], down_weight, ((1,), (0,))).astype(BF16))
+        main.add(("grad", r), scatter_tokens(part, chips, place, core))
+
+    def over_tokens(left, right, start, size):
+        total = 0.0
+        for r in range(rows_here):
+            part = left[r][:, start : start + size]
+            total += dot(part, right[r], ((0,), (0,)))
+        return total.astype(BF16)
+
+    gate_part = over_tokens(grad_gate_up, normed_group, 0, units)
+    up_part = over_tokens(grad_gate_up, normed_group, units, units)
+    down_part = over_tokens(hidden, grad_group, 0, units)
+    parts = (gate_part, up_part, down_part)
+    summed = lax.psum(parts, "rows")
 
     grad_middle, gain_two_grad = [], 0.0
     for r in range(rows_here):
         grad_normed_two = main.result(("grad", r))
+        if r:
+            grad_normed_two, parts = lax.optimization_barrier((grad_normed_two, parts))
         scaled_two = middle[r] * inverse_two[r]
         gain_two_grad += jnp.sum(grad_normed_two * scaled_two, axis=0)
         grad_middle.append(
             grad_out[r] + norm_back(grad_normed_two, scaled_two, inverse_two[r], gain_two)
         )
+    for r in range(rows_here):
+        part = tie(ffn_part[r], grad_middle[-1]) if r else ffn_part[r]
+        fill.add(("ffn", r), scatter_tokens(part, chips, place, core))
     grad_middle = jnp.concatenate(grad_middle, axis=0)
     grad_branch = beside(grad_middle.astype(BF16), fill)
     output_part = [dot(half, grad_branch, ((0,), (0,))).astype(BF16) for half in mixed]
@@ -407,16 +419,18 @@
     input_grad = grad_middle + norm_back(grad_normed_one, scaled_one, inverse_one, gain_one)
     gain_grad = sum_all(jnp.stack([gain_one_grad, gain_two_grad]), rows, seq)
 
-    output_grad = sum_rows(main.result("output"), rows)
     layer_out = [
         (live[r] * (middle[r] + fill.result(("ffn", r)))).astype(BF16) for r in range(rows_here)
     ]
     cache_grad = fill.result("cache")
     cache_grad = cache_grad.transpose(1, 3, 0, 2, 4).reshape(rows_here, seg_len, 2, KV * HEAD)
-    query_grad = sum_rows(main.result("query"), rows)
-    down_grad = sum_rows(down_part, rows)
-    gate_grad, up_grad = lax.optimization_barrier((gate_grad, up_grad, query_grad))[:2]
-    in_grad = jnp.stack([gate_grad, up_grad], axis=1)
+    summed, output_sum, query_sum = lax.optimization_barrier(
+        (summed, main.result("output").astype(BF16), main.result("query").astype(BF16))
+    )
+    gate_grad, up_grad, down_grad = summed
+    output_grad, query_grad = sum_rows(output_sum, rows), sum_rows(query_sum, rows)
+    in_grad = jnp.concatenate([gate_grad, up_grad], axis=1)
+    in_grad = lax.optimization_barrier(in_grad.reshape(units, 2, width))
     return (
         jnp.stack(layer_out),
         input_grad.reshape(rows_here, seg_len, width),
@@ -425,7 +439,7 @@
         query_grad,
         output_grad,
         in_grad.astype(F32),
-        down_grad,
+        down_grad.astype(F32),
     )
 
 

time: 948 us -> 954 us (level)
  local copies, waits for them, and re-layouts: 116 us -> 147 us
  starting transfers between devices: 72.2 us -> 51.4 us
  waiting for transfers between devices: 384 us -> 366 us
  other arithmetic: 122 us -> 136 us
    dot_general x4 -> x0, matrix products: 57.8 us -> none  [the longest x2 33 us: local(): jnp.einsum('td,nkd->tkn', beside(normed_group[r], main), ffn_in_weight, p...]
    ppermute x22 -> x18, waiting for transfers between devices: 91.7 us -> 34.9 us  [swap_row(): return lax.ppermute(value, 'rows', [(r, r ^ mask) for r in range(rows)])]
    dot_general x22 -> x26, matrix products: 102 us -> 157 us  [dot(): lax.dot_general(left, right, (dims, ((), ())), preferred_element_type=F32)]
    ppermute x3, waiting for transfers between devices: 1.33 us -> 42 us  [sum_all(): lax.ppermute(value, 'seq', [(s, s ^ mask) for s in range(seq)])]
    unnamed x179 -> x204, local copies, waits for them, and re-layouts: 52.7 us -> 32.7 us
    concatenate x0 -> x3, other arithmetic: none -> 16.9 us  [the longest x1 8.62 us: local(): jnp.concatenate([ffn_in_weight[:, 0], ffn_in_weight[:, 1]], axis=0)]
    slice x0 -> x1, local copies, waits for them, and re-layouts: none -> 16.6 us  [local(): ffn_in_weight[:, 0]]
    reshape x0 -> x1, local copies, waits for them, and re-layouts: none -> 14.5 us  [local(): in_grad = lax.optimization_barrier(in_grad.reshape(units, 2, width))]
  transfers between devices with their start and end apart: 72 -> 68, of which waited for: 34 -> 31; matrix products, arithmetic and copies ran while one was open for 43% -> 51% of each run, Pallas kernels for 0% -> 0%
where the time goes in v4:
time: 954 us; the launch traced here: 942 us
  waiting for transfers between devices  366 us (38%)
  matrix products  225 us (24%)
  local copies, waits for them, and re-layouts  147 us (15%)
  other arithmetic  136 us (14%)
  starting transfers between devices  51.4 us (5%)
  between operations  16.2 us (2%)
    ppermute x30, waiting for transfers between devices, ring(): return lax.ppermute(value, 'seq', pairs)  241 us
    dot_general x26, matrix products, dot(): lax.dot_general(left, right, (dims, ((), ())), preferred_element_type=F32)  157 us
    all_gather x2, waiting for transfers between devices, local(): lax.all_gather(n, 'seq', axis=0, tiled=True)  47.7 us
    dot_general x6, matrix products, heads_dot(): return jnp.einsum(spec, left, right, preferred_element_type=F32)  43.9 us
    ppermute x3, waiting for transfers between devices, sum_all(): lax.ppermute(value, 'seq', [(s, s ^ mask) for s in range(seq)])  42 us
    ppermute x18, waiting for transfers between devices, swap_row(): return lax.ppermute(value, 'rows', [(r, r ^ mask) for r in range(rows)])  34.9 us
    unnamed x204, local copies, waits for them, and re-layouts  32.7 us
    ppermute x30, starting transfers between devices, ring(): return lax.ppermute(value, 'seq', pairs)  25.4 us
  transfers between devices with their start and end apart: 68, of which 31 were waited for; matrix products, arithmetic and copies ran while one was open for 51% of the time, Pallas kernels for 0%

profile of v4, /device:TPU:0, one launch (start us, length us, event | category | flops | bytes accessed | tf_op | source)
XLA Modules:
  0.0 942.0 jit_solution(3731489266950948146)
XLA Ops:
  29.0 16.6 %fusion.71 = (bf16[1024,1,2048]{2,1,0:T(2,128)(2,1)S(1)}, bf16[1024,1,2048]{2,1,0:T(2,128)(2,1)S(1)}) fusion(bf16[1024,2,2048]{2,1,0:T(2,128)(2,1)} %param.15), kind=kLoop, calls=%fused_computation.286 | loop fusion | bytes 16777216 | tf_op jit(solution)/shard_map/slice | solution.py:261
  53.6 8.6 pad_maximum_fusion
  78.3 12.8 %collective-permute-done.2 = bf16[256,512]{1,0:T(8,128)(2,1)S(1)} collective-permute-done((bf16[256,512]{1,0:T(8,128)(2,1)S(1)}, bf16[256,512]{1,0:T(8,128)(2,1)S(1)}, u32[]{:S(2)}, u32[]{:S(2)}) %collective-permute-start.2) | collective-permute-done | bytes 262176 | tf_op jit(solution)/shard_map/ppermute | solution.py:37
  94.6 18.6 %collective-permute-done.9 = bf16[2,2,4,128,128]{4,3,2,1,0:T(8,128)(2,1)} collective-permute-done((bf16[2,2,4,128,128]{4,3,2,1,0:T(8,128)(2,1)}, bf16[2,2,4,128,128]{4,3,2,1,0:T(8,128)(2,1)}, u32[]{:S(2)}, u32[]{:S(2)}) %collective-permute-start.9) | collective-permute-done | bytes 524320 | tf_op jit(solution)/shard_map/ppermute | solution.py:37
  113.2 10.8 %collective-permute-start.10 = (bf16[2,2,4,128,128]{4,3,2,1,0:T(8,128)(2,1)}, bf16[2,2,4,128,128]{4,3,2,1,0:T(8,128)(2,1)}, u32[]{:S(2)}, u32[]{:S(2)}) collective-permute-start(bf16[2,2,4,128,128]{4,3,2,1,0:T(8,128)(2,1)} %collective-permute-done.9), channel_id=1, source_target_pairs={{0,2},{1,3},{2,4},{3,5},{4,6},{5,7},{6,0},{7,1},{8,10},{9,11},{10,... | collective-permute-start | bytes 1572872 | tf_op jit(solution)/shard_map/ppermute | solution.py:37
  284.3 47.7 %all-gather.9.cloned.1.call-done = bf16[1024,2048]{1,0:T(8,128)(2,1)} async-done(((bf16[128,2048]{1,0:T(8,128)(2,1)}), bf16[1024,2048]{1,0:T(8,128)(2,1)}) %all-gather.9.cloned.1.call-update) | async-done | bytes 4194320 | tf_op jit(solution)/shard_map/all_gather | solution.py:331
  331.9 14.9 %fusion.83 = f32[1024,2048]{1,0:T(8,128)} fusion(bf16[1024,2048]{1,0:T(8,128)(2,1)} %all-gather.9.cloned.1.call-done, bf16[2048,2048]{1,0:T(8,128)(2,1)} %pad_maximum_fusion), kind=kOutput, calls=%fused_computation.298 | convolution fusion | flops 8589934592 | bytes 20971520 | tf_op jit(solution)/shard_map/dot_general | solution.py:17
  346.8 10.2 %multiply_convert_fusion.6 = (bf16[1024,1024]{1,0:T(8,128)(2,1)}, bf16[1024,1024]{1,0:T(8,128)(2,1)S(1)}, bf16[1024,1024]{1,0:T(8,128)(2,1)}) fusion(f32[1024,2048]{1,0:T(8,128)} %fusion.83, bf16[1024,2048]{1,0:T(8,128)(2,1)S(1)} %copy-done.83, bf16[1024,2048]{1,0:T(8,128)(2,1)S(1)} %copy-done.81), kind=kOutput, calls=%fused_computation.42 | convolution fusion | flops 4311744512 | bytes 23068672 | tf_op jit(solution)/shard_map/dot_general | solution.py:17
  357.1 11.2 %fusion.20 = bf16[1024,2048]{1,0:T(8,128)(2,1)S(1)} fusion(bf16[2048,2048]{1,0:T(8,128)(2,1)S(1)} %bitcast.258, bf16[1024,1024]{1,0:T(8,128)(2,1)S(1)} %get-tuple-element.89, bf16[1024,1024]{1,0:T(8,128)(2,1)} %get-tuple-element.88), kind=kOutput, calls=%fused_computation.52 | convolution fusion | flops 8600420352 | bytes 16777216 | tf_op jit(solution)/shard_map/dot_general | solution.py:17
  396.3 14.8 %fusion.84 = f32[1024,2048]{1,0:T(8,128)} fusion(bf16[1024,2048]{1,0:T(8,128)(2,1)} %all-gather.11.cloned.1.call-done, bf16[2048,2048]{1,0:T(8,128)(2,1)} %pad_maximum_fusion), kind=kOutput, calls=%fused_computation.299 | convolution fusion | flops 8589934592 | bytes 20971520 | tf_op jit(solution)/shard_map/dot_general | solution.py:17
  416.7 13.3 %multiply_convert_fusion.3 = (bf16[1024,1024]{1,0:T(8,128)(2,1)S(1)}, bf16[1024,1024]{1,0:T(8,128)(2,1)S(1)}, bf16[1024,1024]{1,0:T(8,128)(2,1)}) fusion(f32[1024,2048]{1,0:T(8,128)} %fusion.84, bf16[1024,2048]{1,0:T(8,128)(2,1)} %all-gather.7.cloned.1.call-done, bf16[1024,2048]{1,0:T(8,128)(2,1)} %param.16), kind=kOutput, calls=%fused_computation.38 | convolution fusion | flops 4311744512 | bytes 23068672 | tf_op jit(solution)/shard_map/dot_general | solution.py:17
  441.8 9.1 convolution_convert_fusion.4
  473.5 9.2 add_convert_fusion.2
  524.7 9.8 %collective-permute-done.37 = bf16[128,2048]{1,0:T(8,128)(2,1)S(1)} collective-permute-done((bf16[128,2048]{1,0:T(8,128)(2,1)S(1)}, bf16[128,2048]{1,0:T(8,128)(2,1)S(1)}, u32[]{:S(2)}, u32[]{:S(2)}) %collective-permute-start.37) | collective-permute-done | bytes 524320 | tf_op jit(solution)/shard_map/ppermute | solution.py:37
  550.3 16.1 %collective-permute-done.34 = bf16[128,2048]{1,0:T(8,128)(2,1)S(1)} collective-permute-done((bf16[128,2048]{1,0:T(8,128)(2,1)S(1)}, bf16[128,2048]{1,0:T(8,128)(2,1)S(1)}, u32[]{:S(2)}, u32[]{:S(2)}) %collective-permute-start.34) | collective-permute-done | bytes 524320 | tf_op jit(solution)/shard_map/ppermute | solution.py:37
  568.8 14.3 %collective-permute-done.35 = bf16[128,2048]{1,0:T(8,128)(2,1)} collective-permute-done((bf16[128,2048]{1,0:T(8,128)(2,1)}, bf16[128,2048]{1,0:T(8,128)(2,1)}, u32[]{:S(2)}, u32[]{:S(2)}) %collective-permute-start.35) | collective-permute-done | bytes 524320 | tf_op jit(solution)/shard_map/ppermute | solution.py:37
  588.9 11.4 %collective-permute-done.36 = bf16[128,2048]{1,0:T(8,128)(2,1)} collective-permute-done((bf16[128,2048]{1,0:T(8,128)(2,1)}, bf16[128,2048]{1,0:T(8,128)(2,1)}, u32[]{:S(2)}, u32[]{:S(2)}) %collective-permute-start.36) | collective-permute-done | bytes 524320 | tf_op jit(solution)/shard_map/ppermute | solution.py:37
  635.3 12.0 %multiply_convert_fusion = bf16[2,4,512,1024]{3,2,1,0:T(8,128)(2,1)} fusion(f32[2,4,512,1024]{3,2,1,0:T(8,128)} %copy-done, f32[2,4,512]{2,1,0:T(4,128)S(1)} %multiply_reduce_fusion.2, f32[2,4,512]{2,1,0:T(4,128)S(1)} %bitcast.306, pred[2,512,1024]{2,1,0:T(8,128)(4,1)S(1)} %copy-done.16, bf16[2,4,512,128]{3,2,1,0:T(8,128)(2,1)S(1)} %bitcast.270, ...), kind=kOutput, calls=%fused_computation | convolution fusion | flops 1098907648 | bytes 29392896 | tf_op jit(solution)/shard_map/rjqd,rjkd->rjqk/dot_general | solution.py:298
  709.4 42.0 %collective-permute-done.46 = f32[2,2048]{1,0:T(2,128)S(1)} collective-permute-done((f32[2,2048]{1,0:T(2,128)S(1)}, f32[2,2048]{1,0:T(2,128)S(1)}, u32[]{:S(2)}, u32[]{:S(2)}) %collective-permute-start.46) | collective-permute-done | bytes 16416 | tf_op jit(solution)/shard_map/ppermute | solution.py:223
  764.2 22.4 %collective-permute-done.53 = bf16[256,2048]{1,0:T(8,128)(2,1)S(1)} collective-permute-done((bf16[256,2048]{1,0:T(8,128)(2,1)S(1)}, bf16[256,2048]{1,0:T(8,128)(2,1)S(1)}, u32[]{:S(2)}, u32[]{:S(2)}) %collective-permute-start.53) | collective-permute-done | bytes 1048608 | tf_op jit(solution)/shard_map/ppermute | solution.py:37
  788.5 31.8 %collective-permute-done.41 = bf16[2,2,4,128,128]{3,4,2,1,0:T(8,128)(2,1)S(1)} collective-permute-done((bf16[2,2,4,128,128]{3,4,2,1,0:T(8,128)(2,1)S(1)}, bf16[2,2,4,128,128]{3,4,2,1,0:T(8,128)(2,1)S(1)}, u32[]{:S(2)}, u32[]{:S(2)}) %collective-permute-start.41) | collective-permute-done | bytes 524320 | tf_op jit(solution)/shard_map/ppermute | solution.py:37
  822.4 29.1 %collective-permute-done.42 = bf16[2,2,4,128,128]{3,4,2,1,0:T(8,128)(2,1)S(1)} collective-permute-done((bf16[2,2,4,128,128]{3,4,2,1,0:T(8,128)(2,1)S(1)}, bf16[2,2,4,128,128]{3,4,2,1,0:T(8,128)(2,1)S(1)}, u32[]{:S(2)}, u32[]{:S(2)}) %collective-permute-start.42) | collective-permute-done | bytes 524320 | tf_op jit(solution)/shard_map/ppermute | solution.py:37
  881.6 14.5 %reshape.307 = bf16[1024,2,2048]{2,1,0:T(2,128)(2,1)} reshape(bf16[1024,4096]{1,0:T(8,128)(2,1)} %pad_maximum_fusion.1) | data formatting | bytes 16777216 | tf_op jit(solution)/shard_map/reshape | solution.py:433
  896.1 11.9 %convert_element_type.848 = f32[1024,2,2048]{2,1,0:T(2,128)} convert(bf16[1024,2,2048]{2,1,0:T(2,128)(2,1)} %reshape.307) | non-fusion elementwise | flops 4194304 | bytes 25165824 | tf_op jit(solution)/shard_map/convert_element_type | solution.py:441
  (529 shorter events, 512.8 us)
Async XLA Ops:
  7.2 225.1 %all-gather.5.cloned.1.call-start = ((), (), s32[]{:S(2)}) async-start(), calls=%async_computation | async-start | bytes 4718592 | tf_op jit(solution)/shard_map/all_gather | solution.py:270
  12.9 254.3 %all-gather.7.cloned.1.call-start = ((), (), s32[]{:S(2)}) async-start(), calls=%async_computation.1 | async-start | bytes 4718592 | tf_op jit(solution)/shard_map/all_gather | solution.py:270
  13.0 165.6 %collective-permute-start.7 = (bf16[256,2048]{1,0:T(8,128)(2,1)}, bf16[256,2048]{1,0:T(8,128)(2,1)}, u32[]{:S(2)}, u32[]{:S(2)}) collective-permute-start(bf16[256,2048]{1,0:T(8,128)(2,1)} %param.13), channel_id=1, source_target_pairs={{0,1},{1,0},{2,3},{3,2},{4,5},{5,4},{6,7},{7,6},{8,9},{9,8},{10,11... | collective-permute-start | bytes 3145736 | tf_op jit(solution)/shard_map/ppermute | solution.py:32
  14.5 49.4 %collective-permute-start = (bf16[256,512]{1,0:T(8,128)(2,1)S(1)}, bf16[256,512]{1,0:T(8,128)(2,1)}, u32[]{:S(2)}, u32[]{:S(2)}) collective-permute-start(bf16[256,512]{1,0:T(8,128)(2,1)S(1)} %constant_dynamic-slice_fusion.17), channel_id=1, source_target_pairs={{0,2},{1,3},{2,4},{3,5},{4,6},{5,7},{6,0},{7,1},{8,10},{9,11},{10,... | collective-permute-start | bytes 786440 | tf_op jit(solution)/shard_map/ppermute | solution.py:37
  17.1 261.6 %collective-permute-start.13 = (bf16[256,2048]{1,0:T(8,128)(2,1)}, bf16[256,2048]{1,0:T(8,128)(2,1)}, u32[]{:S(2)}, u32[]{:S(2)}) collective-permute-start(bf16[256,2048]{1,0:T(8,128)(2,1)} %param.14), channel_id=1, source_target_pairs={{0,1},{1,0},{2,3},{3,2},{4,5},{5,4},{6,7},{7,6},{8,9},{9,8},{10,11... | collective-permute-start | bytes 3145736 | tf_op jit(solution)/shard_map/ppermute | solution.py:32
  17.3 314.6 %all-gather.9.cloned.1.call-start = ((), (), s32[]{:S(2)}) async-start(), calls=%async_computation.2 | async-start | bytes 4718592 | tf_op jit(solution)/shard_map/all_gather | solution.py:331
  93.0 45.7 %collective-permute-start.3 = (bf16[3,128,512]{2,1,0:T(8,128)(2,1)S(1)}, bf16[3,128,512]{2,1,0:T(8,128)(2,1)}, u32[]{:S(2)}, u32[]{:S(2)}) collective-permute-start(bf16[3,128,512]{2,1,0:T(8,128)(2,1)S(1)} %pad_maximum_fusion.23), channel_id=1, source_target_pairs={{0,8},{8,0},{16,24},{24,16},{1,9},{9,1},{17,25},{25,17},{2,10},{10... | collective-permute-start | bytes 1179656 | tf_op jit(solution)/shard_map/ppermute | solution.py:41
  161.7 66.8 %collective-permute-start.8 = (bf16[4,768,512]{2,1,0:T(8,128)(2,1)}, bf16[4,768,512]{2,1,0:T(8,128)(2,1)}, u32[]{:S(2)}, u32[]{:S(2)}) collective-permute-start(bf16[4,768,512]{2,1,0:T(8,128)(2,1)} %bitcast.22), channel_id=1, source_target_pairs={{0,1},{1,0},{2,3},{3,2},{4,5},{5,4},{6,7},{7,6},{8,9},{9,8},{10,11... | collective-permute-start | bytes 9437192 | tf_op jit(solution)/shard_map/ppermute | solution.py:32
  170.6 48.9 %collective-permute-start.12 = (bf16[2,2,4,512,128]{4,3,2,1,0:T(8,128)(2,1)}, bf16[2,2,4,512,128]{4,3,2,1,0:T(8,128)(2,1)}, u32[]{:S(2)}, u32[]{:S(2)}) collective-permute-start(bf16[2,2,4,512,128]{4,3,2,1,0:T(8,128)(2,1)} %pad_maximum_fusion.5), channel_id=1, source_target_pairs={{0,1},{1,0},{2,3},{3,2},{4,5},{5,4},{6,7},{7,6},{8,9},{9,8},{10,11... | collective-permute-start | bytes 6291464 | tf_op jit(solution)/shard_map/ppermute | solution.py:32
  219.4 50.0 %collective-permute-start.21 = (bf16[4,768,512]{1,2,0:T(8,128)(2,1)S(1)}, bf16[4,768,512]{1,2,0:T(8,128)(2,1)}, u32[]{:S(2)}, u32[]{:S(2)}) collective-permute-start(bf16[4,768,512]{1,2,0:T(8,128)(2,1)S(1)} %reshape.293), channel_id=1, source_target_pairs={{0,1},{1,0},{2,3},{3,2},{4,5},{5,4},{6,7},{7,6},{8,9},{9,8},{10,11... | collective-permute-start | bytes 9437192 | tf_op jit(solution)/shard_map/ppermute | solution.py:32
  283.4 112.8 %all-gather.11.cloned.1.call-start = ((), (), s32[]{:S(2)}) async-start(), calls=%async_computation.3 | async-start | bytes 4718592 | tf_op jit(solution)/shard_map/all_gather | solution.py:331
  284.2 569.3 %all-reduce.3.cloned.1.call-start = ((), (), s32[]{:S(2)}) async-start(), calls=%async_computation.4 | async-start | bytes 25165824 | tf_op jit(solution)/shard_map/psum | solution.py:361
  412.6 49.5 %collective-permute-start.23 = (bf16[128,2048]{1,0:T(8,128)(2,1)S(1)}, bf16[128,2048]{1,0:T(8,128)(2,1)S(1)}, u32[]{:S(2)}, u32[]{:S(2)}) collective-permute-start(bf16[128,2048]{1,0:T(8,128)(2,1)S(1)} %add_convert_fusion.50), channel_id=1, source_target_pairs={{0,2},{1,3},{2,4},{3,5},{4,6},{5,7},{6,0},{7,1},{8,10},{9,11},{10,... | collective-permute-start | bytes 1572872 | tf_op jit(solution)/shard_map/ppermute | solution.py:37
  464.2 50.1 %collective-permute-start.24 = (bf16[128,2048]{1,0:T(8,128)(2,1)}, bf16[128,2048]{1,0:T(8,128)(2,1)S(1)}, u32[]{:S(2)}, u32[]{:S(2)}) collective-permute-start(bf16[128,2048]{1,0:T(8,128)(2,1)} %add_convert_fusion.48), channel_id=1, source_target_pairs={{0,2},{1,3},{2,4},{3,5},{4,6},{5,7},{6,0},{7,1},{8,10},{9,11},{10,... | collective-permute-start | bytes 1572872 | tf_op jit(solution)/shard_map/ppermute | solution.py:37
  550.1 53.0 %collective-permute-start.38 = (bf16[1024,2048]{1,0:T(8,128)(2,1)}, bf16[1024,2048]{1,0:T(8,128)(2,1)}, u32[]{:S(2)}, u32[]{:S(2)}) collective-permute-start(bf16[1024,2048]{1,0:T(8,128)(2,1)} %convolution_convert_fusion.2), channel_id=1, source_target_pairs={{0,1},{1,0},{2,3},{3,2},{4,5},{5,4},{6,7},{7,6},{8,9},{9,8},{10,11... | collective-permute-start | bytes 12582920 | tf_op jit(solution)/shard_map/ppermute | solution.py:32
  701.1 55.7 %collective-permute-start.52 = (bf16[256,2048]{1,0:T(8,128)(2,1)S(1)}, bf16[256,2048]{1,0:T(8,128)(2,1)S(1)}, u32[]{:S(2)}, u32[]{:S(2)}) collective-permute-start(bf16[256,2048]{1,0:T(8,128)(2,1)S(1)} %add_convert_fusion.9), channel_id=1, source_target_pairs={{0,2},{1,3},{2,4},{3,5},{4,6},{5,7},{6,0},{7,1},{8,10},{9,11},{10,... | collective-permute-start | bytes 3145736 | tf_op jit(solution)/shard_map/ppermute | solution.py:37
  705.6 58.3 %collective-permute-start.40 = (bf16[2,2,4,512,128]{3,4,2,1,0:T(8,128)(2,1)S(1)}, bf16[2,2,4,512,128]{3,4,2,1,0:T(8,128)(2,1)S(1)}, u32[]{:S(2)}, u32[]{:S(2)}) collective-permute-start(bf16[2,2,4,512,128]{3,4,2,1,0:T(8,128)(2,1)S(1)} %slice.455), channel_id=1, source_target_pairs={{0,1},{1,0},{2,3},{3,2},{4,5},{5,4},{6,7},{7,6},{8,9},{9,8},{10,11... | collective-permute-start | bytes 6291464 | tf_op jit(solution)/shard_map/ppermute | solution.py:32
  705.8 45.6 %collective-permute-start.46 = (f32[2,2048]{1,0:T(2,128)S(1)}, f32[2,2048]{1,0:T(2,128)S(1)}, u32[]{:S(2)}, u32[]{:S(2)}) collective-permute-start(f32[2,2048]{1,0:T(2,128)S(1)} %fusion.153), channel_id=1, source_target_pairs={{0,4},{1,5},{2,6},{3,7},{4,0},{5,1},{6,2},{7,3},{8,12},{9,13},{10,... | collective-permute-start | bytes 49160 | tf_op jit(solution)/shard_map/ppermute | solution.py:223
  708.5 52.8 %collective-permute-start.49 = (bf16[256,2048]{1,0:T(8,128)(2,1)S(1)}, bf16[256,2048]{1,0:T(8,128)(2,1)S(1)}, u32[]{:S(2)}, u32[]{:S(2)}) collective-permute-start(bf16[256,2048]{1,0:T(8,128)(2,1)S(1)} %copy-done.58), channel_id=1, source_target_pairs={{0,2},{1,3},{2,4},{3,5},{4,6},{5,7},{6,0},{7,1},{8,10},{9,11},{10,... | collective-permute-start | bytes 3145736 | tf_op jit(solution)/shard_map/ppermute | solution.py:37
  763.8 56.8 %collective-permute-start.50 = (bf16[256,2048]{1,0:T(8,128)(2,1)S(1)}, bf16[256,2048]{1,0:T(8,128)(2,1)S(1)}, u32[]{:S(2)}, u32[]{:S(2)}) collective-permute-start(bf16[256,2048]{1,0:T(8,128)(2,1)S(1)} %add_convert_fusion.12), channel_id=1, source_target_pairs={{0,2},{1,3},{2,4},{3,5},{4,6},{5,7},{6,0},{7,1},{8,10},{9,11},{10,... | collective-permute-start | bytes 3145736 | tf_op jit(solution)/shard_map/ppermute | solution.py:37
  764.1 56.2 %collective-permute-start.41 = (bf16[2,2,4,128,128]{3,4,2,1,0:T(8,128)(2,1)S(1)}, bf16[2,2,4,128,128]{3,4,2,1,0:T(8,128)(2,1)S(1)}, u32[]{:S(2)}, u32[]{:S(2)}) collective-permute-start(bf16[2,2,4,128,128]{3,4,2,1,0:T(8,128)(2,1)S(1)} %add_convert_fusion.26), channel_id=1, source_target_pairs={{0,2},{1,3},{2,4},{3,5},{4,6},{5,7},{6,0},{7,1},{8,10},{9,11},{10,... | collective-permute-start | bytes 1572872 | tf_op jit(solution)/shard_map/ppermute | solution.py:37
  788.5 63.3 %collective-permute-start.54 = (bf16[256,2048]{1,0:T(8,128)(2,1)S(1)}, bf16[256,2048]{1,0:T(8,128)(2,1)S(1)}, u32[]{:S(2)}, u32[]{:S(2)}) collective-permute-start(bf16[256,2048]{1,0:T(8,128)(2,1)S(1)} %add_convert_fusion.5), channel_id=1, source_target_pairs={{0,2},{1,3},{2,4},{3,5},{4,6},{5,7},{6,0},{7,1},{8,10},{9,11},{10,... | collective-permute-start | bytes 3145736 | tf_op jit(solution)/shard_map/ppermute | solution.py:37
  869.2 44.5 %collective-permute-start.59 = (bf16[128,2048]{1,0:T(8,128)(2,1)}, bf16[128,2048]{1,0:T(8,128)(2,1)}, u32[]{:S(2)}, u32[]{:S(2)}) collective-permute-start(bf16[128,2048]{1,0:T(8,128)(2,1)} %get-tuple-element.115), channel_id=1, source_target_pairs={{0,8},{8,0},{16,24},{24,16},{1,9},{9,1},{17,25},{25,17},{2,10},{10... | collective-permute-start | bytes 1572872 | tf_op jit(solution)/shard_map/ppermute | solution.py:41
  873.1 44.6 %collective-permute-start.58 = (bf16[128,2048]{1,0:T(8,128)(2,1)S(1)}, bf16[128,2048]{1,0:T(8,128)(2,1)}, u32[]{:S(2)}, u32[]{:S(2)}) collective-permute-start(bf16[128,2048]{1,0:T(8,128)(2,1)S(1)} %get-tuple-element.118), channel_id=1, source_target_pairs={{0,8},{8,0},{16,24},{24,16},{1,9},{9,1},{17,25},{25,17},{2,10},{10... | collective-permute-start | bytes 1572872 | tf_op jit(solution)/shard_map/ppermute | solution.py:41
  (141 other events, 2593.4 us)
Sparse Core Ops, SparseCore 0:
  13.0 49.8 all-gather.4
  64.5 62.5 all-gather.6
  283.5 48.3 all-gather.8
  333.4 45.8 all-gather.10
  586.3 242.6 all-reduce.2

commit v5 on v4

--- a/solution.py
+++ b/solution.py
@@ -115,13 +115,12 @@
 
 
 class Weight:
-    def __init__(self, shard, chips, rows, row_at, order, dep=None, beside=None):
+    def __init__(self, shard, chips, rows, row_at, order, dep=None):
         seq = 2 * chips
         self.chips, self.row_at, self.order = chips, row_at, order
         depth, width = shard.shape
         self.depth = depth
         self.split = rows == 4 and depth % 32 == 0 and width % 512 == 0
-        self.beside = beside
         if not self.split:
             self.whole = lax.all_gather(shard, "seq", axis=0, tiled=True)
             self.token = dep
@@ -131,22 +130,14 @@
         mine = lax.dynamic_slice_in_dim(shard, row_at * part, part, axis=1)
         slots, self.token = ring_gather(mine, chips, dep=dep)
         first = jnp.stack([v[:half] for v in slots[1:]])
-        self.beside = beside
-        if beside is not None:
-            first, self.beside = lax.optimization_barrier((first, beside))
         second = jnp.stack([v[half:] for v in slots[1:]])
         first_x = swap_row(first, rows, 1)
         second_y = swap_row(second, rows, 2)
         first_pair = swap_row(jnp.stack([first, first_x]), rows, 2)
         second_pair = swap_row(jnp.stack([second, second_y]), rows, 1)
-        parts = jnp.stack(
-            [
-                jnp.stack([first, first_x, first_pair[0], first_pair[1]]),
-                jnp.stack([second, second_pair[0], second_y, second_pair[1]]),
-            ],
-            axis=2,
-        )
-        parts = parts.reshape(rows, (chips - 1) * depth, part)
+        parts = [first, second, first_x, second_pair[0]]
+        parts += [first_pair[0], second_y, first_pair[1], second_pair[1]]
+        parts = jnp.concatenate(parts, axis=0).reshape(rows, (chips - 1) * depth, part)
         self.far = [parts, swap_core(parts, seq)]
         self.near = [shard, swap_core(shard, seq)]
 
@@ -162,6 +153,8 @@
         for near, far in zip(self.near, self.far, strict=True):
             term = jnp.einsum("ktc,kfc->ktf", blocks, far, preferred_element_type=F32)
             term = jnp.sum(term, axis=0).astype(BF16)
+            term = term.reshape(count, 2, self.chips - 1, -1).transpose(0, 2, 1, 3)
+            term = term.reshape(count, -1)
             out.append(jnp.concatenate([dot(value, near, ((1,), (1,))).astype(BF16), term], axis=1))
         return out
 
@@ -173,9 +166,9 @@
         near_sum = far_sum = 0.0
         for part, near, far in zip(halves, self.near, self.far, strict=True):
             near_sum += dot(part[:, : self.depth], near, ((1,), (0,)))
-            far_sum += jnp.einsum(
-                "tf,kfc->ktc", part[:, self.depth :], far, preferred_element_type=F32
-            )
+            rest = part[:, self.depth :].reshape(count, self.chips - 1, 2, -1)
+            rest = rest.transpose(0, 2, 1, 3).reshape(count, -1)
+            far_sum += jnp.einsum("tf,kfc->ktc", rest, far, preferred_element_type=F32)
         far_sum = xor_order(far_sum, self.row_at).transpose(1, 0, 2).reshape(count, -1)
         return near_sum + far_sum
 
@@ -259,15 +252,15 @@
     ]
     grad_out = [cotangent[r].astype(F32) * live[r] for r in range(rows_here)]
     gate_up_weight = jnp.concatenate([ffn_in_weight[:, 0], ffn_in_weight[:, 1]], axis=0)
-    query_proj = Weight(query_weight, chips, rows, row_at, order, beside=gate_up_weight)
-    gate_up_weight = query_proj.beside
+    query_proj = Weight(query_weight, chips, rows, row_at, order)
     cache_own = kv_cache.reshape(rows_here, seg_len, 2, KV, HEAD).transpose(2, 0, 3, 1, 4)
     cache_slots, token = ring_gather(cache_own, chips, dep=query_proj.token)
     cache_block = jnp.concatenate(cache_slots, axis=3)
     cache_all = jnp.concatenate([cache_block, swap_core(cache_block, seq)], axis=3)
     output_proj = Weight(output_weight, chips, rows, row_at, order, dep=token)
     grad_group = [
-        lax.all_gather(g.astype(BF16), "seq", axis=0, tiled=True) for g in grad_out
+        lax.all_gather(tie(g.astype(BF16), output_proj.token), "seq", axis=0, tiled=True)
+        for g in grad_out
     ]
     per = chips // KV
 
@@ -307,7 +300,6 @@
     inverse_one = lax.rsqrt(jnp.mean(inputs * inputs, axis=-1, keepdims=True) + EPS)
     normed_one = (inputs * inverse_one * gain_one).astype(BF16)
     query = query_proj.features(normed_one)
-    query, grad_group[0] = lax.optimization_barrier((query, grad_group[0]))
     cache_slot = to_slots(cache_all)
     keys, values = cache_slot[0], cache_slot[1]
     query_heads = to_heads(query)
@@ -319,10 +311,11 @@
     mixed_heads = heads_dot("rjqk,rjkd->rjqd", weights.astype(BF16), values) / total
     lse = best + jnp.log(total)
     mixed = from_heads(mixed_heads.astype(BF16))
-    mixed, grad_group[1:] = lax.optimization_barrier((mixed, grad_group[1:]))
+    mixed, grad_group[0] = lax.optimization_barrier((mixed, grad_group[0]))
     middle_all = inputs + output_proj.back(mixed)
     inverse_all = lax.rsqrt(jnp.mean(middle_all * middle_all, axis=-1, keepdims=True) + EPS)
     normed_all = (middle_all * inverse_all * gain_two).astype(BF16)
+    normed_all, grad_group[1:] = lax.optimization_barrier((normed_all, grad_group[1:]))
 
     def split(value):
         return [value[r * seg_len : (r + 1) * seg_len] for r in range(rows_here)]
@@ -357,6 +350,8 @@
     gate_part = over_tokens(grad_gate_up, normed_group, 0, units)
     up_part = over_tokens(grad_gate_up, normed_group, units, units)
     down_part = over_tokens(hidden, grad_group, 0, units)
+    for r in range(rows_here):
+        fill.add(("ffn", r), scatter_tokens(ffn_part[r], chips, place, core))
     parts = (gate_part, up_part, down_part)
     summed = lax.psum(parts, "rows")
 
@@ -370,11 +365,8 @@
         grad_middle.append(
             grad_out[r] + norm_back(grad_normed_two, scaled_two, inverse_two[r], gain_two)
         )
-    for r in range(rows_here):
-        part = tie(ffn_part[r], grad_middle[-1]) if r else ffn_part[r]
-        fill.add(("ffn", r), scatter_tokens(part, chips, place, core))
     grad_middle = jnp.concatenate(grad_middle, axis=0)
-    grad_branch = beside(grad_middle.astype(BF16), fill)
+    grad_branch = grad_middle.astype(BF16)
     output_part = [dot(half, grad_branch, ((0,), (0,))).astype(BF16) for half in mixed]
 
     def scatter_rows(parts):
@@ -384,8 +376,7 @@
         return scatter_halves(lambda j: take(parts[0], j), parts[1], take, chips)
 
     main.add("output", scatter_rows(output_part))
-    grad_heads = to_heads(output_proj.features(beside(grad_branch, main, fill)))
-    grad_heads = beside(grad_heads, main, fill)
+    grad_heads = to_heads(output_proj.features(grad_branch))
     delta = jnp.sum(grad_heads.astype(F32) * mixed_heads, axis=-1, keepdims=True)
     scores = heads_dot("rjqd,rjkd->rjqk", query_heads, keys) * scale
     probs = jnp.where(valid, jnp.exp(scores - lse), 0.0)
@@ -402,8 +393,6 @@
     def positions_of(value, j):
         return value[:, :, :, j * seg_len : (j + 1) * seg_len]
 
-    main.step()
-    fill.step()
     fill.add(
         "cache",
         scatter_halves(

time: 954 us -> 915 us (0.959)
  other arithmetic: 136 us -> 121 us
  starting transfers between devices: 51.4 us -> 37.2 us
    all_gather x2, waiting for transfers between devices: 47.7 us -> 21 us  [local(): lax.all_gather(n, 'seq', axis=0, tiled=True)]
    unnamed x204 -> x214, local copies, waits for them, and re-layouts: 32.7 us -> 48.3 us
    ppermute x30, starting transfers between devices: 25.4 us -> 12.2 us  [ring(): return lax.ppermute(value, 'seq', pairs)]
    ppermute x18, waiting for transfers between devices: 34.9 us -> 47.2 us  [swap_row(): return lax.ppermute(value, 'rows', [(r, r ^ mask) for r in range(rows)])]
  transfers between devices with their start and end apart: 68 -> 68, of which waited for: 31 -> 33; matrix products, arithmetic and copies ran while one was open for 51% -> 52% of each run, Pallas kernels for 0% -> 0%
where the time goes in v5:
time: 915 us; the launch traced here: 906 us
  waiting for transfers between devices  363 us (40%)
  matrix products  229 us (25%)
  local copies, waits for them, and re-layouts  140 us (15%)
  other arithmetic  121 us (13%)
  starting transfers between devices  37.2 us (4%)
  between operations  16.3 us (2%)
    ppermute x30, waiting for transfers between devices, ring(): return lax.ppermute(value, 'seq', pairs)  251 us
    dot_general x26, matrix products, dot(): lax.dot_general(left, right, (dims, ((), ())), preferred_element_type=F32)  158 us
    unnamed x214, local copies, waits for them, and re-layouts  48.3 us
    ppermute x18, waiting for transfers between devices, swap_row(): return lax.ppermute(value, 'rows', [(r, r ^ mask) for r in range(rows)])  47.2 us
    dot_general x6, matrix products, heads_dot(): return jnp.einsum(spec, left, right, preferred_element_type=F32)  45.8 us
    ppermute x3, waiting for transfers between devices, sum_all(): lax.ppermute(value, 'seq', [(s, s ^ mask) for s in range(seq)])  43.9 us
    convert_element_type x14, other arithmetic, ring_scatter(): sent = total.astype(BF16)  23.1 us
    all_gather x2, waiting for transfers between devices, local(): lax.all_gather(n, 'seq', axis=0, tiled=True)  21 us
  transfers between devices with their start and end apart: 68, of which 33 were waited for; matrix products, arithmetic and copies ran while one was open for 52% of the time, Pallas kernels for 0%

profile of v5, /device:TPU:0, one launch (start us, length us, event | category | flops | bytes accessed | tf_op | source)
XLA Modules:
  0.0 905.8 jit_solution(15769204520296702819)
XLA Ops:
  29.8 13.2 %collective-permute-done.9 = bf16[2,2,4,128,128]{4,3,2,1,0:T(8,128)(2,1)S(1)} collective-permute-done((bf16[2,2,4,128,128]{4,3,2,1,0:T(8,128)(2,1)S(1)}, bf16[2,2,4,128,128]{4,3,2,1,0:T(8,128)(2,1)S(1)}, u32[]{:S(2)}, u32[]{:S(2)}) %collective-permute-start.9) | collective-permute-done | bytes 524320 | tf_op jit(solution)/shard_map/ppermute | solution.py:37
  82.0 13.7 %collective-permute-done.2 = bf16[256,512]{1,0:T(8,128)(2,1)S(1)} collective-permute-done((bf16[256,512]{1,0:T(8,128)(2,1)S(1)}, bf16[256,512]{1,0:T(8,128)(2,1)S(1)}, u32[]{:S(2)}, u32[]{:S(2)}) %collective-permute-start.2) | collective-permute-done | bytes 262176 | tf_op jit(solution)/shard_map/ppermute | solution.py:37
  164.7 11.8 %collective-permute-done.19 = bf16[2,3,128,512]{3,2,1,0:T(8,128)(2,1)S(1)} collective-permute-done((bf16[2,3,128,512]{3,2,1,0:T(8,128)(2,1)S(1)}, bf16[2,3,128,512]{3,2,1,0:T(8,128)(2,1)S(1)}, u32[]{:S(2)}, u32[]{:S(2)}) %collective-permute-start.19) | collective-permute-done | bytes 786464 | tf_op jit(solution)/shard_map/ppermute | solution.py:41
  240.5 16.6 %fusion.80 = (bf16[1024,1,2048]{2,1,0:T(2,128)(2,1)S(1)}, bf16[1024,1,2048]{2,1,0:T(2,128)(2,1)S(1)}) fusion(bf16[1024,2,2048]{2,1,0:T(2,128)(2,1)} %param.15), kind=kLoop, calls=%fused_computation.312 | loop fusion | bytes 16777216 | tf_op jit(solution)/shard_map/slice | solution.py:254
  266.0 21.0 %all-gather.9.cloned.1.call-done = bf16[1024,2048]{1,0:T(8,128)(2,1)} async-done(((bf16[128,2048]{1,0:T(8,128)(2,1)}), bf16[1024,2048]{1,0:T(8,128)(2,1)}) %all-gather.9.cloned.1.call-update) | async-done | bytes 4194320 | tf_op jit(solution)/shard_map/all_gather | solution.py:324
  287.0 15.4 %fusion.75 = f32[1024,2048]{1,0:T(8,128)} fusion(bf16[1024,2048]{1,0:T(8,128)(2,1)} %all-gather.9.cloned.1.call-done, bf16[1024,2048]{1,0:T(8,128)(2,1)} %get-tuple-element.160, bf16[1024,2048]{1,0:T(8,128)(2,1)} %get-tuple-element.161), kind=kOutput, calls=%fused_computation.309 | convolution fusion | flops 8606711808 | bytes 20971520 | tf_op jit(solution)/shard_map/dot_general | solution.py:17
  302.4 11.4 %multiply_convert_fusion.6 = (bf16[1024,1024]{1,0:T(8,128)(2,1)}, bf16[1024,1024]{1,0:T(8,128)(2,1)S(1)}, bf16[1024,1024]{1,0:T(8,128)(2,1)}) fusion(f32[1024,2048]{1,0:T(8,128)} %fusion.75, bf16[1024,2048]{1,0:T(8,128)(2,1)} %all-gather.5.cloned.1.call-done, bf16[1024,2048]{1,0:T(8,128)(2,1)S(1)} %copy-done.80), kind=kOutput, calls=%fused_computation.42 | convolution fusion | flops 4311744512 | bytes 23068672 | tf_op jit(solution)/shard_map/dot_general | solution.py:17
  313.9 11.5 %fusion.20 = bf16[1024,2048]{1,0:T(8,128)(2,1)S(1)} fusion(bf16[1024,1024]{1,0:T(8,128)(2,1)S(1)} %get-tuple-element.79, bf16[1024,1024]{1,0:T(8,128)(2,1)} %get-tuple-element.78, bf16[1024,2048]{1,0:T(8,128)(2,1)S(1)} %copy-done.42, bf16[1024,2048]{1,0:T(8,128)(2,1)S(1)} %copy-done.44), kind=kOutput, calls=%fused_computation.52 | convolution fusion | flops 8617197568 | bytes 16777216 | tf_op jit(solution)/shard_map/dot_general | solution.py:17
  361.1 15.7 %fusion.74 = f32[1024,2048]{1,0:T(8,128)} fusion(bf16[1024,2048]{1,0:T(8,128)(2,1)} %all-gather.11.cloned.1.call-done, bf16[1024,2048]{1,0:T(8,128)(2,1)} %get-tuple-element.160, bf16[1024,2048]{1,0:T(8,128)(2,1)} %get-tuple-element.161), kind=kOutput, calls=%fused_computation.308 | convolution fusion | flops 8606711808 | bytes 20971520 | tf_op jit(solution)/shard_map/dot_general | solution.py:17
  382.1 11.2 %multiply_convert_fusion.3 = (bf16[1024,1024]{1,0:T(8,128)(2,1)S(1)}, bf16[1024,1024]{1,0:T(8,128)(2,1)S(1)}, bf16[1024,1024]{1,0:T(8,128)(2,1)}) fusion(f32[1024,2048]{1,0:T(8,128)} %fusion.74, bf16[1024,2048]{1,0:T(8,128)(2,1)} %all-gather.7.cloned.1.call-done, bf16[1024,2048]{1,0:T(8,128)(2,1)S(1)} %copy-done.81), kind=kOutput, calls=%fused_computation.38 | convolution fusion | flops 4311744512 | bytes 23068672 | tf_op jit(solution)/shard_map/dot_general | solution.py:17
  393.7 12.5 %collective-permute-done.32 = bf16[128,2048]{1,0:T(8,128)(2,1)S(1)} collective-permute-done((bf16[128,2048]{1,0:T(8,128)(2,1)S(1)}, bf16[128,2048]{1,0:T(8,128)(2,1)S(1)}, u32[]{:S(2)}, u32[]{:S(2)}) %collective-permute-start.32) | collective-permute-done | bytes 524320 | tf_op jit(solution)/shard_map/ppermute | solution.py:37
  438.5 9.7 %add_convert_fusion.2 = bf16[1024,2048]{1,0:T(8,128)(2,1)} fusion(f32[1024,2048]{1,0:T(8,128)} %fusion.91, bf16[1024,1024]{1,0:T(8,128)(2,1)S(1)} %get-tuple-element.76, bf16[1024,2048]{1,0:T(8,128)(2,1)} %all-gather.11.cloned.1.call-done), kind=kOutput, calls=%fused_computation.20 | convolution fusion | flops 4299161600 | bytes 18874368 | tf_op jit(solution)/shard_map/dot_general | solution.py:17
  451.6 14.4 %collective-permute-done.35 = bf16[128,2048]{1,0:T(8,128)(2,1)S(1)} collective-permute-done((bf16[128,2048]{1,0:T(8,128)(2,1)S(1)}, bf16[128,2048]{1,0:T(8,128)(2,1)S(1)}, u32[]{:S(2)}, u32[]{:S(2)}) %collective-permute-start.35) | collective-permute-done | bytes 524320 | tf_op jit(solution)/shard_map/ppermute | solution.py:37
  492.3 18.6 %collective-permute-done.29 = bf16[128,2048]{1,0:T(8,128)(2,1)S(1)} collective-permute-done((bf16[128,2048]{1,0:T(8,128)(2,1)S(1)}, bf16[128,2048]{1,0:T(8,128)(2,1)S(1)}, u32[]{:S(2)}, u32[]{:S(2)}) %collective-permute-start.29) | collective-permute-done | bytes 524320 | tf_op jit(solution)/shard_map/ppermute | solution.py:37
  523.5 10.0 %collective-permute-done.25 = bf16[128,2048]{1,0:T(8,128)(2,1)} collective-permute-done((bf16[128,2048]{1,0:T(8,128)(2,1)}, bf16[128,2048]{1,0:T(8,128)(2,1)}, u32[]{:S(2)}, u32[]{:S(2)}) %collective-permute-start.25) | collective-permute-done | bytes 524320 | tf_op jit(solution)/shard_map/ppermute | solution.py:37
  572.4 12.7 %multiply_convert_fusion = bf16[2,4,512,1024]{3,2,1,0:T(8,128)(2,1)} fusion(f32[2,4,512,1024]{3,2,1,0:T(8,128)} %copy-done, f32[2,4,512]{2,1,0:T(4,128)S(1)} %multiply_reduce_fusion.2, f32[2,4,512]{2,1,0:T(4,128)S(1)} %bitcast.404, pred[2,512,1024]{2,1,0:T(8,128)(4,1)S(1)} %copy-done.7, bf16[2,4,512,128]{3,2,1,0:T(8,128)(2,1)S(1)} %bitcast.355, ...), kind=kOutput, calls=%fused_computation | convolution fusion | flops 1098907648 | bytes 29392896 | tf_op jit(solution)/shard_map/rjqd,rjkd->rjqk/dot_general | solution.py:291
  653.8 43.9 %collective-permute-done.44 = f32[2,2048]{1,0:T(2,128)S(1)} collective-permute-done((f32[2,2048]{1,0:T(2,128)S(1)}, f32[2,2048]{1,0:T(2,128)S(1)}, u32[]{:S(2)}, u32[]{:S(2)}) %collective-permute-start.44) | collective-permute-done | bytes 16416 | tf_op jit(solution)/shard_map/ppermute | solution.py:216
  716.2 22.2 %collective-permute-done.49 = bf16[256,2048]{1,0:T(8,128)(2,1)S(1)} collective-permute-done((bf16[256,2048]{1,0:T(8,128)(2,1)S(1)}, bf16[256,2048]{1,0:T(8,128)(2,1)S(1)}, u32[]{:S(2)}, u32[]{:S(2)}) %collective-permute-start.49) | collective-permute-done | bytes 1048608 | tf_op jit(solution)/shard_map/ppermute | solution.py:37
  740.2 20.6 %collective-permute-done.53 = bf16[256,2048]{1,0:T(8,128)(2,1)S(1)} collective-permute-done((bf16[256,2048]{1,0:T(8,128)(2,1)S(1)}, bf16[256,2048]{1,0:T(8,128)(2,1)S(1)}, u32[]{:S(2)}, u32[]{:S(2)}) %collective-permute-start.53) | collective-permute-done | bytes 1048608 | tf_op jit(solution)/shard_map/ppermute | solution.py:37
  772.4 22.2 %collective-permute-done.50 = bf16[256,2048]{1,0:T(8,128)(2,1)S(1)} collective-permute-done((bf16[256,2048]{1,0:T(8,128)(2,1)S(1)}, bf16[256,2048]{1,0:T(8,128)(2,1)S(1)}, u32[]{:S(2)}, u32[]{:S(2)}) %collective-permute-start.50) | collective-permute-done | bytes 1048608 | tf_op jit(solution)/shard_map/ppermute | solution.py:37
  796.3 20.7 %collective-permute-done.54 = bf16[256,2048]{1,0:T(8,128)(2,1)S(1)} collective-permute-done((bf16[256,2048]{1,0:T(8,128)(2,1)S(1)}, bf16[256,2048]{1,0:T(8,128)(2,1)S(1)}, u32[]{:S(2)}, u32[]{:S(2)}) %collective-permute-start.54) | collective-permute-done | bytes 1048608 | tf_op jit(solution)/shard_map/ppermute | solution.py:37
  843.5 14.5 %reshape.372 = bf16[1024,2,2048]{2,1,0:T(2,128)(2,1)} reshape(bf16[1024,4096]{1,0:T(8,128)(2,1)} %pad_maximum_fusion.1) | data formatting | bytes 16777216 | tf_op jit(solution)/shard_map/reshape | solution.py:422
  858.0 11.9 %convert_element_type.849 = f32[1024,2,2048]{2,1,0:T(2,128)} convert(bf16[1024,2,2048]{2,1,0:T(2,128)(2,1)} %reshape.372) | non-fusion elementwise | flops 4194304 | bytes 25165824 | tf_op jit(solution)/shard_map/convert_element_type | solution.py:430
  879.4 9.8 %collective-permute-done.56 = bf16[128,2048]{1,0:T(8,128)(2,1)S(1)} collective-permute-done((bf16[128,2048]{1,0:T(8,128)(2,1)S(1)}, bf16[128,2048]{1,0:T(8,128)(2,1)S(1)}, u32[]{:S(2)}, u32[]{:S(2)}) %collective-permute-start.56) | collective-permute-done | bytes 524320 | tf_op jit(solution)/shard_map/ppermute | solution.py:41
  (546 shorter events, 504.6 us)
Async XLA Ops:
  7.2 214.3 %all-gather.5.cloned.1.call-start = ((), (), s32[]{:S(2)}) async-start(), calls=%async_computation | async-start | bytes 4718592 | tf_op jit(solution)/shard_map/all_gather | solution.py:262
  19.7 91.7 %collective-permute-start.7 = (bf16[256,2048]{1,0:T(8,128)(2,1)}, bf16[256,2048]{1,0:T(8,128)(2,1)}, u32[]{:S(2)}, u32[]{:S(2)}) collective-permute-start(bf16[256,2048]{1,0:T(8,128)(2,1)} %param.13), channel_id=1, source_target_pairs={{0,1},{1,0},{2,3},{3,2},{4,5},{5,4},{6,7},{7,6},{8,9},{9,8},{10,11... | collective-permute-start | bytes 3145736 | tf_op jit(solution)/shard_map/ppermute | solution.py:32
  19.7 214.5 %collective-permute-start.15 = (bf16[256,2048]{1,0:T(8,128)(2,1)}, bf16[256,2048]{1,0:T(8,128)(2,1)}, u32[]{:S(2)}, u32[]{:S(2)}) collective-permute-start(bf16[256,2048]{1,0:T(8,128)(2,1)} %param.14), channel_id=1, source_target_pairs={{0,1},{1,0},{2,3},{3,2},{4,5},{5,4},{6,7},{7,6},{8,9},{9,8},{10,11... | collective-permute-start | bytes 3145736 | tf_op jit(solution)/shard_map/ppermute | solution.py:32
  73.6 164.3 %all-gather.7.cloned.1.call-start = ((), (), s32[]{:S(2)}) async-start(), calls=%async_computation.1 | async-start | bytes 4718592 | tf_op jit(solution)/shard_map/all_gather | solution.py:262
  125.0 68.1 %collective-permute-start.8 = (bf16[4,768,512]{2,1,0:T(8,128)(2,1)}, bf16[4,768,512]{2,1,0:T(8,128)(2,1)}, u32[]{:S(2)}, u32[]{:S(2)}) collective-permute-start(bf16[4,768,512]{2,1,0:T(8,128)(2,1)} %bitcast.22), channel_id=1, source_target_pairs={{0,1},{1,0},{2,3},{3,2},{4,5},{5,4},{6,7},{7,6},{8,9},{9,8},{10,11... | collective-permute-start | bytes 9437192 | tf_op jit(solution)/shard_map/ppermute | solution.py:32
  135.4 151.6 %all-gather.9.cloned.1.call-start = ((), (), s32[]{:S(2)}) async-start(), calls=%async_computation.2 | async-start | bytes 4718592 | tf_op jit(solution)/shard_map/all_gather | solution.py:324
  139.6 45.7 %collective-permute-start.12 = (bf16[2,2,4,512,128]{4,3,2,1,0:T(8,128)(2,1)}, bf16[2,2,4,512,128]{4,3,2,1,0:T(8,128)(2,1)}, u32[]{:S(2)}, u32[]{:S(2)}) collective-permute-start(bf16[2,2,4,512,128]{4,3,2,1,0:T(8,128)(2,1)} %pad_maximum_fusion.3), channel_id=1, source_target_pairs={{0,1},{1,0},{2,3},{3,2},{4,5},{5,4},{6,7},{7,6},{8,9},{9,8},{10,11... | collective-permute-start | bytes 6291464 | tf_op jit(solution)/shard_map/ppermute | solution.py:32
  239.0 122.1 %all-gather.11.cloned.1.call-start = ((), (), s32[]{:S(2)}) async-start(), calls=%async_computation.3 | async-start | bytes 4718592 | tf_op jit(solution)/shard_map/all_gather | solution.py:324
  266.0 552.8 %all-reduce.3.cloned.1.call-start = ((), (), s32[]{:S(2)}) async-start(), calls=%async_computation.4 | async-start | bytes 25165824 | tf_op jit(solution)/shard_map/psum | solution.py:356
  378.9 56.5 %collective-permute-start.23 = (bf16[128,2048]{1,0:T(8,128)(2,1)}, bf16[128,2048]{1,0:T(8,128)(2,1)}, u32[]{:S(2)}, u32[]{:S(2)}) collective-permute-start(bf16[128,2048]{1,0:T(8,128)(2,1)} %add_convert_fusion.50), channel_id=1, source_target_pairs={{0,2},{1,3},{2,4},{3,5},{4,6},{5,7},{6,0},{7,1},{8,10},{9,11},{10,... | collective-permute-start | bytes 1572872 | tf_op jit(solution)/shard_map/ppermute | solution.py:37
  438.0 52.0 %collective-permute-start.24 = (bf16[128,2048]{1,0:T(8,128)(2,1)S(1)}, bf16[128,2048]{1,0:T(8,128)(2,1)S(1)}, u32[]{:S(2)}, u32[]{:S(2)}) collective-permute-start(bf16[128,2048]{1,0:T(8,128)(2,1)S(1)} %add_convert_fusion.48), channel_id=1, source_target_pairs={{0,2},{1,3},{2,4},{3,5},{4,6},{5,7},{6,0},{7,1},{8,10},{9,11},{10,... | collective-permute-start | bytes 1572872 | tf_op jit(solution)/shard_map/ppermute | solution.py:37
  476.6 46.9 %collective-permute-start.33 = (bf16[128,2048]{1,0:T(8,128)(2,1)}, bf16[128,2048]{1,0:T(8,128)(2,1)}, u32[]{:S(2)}, u32[]{:S(2)}) collective-permute-start(bf16[128,2048]{1,0:T(8,128)(2,1)} %add_convert_fusion.34), channel_id=1, source_target_pairs={{0,2},{1,3},{2,4},{3,5},{4,6},{5,7},{6,0},{7,1},{8,10},{9,11},{10,... | collective-permute-start | bytes 1572872 | tf_op jit(solution)/shard_map/ppermute | solution.py:37
  599.7 46.2 %collective-permute-start.47 = (bf16[1024,2048]{1,0:T(8,128)(2,1)}, bf16[1024,2048]{1,0:T(8,128)(2,1)}, u32[]{:S(2)}, u32[]{:S(2)}) collective-permute-start(bf16[1024,2048]{1,0:T(8,128)(2,1)} %convolution_convert_fusion.2), channel_id=1, source_target_pairs={{0,1},{1,0},{2,3},{3,2},{4,5},{5,4},{6,7},{7,6},{8,9},{9,8},{10,11... | collective-permute-start | bytes 12582920 | tf_op jit(solution)/shard_map/ppermute | solution.py:32
  645.3 53.7 %collective-permute-start.38 = (bf16[2,2,4,512,128]{3,4,2,1,0:T(8,128)(2,1)S(1)}, bf16[2,2,4,512,128]{3,4,2,1,0:T(8,128)(2,1)S(1)}, u32[]{:S(2)}, u32[]{:S(2)}) collective-permute-start(bf16[2,2,4,512,128]{3,4,2,1,0:T(8,128)(2,1)S(1)} %slice.463), channel_id=1, source_target_pairs={{0,1},{1,0},{2,3},{3,2},{4,5},{5,4},{6,7},{7,6},{8,9},{9,8},{10,11... | collective-permute-start | bytes 6291464 | tf_op jit(solution)/shard_map/ppermute | solution.py:32
  647.5 52.1 %collective-permute-start.48 = (bf16[256,2048]{1,0:T(8,128)(2,1)S(1)}, bf16[256,2048]{1,0:T(8,128)(2,1)S(1)}, u32[]{:S(2)}, u32[]{:S(2)}) collective-permute-start(bf16[256,2048]{1,0:T(8,128)(2,1)S(1)} %add_convert_fusion.16), channel_id=1, source_target_pairs={{0,2},{1,3},{2,4},{3,5},{4,6},{5,7},{6,0},{7,1},{8,10},{9,11},{10,... | collective-permute-start | bytes 3145736 | tf_op jit(solution)/shard_map/ppermute | solution.py:37
  651.4 51.9 %collective-permute-start.52 = (bf16[256,2048]{1,0:T(8,128)(2,1)S(1)}, bf16[256,2048]{1,0:T(8,128)(2,1)S(1)}, u32[]{:S(2)}, u32[]{:S(2)}) collective-permute-start(bf16[256,2048]{1,0:T(8,128)(2,1)S(1)} %add_convert_fusion.9), channel_id=1, source_target_pairs={{0,2},{1,3},{2,4},{3,5},{4,6},{5,7},{6,0},{7,1},{8,10},{9,11},{10,... | collective-permute-start | bytes 3145736 | tf_op jit(solution)/shard_map/ppermute | solution.py:37
  651.5 46.2 %collective-permute-start.44 = (f32[2,2048]{1,0:T(2,128)S(1)}, f32[2,2048]{1,0:T(2,128)S(1)}, u32[]{:S(2)}, u32[]{:S(2)}) collective-permute-start(f32[2,2048]{1,0:T(2,128)S(1)} %fusion.160), channel_id=1, source_target_pairs={{0,4},{1,5},{2,6},{3,7},{4,0},{5,1},{6,2},{7,3},{8,12},{9,13},{10,... | collective-permute-start | bytes 49160 | tf_op jit(solution)/shard_map/ppermute | solution.py:216
  705.1 55.7 %collective-permute-start.53 = (bf16[256,2048]{1,0:T(8,128)(2,1)S(1)}, bf16[256,2048]{1,0:T(8,128)(2,1)S(1)}, u32[]{:S(2)}, u32[]{:S(2)}) collective-permute-start(bf16[256,2048]{1,0:T(8,128)(2,1)S(1)} %add_convert_fusion.7), channel_id=1, source_target_pairs={{0,2},{1,3},{2,4},{3,5},{4,6},{5,7},{6,0},{7,1},{8,10},{9,11},{10,... | collective-permute-start | bytes 3145736 | tf_op jit(solution)/shard_map/ppermute | solution.py:37
  707.3 56.4 %collective-permute-start.46 = (f32[2,2048]{1,0:T(2,128)S(1)}, f32[2,2048]{1,0:T(2,128)S(1)}, u32[]{:S(2)}, u32[]{:S(2)}) collective-permute-start(f32[2,2048]{1,0:T(2,128)S(1)} %add.667), channel_id=1, source_target_pairs={{0,16},{8,24},{16,0},{24,8},{1,17},{9,25},{17,1},{25,9},{2,18},{10... | collective-permute-start | bytes 49160 | tf_op jit(solution)/shard_map/ppermute | solution.py:41
  716.1 55.9 %collective-permute-start.40 = (bf16[2,2,4,128,128]{3,4,2,1,0:T(8,128)(2,1)S(1)}, bf16[2,2,4,128,128]{3,4,2,1,0:T(8,128)(2,1)S(1)}, u32[]{:S(2)}, u32[]{:S(2)}) collective-permute-start(bf16[2,2,4,128,128]{3,4,2,1,0:T(8,128)(2,1)S(1)} %add_convert_fusion.24), channel_id=1, source_target_pairs={{0,2},{1,3},{2,4},{3,5},{4,6},{5,7},{6,0},{7,1},{8,10},{9,11},{10,... | collective-permute-start | bytes 1572872 | tf_op jit(solution)/shard_map/ppermute | solution.py:37
  740.2 54.4 %collective-permute-start.50 = (bf16[256,2048]{1,0:T(8,128)(2,1)S(1)}, bf16[256,2048]{1,0:T(8,128)(2,1)S(1)}, u32[]{:S(2)}, u32[]{:S(2)}) collective-permute-start(bf16[256,2048]{1,0:T(8,128)(2,1)S(1)} %add_convert_fusion.12), channel_id=1, source_target_pairs={{0,2},{1,3},{2,4},{3,5},{4,6},{5,7},{6,0},{7,1},{8,10},{9,11},{10,... | collective-permute-start | bytes 3145736 | tf_op jit(solution)/shard_map/ppermute | solution.py:37
  762.6 54.4 %collective-permute-start.54 = (bf16[256,2048]{1,0:T(8,128)(2,1)S(1)}, bf16[256,2048]{1,0:T(8,128)(2,1)S(1)}, u32[]{:S(2)}, u32[]{:S(2)}) collective-permute-start(bf16[256,2048]{1,0:T(8,128)(2,1)S(1)} %add_convert_fusion.5), channel_id=1, source_target_pairs={{0,2},{1,3},{2,4},{3,5},{4,6},{5,7},{6,0},{7,1},{8,10},{9,11},{10,... | collective-permute-start | bytes 3145736 | tf_op jit(solution)/shard_map/ppermute | solution.py:37
  772.3 54.8 %collective-permute-start.41 = (bf16[2,2,4,128,128]{3,4,2,1,0:T(8,128)(2,1)S(1)}, bf16[2,2,4,128,128]{3,4,2,1,0:T(8,128)(2,1)}, u32[]{:S(2)}, u32[]{:S(2)}) collective-permute-start(bf16[2,2,4,128,128]{3,4,2,1,0:T(8,128)(2,1)S(1)} %add_convert_fusion.22), channel_id=1, source_target_pairs={{0,2},{1,3},{2,4},{3,5},{4,6},{5,7},{6,0},{7,1},{8,10},{9,11},{10,... | collective-permute-start | bytes 1572872 | tf_op jit(solution)/shard_map/ppermute | solution.py:37
  834.7 44.6 %collective-permute-start.58 = (bf16[128,2048]{1,0:T(8,128)(2,1)S(1)}, bf16[128,2048]{1,0:T(8,128)(2,1)S(1)}, u32[]{:S(2)}, u32[]{:S(2)}) collective-permute-start(bf16[128,2048]{1,0:T(8,128)(2,1)S(1)} %get-tuple-element.109), channel_id=1, source_target_pairs={{0,8},{8,0},{16,24},{24,16},{1,9},{9,1},{17,25},{25,17},{2,10},{10... | collective-permute-start | bytes 1572872 | tf_op jit(solution)/shard_map/ppermute | solution.py:41
  (135 other events, 2666.1 us)
Sparse Core Ops, SparseCore 0:
  73.7 57.2 all-gather.4
  135.5 46.6 all-gather.6
  239.1 47.8 all-gather.8
  288.5 45.8 all-gather.10
  523.6 239.4 all-reduce.2

commit v6 on v5

--- a/solution.py
+++ b/solution.py
@@ -115,31 +115,10 @@
 
 
 class Weight:
-    def __init__(self, shard, chips, rows, row_at, order, dep=None):
-        seq = 2 * chips
+    def __init__(self, chips, row_at, order, near=None, far=None, whole=None):
         self.chips, self.row_at, self.order = chips, row_at, order
-        depth, width = shard.shape
-        self.depth = depth
-        self.split = rows == 4 and depth % 32 == 0 and width % 512 == 0
-        if not self.split:
-            self.whole = lax.all_gather(shard, "seq", axis=0, tiled=True)
-            self.token = dep
-            return
-        part = width // rows
-        half = depth // 2
-        mine = lax.dynamic_slice_in_dim(shard, row_at * part, part, axis=1)
-        slots, self.token = ring_gather(mine, chips, dep=dep)
-        first = jnp.stack([v[:half] for v in slots[1:]])
-        second = jnp.stack([v[half:] for v in slots[1:]])
-        first_x = swap_row(first, rows, 1)
-        second_y = swap_row(second, rows, 2)
-        first_pair = swap_row(jnp.stack([first, first_x]), rows, 2)
-        second_pair = swap_row(jnp.stack([second, second_y]), rows, 1)
-        parts = [first, second, first_x, second_pair[0]]
-        parts += [first_pair[0], second_y, first_pair[1], second_pair[1]]
-        parts = jnp.concatenate(parts, axis=0).reshape(rows, (chips - 1) * depth, part)
-        self.far = [parts, swap_core(parts, seq)]
-        self.near = [shard, swap_core(shard, seq)]
+        self.near, self.far, self.whole = near, far, whole
+        self.split = whole is None
 
     def features(self, value):
         if not self.split:
@@ -153,8 +132,6 @@
         for near, far in zip(self.near, self.far, strict=True):
             term = jnp.einsum("ktc,kfc->ktf", blocks, far, preferred_element_type=F32)
             term = jnp.sum(term, axis=0).astype(BF16)
-            term = term.reshape(count, 2, self.chips - 1, -1).transpose(0, 2, 1, 3)
-            term = term.reshape(count, -1)
             out.append(jnp.concatenate([dot(value, near, ((1,), (1,))).astype(BF16), term], axis=1))
         return out
 
@@ -165,12 +142,37 @@
         count = halves[0].shape[0]
         near_sum = far_sum = 0.0
         for part, near, far in zip(halves, self.near, self.far, strict=True):
-            near_sum += dot(part[:, : self.depth], near, ((1,), (0,)))
-            rest = part[:, self.depth :].reshape(count, self.chips - 1, 2, -1)
-            rest = rest.transpose(0, 2, 1, 3).reshape(count, -1)
-            far_sum += jnp.einsum("tf,kfc->ktc", rest, far, preferred_element_type=F32)
+            depth = near.shape[0]
+            near_sum += dot(part[:, :depth], near, ((1,), (0,)))
+            far_sum += jnp.einsum("tf,kfc->ktc", part[:, depth:], far, preferred_element_type=F32)
         far_sum = xor_order(far_sum, self.row_at).transpose(1, 0, 2).reshape(count, -1)
         return near_sum + far_sum
+
+
+def gather_weights(shards, chips, rows, row_at, order):
+    seq = 2 * chips
+    depth, width = shards[0].shape
+    if rows != 4 or depth % 32 or width % 512:
+        whole = [lax.all_gather(w, "seq", axis=0, tiled=True) for w in shards]
+        return [Weight(chips, row_at, order, whole=w) for w in whole], None
+    part = width // rows
+    mine = jnp.stack([lax.dynamic_slice_in_dim(w, row_at * part, part, axis=1) for w in shards])
+    slots, token = ring_gather(mine, chips)
+    first, second = (jnp.stack([v[n] for v in slots[1:]]) for n in range(2))
+    first_x = swap_row(first, rows, 1)
+    second_y = swap_row(second, rows, 2)
+    first_pair = swap_row(jnp.stack([first, first_x]), rows, 2)
+    second_pair = swap_row(jnp.stack([second, second_y]), rows, 1)
+    pieces = [
+        jnp.stack([first, first_x, first_pair[0], first_pair[1]]),
+        jnp.stack([second, second_pair[0], second_y, second_pair[1]]),
+    ]
+    out = []
+    for shard, piece in zip(shards, pieces, strict=True):
+        far = piece.reshape(rows, (chips - 1) * depth, part)
+        far, near = [far, swap_core(far, seq)], [shard, swap_core(shard, seq)]
+        out.append(Weight(chips, row_at, order, near=near, far=far))
+    return out, token
 
 
 def scatter_halves(own, sib, got_at, chips):
@@ -197,17 +199,22 @@
     )
 
 
-def sum_rows(value, rows):
+def sum_rows(values, rows, other):
     if rows != 4:
-        return lax.psum(value.astype(BF16), "rows").astype(F32)
-    half = value.shape[0] // 2
-    first, second = value[:half].astype(BF16), value[half:].astype(BF16)
+        return [lax.psum(v.astype(BF16), "rows").astype(F32) for v in values], other
 
     def pair(item, mask):
         return item.astype(F32) + swap_row(item, rows, mask).astype(F32)
 
-    first, second = pair(first, 1).astype(BF16), pair(second, 2).astype(BF16)
-    return jnp.concatenate([pair(first, 2), pair(second, 1)], axis=0)
+    halves = []
+    for value in values:
+        half = value.shape[0] // 2
+        halves.append(pair(value[:half].astype(BF16), 1).astype(BF16))
+        halves.append(pair(value[half:].astype(BF16), 2).astype(BF16))
+    halves, other = lax.optimization_barrier((halves, other))
+    masks = [2, 1] * len(values)
+    sums = [pair(h, m) for h, m in zip(halves, masks, strict=True)]
+    return [jnp.concatenate(sums[2 * n : 2 * n + 2], axis=0) for n in range(len(values))], other
 
 
 def sum_all(value, rows, seq):
@@ -252,14 +259,15 @@
     ]
     grad_out = [cotangent[r].astype(F32) * live[r] for r in range(rows_here)]
     gate_up_weight = jnp.concatenate([ffn_in_weight[:, 0], ffn_in_weight[:, 1]], axis=0)
-    query_proj = Weight(query_weight, chips, rows, row_at, order)
+    (query_proj, output_proj), token = gather_weights(
+        (query_weight, output_weight), chips, rows, row_at, order
+    )
     cache_own = kv_cache.reshape(rows_here, seg_len, 2, KV, HEAD).transpose(2, 0, 3, 1, 4)
-    cache_slots, token = ring_gather(cache_own, chips, dep=query_proj.token)
+    cache_slots, token = ring_gather(cache_own, chips, dep=token)
     cache_block = jnp.concatenate(cache_slots, axis=3)
     cache_all = jnp.concatenate([cache_block, swap_core(cache_block, seq)], axis=3)
-    output_proj = Weight(output_weight, chips, rows, row_at, order, dep=token)
     grad_group = [
-        lax.all_gather(tie(g.astype(BF16), output_proj.token), "seq", axis=0, tiled=True)
+        lax.all_gather(tie(g.astype(BF16), token), "seq", axis=0, tiled=True)
         for g in grad_out
     ]
     per = chips // KV
@@ -325,7 +333,7 @@
 
     main, fill = Lane(), Lane()
     units = down_weight.shape[0]
-    hidden, grad_gate_up, grad_part, ffn_part = [], [], [], []
+    hidden, grad_gate_up, ffn_part = [], [], []
     for r in range(rows_here):
         kept = dot(beside(normed_group[r], main), gate_up_weight, ((1,), (1,)))
         gate, upper = kept[:, :units], kept[:, units:]
@@ -336,9 +344,10 @@
         grad_up = grad_hidden * gate * sigma
         grad_gate_up.append(jnp.concatenate([grad_gate, grad_up], axis=1).astype(BF16))
         part = dot(beside(grad_gate_up[r], main), gate_up_weight, ((1,), (0,))).astype(BF16)
-        grad_part.append(part)
         ffn_part.append(dot(hidden[r], down_weight, ((1,), (0,))).astype(BF16))
         main.add(("grad", r), scatter_tokens(part, chips, place, core))
+        if r == 0:
+            fill.add(("ffn", 0), scatter_tokens(ffn_part[0], chips, place, core))
 
     def over_tokens(left, right, start, size):
         total = 0.0
@@ -350,8 +359,6 @@
     gate_part = over_tokens(grad_gate_up, normed_group, 0, units)
     up_part = over_tokens(grad_gate_up, normed_group, units, units)
     down_part = over_tokens(hidden, grad_group, 0, units)
-    for r in range(rows_here):
-        fill.add(("ffn", r), scatter_tokens(ffn_part[r], chips, place, core))
     parts = (gate_part, up_part, down_part)
     summed = lax.psum(parts, "rows")
 
@@ -365,6 +372,9 @@
         grad_middle.append(
             grad_out[r] + norm_back(grad_normed_two, scaled_two, inverse_two[r], gain_two)
         )
+    for r in range(1, rows_here):
+        part = tie(ffn_part[r], grad_middle[-1])
+        fill.add(("ffn", r), scatter_tokens(part, chips, place, core))
     grad_middle = jnp.concatenate(grad_middle, axis=0)
     grad_branch = grad_middle.astype(BF16)
     output_part = [dot(half, grad_branch, ((0,), (0,))).astype(BF16) for half in mixed]
@@ -376,15 +386,17 @@
         return scatter_halves(lambda j: take(parts[0], j), parts[1], take, chips)
 
     main.add("output", scatter_rows(output_part))
-    grad_heads = to_heads(output_proj.features(grad_branch))
+    grad_heads = to_heads(output_proj.features(tie(grad_branch, output_part[1])))
+    grad_heads = beside(grad_heads, main)
     delta = jnp.sum(grad_heads.astype(F32) * mixed_heads, axis=-1, keepdims=True)
     scores = heads_dot("rjqd,rjkd->rjqk", query_heads, keys) * scale
     probs = jnp.where(valid, jnp.exp(scores - lse), 0.0)
     grad_probs = heads_dot("rjqd,rjkd->rjqk", grad_heads, values)
-    grad_scores = (probs * (grad_probs - delta)).astype(BF16)
+    grad_scores = beside((probs * (grad_probs - delta)).astype(BF16), main)
     query_term = from_heads(
         (heads_dot("rjqk,rjkd->rjqd", grad_scores, keys) * scale).astype(BF16)
     )
+    query_term[0] = beside(query_term[0], main)
     grad_keys = heads_dot("rjqk,rjqd->rjkd", grad_scores, query_heads) * scale
     grad_values = heads_dot("rjqk,rjqd->rjkd", probs.astype(BF16), grad_heads)
     cache_part = from_slots(jnp.stack([grad_keys.astype(BF16), grad_values.astype(BF16)]))
@@ -417,8 +429,8 @@
         (summed, main.result("output").astype(BF16), main.result("query").astype(BF16))
     )
     gate_grad, up_grad, down_grad = summed
-    output_grad, query_grad = sum_rows(output_sum, rows), sum_rows(query_sum, rows)
     in_grad = jnp.concatenate([gate_grad, up_grad], axis=1)
+    (output_grad, query_grad), in_grad = sum_rows([output_sum, query_sum], rows, in_grad)
     in_grad = lax.optimization_barrier(in_grad.reshape(units, 2, width))
     return (
         jnp.stack(layer_out),

time: 915 us -> 933 us (1.020)
  other arithmetic: 121 us -> 156 us
    ppermute x30 -> x27, waiting for transfers between devices: 251 us -> 192 us  [ring(): return lax.ppermute(value, 'seq', pairs)]
    ppermute x18 -> x14, waiting for transfers between devices: 47.2 us -> 81.8 us  [swap_row(): return lax.ppermute(value, 'rows', [(r, r ^ mask) for r in range(rows)])]
    unnamed x214 -> x212, local copies, waits for them, and re-layouts: 48.3 us -> 25.2 us
    ppermute x3, waiting for transfers between devices: 43.9 us -> 66 us  [sum_all(): lax.ppermute(value, 'seq', [(s, s ^ mask) for s in range(seq)])]
    ppermute x18 -> x14, starting transfers between devices: 19.4 us -> 14.6 us  [swap_row(): return lax.ppermute(value, 'rows', [(r, r ^ mask) for r in range(rows)])]
  transfers between devices with their start and end apart: 68 -> 61, of which waited for: 33 -> 27; matrix products, arithmetic and copies ran while one was open for 52% -> 53% of each run, Pallas kernels for 0% -> 0%
where the time goes in v6:
time: 933 us; the launch traced here: 923 us
  waiting for transfers between devices  358 us (38%)
  matrix products  229 us (25%)
  other arithmetic  156 us (17%)
  local copies, waits for them, and re-layouts  133 us (14%)
  starting transfers between devices  30.3 us (3%)
  between operations  16 us (2%)
    ppermute x27, waiting for transfers between devices, ring(): return lax.ppermute(value, 'seq', pairs)  192 us
    dot_general x26, matrix products, dot(): lax.dot_general(left, right, (dims, ((), ())), preferred_element_type=F32)  163 us
    ppermute x14, waiting for transfers between devices, swap_row(): return lax.ppermute(value, 'rows', [(r, r ^ mask) for r in range(rows)])  81.8 us
    ppermute x3, waiting for transfers between devices, sum_all(): lax.ppermute(value, 'seq', [(s, s ^ mask) for s in range(seq)])  66 us
    dot_general x6, matrix products, heads_dot(): return jnp.einsum(spec, left, right, preferred_element_type=F32)  42.1 us
    convert_element_type x14, other arithmetic, ring_scatter(): sent = total.astype(BF16)  28.4 us
    unnamed x212, local copies, waits for them, and re-layouts  25.2 us
  transfers between devices with their start and end apart: 61, of which 27 were waited for; matrix products, arithmetic and copies ran while one was open for 53% of the time, Pallas kernels for 0%

profile of v6, /device:TPU:0, one launch (start us, length us, event | category | flops | bytes accessed | tf_op | source)
XLA Modules:
  0.0 922.9 jit_solution(15665944906800565964)
XLA Ops:
  12.5 14.1 %collective-permute-done = bf16[2,256,512]{2,1,0:T(8,128)(2,1)} collective-permute-done((bf16[2,256,512]{2,1,0:T(8,128)(2,1)S(1)}, bf16[2,256,512]{2,1,0:T(8,128)(2,1)}, u32[]{:S(2)}, u32[]{:S(2)}) %collective-permute-start) | collective-permute-done | bytes 524320 | tf_op jit(solution)/shard_map/ppermute | solution.py:37
  28.2 13.5 %collective-permute-done.1 = bf16[2,256,512]{2,1,0:T(8,128)(2,1)} collective-permute-done((bf16[2,256,512]{2,1,0:T(8,128)(2,1)}, bf16[2,256,512]{2,1,0:T(8,128)(2,1)}, u32[]{:S(2)}, u32[]{:S(2)}) %collective-permute-start.1) | collective-permute-done | bytes 524320 | tf_op jit(solution)/shard_map/ppermute | solution.py:37
  42.4 13.4 %collective-permute-done.7 = bf16[2,2,4,128,128]{4,3,2,1,0:T(8,128)(2,1)S(1)} collective-permute-done((bf16[2,2,4,128,128]{4,3,2,1,0:T(8,128)(2,1)S(1)}, bf16[2,2,4,128,128]{4,3,2,1,0:T(8,128)(2,1)S(1)}, u32[]{:S(2)}, u32[]{:S(2)}) %collective-permute-start.7) | collective-permute-done | bytes 524320 | tf_op jit(solution)/shard_map/ppermute | solution.py:37
  58.3 10.5 %collective-permute-done.8 = bf16[2,2,4,128,128]{4,3,2,1,0:T(8,128)(2,1)S(1)} collective-permute-done((bf16[2,2,4,128,128]{4,3,2,1,0:T(8,128)(2,1)S(1)}, bf16[2,2,4,128,128]{4,3,2,1,0:T(8,128)(2,1)S(1)}, u32[]{:S(2)}, u32[]{:S(2)}) %collective-permute-start.8) | collective-permute-done | bytes 524320 | tf_op jit(solution)/shard_map/ppermute | solution.py:37
  78.3 23.4 %collective-permute-done.2 = bf16[2,256,512]{2,1,0:T(8,128)(2,1)S(1)} collective-permute-done((bf16[2,256,512]{2,1,0:T(8,128)(2,1)}, bf16[2,256,512]{2,1,0:T(8,128)(2,1)S(1)}, u32[]{:S(2)}, u32[]{:S(2)}) %collective-permute-start.2) | collective-permute-done | bytes 524320 | tf_op jit(solution)/shard_map/ppermute | solution.py:37
  103.4 16.9 %collective-permute-done.3 = bf16[3,256,512]{2,1,0:T(8,128)(2,1)S(1)} collective-permute-done((bf16[3,256,512]{2,1,0:T(8,128)(2,1)S(1)}, bf16[3,256,512]{2,1,0:T(8,128)(2,1)S(1)}, u32[]{:S(2)}, u32[]{:S(2)}) %collective-permute-start.3) | collective-permute-done | bytes 786464 | tf_op jit(solution)/shard_map/ppermute | solution.py:41
  131.4 28.0 %collective-permute-done.4 = bf16[2,3,256,512]{3,2,1,0:T(8,128)(2,1)} collective-permute-done((bf16[2,3,256,512]{3,2,1,0:T(8,128)(2,1)}, bf16[2,3,256,512]{3,2,1,0:T(8,128)(2,1)}, u32[]{:S(2)}, u32[]{:S(2)}) %collective-permute-start.4) | collective-permute-done | bytes 1572896 | tf_op jit(solution)/shard_map/ppermute | solution.py:41
  162.8 10.5 %collective-permute-done.12 = bf16[3,256,512]{2,1,0:T(8,128)(2,1)} collective-permute-done((bf16[3,256,512]{2,1,0:T(8,128)(2,1)}, bf16[3,256,512]{2,1,0:T(8,128)(2,1)}, u32[]{:S(2)}, u32[]{:S(2)}) %collective-permute-start.12) | collective-permute-done | bytes 786464 | tf_op jit(solution)/shard_map/ppermute | solution.py:41
  190.0 19.6 %collective-permute-done.13 = bf16[2,3,256,512]{3,2,1,0:T(8,128)(2,1)} collective-permute-done((bf16[2,3,256,512]{3,2,1,0:T(8,128)(2,1)}, bf16[2,3,256,512]{3,2,1,0:T(8,128)(2,1)}, u32[]{:S(2)}, u32[]{:S(2)}) %collective-permute-start.13) | collective-permute-done | bytes 1572896 | tf_op jit(solution)/shard_map/ppermute | solution.py:41
  283.6 16.6 %fusion.78 = (bf16[1024,1,2048]{2,1,0:T(2,128)(2,1)S(1)}, bf16[1024,1,2048]{2,1,0:T(2,128)(2,1)S(1)}) fusion(bf16[1024,2,2048]{2,1,0:T(2,128)(2,1)} %param.15), kind=kLoop, calls=%fused_computation.270 | loop fusion | bytes 16777216 | tf_op jit(solution)/shard_map/slice | solution.py:261
  308.5 18.5 %all-gather.9.cloned.1.call-done = bf16[1024,2048]{1,0:T(8,128)(2,1)} async-done(((bf16[128,2048]{1,0:T(8,128)(2,1)}), bf16[1024,2048]{1,0:T(8,128)(2,1)}) %all-gather.9.cloned.1.call-update) | async-done | bytes 4194320 | tf_op jit(solution)/shard_map/all_gather | solution.py:332
  327.0 15.5 %fusion.77 = f32[1024,2048]{1,0:T(8,128)} fusion(bf16[1024,2048]{1,0:T(8,128)(2,1)} %all-gather.9.cloned.1.call-done, bf16[1024,2048]{1,0:T(8,128)(2,1)} %get-tuple-element.165, bf16[1024,2048]{1,0:T(8,128)(2,1)} %get-tuple-element.166), kind=kOutput, calls=%fused_computation.269 | convolution fusion | flops 8606711808 | bytes 20971520 | tf_op jit(solution)/shard_map/dot_general | solution.py:17
  342.5 10.5 %multiply_convert_fusion.6 = (bf16[1024,1024]{1,0:T(8,128)(2,1)}, bf16[1024,1024]{1,0:T(8,128)(2,1)}, bf16[1024,1024]{1,0:T(8,128)(2,1)}) fusion(f32[1024,2048]{1,0:T(8,128)} %fusion.77, bf16[1024,2048]{1,0:T(8,128)(2,1)S(1)} %copy-done.92, bf16[1024,2048]{1,0:T(8,128)(2,1)S(1)} %copy-done.90), kind=kOutput, calls=%fused_computation.42 | convolution fusion | flops 4311744512 | bytes 23068672 | tf_op jit(solution)/shard_map/dot_general | solution.py:17
  353.0 10.8 %fusion.20 = bf16[1024,2048]{1,0:T(8,128)(2,1)S(1)} fusion(bf16[1024,1024]{1,0:T(8,128)(2,1)} %get-tuple-element.93, bf16[1024,1024]{1,0:T(8,128)(2,1)} %get-tuple-element.92, bf16[1024,2048]{1,0:T(8,128)(2,1)S(1)} %copy-done.33, bf16[1024,2048]{1,0:T(8,128)(2,1)S(1)} %copy-done.35), kind=kOutput, calls=%fused_computation.52 | convolution fusion | flops 8617197568 | bytes 16777216 | tf_op jit(solution)/shard_map/dot_general | solution.py:17
  391.6 15.3 %fusion.76 = f32[1024,2048]{1,0:T(8,128)} fusion(bf16[1024,2048]{1,0:T(8,128)(2,1)} %all-gather.11.cloned.1.call-done, bf16[1024,2048]{1,0:T(8,128)(2,1)} %get-tuple-element.165, bf16[1024,2048]{1,0:T(8,128)(2,1)} %get-tuple-element.166), kind=kOutput, calls=%fused_computation.268 | convolution fusion | flops 8606711808 | bytes 20971520 | tf_op jit(solution)/shard_map/dot_general | solution.py:17
  412.8 11.4 %multiply_convert_fusion.3 = (bf16[1024,1024]{1,0:T(8,128)(2,1)}, bf16[1024,1024]{1,0:T(8,128)(2,1)S(1)}, bf16[1024,1024]{1,0:T(8,128)(2,1)}) fusion(f32[1024,2048]{1,0:T(8,128)} %fusion.76, bf16[1024,2048]{1,0:T(8,128)(2,1)} %all-gather.7.cloned.1.call-done, bf16[1024,2048]{1,0:T(8,128)(2,1)S(1)} %copy-done.91), kind=kOutput, calls=%fused_computation.38 | convolution fusion | flops 4311744512 | bytes 23068672 | tf_op jit(solution)/shard_map/dot_general | solution.py:17
  426.4 10.2 %collective-permute-done.21 = bf16[128,2048]{1,0:T(8,128)(2,1)S(1)} collective-permute-done((bf16[128,2048]{1,0:T(8,128)(2,1)S(1)}, bf16[128,2048]{1,0:T(8,128)(2,1)S(1)}, u32[]{:S(2)}, u32[]{:S(2)}) %collective-permute-start.21) | collective-permute-done | bytes 524320 | tf_op jit(solution)/shard_map/ppermute | solution.py:37
  608.6 12.4 %multiply_convert_fusion = bf16[2,4,512,1024]{3,2,1,0:T(8,128)(2,1)} fusion(f32[2,4,512,1024]{3,2,1,0:T(8,128)} %copy-done, f32[2,4,512]{2,1,0:T(4,128)S(1)} %multiply_reduce_fusion.2, f32[2,4,512]{2,1,0:T(4,128)S(1)} %bitcast.269, pred[2,512,1024]{2,1,0:T(8,128)(4,1)S(1)} %copy-done.16, bf16[2,4,512,128]{3,2,1,0:T(8,128)(2,1)S(1)} %bitcast.230, ...), kind=kOutput, calls=%fused_computation | convolution fusion | flops 1098907648 | bytes 29392896 | tf_op jit(solution)/shard_map/rjqd,rjkd->rjqk/dot_general | solution.py:299
  630.1 12.3 %collective-permute-done.32 = bf16[256,2048]{1,0:T(8,128)(2,1)} collective-permute-done((bf16[256,2048]{1,0:T(8,128)(2,1)}, bf16[256,2048]{1,0:T(8,128)(2,1)}, u32[]{:S(2)}, u32[]{:S(2)}) %collective-permute-start.32) | collective-permute-done | bytes 1048608 | tf_op jit(solution)/shard_map/ppermute | solution.py:37
  702.8 23.8 %collective-permute-done.45 = bf16[256,2048]{1,0:T(8,128)(2,1)S(1)} collective-permute-done((bf16[256,2048]{1,0:T(8,128)(2,1)S(1)}, bf16[256,2048]{1,0:T(8,128)(2,1)S(1)}, u32[]{:S(2)}, u32[]{:S(2)}) %collective-permute-start.45) | collective-permute-done | bytes 1048608 | tf_op jit(solution)/shard_map/ppermute | solution.py:37
  733.9 66.0 %collective-permute-done.40 = f32[2,2048]{1,0:T(2,128)S(1)} collective-permute-done((f32[2,2048]{1,0:T(2,128)S(1)}, f32[2,2048]{1,0:T(2,128)S(1)}, u32[]{:S(2)}, u32[]{:S(2)}) %collective-permute-start.40) | collective-permute-done | bytes 16416 | tf_op jit(solution)/shard_map/ppermute | solution.py:223
  821.8 18.6 %collective-permute-done.36 = bf16[2,2,4,128,128]{3,4,2,1,0:T(8,128)(2,1)S(1)} collective-permute-done((bf16[2,2,4,128,128]{3,4,2,1,0:T(8,128)(2,1)S(1)}, bf16[2,2,4,128,128]{3,4,2,1,0:T(8,128)(2,1)S(1)}, u32[]{:S(2)}, u32[]{:S(2)}) %collective-permute-start.36) | collective-permute-done | bytes 524320 | tf_op jit(solution)/shard_map/ppermute | solution.py:37
  884.2 14.5 %reshape.301 = bf16[1024,2,2048]{2,1,0:T(2,128)(2,1)} reshape(bf16[1024,4096]{1,0:T(8,128)(2,1)} %pad_maximum_fusion.1) | data formatting | bytes 16777216 | tf_op jit(solution)/shard_map/reshape | solution.py:434
  898.6 11.7 %convert_element_type.847 = f32[1024,2,2048]{2,1,0:T(2,128)} convert(bf16[1024,2,2048]{2,1,0:T(2,128)(2,1)} %reshape.301) | non-fusion elementwise | flops 4194304 | bytes 25165824 | tf_op jit(solution)/shard_map/convert_element_type | solution.py:442
  (510 shorter events, 489.1 us)
Async XLA Ops:
  7.2 260.5 %all-gather.5.cloned.1.call-start = ((), (), s32[]{:S(2)}) async-start(), calls=%async_computation | async-start | bytes 4718592 | tf_op jit(solution)/shard_map/all_gather | solution.py:270
  69.7 212.7 %all-gather.7.cloned.1.call-start = ((), (), s32[]{:S(2)}) async-start(), calls=%async_computation.1 | async-start | bytes 4718592 | tf_op jit(solution)/shard_map/all_gather | solution.py:270
  69.7 111.0 %collective-permute-start.5 = (bf16[256,2048]{1,0:T(8,128)(2,1)}, bf16[256,2048]{1,0:T(8,128)(2,1)}, u32[]{:S(2)}, u32[]{:S(2)}) collective-permute-start(bf16[256,2048]{1,0:T(8,128)(2,1)} %param.13), channel_id=1, source_target_pairs={{0,1},{1,0},{2,3},{3,2},{4,5},{5,4},{6,7},{7,6},{8,9},{9,8},{10,11... | collective-permute-start | bytes 3145736 | tf_op jit(solution)/shard_map/ppermute | solution.py:32
  69.8 208.8 %collective-permute-start.11 = (bf16[256,2048]{1,0:T(8,128)(2,1)}, bf16[256,2048]{1,0:T(8,128)(2,1)}, u32[]{:S(2)}, u32[]{:S(2)}) collective-permute-start(bf16[256,2048]{1,0:T(8,128)(2,1)} %param.14), channel_id=1, source_target_pairs={{0,1},{1,0},{2,3},{3,2},{4,5},{5,4},{6,7},{7,6},{8,9},{9,8},{10,11... | collective-permute-start | bytes 3145736 | tf_op jit(solution)/shard_map/ppermute | solution.py:32
  124.5 48.8 %collective-permute-start.12 = (bf16[3,256,512]{2,1,0:T(8,128)(2,1)}, bf16[3,256,512]{2,1,0:T(8,128)(2,1)}, u32[]{:S(2)}, u32[]{:S(2)}) collective-permute-start(bf16[3,256,512]{2,1,0:T(8,128)(2,1)} %get-tuple-element.138), channel_id=1, source_target_pairs={{0,16},{8,24},{16,0},{24,8},{1,17},{9,25},{17,1},{25,9},{2,18},{10... | collective-permute-start | bytes 2359304 | tf_op jit(solution)/shard_map/ppermute | solution.py:41
  131.3 44.5 %collective-permute-start.9 = (bf16[2,2,4,128,128]{4,3,2,1,0:T(8,128)(2,1)S(1)}, bf16[2,2,4,128,128]{4,3,2,1,0:T(8,128)(2,1)S(1)}, u32[]{:S(2)}, u32[]{:S(2)}) collective-permute-start(bf16[2,2,4,128,128]{4,3,2,1,0:T(8,128)(2,1)S(1)} %copy-done.60), channel_id=1, source_target_pairs={{0,2},{1,3},{2,4},{3,5},{4,6},{5,7},{6,0},{7,1},{8,10},{9,11},{10,... | collective-permute-start | bytes 1572872 | tf_op jit(solution)/shard_map/ppermute | solution.py:37
  162.8 68.6 %collective-permute-start.6 = (bf16[4,768,512]{2,1,0:T(8,128)(2,1)}, bf16[4,768,512]{2,1,0:T(8,128)(2,1)}, u32[]{:S(2)}, u32[]{:S(2)}) collective-permute-start(bf16[4,768,512]{2,1,0:T(8,128)(2,1)} %pad_maximum_fusion.3), channel_id=1, source_target_pairs={{0,1},{1,0},{2,3},{3,2},{4,5},{5,4},{6,7},{7,6},{8,9},{9,8},{10,11... | collective-permute-start | bytes 9437192 | tf_op jit(solution)/shard_map/ppermute | solution.py:32
  177.3 46.1 %collective-permute-start.10 = (bf16[2,2,4,512,128]{4,3,2,1,0:T(8,128)(2,1)}, bf16[2,2,4,512,128]{4,3,2,1,0:T(8,128)(2,1)}, u32[]{:S(2)}, u32[]{:S(2)}) collective-permute-start(bf16[2,2,4,512,128]{4,3,2,1,0:T(8,128)(2,1)} %pad_maximum_fusion.5), channel_id=1, source_target_pairs={{0,1},{1,0},{2,3},{3,2},{4,5},{5,4},{6,7},{7,6},{8,9},{9,8},{10,11... | collective-permute-start | bytes 6291464 | tf_op jit(solution)/shard_map/ppermute | solution.py:32
  185.0 142.0 %all-gather.9.cloned.1.call-start = ((), (), s32[]{:S(2)}) async-start(), calls=%async_computation.2 | async-start | bytes 4718592 | tf_op jit(solution)/shard_map/all_gather | solution.py:332
  215.9 51.8 %collective-permute-start.14 = (bf16[4,768,512]{1,2,0:T(8,128)(2,1)S(1)}, bf16[4,768,512]{1,2,0:T(8,128)(2,1)}, u32[]{:S(2)}, u32[]{:S(2)}) collective-permute-start(bf16[4,768,512]{1,2,0:T(8,128)(2,1)S(1)} %pad_maximum_fusion.4), channel_id=1, source_target_pairs={{0,1},{1,0},{2,3},{3,2},{4,5},{5,4},{6,7},{7,6},{8,9},{9,8},{10,11... | collective-permute-start | bytes 9437192 | tf_op jit(solution)/shard_map/ppermute | solution.py:32
  283.4 108.2 %all-gather.11.cloned.1.call-start = ((), (), s32[]{:S(2)}) async-start(), calls=%async_computation.3 | async-start | bytes 4718592 | tf_op jit(solution)/shard_map/all_gather | solution.py:332
  308.4 536.0 %all-reduce.3.cloned.1.call-start = ((), (), s32[]{:S(2)}) async-start(), calls=%async_computation.4 | async-start | bytes 25165824 | tf_op jit(solution)/shard_map/psum | solution.py:363
  409.2 49.6 %collective-permute-start.16 = (bf16[128,2048]{1,0:T(8,128)(2,1)}, bf16[128,2048]{1,0:T(8,128)(2,1)S(1)}, u32[]{:S(2)}, u32[]{:S(2)}) collective-permute-start(bf16[128,2048]{1,0:T(8,128)(2,1)} %add_convert_fusion.50), channel_id=1, source_target_pairs={{0,2},{1,3},{2,4},{3,5},{4,6},{5,7},{6,0},{7,1},{8,10},{9,11},{10,... | collective-permute-start | bytes 1572872 | tf_op jit(solution)/shard_map/ppermute | solution.py:37
  460.9 50.1 %collective-permute-start.17 = (bf16[128,2048]{1,0:T(8,128)(2,1)}, bf16[128,2048]{1,0:T(8,128)(2,1)S(1)}, u32[]{:S(2)}, u32[]{:S(2)}) collective-permute-start(bf16[128,2048]{1,0:T(8,128)(2,1)} %add_convert_fusion.48), channel_id=1, source_target_pairs={{0,2},{1,3},{2,4},{3,5},{4,6},{5,7},{6,0},{7,1},{8,10},{9,11},{10,... | collective-permute-start | bytes 1572872 | tf_op jit(solution)/shard_map/ppermute | solution.py:37
  552.8 52.4 %collective-permute-start.31 = (bf16[1024,2048]{1,0:T(8,128)(2,1)}, bf16[1024,2048]{1,0:T(8,128)(2,1)}, u32[]{:S(2)}, u32[]{:S(2)}) collective-permute-start(bf16[1024,2048]{1,0:T(8,128)(2,1)} %convolution_convert_fusion.3), channel_id=1, source_target_pairs={{0,1},{1,0},{2,3},{3,2},{4,5},{5,4},{6,7},{7,6},{8,9},{9,8},{10,11... | collective-permute-start | bytes 12582920 | tf_op jit(solution)/shard_map/ppermute | solution.py:32
  605.2 94.2 %collective-permute-start.29 = (bf16[128,2048]{1,0:T(8,128)(2,1)}, bf16[128,2048]{1,0:T(8,128)(2,1)}, u32[]{:S(2)}, u32[]{:S(2)}) collective-permute-start(bf16[128,2048]{1,0:T(8,128)(2,1)} %add_convert_fusion.29), channel_id=1, source_target_pairs={{0,2},{1,3},{2,4},{3,5},{4,6},{5,7},{6,0},{7,1},{8,10},{9,11},{10,... | collective-permute-start | bytes 1572872 | tf_op jit(solution)/shard_map/ppermute | solution.py:37
  657.4 40.2 %collective-permute-start.44 = (bf16[1024,2048]{1,0:T(8,128)(2,1)}, bf16[1024,2048]{1,0:T(8,128)(2,1)}, u32[]{:S(2)}, u32[]{:S(2)}) collective-permute-start(bf16[1024,2048]{1,0:T(8,128)(2,1)} %convolution_convert_fusion), channel_id=1, source_target_pairs={{0,1},{1,0},{2,3},{3,2},{4,5},{5,4},{6,7},{7,6},{8,9},{9,8},{10,11... | collective-permute-start | bytes 12582920 | tf_op jit(solution)/shard_map/ppermute | solution.py:32
  672.7 132.9 %collective-permute-start.34 = (bf16[2,2,4,512,128]{3,4,2,1,0:T(8,128)(2,1)}, bf16[2,2,4,512,128]{3,4,2,1,0:T(8,128)(2,1)}, u32[]{:S(2)}, u32[]{:S(2)}) collective-permute-start(bf16[2,2,4,512,128]{3,4,2,1,0:T(8,128)(2,1)} %slice.410), channel_id=1, source_target_pairs={{0,1},{1,0},{2,3},{3,2},{4,5},{5,4},{6,7},{7,6},{8,9},{9,8},{10,11... | collective-permute-start | bytes 6291464 | tf_op jit(solution)/shard_map/ppermute | solution.py:32
  728.3 78.7 %collective-permute-start.46 = (bf16[256,2048]{1,0:T(8,128)(2,1)S(1)}, bf16[256,2048]{1,0:T(8,128)(2,1)S(1)}, u32[]{:S(2)}, u32[]{:S(2)}) collective-permute-start(bf16[256,2048]{1,0:T(8,128)(2,1)S(1)} %add_convert_fusion.7), channel_id=1, source_target_pairs={{0,2},{1,3},{2,4},{3,5},{4,6},{5,7},{6,0},{7,1},{8,10},{9,11},{10,... | collective-permute-start | bytes 3145736 | tf_op jit(solution)/shard_map/ppermute | solution.py:37
  728.4 71.5 %collective-permute-start.40 = (f32[2,2048]{1,0:T(2,128)S(1)}, f32[2,2048]{1,0:T(2,128)S(1)}, u32[]{:S(2)}, u32[]{:S(2)}) collective-permute-start(f32[2,2048]{1,0:T(2,128)S(1)} %fusion.154), channel_id=1, source_target_pairs={{0,4},{1,5},{2,6},{3,7},{4,0},{5,1},{6,2},{7,3},{8,12},{9,13},{10,... | collective-permute-start | bytes 49160 | tf_op jit(solution)/shard_map/ppermute | solution.py:223
  731.8 87.9 %collective-permute-start.43 = (bf16[256,2048]{1,0:T(8,128)(2,1)S(1)}, bf16[256,2048]{1,0:T(8,128)(2,1)S(1)}, u32[]{:S(2)}, u32[]{:S(2)}) collective-permute-start(bf16[256,2048]{1,0:T(8,128)(2,1)S(1)} %copy-done.65), channel_id=1, source_target_pairs={{0,2},{1,3},{2,4},{3,5},{4,6},{5,7},{6,0},{7,1},{8,10},{9,11},{10,... | collective-permute-start | bytes 3145736 | tf_op jit(solution)/shard_map/ppermute | solution.py:37
  803.7 68.1 %collective-permute-start.42 = (f32[2,2048]{1,0:T(2,128)S(1)}, f32[2,2048]{1,0:T(2,128)S(1)}, u32[]{:S(2)}, u32[]{:S(2)}) collective-permute-start(f32[2,2048]{1,0:T(2,128)S(1)} %add.672), channel_id=1, source_target_pairs={{0,16},{8,24},{16,0},{24,8},{1,17},{9,25},{17,1},{25,9},{2,18},{10... | collective-permute-start | bytes 49160 | tf_op jit(solution)/shard_map/ppermute | solution.py:41
  868.1 42.3 %collective-permute-start.53 = (bf16[128,2048]{1,0:T(8,128)(2,1)S(1)}, bf16[128,2048]{1,0:T(8,128)(2,1)S(1)}, u32[]{:S(2)}, u32[]{:S(2)}) collective-permute-start(bf16[128,2048]{1,0:T(8,128)(2,1)S(1)} %get-tuple-element.57), channel_id=1, source_target_pairs={{0,8},{8,0},{16,24},{24,16},{1,9},{9,1},{17,25},{25,17},{2,10},{10... | collective-permute-start | bytes 1572872 | tf_op jit(solution)/shard_map/ppermute | solution.py:41
  872.4 38.1 %collective-permute-start.52 = (bf16[128,2048]{1,0:T(8,128)(2,1)S(1)}, bf16[128,2048]{1,0:T(8,128)(2,1)S(1)}, u32[]{:S(2)}, u32[]{:S(2)}) collective-permute-start(bf16[128,2048]{1,0:T(8,128)(2,1)S(1)} %get-tuple-element.56), channel_id=1, source_target_pairs={{0,16},{8,24},{16,0},{24,8},{1,17},{9,25},{17,1},{25,9},{2,18},{10... | collective-permute-start | bytes 1572872 | tf_op jit(solution)/shard_map/ppermute | solution.py:41
  (138 other events, 2615.1 us)
Sparse Core Ops, SparseCore 0:
  69.8 55.8 all-gather.4
  185.1 45.0 all-gather.6
  283.5 43.4 all-gather.8
  328.4 45.8 all-gather.10
  554.0 239.2 all-reduce.2

commit v7 on v5

--- a/solution.py
+++ b/solution.py
@@ -45,7 +45,7 @@
     got = [tie(own, dep)]
     for _ in range(1, chips):
         got.append(ring(got[-1], chips))
-    return [own] + got[:0:-1], got[-2]
+    return [own] + got[:0:-1], got[-1]
 
 
 def ring_scatter(parts, chips):
@@ -124,6 +124,7 @@
         if not self.split:
             self.whole = lax.all_gather(shard, "seq", axis=0, tiled=True)
             self.token = dep
+            self.steps = [None, None]
             return
         part = width // rows
         half = depth // 2
@@ -138,19 +139,22 @@
         parts = [first, second, first_x, second_pair[0]]
         parts += [first_pair[0], second_y, first_pair[1], second_pair[1]]
         parts = jnp.concatenate(parts, axis=0).reshape(rows, (chips - 1) * depth, part)
+        self.steps = [(first_x, second_y), (first_pair, second_pair)]
         self.far = [parts, swap_core(parts, seq)]
         self.near = [shard, swap_core(shard, seq)]
 
-    def features(self, value):
+    def features(self, value, lane=None):
         if not self.split:
             out = own_order(dot(value, self.whole, ((1,), (1,))), *self.order)
             half = out.shape[1] // 2
             return [out[:, :half].astype(BF16), out[:, half:].astype(BF16)]
         count = value.shape[0]
-        blocks = value.reshape(count, 4, -1).transpose(1, 0, 2)
-        blocks = xor_order(blocks, self.row_at)
         out = []
         for near, far in zip(self.near, self.far, strict=True):
+            if out and lane is not None:
+                value = beside(value, lane)
+            blocks = value.reshape(count, 4, -1).transpose(1, 0, 2)
+            blocks = xor_order(blocks, self.row_at)
             term = jnp.einsum("ktc,kfc->ktf", blocks, far, preferred_element_type=F32)
             term = jnp.sum(term, axis=0).astype(BF16)
             term = term.reshape(count, 2, self.chips - 1, -1).transpose(0, 2, 1, 3)
@@ -197,17 +201,22 @@
     )
 
 
-def sum_rows(value, rows):
+def sum_rows(values, rows, other):
     if rows != 4:
-        return lax.psum(value.astype(BF16), "rows").astype(F32)
-    half = value.shape[0] // 2
-    first, second = value[:half].astype(BF16), value[half:].astype(BF16)
+        return [lax.psum(v.astype(BF16), "rows").astype(F32) for v in values], other
 
     def pair(item, mask):
         return item.astype(F32) + swap_row(item, rows, mask).astype(F32)
 
-    first, second = pair(first, 1).astype(BF16), pair(second, 2).astype(BF16)
-    return jnp.concatenate([pair(first, 2), pair(second, 1)], axis=0)
+    halves = []
+    for value in values:
+        half = value.shape[0] // 2
+        halves.append(pair(value[:half].astype(BF16), 1).astype(BF16))
+        halves.append(pair(value[half:].astype(BF16), 2).astype(BF16))
+    halves, other = lax.optimization_barrier((halves, other))
+    masks = [2, 1] * len(values)
+    sums = [pair(h, m) for h, m in zip(halves, masks, strict=True)]
+    return [jnp.concatenate(sums[2 * n : 2 * n + 2], axis=0) for n in range(len(values))], other
 
 
 def sum_all(value, rows, seq):
@@ -254,13 +263,13 @@
     gate_up_weight = jnp.concatenate([ffn_in_weight[:, 0], ffn_in_weight[:, 1]], axis=0)
     query_proj = Weight(query_weight, chips, rows, row_at, order)
     cache_own = kv_cache.reshape(rows_here, seg_len, 2, KV, HEAD).transpose(2, 0, 3, 1, 4)
-    cache_slots, token = ring_gather(cache_own, chips, dep=query_proj.token)
+    output_proj = Weight(output_weight, chips, rows, row_at, order, dep=query_proj.token)
+    cache_slots, token = ring_gather(cache_own, chips, dep=output_proj.token)
     cache_block = jnp.concatenate(cache_slots, axis=3)
+    cache_block = tie(cache_block, output_proj.steps[0])
     cache_all = jnp.concatenate([cache_block, swap_core(cache_block, seq)], axis=3)
-    output_proj = Weight(output_weight, chips, rows, row_at, order, dep=token)
     grad_group = [
-        lax.all_gather(tie(g.astype(BF16), output_proj.token), "seq", axis=0, tiled=True)
-        for g in grad_out
+        lax.all_gather(tie(g.astype(BF16), token), "seq", axis=0, tiled=True) for g in grad_out
     ]
     per = chips // KV
 
@@ -299,7 +308,7 @@
     inputs = tokens.astype(F32).reshape(rows_here * seg_len, width)
     inverse_one = lax.rsqrt(jnp.mean(inputs * inputs, axis=-1, keepdims=True) + EPS)
     normed_one = (inputs * inverse_one * gain_one).astype(BF16)
-    query = query_proj.features(normed_one)
+    query = tie(query_proj.features(normed_one), output_proj.steps[1])
     cache_slot = to_slots(cache_all)
     keys, values = cache_slot[0], cache_slot[1]
     query_heads = to_heads(query)
@@ -327,18 +336,19 @@
     units = down_weight.shape[0]
     hidden, grad_gate_up, grad_part, ffn_part = [], [], [], []
     for r in range(rows_here):
-        kept = dot(beside(normed_group[r], main), gate_up_weight, ((1,), (1,)))
+        kept = dot(normed_group[r], gate_up_weight, ((1,), (1,)))
         gate, upper = kept[:, :units], kept[:, units:]
         sigma = jax.nn.sigmoid(gate)
-        grad_hidden = dot(beside(grad_group[r], main), down_weight, ((1,), (1,)))
+        grad_hidden = dot(beside(grad_group[r], fill), down_weight, ((1,), (1,)))
         hidden.append((gate * sigma * upper).astype(BF16))
         grad_gate = grad_hidden * upper * sigma * (1.0 + gate * (1.0 - sigma))
         grad_up = grad_hidden * gate * sigma
         grad_gate_up.append(jnp.concatenate([grad_gate, grad_up], axis=1).astype(BF16))
-        part = dot(beside(grad_gate_up[r], main), gate_up_weight, ((1,), (0,))).astype(BF16)
-        grad_part.append(part)
+        part = dot(beside(grad_gate_up[r], fill), gate_up_weight, ((1,), (0,))).astype(BF16)
+        grad_part.append(lax.psum_scatter(part, "seq", scatter_dimension=0, tiled=True))
         ffn_part.append(dot(hidden[r], down_weight, ((1,), (0,))).astype(BF16))
-        main.add(("grad", r), scatter_tokens(part, chips, place, core))
+        if r == 0:
+            fill.add(("ffn", 0), scatter_tokens(ffn_part[0], chips, place, core))
 
     def over_tokens(left, right, start, size):
         total = 0.0
@@ -350,14 +360,12 @@
     gate_part = over_tokens(grad_gate_up, normed_group, 0, units)
     up_part = over_tokens(grad_gate_up, normed_group, units, units)
     down_part = over_tokens(hidden, grad_group, 0, units)
-    for r in range(rows_here):
-        fill.add(("ffn", r), scatter_tokens(ffn_part[r], chips, place, core))
     parts = (gate_part, up_part, down_part)
     summed = lax.psum(parts, "rows")
 
     grad_middle, gain_two_grad = [], 0.0
     for r in range(rows_here):
-        grad_normed_two = main.result(("grad", r))
+        grad_normed_two = grad_part[r].astype(F32)
         if r:
             grad_normed_two, parts = lax.optimization_barrier((grad_normed_two, parts))
         scaled_two = middle[r] * inverse_two[r]
@@ -365,6 +373,9 @@
         grad_middle.append(
             grad_out[r] + norm_back(grad_normed_two, scaled_two, inverse_two[r], gain_two)
         )
+    for r in range(1, rows_here):
+        part = tie(ffn_part[r], grad_middle[-1])
+        fill.add(("ffn", r), scatter_tokens(part, chips, place, core))
     grad_middle = jnp.concatenate(grad_middle, axis=0)
     grad_branch = grad_middle.astype(BF16)
     output_part = [dot(half, grad_branch, ((0,), (0,))).astype(BF16) for half in mixed]
@@ -376,15 +387,16 @@
         return scatter_halves(lambda j: take(parts[0], j), parts[1], take, chips)
 
     main.add("output", scatter_rows(output_part))
-    grad_heads = to_heads(output_proj.features(grad_branch))
+    grad_heads = to_heads(output_proj.features(tie(grad_branch, output_part[1]), main))
     delta = jnp.sum(grad_heads.astype(F32) * mixed_heads, axis=-1, keepdims=True)
     scores = heads_dot("rjqd,rjkd->rjqk", query_heads, keys) * scale
     probs = jnp.where(valid, jnp.exp(scores - lse), 0.0)
     grad_probs = heads_dot("rjqd,rjkd->rjqk", grad_heads, values)
-    grad_scores = (probs * (grad_probs - delta)).astype(BF16)
+    grad_scores = beside((probs * (grad_probs - delta)).astype(BF16), main)
     query_term = from_heads(
         (heads_dot("rjqk,rjkd->rjqd", grad_scores, keys) * scale).astype(BF16)
     )
+    query_term[0] = beside(query_term[0], main)
     grad_keys = heads_dot("rjqk,rjqd->rjkd", grad_scores, query_heads) * scale
     grad_values = heads_dot("rjqk,rjqd->rjkd", probs.astype(BF16), grad_heads)
     cache_part = from_slots(jnp.stack([grad_keys.astype(BF16), grad_values.astype(BF16)]))
@@ -406,19 +418,19 @@
     scaled_one = inputs * inverse_one
     gain_one_grad = jnp.sum(grad_normed_one * scaled_one, axis=0)
     input_grad = grad_middle + norm_back(grad_normed_one, scaled_one, inverse_one, gain_one)
-    gain_grad = sum_all(jnp.stack([gain_one_grad, gain_two_grad]), rows, seq)
+    gain_grad = jnp.stack([gain_one_grad, gain_two_grad])
 
     layer_out = [
         (live[r] * (middle[r] + fill.result(("ffn", r)))).astype(BF16) for r in range(rows_here)
     ]
     cache_grad = fill.result("cache")
     cache_grad = cache_grad.transpose(1, 3, 0, 2, 4).reshape(rows_here, seg_len, 2, KV * HEAD)
-    summed, output_sum, query_sum = lax.optimization_barrier(
-        (summed, main.result("output").astype(BF16), main.result("query").astype(BF16))
-    )
+    sums = (main.result("output").astype(BF16), main.result("query").astype(BF16))
+    summed, sums, gain_grad = lax.optimization_barrier((summed, sums, gain_grad))
+    gain_grad = sum_all(gain_grad, rows, seq)
     gate_grad, up_grad, down_grad = summed
-    output_grad, query_grad = sum_rows(output_sum, rows), sum_rows(query_sum, rows)
     in_grad = jnp.concatenate([gate_grad, up_grad], axis=1)
+    (output_grad, query_grad), in_grad = sum_rows(sums, rows, in_grad)
     in_grad = lax.optimization_barrier(in_grad.reshape(units, 2, width))
     return (
         jnp.stack(layer_out),

time: 915 us -> 896 us (0.979)
  waiting for transfers between devices: 363 us -> 278 us
  other arithmetic: 121 us -> 156 us
  local copies, waits for them, and re-layouts: 140 us -> 173 us
    ppermute x30 -> x24, waiting for transfers between devices: 251 us -> 186 us  [ring(): return lax.ppermute(value, 'seq', pairs)]
    ppermute x3, waiting for transfers between devices: 43.9 us -> 1.41 us  [sum_all(): lax.ppermute(value, 'seq', [(s, s ^ mask) for s in range(seq)])]
    reduce_scatter x0 -> x2, waiting for transfers between devices: none -> 31.3 us  [local(): lax.psum_scatter(part, 'seq', scatter_dimension=0, tiled=True)]
    ppermute x18, waiting for transfers between devices: 47.2 us -> 32.9 us  [swap_row(): return lax.ppermute(value, 'rows', [(r, r ^ mask) for r in range(rows)])]
    another operation x8, local copies, waits for them, and re-layouts: 8.53 us -> 21.3 us  [to_heads(): jnp.stack([h.reshape(rows_here, seg_len, chips, -1, HEAD) for h in halves])]
    unnamed x214 -> x230, local copies, waits for them, and re-layouts: 48.3 us -> 36.7 us
    convert_element_type x14 -> x10, other arithmetic: 23.1 us -> 23.8 us  [ring_scatter(): sent = total.astype(BF16)]
  transfers between devices with their start and end apart: 68 -> 62, of which waited for: 33 -> 29; matrix products, arithmetic and copies ran while one was open for 52% -> 59% of each run, Pallas kernels for 0% -> 0%
where the time goes in v7:
time: 896 us; the launch traced here: 885 us
  waiting for transfers between devices  278 us (31%)
  matrix products  226 us (25%)
  local copies, waits for them, and re-layouts  173 us (19%)
  other arithmetic  156 us (17%)
  starting transfers between devices  36 us (4%)
  between operations  16.3 us (2%)
    ppermute x24, waiting for transfers between devices, ring(): return lax.ppermute(value, 'seq', pairs)  186 us
    dot_general x26, matrix products, dot(): lax.dot_general(left, right, (dims, ((), ())), preferred_element_type=F32)  162 us
    dot_general x6, matrix products, heads_dot(): return jnp.einsum(spec, left, right, preferred_element_type=F32)  41.7 us
    unnamed x230, local copies, waits for them, and re-layouts  36.7 us
    ppermute x18, waiting for transfers between devices, swap_row(): return lax.ppermute(value, 'rows', [(r, r ^ mask) for r in range(rows)])  32.9 us
    reduce_scatter x2, waiting for transfers between devices, local(): lax.psum_scatter(part, 'seq', scatter_dimension=0, tiled=True)  31.3 us
    all_gather x2, waiting for transfers between devices, local(): lax.all_gather(n, 'seq', axis=0, tiled=True)  25.1 us
    convert_element_type x10, other arithmetic, ring_scatter(): sent = total.astype(BF16)  23.8 us
  transfers between devices with their start and end apart: 62, of which 29 were waited for; matrix products, arithmetic and copies ran while one was open for 59% of the time, Pallas kernels for 0%

profile of v7, /device:TPU:0, one launch (start us, length us, event | category | flops | bytes accessed | tf_op | source)
XLA Modules:
  0.0 884.9 jit_solution(2696197464970395482)
XLA Ops:
  87.0 9.6 %collective-permute-done.17 = bf16[2,2,4,128,128]{4,3,2,1,0:T(8,128)(2,1)} collective-permute-done((bf16[2,2,4,128,128]{4,3,2,1,0:T(8,128)(2,1)}, bf16[2,2,4,128,128]{4,3,2,1,0:T(8,128)(2,1)}, u32[]{:S(2)}, u32[]{:S(2)}) %collective-permute-start.17) | collective-permute-done | bytes 524320 | tf_op jit(solution)/shard_map/ppermute | solution.py:37
  122.2 10.1 %collective-permute-done.5 = bf16[2,3,128,512]{3,2,1,0:T(8,128)(2,1)S(1)} collective-permute-done((bf16[2,3,128,512]{3,2,1,0:T(8,128)(2,1)S(1)}, bf16[2,3,128,512]{3,2,1,0:T(8,128)(2,1)S(1)}, u32[]{:S(2)}, u32[]{:S(2)}) %collective-permute-start.5) | collective-permute-done | bytes 786464 | tf_op jit(solution)/shard_map/ppermute | solution.py:41
  244.8 17.7 %fusion.81 = (bf16[1024,1,2048]{2,1,0:T(2,128)(2,1)}, bf16[1024,1,2048]{2,1,0:T(2,128)(2,1)}) fusion(bf16[1024,2,2048]{2,1,0:T(2,128)(2,1)} %param.15), kind=kLoop, calls=%fused_computation.289 | loop fusion | bytes 16777216 | tf_op jit(solution)/shard_map/slice | solution.py:263
  262.7 15.0 %copy_bitcast_fusion = (bf16[1024,2048]{1,0:T(8,128)(2,1)}, bf16[1024,2048]{1,0:T(8,128)(2,1)}) fusion(bf16[1024,1,2048]{2,1,0:T(2,128)(2,1)} %get-tuple-element.104, bf16[1024,1,2048]{2,1,0:T(2,128)(2,1)} %get-tuple-element.103), kind=kLoop, calls=%fused_computation.38 | loop fusion | bytes 16777216 | tf_op jit(solution)/shard_map/squeeze | solution.py:263
  277.7 10.7 %all-gather.9.cloned.1.call-done = bf16[1024,2048]{1,0:T(8,128)(2,1)} async-done(((bf16[128,2048]{1,0:T(8,128)(2,1)}), bf16[1024,2048]{1,0:T(8,128)(2,1)}) %all-gather.9.cloned.1.call-update) | async-done | bytes 4194320 | tf_op jit(solution)/shard_map/all_gather | solution.py:333
  288.4 15.3 %fusion.80 = f32[1024,2048]{1,0:T(8,128)} fusion(bf16[1024,2048]{1,0:T(8,128)(2,1)} %all-gather.9.cloned.1.call-done, bf16[1024,2048]{1,0:T(8,128)(2,1)} %get-tuple-element.172, bf16[1024,2048]{1,0:T(8,128)(2,1)} %get-tuple-element.173), kind=kOutput, calls=%fused_computation.288 | convolution fusion | flops 8606711808 | bytes 20971520 | tf_op jit(solution)/shard_map/dot_general | solution.py:17
  303.6 10.3 %multiply_convert_fusion.2 = (bf16[1024,1024]{1,0:T(8,128)(2,1)}, bf16[1024,1024]{1,0:T(8,128)(2,1)}, bf16[1024,1024]{1,0:T(8,128)(2,1)S(1)}) fusion(f32[1024,2048]{1,0:T(8,128)} %fusion.80, bf16[1024,2048]{1,0:T(8,128)(2,1)S(1)} %copy-done.90, bf16[1024,2048]{1,0:T(8,128)(2,1)S(1)} %copy-done.88), kind=kOutput, calls=%fused_computation.41 | convolution fusion | flops 4311744512 | bytes 23068672 | tf_op jit(solution)/shard_map/dot_general | solution.py:17
  321.4 14.4 %all-gather.11.cloned.1.call-done = bf16[1024,2048]{1,0:T(8,128)(2,1)} async-done(((bf16[128,2048]{1,0:T(8,128)(2,1)}), bf16[1024,2048]{1,0:T(8,128)(2,1)}) %all-gather.11.cloned.1.call-update) | async-done | bytes 4194320 | tf_op jit(solution)/shard_map/all_gather | solution.py:333
  335.8 15.3 %fusion.79 = f32[1024,2048]{1,0:T(8,128)} fusion(bf16[1024,2048]{1,0:T(8,128)(2,1)} %all-gather.11.cloned.1.call-done, bf16[1024,2048]{1,0:T(8,128)(2,1)} %get-tuple-element.172, bf16[1024,2048]{1,0:T(8,128)(2,1)} %get-tuple-element.173), kind=kOutput, calls=%fused_computation.287 | convolution fusion | flops 8606711808 | bytes 20971520 | tf_op jit(solution)/shard_map/dot_general | solution.py:17
  352.6 11.3 %multiply_convert_fusion.5 = (bf16[1024,1024]{1,0:T(8,128)(2,1)S(1)}, bf16[1024,1024]{1,0:T(8,128)(2,1)S(1)}, bf16[1024,1024]{1,0:T(8,128)(2,1)}) fusion(f32[1024,2048]{1,0:T(8,128)} %fusion.79, bf16[1024,2048]{1,0:T(8,128)(2,1)} %all-gather.7.cloned.1.call-done, bf16[1024,2048]{1,0:T(8,128)(2,1)S(1)} %copy-done.89), kind=kOutput, calls=%fused_computation.44 | convolution fusion | flops 4311744512 | bytes 23068672 | tf_op jit(solution)/shard_map/dot_general | solution.py:17
  369.8 10.4 %convolution_convert_fusion.4 = bf16[1024,2048]{1,0:T(8,128)(2,1)} fusion(bf16[1024,2048]{1,0:T(8,128)(2,1)S(1)} %pad_maximum_fusion.2, bf16[1024,2048]{1,0:T(8,128)(2,1)S(1)} %copy-done.40, bf16[1024,2048]{1,0:T(8,128)(2,1)S(1)} %copy-done.41), kind=kOutput, calls=%fused_computation.53 | convolution fusion | flops 8608808960 | bytes 16777216 | tf_op jit(solution)/shard_map/dot_general | solution.py:17
  381.7 13.2 %fusion.22 = bf16[1024,2048]{1,0:T(8,128)(2,1)} fusion(bf16[1024,1024]{1,0:T(8,128)(2,1)} %get-tuple-element.97, bf16[1024,1024]{1,0:T(8,128)(2,1)S(1)} %copy-done.94, bf16[1024,2048]{1,0:T(8,128)(2,1)} %get-tuple-element.172, bf16[1024,2048]{1,0:T(8,128)(2,1)} %get-tuple-element.173), kind=kOutput, calls=%fused_computation.56 | convolution fusion | flops 8617197568 | bytes 16777216 | tf_op jit(solution)/shard_map/dot_general | solution.py:17
  395.6 10.8 %fusion.94 = f32[1024,2048]{1,0:T(8,128)} fusion(bf16[1024,1024]{1,0:T(8,128)(2,1)} %copy-done.97, bf16[1024,2048]{1,0:T(8,128)(2,1)} %all-gather.5.cloned.1.call-done), kind=kOutput, calls=%fused_computation.302 | convolution fusion | flops 4294967296 | bytes 14680064 | tf_op jit(solution)/shard_map/dot_general | solution.py:17
  450.7 18.3 %collective-permute-done.24 = bf16[128,2048]{1,0:T(8,128)(2,1)S(1)} collective-permute-done((bf16[128,2048]{1,0:T(8,128)(2,1)S(1)}, bf16[128,2048]{1,0:T(8,128)(2,1)S(1)}, u32[]{:S(2)}, u32[]{:S(2)}) %collective-permute-start.24) | collective-permute-done | bytes 524320 | tf_op jit(solution)/shard_map/ppermute | solution.py:37
  472.4 31.3 %reduce-scatter.5.cloned.1.call-done = bf16[128,2048]{1,0:T(8,128)(2,1)} async-done(((bf16[1024,2048]{1,0:T(8,128)(2,1)}), bf16[128,2048]{1,0:T(8,128)(2,1)}) %reduce-scatter.5.cloned.1.call-update) | async-done | bytes 524304 | tf_op jit(solution)/shard_map/reduce_scatter | solution.py:348
  526.5 14.4 %collective-permute-done.27 = bf16[128,2048]{1,0:T(8,128)(2,1)S(1)} collective-permute-done((bf16[128,2048]{1,0:T(8,128)(2,1)S(1)}, bf16[128,2048]{1,0:T(8,128)(2,1)S(1)}, u32[]{:S(2)}, u32[]{:S(2)}) %collective-permute-start.27) | collective-permute-done | bytes 524320 | tf_op jit(solution)/shard_map/ppermute | solution.py:37
  586.1 11.9 %multiply_convert_fusion = bf16[2,4,512,1024]{3,2,1,0:T(8,128)(2,1)} fusion(f32[2,4,512,1024]{3,2,1,0:T(8,128)} %copy-done, f32[2,4,512]{2,1,0:T(4,128)S(1)} %multiply_reduce_fusion.2, f32[2,4,512]{2,1,0:T(4,128)S(1)} %bitcast.404, pred[2,512,1024]{2,1,0:T(8,128)(4,1)S(1)} %copy-done.20, bf16[2,4,512,128]{3,2,1,0:T(8,128)(2,1)S(1)} %bitcast.354, ...), kind=kOutput, calls=%fused_computation | convolution fusion | flops 1098907648 | bytes 29392896 | tf_op jit(solution)/shard_map/rjqd,rjkd->rjqk/dot_general | solution.py:300
  621.0 9.5 %convert_bitcast_fusion = bf16[1,2,4,1024,128]{3,4,2,1,0:T(8,128)(2,1)} fusion(bf16[2,4,512,128]{3,2,1,0:T(8,128)(2,1)S(1)} %bitcast.355, f32[2,4,512,1024]{3,2,1,0:T(8,128)} %copy-done, f32[2,4,512]{2,1,0:T(4,128)S(1)} %bitcast.405, pred[2,512,1024]{2,1,0:T(8,128)(4,1)S(1)} %copy-done.20), kind=kOutput, calls=%fused_computation.86 | convolution fusion | flops 1091567616 | bytes 20987904 | tf_op jit(solution)/shard_map/rjqk,rjqd->rjkd/dot_general | solution.py:300
  684.3 27.1 %collective-permute-done.39 = bf16[256,2048]{1,0:T(8,128)(2,1)} collective-permute-done((bf16[256,2048]{1,0:T(8,128)(2,1)}, bf16[256,2048]{1,0:T(8,128)(2,1)}, u32[]{:S(2)}, u32[]{:S(2)}) %collective-permute-start.39) | collective-permute-done | bytes 1048608 | tf_op jit(solution)/shard_map/ppermute | solution.py:37
  718.8 22.8 %collective-permute-done.40 = bf16[256,2048]{1,0:T(8,128)(2,1)S(1)} collective-permute-done((bf16[256,2048]{1,0:T(8,128)(2,1)S(1)}, bf16[256,2048]{1,0:T(8,128)(2,1)S(1)}, u32[]{:S(2)}, u32[]{:S(2)}) %collective-permute-start.40) | collective-permute-done | bytes 1048608 | tf_op jit(solution)/shard_map/ppermute | solution.py:37
  743.5 9.4 %collective-permute-done.34 = bf16[2,2,4,128,128]{3,4,2,1,0:T(8,128)(2,1)S(1)} collective-permute-done((bf16[2,2,4,128,128]{3,4,2,1,0:T(8,128)(2,1)S(1)}, bf16[2,2,4,128,128]{3,4,2,1,0:T(8,128)(2,1)S(1)}, u32[]{:S(2)}, u32[]{:S(2)}) %collective-permute-start.34) | collective-permute-done | bytes 524320 | tf_op jit(solution)/shard_map/ppermute | solution.py:37
  757.0 27.4 %collective-permute-done.35 = bf16[2,2,4,128,128]{3,4,2,1,0:T(8,128)(2,1)S(1)} collective-permute-done((bf16[2,2,4,128,128]{3,4,2,1,0:T(8,128)(2,1)S(1)}, bf16[2,2,4,128,128]{3,4,2,1,0:T(8,128)(2,1)S(1)}, u32[]{:S(2)}, u32[]{:S(2)}) %collective-permute-start.35) | collective-permute-done | bytes 524320 | tf_op jit(solution)/shard_map/ppermute | solution.py:37
  836.2 14.4 %reshape.375 = bf16[1024,2,2048]{2,1,0:T(2,128)(2,1)} reshape(bf16[1024,4096]{1,0:T(8,128)(2,1)} %pad_maximum_fusion.1) | data formatting | bytes 16777216 | tf_op jit(solution)/shard_map/reshape | solution.py:434
  850.6 11.8 %convert_element_type.695 = f32[1024,2,2048]{2,1,0:T(2,128)} convert(bf16[1024,2,2048]{2,1,0:T(2,128)(2,1)} %reshape.375) | non-fusion elementwise | flops 4194304 | bytes 25165824 | tf_op jit(solution)/shard_map/convert_element_type | solution.py:442
  (548 shorter events, 506.4 us)
Async XLA Ops:
  7.2 215.3 %all-gather.5.cloned.1.call-start = ((), (), s32[]{:S(2)}) async-start(), calls=%async_computation.2 | async-start | bytes 4718592 | tf_op jit(solution)/shard_map/all_gather | solution.py:272
  7.2 106.8 %collective-permute-start.7 = (bf16[256,2048]{1,0:T(8,128)(2,1)}, bf16[256,2048]{1,0:T(8,128)(2,1)}, u32[]{:S(2)}, u32[]{:S(2)}) collective-permute-start(bf16[256,2048]{1,0:T(8,128)(2,1)} %param.13), channel_id=1, source_target_pairs={{0,1},{1,0},{2,3},{3,2},{4,5},{5,4},{6,7},{7,6},{8,9},{9,8},{10,11... | collective-permute-start | bytes 3145736 | tf_op jit(solution)/shard_map/ppermute | solution.py:32
  12.0 227.4 %collective-permute-start.20 = (bf16[256,2048]{1,0:T(8,128)(2,1)}, bf16[256,2048]{1,0:T(8,128)(2,1)}, u32[]{:S(2)}, u32[]{:S(2)}) collective-permute-start(bf16[256,2048]{1,0:T(8,128)(2,1)} %param.14), channel_id=1, source_target_pairs={{0,1},{1,0},{2,3},{3,2},{4,5},{5,4},{6,7},{7,6},{8,9},{9,8},{10,11... | collective-permute-start | bytes 3145736 | tf_op jit(solution)/shard_map/ppermute | solution.py:32
  107.9 135.2 %all-gather.7.cloned.1.call-start = ((), (), s32[]{:S(2)}) async-start(), calls=%async_computation.3 | async-start | bytes 4718592 | tf_op jit(solution)/shard_map/all_gather | solution.py:272
  136.7 33.2 %collective-permute-start.8 = (bf16[4,768,512]{2,1,0:T(8,128)(2,1)}, bf16[4,768,512]{2,1,0:T(8,128)(2,1)}, u32[]{:S(2)}, u32[]{:S(2)}) collective-permute-start(bf16[4,768,512]{2,1,0:T(8,128)(2,1)} %bitcast.22), channel_id=1, source_target_pairs={{0,1},{1,0},{2,3},{3,2},{4,5},{5,4},{6,7},{7,6},{8,9},{9,8},{10,11... | collective-permute-start | bytes 9437192 | tf_op jit(solution)/shard_map/ppermute | solution.py:32
  145.2 45.6 %collective-permute-start.19 = (bf16[2,2,4,512,128]{4,3,2,1,0:T(8,128)(2,1)}, bf16[2,2,4,512,128]{4,3,2,1,0:T(8,128)(2,1)}, u32[]{:S(2)}, u32[]{:S(2)}) collective-permute-start(bf16[2,2,4,512,128]{4,3,2,1,0:T(8,128)(2,1)} %pad_maximum_fusion.3), channel_id=1, source_target_pairs={{0,1},{1,0},{2,3},{3,2},{4,5},{5,4},{6,7},{7,6},{8,9},{9,8},{10,11... | collective-permute-start | bytes 6291464 | tf_op jit(solution)/shard_map/ppermute | solution.py:32
  169.6 60.3 %collective-permute-start.21 = (bf16[4,768,512]{1,2,0:T(8,128)(2,1)}, bf16[4,768,512]{1,2,0:T(8,128)(2,1)S(1)}, u32[]{:S(2)}, u32[]{:S(2)}) collective-permute-start(bf16[4,768,512]{1,2,0:T(8,128)(2,1)} %copy.59), channel_id=1, source_target_pairs={{0,1},{1,0},{2,3},{3,2},{4,5},{5,4},{6,7},{7,6},{8,9},{9,8},{10,11... | collective-permute-start | bytes 9437192 | tf_op jit(solution)/shard_map/ppermute | solution.py:32
  169.6 118.7 %all-gather.9.cloned.1.call-start = ((), (), s32[]{:S(2)}) async-start(), calls=%async_computation.4 | async-start | bytes 4718592 | tf_op jit(solution)/shard_map/all_gather | solution.py:333
  244.2 91.5 %all-gather.11.cloned.1.call-start = ((), (), s32[]{:S(2)}) async-start(), calls=%async_computation.5 | async-start | bytes 4718592 | tf_op jit(solution)/shard_map/all_gather | solution.py:333
  244.8 226.5 %reduce-scatter.3.cloned.1.call-start = ((), (), s32[]{:S(2)}) async-start(), calls=%async_computation.6 | async-start | bytes 4718592 | tf_op jit(solution)/shard_map/reduce_scatter | solution.py:348
  380.2 123.5 %reduce-scatter.5.cloned.1.call-start = ((), (), s32[]{:S(2)}) async-start(), calls=%async_computation.7 | async-start | bytes 4718592 | tf_op jit(solution)/shard_map/reduce_scatter | solution.py:348
  395.0 394.4 %all-reduce.3.cloned.1.call-start = ((), (), s32[]{:S(2)}) async-start(), calls=%async_computation.8 | async-start | bytes 25165824 | tf_op jit(solution)/shard_map/psum | solution.py:364
  471.3 34.8 %collective-permute-start.25 = (bf16[128,2048]{1,0:T(8,128)(2,1)}, bf16[128,2048]{1,0:T(8,128)(2,1)}, u32[]{:S(2)}, u32[]{:S(2)}) collective-permute-start(bf16[128,2048]{1,0:T(8,128)(2,1)} %add_convert_fusion.34), channel_id=1, source_target_pairs={{0,2},{1,3},{2,4},{3,5},{4,6},{5,7},{6,0},{7,1},{8,10},{9,11},{10,... | collective-permute-start | bytes 1572872 | tf_op jit(solution)/shard_map/ppermute | solution.py:37
  515.1 46.4 %collective-permute-start.30 = (bf16[1024,2048]{1,0:T(8,128)(2,1)}, bf16[1024,2048]{1,0:T(8,128)(2,1)}, u32[]{:S(2)}, u32[]{:S(2)}) collective-permute-start(bf16[1024,2048]{1,0:T(8,128)(2,1)} %convolution_convert_fusion.3), channel_id=1, source_target_pairs={{0,1},{1,0},{2,3},{3,2},{4,5},{5,4},{6,7},{7,6},{8,9},{9,8},{10,11... | collective-permute-start | bytes 12582920 | tf_op jit(solution)/shard_map/ppermute | solution.py:32
  561.5 56.5 %collective-permute-start.29 = (bf16[128,2048]{1,0:T(8,128)(2,1)}, bf16[128,2048]{1,0:T(8,128)(2,1)}, u32[]{:S(2)}, u32[]{:S(2)}) collective-permute-start(bf16[128,2048]{1,0:T(8,128)(2,1)} %add_convert_fusion.28), channel_id=1, source_target_pairs={{0,2},{1,3},{2,4},{3,5},{4,6},{5,7},{6,0},{7,1},{8,10},{9,11},{10,... | collective-permute-start | bytes 1572872 | tf_op jit(solution)/shard_map/ppermute | solution.py:37
  564.1 34.9 %collective-permute-start.31 = (bf16[256,2048]{1,0:T(8,128)(2,1)}, bf16[256,2048]{1,0:T(8,128)(2,1)}, u32[]{:S(2)}, u32[]{:S(2)}) collective-permute-start(bf16[256,2048]{1,0:T(8,128)(2,1)} %add_convert_fusion.16), channel_id=1, source_target_pairs={{0,2},{1,3},{2,4},{3,5},{4,6},{5,7},{6,0},{7,1},{8,10},{9,11},{10,... | collective-permute-start | bytes 3145736 | tf_op jit(solution)/shard_map/ppermute | solution.py:37
  618.0 50.3 %collective-permute-start.38 = (bf16[1024,2048]{1,0:T(8,128)(2,1)}, bf16[1024,2048]{1,0:T(8,128)(2,1)}, u32[]{:S(2)}, u32[]{:S(2)}) collective-permute-start(bf16[1024,2048]{1,0:T(8,128)(2,1)} %convolution_convert_fusion), channel_id=1, source_target_pairs={{0,1},{1,0},{2,3},{3,2},{4,5},{5,4},{6,7},{7,6},{8,9},{9,8},{10,11... | collective-permute-start | bytes 12582920 | tf_op jit(solution)/shard_map/ppermute | solution.py:32
  644.2 73.1 %collective-permute-start.33 = (bf16[2,2,4,512,128]{3,4,2,1,0:T(8,128)(2,1)}, bf16[2,2,4,512,128]{3,4,2,1,0:T(8,128)(2,1)}, u32[]{:S(2)}, u32[]{:S(2)}) collective-permute-start(bf16[2,2,4,512,128]{3,4,2,1,0:T(8,128)(2,1)} %slice.427), channel_id=1, source_target_pairs={{0,1},{1,0},{2,3},{3,2},{4,5},{5,4},{6,7},{7,6},{8,9},{9,8},{10,11... | collective-permute-start | bytes 6291464 | tf_op jit(solution)/shard_map/ppermute | solution.py:32
  662.0 92.6 %collective-permute-start.37 = (bf16[256,2048]{1,0:T(8,128)(2,1)}, bf16[256,2048]{1,0:T(8,128)(2,1)}, u32[]{:S(2)}, u32[]{:S(2)}) collective-permute-start(bf16[256,2048]{1,0:T(8,128)(2,1)} %add_convert_fusion.12), channel_id=1, source_target_pairs={{0,2},{1,3},{2,4},{3,5},{4,6},{5,7},{6,0},{7,1},{8,10},{9,11},{10,... | collective-permute-start | bytes 3145736 | tf_op jit(solution)/shard_map/ppermute | solution.py:37
  671.7 39.8 %collective-permute-start.39 = (bf16[256,2048]{1,0:T(8,128)(2,1)}, bf16[256,2048]{1,0:T(8,128)(2,1)}, u32[]{:S(2)}, u32[]{:S(2)}) collective-permute-start(bf16[256,2048]{1,0:T(8,128)(2,1)} %add_convert_fusion.9), channel_id=1, source_target_pairs={{0,2},{1,3},{2,4},{3,5},{4,6},{5,7},{6,0},{7,1},{8,10},{9,11},{10,... | collective-permute-start | bytes 3145736 | tf_op jit(solution)/shard_map/ppermute | solution.py:37
  718.7 34.2 %collective-permute-start.34 = (bf16[2,2,4,128,128]{3,4,2,1,0:T(8,128)(2,1)S(1)}, bf16[2,2,4,128,128]{3,4,2,1,0:T(8,128)(2,1)S(1)}, u32[]{:S(2)}, u32[]{:S(2)}) collective-permute-start(bf16[2,2,4,128,128]{3,4,2,1,0:T(8,128)(2,1)S(1)} %add_convert_fusion.26), channel_id=1, source_target_pairs={{0,2},{1,3},{2,4},{3,5},{4,6},{5,7},{6,0},{7,1},{8,10},{9,11},{10,... | collective-permute-start | bytes 1572872 | tf_op jit(solution)/shard_map/ppermute | solution.py:37
  743.4 43.2 %collective-permute-start.41 = (bf16[256,2048]{1,0:T(8,128)(2,1)S(1)}, bf16[256,2048]{1,0:T(8,128)(2,1)S(1)}, u32[]{:S(2)}, u32[]{:S(2)}) collective-permute-start(bf16[256,2048]{1,0:T(8,128)(2,1)S(1)} %add_convert_fusion.5), channel_id=1, source_target_pairs={{0,2},{1,3},{2,4},{3,5},{4,6},{5,7},{6,0},{7,1},{8,10},{9,11},{10,... | collective-permute-start | bytes 3145736 | tf_op jit(solution)/shard_map/ppermute | solution.py:37
  821.2 44.1 %collective-permute-start.53 = (bf16[128,2048]{1,0:T(8,128)(2,1)}, bf16[128,2048]{1,0:T(8,128)(2,1)}, u32[]{:S(2)}, u32[]{:S(2)}) collective-permute-start(bf16[128,2048]{1,0:T(8,128)(2,1)} %get-tuple-element.66), channel_id=1, source_target_pairs={{0,16},{8,24},{16,0},{24,8},{1,17},{9,25},{17,1},{25,9},{2,18},{10... | collective-permute-start | bytes 1572872 | tf_op jit(solution)/shard_map/ppermute | solution.py:41
  825.2 41.5 %collective-permute-start.54 = (bf16[128,2048]{1,0:T(8,128)(2,1)}, bf16[128,2048]{1,0:T(8,128)(2,1)S(1)}, u32[]{:S(2)}, u32[]{:S(2)}) collective-permute-start(bf16[128,2048]{1,0:T(8,128)(2,1)} %get-tuple-element.67), channel_id=1, source_target_pairs={{0,8},{8,0},{16,24},{24,16},{1,9},{9,1},{17,25},{25,17},{2,10},{10... | collective-permute-start | bytes 1572872 | tf_op jit(solution)/shard_map/ppermute | solution.py:41
  (142 other events, 2157.0 us)
Sparse Core Ops, SparseCore 0:
  108.0 45.1 all-gather.4
  169.7 43.9 all-gather.6
  244.3 43.9 all-gather.8
  289.8 45.9 all-gather.10
  380.3 50.5 reduce-scatter.2
  433.1 70.6 reduce-scatter.4
  517.7 239.0 all-reduce.2

commit v8 on v7

--- a/solution.py
+++ b/solution.py
@@ -127,18 +127,18 @@
             self.steps = [None, None]
             return
         part = width // rows
-        half = depth // 2
+        half = part // 2
         mine = lax.dynamic_slice_in_dim(shard, row_at * part, part, axis=1)
         slots, self.token = ring_gather(mine, chips, dep=dep)
-        first = jnp.stack([v[:half] for v in slots[1:]])
-        second = jnp.stack([v[half:] for v in slots[1:]])
+        first = jnp.stack([v[:, :half] for v in slots[1:]])
+        second = jnp.stack([v[:, half:] for v in slots[1:]])
         first_x = swap_row(first, rows, 1)
         second_y = swap_row(second, rows, 2)
         first_pair = swap_row(jnp.stack([first, first_x]), rows, 2)
         second_pair = swap_row(jnp.stack([second, second_y]), rows, 1)
         parts = [first, second, first_x, second_pair[0]]
         parts += [first_pair[0], second_y, first_pair[1], second_pair[1]]
-        parts = jnp.concatenate(parts, axis=0).reshape(rows, (chips - 1) * depth, part)
+        parts = jnp.concatenate(parts, axis=0).reshape(rows * 2, (chips - 1) * depth, half)
         self.steps = [(first_x, second_y), (first_pair, second_pair)]
         self.far = [parts, swap_core(parts, seq)]
         self.near = [shard, swap_core(shard, seq)]
@@ -153,12 +153,10 @@
         for near, far in zip(self.near, self.far, strict=True):
             if out and lane is not None:
                 value = beside(value, lane)
-            blocks = value.reshape(count, 4, -1).transpose(1, 0, 2)
-            blocks = xor_order(blocks, self.row_at)
+            blocks = value.reshape(count, 4, 2, -1).transpose(1, 2, 0, 3)
+            blocks = xor_order(blocks, self.row_at).reshape(8, count, -1)
             term = jnp.einsum("ktc,kfc->ktf", blocks, far, preferred_element_type=F32)
             term = jnp.sum(term, axis=0).astype(BF16)
-            term = term.reshape(count, 2, self.chips - 1, -1).transpose(0, 2, 1, 3)
-            term = term.reshape(count, -1)
             out.append(jnp.concatenate([dot(value, near, ((1,), (1,))).astype(BF16), term], axis=1))
         return out
 
@@ -170,10 +168,11 @@
         near_sum = far_sum = 0.0
         for part, near, far in zip(halves, self.near, self.far, strict=True):
             near_sum += dot(part[:, : self.depth], near, ((1,), (0,)))
-            rest = part[:, self.depth :].reshape(count, self.chips - 1, 2, -1)
-            rest = rest.transpose(0, 2, 1, 3).reshape(count, -1)
-            far_sum += jnp.einsum("tf,kfc->ktc", rest, far, preferred_element_type=F32)
-        far_sum = xor_order(far_sum, self.row_at).transpose(1, 0, 2).reshape(count, -1)
+            far_sum += jnp.einsum(
+                "tf,kfc->ktc", part[:, self.depth :], far, preferred_element_type=F32
+            )
+        far_sum = far_sum.reshape(4, 2, count, -1)
+        far_sum = xor_order(far_sum, self.row_at).transpose(2, 0, 1, 3).reshape(count, -1)
         return near_sum + far_sum
 
 
@@ -345,22 +344,24 @@
         grad_up = grad_hidden * gate * sigma
         grad_gate_up.append(jnp.concatenate([grad_gate, grad_up], axis=1).astype(BF16))
         part = dot(beside(grad_gate_up[r], fill), gate_up_weight, ((1,), (0,))).astype(BF16)
+        if r + 1 < rows_here:
+            part, normed_group[r + 1] = lax.optimization_barrier((part, normed_group[r + 1]))
         grad_part.append(lax.psum_scatter(part, "seq", scatter_dimension=0, tiled=True))
         ffn_part.append(dot(hidden[r], down_weight, ((1,), (0,))).astype(BF16))
         if r == 0:
             fill.add(("ffn", 0), scatter_tokens(ffn_part[0], chips, place, core))
 
-    def over_tokens(left, right, start, size):
-        total = 0.0
-        for r in range(rows_here):
-            part = left[r][:, start : start + size]
-            total += dot(part, right[r], ((0,), (0,)))
-        return total.astype(BF16)
-
-    gate_part = over_tokens(grad_gate_up, normed_group, 0, units)
-    up_part = over_tokens(grad_gate_up, normed_group, units, units)
-    down_part = over_tokens(hidden, grad_group, 0, units)
-    parts = (gate_part, up_part, down_part)
+    def over_tokens(left, right):
+        terms = [dot(a, b, ((0,), (0,))) for a, b in zip(left, right, strict=True)]
+        return sum(terms).astype(BF16)
+
+    for r in range(rows_here - 1):
+        grad_part[r], grad_gate_up[-1], hidden[-1] = lax.optimization_barrier(
+            (grad_part[r], grad_gate_up[-1], hidden[-1])
+        )
+    in_part = over_tokens(grad_gate_up, normed_group)
+    down_part = over_tokens(hidden, grad_group)
+    parts = (in_part, down_part)
     summed = lax.psum(parts, "rows")
 
     grad_middle, gain_two_grad = [], 0.0
@@ -373,9 +374,6 @@
         grad_middle.append(
             grad_out[r] + norm_back(grad_normed_two, scaled_two, inverse_two[r], gain_two)
         )
-    for r in range(1, rows_here):
-        part = tie(ffn_part[r], grad_middle[-1])
-        fill.add(("ffn", r), scatter_tokens(part, chips, place, core))
     grad_middle = jnp.concatenate(grad_middle, axis=0)
     grad_branch = grad_middle.astype(BF16)
     output_part = [dot(half, grad_branch, ((0,), (0,))).astype(BF16) for half in mixed]
@@ -393,6 +391,9 @@
     probs = jnp.where(valid, jnp.exp(scores - lse), 0.0)
     grad_probs = heads_dot("rjqd,rjkd->rjqk", grad_heads, values)
     grad_scores = beside((probs * (grad_probs - delta)).astype(BF16), main)
+    for r in range(1, rows_here):
+        part, grad_scores = lax.optimization_barrier((ffn_part[r], grad_scores))
+        fill.add(("ffn", r), scatter_tokens(part, chips, place, core))
     query_term = from_heads(
         (heads_dot("rjqk,rjkd->rjqd", grad_scores, keys) * scale).astype(BF16)
     )
@@ -425,13 +426,16 @@
     ]
     cache_grad = fill.result("cache")
     cache_grad = cache_grad.transpose(1, 3, 0, 2, 4).reshape(rows_here, seg_len, 2, KV * HEAD)
-    sums = (main.result("output").astype(BF16), main.result("query").astype(BF16))
-    summed, sums, gain_grad = lax.optimization_barrier((summed, sums, gain_grad))
+    summed, output_sum = lax.optimization_barrier((summed, main.result("output").astype(BF16)))
+    in_grad, down_grad = summed
+    (output_grad,), in_grad = sum_rows([output_sum], rows, in_grad)
+    in_grad = in_grad.reshape(2, units, width).transpose(1, 0, 2)
+    in_grad = lax.optimization_barrier(in_grad)
+    query_sum, gain_grad = lax.optimization_barrier(
+        (main.result("query").astype(BF16), gain_grad)
+    )
     gain_grad = sum_all(gain_grad, rows, seq)
-    gate_grad, up_grad, down_grad = summed
-    in_grad = jnp.concatenate([gate_grad, up_grad], axis=1)
-    (output_grad, query_grad), in_grad = sum_rows(sums, rows, in_grad)
-    in_grad = lax.optimization_barrier(in_grad.reshape(units, 2, width))
+    (query_grad,), _ = sum_rows([query_sum], rows, ())
     return (
         jnp.stack(layer_out),
         input_grad.reshape(rows_here, seg_len, width),

time: 896 us -> 841 us (0.939)
  other arithmetic: 156 us -> 129 us
  waiting for transfers between devices: 278 us -> 256 us
  local copies, waits for them, and re-layouts: 173 us -> 152 us
  starting transfers between devices: 36 us -> 51.5 us
    reduce_scatter x2, waiting for transfers between devices: 31.3 us -> 0.01 us  [local(): lax.psum_scatter(part, 'seq', scatter_dimension=0, tiled=True)]
    ppermute x24, starting transfers between devices: 13 us -> 26.4 us  [ring(): return lax.ppermute(value, 'seq', pairs)]
    unnamed x230 -> x194, local copies, waits for them, and re-layouts: 36.7 us -> 23.5 us
    reshape x8 -> x6, local copies, waits for them, and re-layouts: 27.6 us -> 37.9 us  [the longest x2 17.1 us: back(): xor_order(far_sum, self.row_at).transpose(2, 0, 1, 3).reshape(count, -1)]
    another operation x8 -> x6, local copies, waits for them, and re-layouts: 21.3 us -> 12.2 us  [to_heads(): jnp.stack([h.reshape(rows_here, seg_len, chips, -1, HEAD) for h in halves])]
    dot_general x26 -> x24, matrix products: 162 us -> 168 us  [dot(): lax.dot_general(left, right, (dims, ((), ())), preferred_element_type=F32)]
  transfers between devices with their start and end apart: 62 -> 62, of which waited for: 29 -> 25; matrix products, arithmetic and copies ran while one was open for 59% -> 59% of each run, Pallas kernels for 0% -> 0%
where the time goes in v8:
time: 841 us; the launch traced here: 830 us
  waiting for transfers between devices  256 us (30%)
  matrix products  225 us (27%)
  local copies, waits for them, and re-layouts  152 us (18%)
  other arithmetic  129 us (15%)
  starting transfers between devices  51.5 us (6%)
  between operations  16.3 us (2%)
    ppermute x24, waiting for transfers between devices, ring(): return lax.ppermute(value, 'seq', pairs)  194 us
    dot_general x24, matrix products, dot(): lax.dot_general(left, right, (dims, ((), ())), preferred_element_type=F32)  168 us
    dot_general x6, matrix products, heads_dot(): return jnp.einsum(spec, left, right, preferred_element_type=F32)  40.3 us
    all_gather x2, waiting for transfers between devices, local(): lax.all_gather(n, 'seq', axis=0, tiled=True)  30.5 us
    ppermute x18, waiting for transfers between devices, swap_row(): return lax.ppermute(value, 'rows', [(r, r ^ mask) for r in range(rows)])  29 us
    ppermute x24, starting transfers between devices, ring(): return lax.ppermute(value, 'seq', pairs)  26.4 us
    unnamed x194, local copies, waits for them, and re-layouts  23.5 us
    ppermute x18, starting transfers between devices, swap_row(): return lax.ppermute(value, 'rows', [(r, r ^ mask) for r in range(rows)])  19.9 us
  transfers between devices with their start and end apart: 62, of which 25 were waited for; matrix products, arithmetic and copies ran while one was open for 59% of the time, Pallas kernels for 0%

profile of v8, /device:TPU:0, one launch (start us, length us, event | category | flops | bytes accessed | tf_op | source)
XLA Modules:
  0.0 830.4 jit_solution(7107890871746065249)
XLA Ops:
  125.3 10.5 %collective-permute-done.5 = bf16[2,3,256,256]{3,2,1,0:T(8,128)(2,1)S(1)} collective-permute-done((bf16[2,3,256,256]{3,2,1,0:T(8,128)(2,1)S(1)}, bf16[2,3,256,256]{3,2,1,0:T(8,128)(2,1)S(1)}, u32[]{:S(2)}, u32[]{:S(2)}) %collective-permute-start.5) | collective-permute-done | bytes 786464 | tf_op jit(solution)/shard_map/ppermute | solution.py:41
  147.3 13.1 %collective-permute-done.15 = bf16[2,3,256,256]{3,2,1,0:T(8,128)(2,1)S(1)} collective-permute-done((bf16[2,3,256,256]{3,2,1,0:T(8,128)(2,1)S(1)}, bf16[2,3,256,256]{3,2,1,0:T(8,128)(2,1)S(1)}, u32[]{:S(2)}, u32[]{:S(2)}) %collective-permute-start.15) | collective-permute-done | bytes 786464 | tf_op jit(solution)/shard_map/ppermute | solution.py:41
  215.6 13.1 %reshape.279 = f32[256,2048]{1,0:T(8,128)} reshape(f32[256,4,2,256]{3,2,1,0:T(2,128)} %bitcast.302) | data formatting | bytes 4194304 | tf_op jit(solution)/shard_map/reshape | solution.py:175
  235.8 16.6 %fusion.84 = (bf16[1024,1,2048]{2,1,0:T(2,128)(2,1)S(1)}, bf16[1024,1,2048]{2,1,0:T(2,128)(2,1)S(1)}) fusion(bf16[1024,2,2048]{2,1,0:T(2,128)(2,1)} %param.15), kind=kLoop, calls=%fused_computation.294 | loop fusion | bytes 16777216 | tf_op jit(solution)/shard_map/slice | solution.py:262
  260.1 20.9 %all-gather.9.cloned.1.call-done = bf16[1024,2048]{1,0:T(8,128)(2,1)} async-done(((bf16[128,2048]{1,0:T(8,128)(2,1)}), bf16[1024,2048]{1,0:T(8,128)(2,1)}) %all-gather.9.cloned.1.call-update) | async-done | bytes 4194320 | tf_op jit(solution)/shard_map/all_gather | solution.py:332
  281.0 15.3 %fusion.83 = f32[1024,2048]{1,0:T(8,128)} fusion(bf16[1024,2048]{1,0:T(8,128)(2,1)} %all-gather.9.cloned.1.call-done, bf16[1024,2048]{1,0:T(8,128)(2,1)} %get-tuple-element.181, bf16[1024,2048]{1,0:T(8,128)(2,1)} %get-tuple-element.182), kind=kOutput, calls=%fused_computation.293 | convolution fusion | flops 8606711808 | bytes 20971520 | tf_op jit(solution)/shard_map/dot_general | solution.py:17
  296.3 10.2 %multiply_convert_fusion.6 = (bf16[1024,1024]{1,0:T(8,128)(2,1)}, bf16[1024,1024]{1,0:T(8,128)(2,1)}, bf16[1024,1024]{1,0:T(8,128)(2,1)S(1)}) fusion(f32[1024,2048]{1,0:T(8,128)} %fusion.83, bf16[1024,2048]{1,0:T(8,128)(2,1)S(1)} %copy-done.79, bf16[1024,2048]{1,0:T(8,128)(2,1)S(1)} %copy-done.77), kind=kOutput, calls=%fused_computation.42 | convolution fusion | flops 4311744512 | bytes 23068672 | tf_op jit(solution)/shard_map/dot_general | solution.py:17
  306.4 12.8 %convolution_convert_fusion.5 = bf16[1024,2048]{1,0:T(8,128)(2,1)} fusion(bf16[1024,1024]{1,0:T(8,128)(2,1)} %get-tuple-element.109, bf16[1024,1024]{1,0:T(8,128)(2,1)} %get-tuple-element.108, bf16[1024,2048]{1,0:T(8,128)(2,1)S(1)} %copy-done.33, bf16[1024,2048]{1,0:T(8,128)(2,1)S(1)} %copy-done.35), kind=kOutput, calls=%fused_computation.50 | convolution fusion | flops 8617197568 | bytes 16777216 | tf_op jit(solution)/shard_map/dot_general | solution.py:17
  338.9 15.3 %fusion.82 = f32[1024,2048]{1,0:T(8,128)} fusion(bf16[1024,2048]{1,0:T(8,128)(2,1)} %all-gather.11.cloned.1.call-done, bf16[1024,2048]{1,0:T(8,128)(2,1)} %get-tuple-element.181, bf16[1024,2048]{1,0:T(8,128)(2,1)} %get-tuple-element.182), kind=kOutput, calls=%fused_computation.292 | convolution fusion | flops 8606711808 | bytes 20971520 | tf_op jit(solution)/shard_map/dot_general | solution.py:17
  355.8 11.4 %multiply_convert_fusion.3 = (bf16[1024,1024]{1,0:T(8,128)(2,1)S(1)}, bf16[1024,1024]{1,0:T(8,128)(2,1)S(1)}, bf16[1024,1024]{1,0:T(8,128)(2,1)}) fusion(f32[1024,2048]{1,0:T(8,128)} %fusion.82, bf16[1024,2048]{1,0:T(8,128)(2,1)} %all-gather.7.cloned.1.call-done, bf16[1024,2048]{1,0:T(8,128)(2,1)S(1)} %copy-done.78), kind=kOutput, calls=%fused_computation.38 | convolution fusion | flops 4311744512 | bytes 23068672 | tf_op jit(solution)/shard_map/dot_general | solution.py:17
  367.6 15.8 %collective-permute-done.23 = bf16[128,2048]{1,0:T(8,128)(2,1)S(1)} collective-permute-done((bf16[128,2048]{1,0:T(8,128)(2,1)S(1)}, bf16[128,2048]{1,0:T(8,128)(2,1)S(1)}, u32[]{:S(2)}, u32[]{:S(2)}) %collective-permute-start.23) | collective-permute-done | bytes 524320 | tf_op jit(solution)/shard_map/ppermute | solution.py:37
  384.8 10.3 %convolution_convert_fusion.4 = bf16[1024,2048]{1,0:T(8,128)(2,1)} fusion(bf16[1024,2048]{1,0:T(8,128)(2,1)S(1)} %pad_maximum_fusion.2, bf16[1024,2048]{1,0:T(8,128)(2,1)S(1)} %copy-done.34, bf16[1024,2048]{1,0:T(8,128)(2,1)S(1)} %copy-done.36), kind=kOutput, calls=%fused_computation.49 | convolution fusion | flops 8608808960 | bytes 16777216 | tf_op jit(solution)/shard_map/dot_general | solution.py:17
  395.8 15.3 %fusion.21 = f32[2048,2048]{1,0:T(8,128)} fusion(bf16[1024,2048]{1,0:T(8,128)(2,1)} %all-gather.9.cloned.1.call-done, bf16[1024,1024]{1,0:T(8,128)(2,1)} %get-tuple-element.109, bf16[1024,1024]{1,0:T(8,128)(2,1)} %get-tuple-element.108), kind=kOutput, calls=%fused_computation.62 | convolution fusion | flops 8598323200 | bytes 25165824 | tf_op jit(solution)/shard_map/dot_general | solution.py:17
  418.3 20.4 %collective-permute-done.24 = bf16[128,2048]{1,0:T(8,128)(2,1)S(1)} collective-permute-done((bf16[128,2048]{1,0:T(8,128)(2,1)S(1)}, bf16[128,2048]{1,0:T(8,128)(2,1)S(1)}, u32[]{:S(2)}, u32[]{:S(2)}) %collective-permute-start.24) | collective-permute-done | bytes 524320 | tf_op jit(solution)/shard_map/ppermute | solution.py:37
  440.8 12.1 %add_convert_fusion.1 = bf16[1024,2048]{1,0:T(8,128)(2,1)} fusion(f32[1024,2048]{1,0:T(8,128)} %fusion.94, bf16[1024,1024]{1,0:T(8,128)(2,1)} %get-tuple-element.62, bf16[1024,2048]{1,0:T(8,128)(2,1)} %all-gather.7.cloned.1.call-done), kind=kOutput, calls=%fused_computation.19 | convolution fusion | flops 4299161600 | bytes 18874368 | tf_op jit(solution)/shard_map/dot_general | solution.py:17
  452.9 15.1 %add_convert_fusion = bf16[2048,2048]{1,0:T(8,128)(2,1)} fusion(f32[2048,2048]{1,0:T(8,128)} %fusion.21, bf16[1024,2048]{1,0:T(8,128)(2,1)S(1)} %copy-done.32, bf16[1024,2048]{1,0:T(8,128)(2,1)S(1)} %copy-done.81), kind=kOutput, calls=%fused_computation.1 | convolution fusion | flops 8598323200 | bytes 33554432 | tf_op jit(solution)/shard_map/dot_general | solution.py:17
  532.2 11.9 %multiply_convert_fusion = bf16[2,4,512,1024]{3,2,1,0:T(8,128)(2,1)} fusion(f32[2,4,512,1024]{3,2,1,0:T(8,128)} %copy-done, f32[2,4,512]{2,1,0:T(4,128)S(1)} %multiply_reduce_fusion.2, f32[2,4,512]{2,1,0:T(4,128)S(1)} %bitcast.340, pred[2,512,1024]{2,1,0:T(8,128)(4,1)S(1)} %copy-done.14, bf16[2,4,512,128]{3,2,1,0:T(8,128)(2,1)S(1)} %bitcast.306, ...), kind=kOutput, calls=%fused_computation | convolution fusion | flops 1098907648 | bytes 29392896 | tf_op jit(solution)/shard_map/rjqd,rjkd->rjqk/dot_general | solution.py:299
  544.1 9.7 %convert_bitcast_fusion = bf16[1,2,4,1024,128]{3,4,2,1,0:T(8,128)(2,1)} fusion(bf16[2,4,512,128]{3,2,1,0:T(8,128)(2,1)S(1)} %bitcast.307, f32[2,4,512,1024]{3,2,1,0:T(8,128)} %copy-done, f32[2,4,512]{2,1,0:T(4,128)S(1)} %bitcast.341, pred[2,512,1024]{2,1,0:T(8,128)(4,1)S(1)} %copy-done.14), kind=kOutput, calls=%fused_computation.83 | convolution fusion | flops 1091567616 | bytes 20987904 | tf_op jit(solution)/shard_map/rjqk,rjqd->rjkd/dot_general | solution.py:299
  618.8 23.8 %collective-permute-done.38 = bf16[256,2048]{1,0:T(8,128)(2,1)S(1)} collective-permute-done((bf16[256,2048]{1,0:T(8,128)(2,1)S(1)}, bf16[256,2048]{1,0:T(8,128)(2,1)S(1)}, u32[]{:S(2)}, u32[]{:S(2)}) %collective-permute-start.38) | collective-permute-done | bytes 1048608 | tf_op jit(solution)/shard_map/ppermute | solution.py:37
  669.0 18.6 %collective-permute-done.39 = bf16[256,2048]{1,0:T(8,128)(2,1)S(1)} collective-permute-done((bf16[256,2048]{1,0:T(8,128)(2,1)S(1)}, bf16[256,2048]{1,0:T(8,128)(2,1)S(1)}, u32[]{:S(2)}, u32[]{:S(2)}) %collective-permute-start.39) | collective-permute-done | bytes 1048608 | tf_op jit(solution)/shard_map/ppermute | solution.py:37
  714.1 18.4 %collective-permute-done.40 = bf16[256,2048]{1,0:T(8,128)(2,1)S(1)} collective-permute-done((bf16[256,2048]{1,0:T(8,128)(2,1)S(1)}, bf16[256,2048]{1,0:T(8,128)(2,1)S(1)}, u32[]{:S(2)}, u32[]{:S(2)}) %collective-permute-start.40) | collective-permute-done | bytes 1048608 | tf_op jit(solution)/shard_map/ppermute | solution.py:37
  734.4 19.9 %collective-permute-done.31 = bf16[128,2048]{1,0:T(8,128)(2,1)S(1)} collective-permute-done((bf16[128,2048]{1,0:T(8,128)(2,1)S(1)}, bf16[128,2048]{1,0:T(8,128)(2,1)S(1)}, u32[]{:S(2)}, u32[]{:S(2)}) %collective-permute-start.31) | collective-permute-done | bytes 524320 | tf_op jit(solution)/shard_map/ppermute | solution.py:37
  791.9 14.5 %copy.104 = bf16[2,1024,2048]{2,0,1:T(2,128)(2,1)S(1)} copy(bf16[2,1024,2048]{2,1,0:T(8,128)(2,1)} %bitcast.301) | data formatting | bytes 16777216 | tf_op jit(solution)/shard_map/reshape | solution.py:432
  807.9 10.7 %convert_element_type.691 = f32[1024,2,2048]{2,1,0:T(2,128)} convert(bf16[1024,2,2048]{2,1,0:T(2,128)(2,1)S(1)} %bitcast.294) | non-fusion elementwise | flops 4194304 | bytes 25165824 | tf_op jit(solution)/shard_map/convert_element_type | solution.py:446
  (490 shorter events, 458.4 us)
Async XLA Ops:
  7.2 201.5 %all-gather.5.cloned.1.call-start = ((), (), s32[]{:S(2)}) async-start(), calls=%async_computation.2 | async-start | bytes 4718592 | tf_op jit(solution)/shard_map/all_gather | solution.py:271
  7.2 108.8 %collective-permute-start.7 = (bf16[256,2048]{1,0:T(8,128)(2,1)}, bf16[256,2048]{1,0:T(8,128)(2,1)}, u32[]{:S(2)}, u32[]{:S(2)}) collective-permute-start(bf16[256,2048]{1,0:T(8,128)(2,1)} %param.13), channel_id=1, source_target_pairs={{0,1},{1,0},{2,3},{3,2},{4,5},{5,4},{6,7},{7,6},{8,9},{9,8},{10,11... | collective-permute-start | bytes 3145736 | tf_op jit(solution)/shard_map/ppermute | solution.py:32
  12.0 218.2 %collective-permute-start.20 = (bf16[256,2048]{1,0:T(8,128)(2,1)}, bf16[256,2048]{1,0:T(8,128)(2,1)}, u32[]{:S(2)}, u32[]{:S(2)}) collective-permute-start(bf16[256,2048]{1,0:T(8,128)(2,1)} %param.14), channel_id=1, source_target_pairs={{0,1},{1,0},{2,3},{3,2},{4,5},{5,4},{6,7},{7,6},{8,9},{9,8},{10,11... | collective-permute-start | bytes 3145736 | tf_op jit(solution)/shard_map/ppermute | solution.py:32
  109.9 124.2 %all-gather.7.cloned.1.call-start = ((), (), s32[]{:S(2)}) async-start(), calls=%async_computation.3 | async-start | bytes 4718592 | tf_op jit(solution)/shard_map/all_gather | solution.py:271
  163.7 44.9 %collective-permute-start.21 = (bf16[8,768,256]{1,2,0:T(8,128)(2,1)}, bf16[8,768,256]{1,2,0:T(8,128)(2,1)}, u32[]{:S(2)}, u32[]{:S(2)}) collective-permute-start(bf16[8,768,256]{1,2,0:T(8,128)(2,1)} %copy.61), channel_id=1, source_target_pairs={{0,1},{1,0},{2,3},{3,2},{4,5},{5,4},{6,7},{7,6},{8,9},{9,8},{10,11... | collective-permute-start | bytes 9437192 | tf_op jit(solution)/shard_map/ppermute | solution.py:32
  163.8 117.2 %all-gather.9.cloned.1.call-start = ((), (), s32[]{:S(2)}) async-start(), calls=%async_computation.4 | async-start | bytes 4718592 | tf_op jit(solution)/shard_map/all_gather | solution.py:332
  235.1 93.7 %all-gather.11.cloned.1.call-start = ((), (), s32[]{:S(2)}) async-start(), calls=%async_computation.5 | async-start | bytes 4718592 | tf_op jit(solution)/shard_map/all_gather | solution.py:332
  235.7 205.1 %reduce-scatter.3.cloned.1.call-start = ((), (), s32[]{:S(2)}) async-start(), calls=%async_computation.6 | async-start | bytes 4718592 | tf_op jit(solution)/shard_map/reduce_scatter | solution.py:349
  328.9 139.1 %reduce-scatter.5.cloned.1.call-start = ((), (), s32[]{:S(2)}) async-start(), calls=%async_computation.7 | async-start | bytes 4718592 | tf_op jit(solution)/shard_map/reduce_scatter | solution.py:349
  395.2 361.3 %all-reduce.3.cloned.1.call-start = ((), (), s32[]{:S(2)}) async-start(), calls=%async_computation.8 | async-start | bytes 25165824 | tf_op jit(solution)/shard_map/psum | solution.py:365
  510.6 43.2 %collective-permute-start.27 = (bf16[256,2048]{1,0:T(8,128)(2,1)}, bf16[256,2048]{1,0:T(8,128)(2,1)}, u32[]{:S(2)}, u32[]{:S(2)}) collective-permute-start(bf16[256,2048]{1,0:T(8,128)(2,1)} %add_convert_fusion.15), channel_id=1, source_target_pairs={{0,2},{1,3},{2,4},{3,5},{4,6},{5,7},{6,0},{7,1},{8,10},{9,11},{10,... | collective-permute-start | bytes 3145736 | tf_op jit(solution)/shard_map/ppermute | solution.py:37
  567.4 44.2 %collective-permute-start.37 = (bf16[1024,2048]{1,0:T(8,128)(2,1)}, bf16[1024,2048]{1,0:T(8,128)(2,1)}, u32[]{:S(2)}, u32[]{:S(2)}) collective-permute-start(bf16[1024,2048]{1,0:T(8,128)(2,1)} %convolution_convert_fusion), channel_id=1, source_target_pairs={{0,1},{1,0},{2,3},{3,2},{4,5},{5,4},{6,7},{7,6},{8,9},{9,8},{10,11... | collective-permute-start | bytes 12582920 | tf_op jit(solution)/shard_map/ppermute | solution.py:32
  582.3 33.5 %collective-permute-start.33 = (bf16[2,2,4,512,128]{3,4,2,1,0:T(8,128)(2,1)}, bf16[2,2,4,512,128]{3,4,2,1,0:T(8,128)(2,1)}, u32[]{:S(2)}, u32[]{:S(2)}) collective-permute-start(bf16[2,2,4,512,128]{3,4,2,1,0:T(8,128)(2,1)} %slice.411), channel_id=1, source_target_pairs={{0,1},{1,0},{2,3},{3,2},{4,5},{5,4},{6,7},{7,6},{8,9},{9,8},{10,11... | collective-permute-start | bytes 6291464 | tf_op jit(solution)/shard_map/ppermute | solution.py:32
  584.1 33.4 %collective-permute-start.28 = (bf16[512,2048]{1,0:T(8,128)(2,1)}, bf16[512,2048]{1,0:T(8,128)(2,1)}, u32[]{:S(2)}, u32[]{:S(2)}) collective-permute-start(bf16[512,2048]{1,0:T(8,128)(2,1)} %pad_maximum_fusion.8), channel_id=1, source_target_pairs={{0,1},{1,0},{2,3},{3,2},{4,5},{5,4},{6,7},{7,6},{8,9},{9,8},{10,11... | collective-permute-start | bytes 6291464 | tf_op jit(solution)/shard_map/ppermute | solution.py:32
  591.3 100.6 %collective-permute-start.50 = (bf16[256,2048]{1,0:T(8,128)(2,1)}, bf16[256,2048]{1,0:T(8,128)(2,1)}, u32[]{:S(2)}, u32[]{:S(2)}) collective-permute-start(bf16[256,2048]{1,0:T(8,128)(2,1)} %add_convert_fusion.11), channel_id=1, source_target_pairs={{0,2},{1,3},{2,4},{3,5},{4,6},{5,7},{6,0},{7,1},{8,10},{9,11},{10,... | collective-permute-start | bytes 3145736 | tf_op jit(solution)/shard_map/ppermute | solution.py:37
  617.4 36.5 %collective-permute-start.34 = (bf16[2,2,4,128,128]{3,4,2,1,0:T(8,128)(2,1)S(1)}, bf16[2,2,4,128,128]{3,4,2,1,0:T(8,128)(2,1)S(1)}, u32[]{:S(2)}, u32[]{:S(2)}) collective-permute-start(bf16[2,2,4,128,128]{3,4,2,1,0:T(8,128)(2,1)S(1)} %add_convert_fusion.25), channel_id=1, source_target_pairs={{0,2},{1,3},{2,4},{3,5},{4,6},{5,7},{6,0},{7,1},{8,10},{9,11},{10,... | collective-permute-start | bytes 1572872 | tf_op jit(solution)/shard_map/ppermute | solution.py:37
  618.8 46.4 %collective-permute-start.29 = (bf16[128,2048]{1,0:T(8,128)(2,1)S(1)}, bf16[128,2048]{1,0:T(8,128)(2,1)S(1)}, u32[]{:S(2)}, u32[]{:S(2)}) collective-permute-start(bf16[128,2048]{1,0:T(8,128)(2,1)S(1)} %add_convert_fusion.31), channel_id=1, source_target_pairs={{0,2},{1,3},{2,4},{3,5},{4,6},{5,7},{6,0},{7,1},{8,10},{9,11},{10,... | collective-permute-start | bytes 1572872 | tf_op jit(solution)/shard_map/ppermute | solution.py:37
  644.4 43.2 %collective-permute-start.39 = (bf16[256,2048]{1,0:T(8,128)(2,1)S(1)}, bf16[256,2048]{1,0:T(8,128)(2,1)S(1)}, u32[]{:S(2)}, u32[]{:S(2)}) collective-permute-start(bf16[256,2048]{1,0:T(8,128)(2,1)S(1)} %add_convert_fusion.8), channel_id=1, source_target_pairs={{0,2},{1,3},{2,4},{3,5},{4,6},{5,7},{6,0},{7,1},{8,10},{9,11},{10,... | collective-permute-start | bytes 3145736 | tf_op jit(solution)/shard_map/ppermute | solution.py:37
  655.3 43.5 %collective-permute-start.35 = (bf16[2,2,4,128,128]{3,4,2,1,0:T(8,128)(2,1)S(1)}, bf16[2,2,4,128,128]{3,4,2,1,0:T(8,128)(2,1)S(1)}, u32[]{:S(2)}, u32[]{:S(2)}) collective-permute-start(bf16[2,2,4,128,128]{3,4,2,1,0:T(8,128)(2,1)S(1)} %add_convert_fusion.23), channel_id=1, source_target_pairs={{0,2},{1,3},{2,4},{3,5},{4,6},{5,7},{6,0},{7,1},{8,10},{9,11},{10,... | collective-permute-start | bytes 1572872 | tf_op jit(solution)/shard_map/ppermute | solution.py:37
  666.4 43.7 %collective-permute-start.30 = (bf16[128,2048]{1,0:T(8,128)(2,1)S(1)}, bf16[128,2048]{1,0:T(8,128)(2,1)S(1)}, u32[]{:S(2)}, u32[]{:S(2)}) collective-permute-start(bf16[128,2048]{1,0:T(8,128)(2,1)S(1)} %add_convert_fusion.29), channel_id=1, source_target_pairs={{0,2},{1,3},{2,4},{3,5},{4,6},{5,7},{6,0},{7,1},{8,10},{9,11},{10,... | collective-permute-start | bytes 1572872 | tf_op jit(solution)/shard_map/ppermute | solution.py:37
  689.5 43.1 %collective-permute-start.40 = (bf16[256,2048]{1,0:T(8,128)(2,1)S(1)}, bf16[256,2048]{1,0:T(8,128)(2,1)S(1)}, u32[]{:S(2)}, u32[]{:S(2)}) collective-permute-start(bf16[256,2048]{1,0:T(8,128)(2,1)S(1)} %add_convert_fusion.6), channel_id=1, source_target_pairs={{0,2},{1,3},{2,4},{3,5},{4,6},{5,7},{6,0},{7,1},{8,10},{9,11},{10,... | collective-permute-start | bytes 3145736 | tf_op jit(solution)/shard_map/ppermute | solution.py:37
  700.3 62.3 %collective-permute-start.36 = (bf16[2,2,4,128,128]{3,4,2,1,0:T(8,128)(2,1)S(1)}, bf16[2,2,4,128,128]{3,4,2,1,0:T(8,128)(2,1)}, u32[]{:S(2)}, u32[]{:S(2)}) collective-permute-start(bf16[2,2,4,128,128]{3,4,2,1,0:T(8,128)(2,1)S(1)} %add_convert_fusion.21), channel_id=1, source_target_pairs={{0,2},{1,3},{2,4},{3,5},{4,6},{5,7},{6,0},{7,1},{8,10},{9,11},{10,... | collective-permute-start | bytes 1572872 | tf_op jit(solution)/shard_map/ppermute | solution.py:37
  711.4 42.9 %collective-permute-start.31 = (bf16[128,2048]{1,0:T(8,128)(2,1)S(1)}, bf16[128,2048]{1,0:T(8,128)(2,1)S(1)}, u32[]{:S(2)}, u32[]{:S(2)}) collective-permute-start(bf16[128,2048]{1,0:T(8,128)(2,1)S(1)} %add_convert_fusion.27), channel_id=1, source_target_pairs={{0,2},{1,3},{2,4},{3,5},{4,6},{5,7},{6,0},{7,1},{8,10},{9,11},{10,... | collective-permute-start | bytes 1572872 | tf_op jit(solution)/shard_map/ppermute | solution.py:37
  777.9 40.6 %collective-permute-start.53 = (bf16[128,2048]{1,0:T(8,128)(2,1)}, bf16[128,2048]{1,0:T(8,128)(2,1)S(1)}, u32[]{:S(2)}, u32[]{:S(2)}) collective-permute-start(bf16[128,2048]{1,0:T(8,128)(2,1)} %get-tuple-element.76), channel_id=1, source_target_pairs={{0,16},{8,24},{16,0},{24,8},{1,17},{9,25},{17,1},{25,9},{2,18},{10... | collective-permute-start | bytes 1572872 | tf_op jit(solution)/shard_map/ppermute | solution.py:41
  (122 other events, 2042.6 us)
Sparse Core Ops, SparseCore 0:
  110.0 45.1 all-gather.4
  163.9 45.5 all-gather.6
  235.3 45.6 all-gather.8
  283.0 45.8 all-gather.10
  331.0 59.9 reduce-scatter.2
  395.3 67.7 reduce-scatter.4
  487.7 241.6 all-reduce.2

commit v9 on v8

--- a/solution.py
+++ b/solution.py
@@ -171,8 +171,8 @@
             far_sum += jnp.einsum(
                 "tf,kfc->ktc", part[:, self.depth :], far, preferred_element_type=F32
             )
-        far_sum = far_sum.reshape(4, 2, count, -1)
-        far_sum = xor_order(far_sum, self.row_at).transpose(2, 0, 1, 3).reshape(count, -1)
+        far_sum = xor_order(far_sum.reshape(4, 2, count, -1), self.row_at)
+        far_sum = jnp.concatenate([far_sum[k, h] for k in range(4) for h in range(2)], axis=1)
         return near_sum + far_sum
 
 
@@ -307,13 +307,13 @@
     inputs = tokens.astype(F32).reshape(rows_here * seg_len, width)
     inverse_one = lax.rsqrt(jnp.mean(inputs * inputs, axis=-1, keepdims=True) + EPS)
     normed_one = (inputs * inverse_one * gain_one).astype(BF16)
-    query = tie(query_proj.features(normed_one), output_proj.steps[1])
+    query = query_proj.features(normed_one)
     cache_slot = to_slots(cache_all)
     keys, values = cache_slot[0], cache_slot[1]
     query_heads = to_heads(query)
     scores = heads_dot("rjqd,rjkd->rjqk", query_heads, keys) * scale
     scores = jnp.where(valid, scores, NEG)
-    best = jnp.max(scores, axis=-1, keepdims=True)
+    best = tie(jnp.max(scores, axis=-1, keepdims=True), output_proj.steps[1])
     weights = jnp.exp(scores - best)
     total = jnp.sum(weights, axis=-1, keepdims=True)
     mixed_heads = heads_dot("rjqk,rjkd->rjqd", weights.astype(BF16), values) / total
@@ -348,8 +348,6 @@
             part, normed_group[r + 1] = lax.optimization_barrier((part, normed_group[r + 1]))
         grad_part.append(lax.psum_scatter(part, "seq", scatter_dimension=0, tiled=True))
         ffn_part.append(dot(hidden[r], down_weight, ((1,), (0,))).astype(BF16))
-        if r == 0:
-            fill.add(("ffn", 0), scatter_tokens(ffn_part[0], chips, place, core))
 
     def over_tokens(left, right):
         terms = [dot(a, b, ((0,), (0,))) for a, b in zip(left, right, strict=True)]
@@ -361,6 +359,8 @@
         )
     in_part = over_tokens(grad_gate_up, normed_group)
     down_part = over_tokens(hidden, grad_group)
+    in_part, ffn_part[0] = lax.optimization_barrier((in_part, ffn_part[0]))
+    fill.add(("ffn", 0), scatter_tokens(ffn_part[0], chips, place, core))
     parts = (in_part, down_part)
     summed = lax.psum(parts, "rows")
 
@@ -374,6 +374,9 @@
         grad_middle.append(
             grad_out[r] + norm_back(grad_normed_two, scaled_two, inverse_two[r], gain_two)
         )
+    for r in range(1, rows_here):
+        part = tie(ffn_part[r], grad_middle[-1])
+        fill.add(("ffn", r), scatter_tokens(part, chips, place, core))
     grad_middle = jnp.concatenate(grad_middle, axis=0)
     grad_branch = grad_middle.astype(BF16)
     output_part = [dot(half, grad_branch, ((0,), (0,))).astype(BF16) for half in mixed]
@@ -386,18 +389,15 @@
 
     main.add("output", scatter_rows(output_part))
     grad_heads = to_heads(output_proj.features(tie(grad_branch, output_part[1]), main))
+    grad_heads = beside(grad_heads, main, fill)
     delta = jnp.sum(grad_heads.astype(F32) * mixed_heads, axis=-1, keepdims=True)
     scores = heads_dot("rjqd,rjkd->rjqk", query_heads, keys) * scale
     probs = jnp.where(valid, jnp.exp(scores - lse), 0.0)
     grad_probs = heads_dot("rjqd,rjkd->rjqk", grad_heads, values)
-    grad_scores = beside((probs * (grad_probs - delta)).astype(BF16), main)
-    for r in range(1, rows_here):
-        part, grad_scores = lax.optimization_barrier((ffn_part[r], grad_scores))
-        fill.add(("ffn", r), scatter_tokens(part, chips, place, core))
+    grad_scores = beside((probs * (grad_probs - delta)).astype(BF16), main, fill)
     query_term = from_heads(
         (heads_dot("rjqk,rjkd->rjqd", grad_scores, keys) * scale).astype(BF16)
     )
-    query_term[0] = beside(query_term[0], main)
     grad_keys = heads_dot("rjqk,rjqd->rjkd", grad_scores, query_heads) * scale
     grad_values = heads_dot("rjqk,rjqd->rjkd", probs.astype(BF16), grad_heads)
     cache_part = from_slots(jnp.stack([grad_keys.astype(BF16), grad_values.astype(BF16)]))
@@ -426,16 +426,13 @@
     ]
     cache_grad = fill.result("cache")
     cache_grad = cache_grad.transpose(1, 3, 0, 2, 4).reshape(rows_here, seg_len, 2, KV * HEAD)
-    summed, output_sum = lax.optimization_barrier((summed, main.result("output").astype(BF16)))
+    sums = (main.result("output").astype(BF16), main.result("query").astype(BF16))
+    summed, sums, gain_grad = lax.optimization_barrier((summed, sums, gain_grad))
+    gain_grad = sum_all(gain_grad, rows, seq)
     in_grad, down_grad = summed
-    (output_grad,), in_grad = sum_rows([output_sum], rows, in_grad)
+    (output_grad, query_grad), in_grad = sum_rows(sums, rows, in_grad)
     in_grad = in_grad.reshape(2, units, width).transpose(1, 0, 2)
     in_grad = lax.optimization_barrier(in_grad)
-    query_sum, gain_grad = lax.optimization_barrier(
-        (main.result("query").astype(BF16), gain_grad)
-    )
-    gain_grad = sum_all(gain_grad, rows, seq)
-    (query_grad,), _ = sum_rows([query_sum], rows, ())
     return (
         jnp.stack(layer_out),
         input_grad.reshape(rows_here, seg_len, width),

time: 841 us -> 828 us (0.985)
  waiting for transfers between devices: 256 us -> 280 us
  starting transfers between devices: 51.5 us -> 28.1 us
  local copies, waits for them, and re-layouts: 152 us -> 143 us
    ppermute x24, waiting for transfers between devices: 194 us -> 223 us  [ring(): return lax.ppermute(value, 'seq', pairs)]
    reshape x4 -> x0, local copies, waits for them, and re-layouts: 24.7 us -> none  [the longest x2 17.1 us: back(): xor_order(far_sum, self.row_at).transpose(2, 0, 1, 3).reshape(count, -1)]
    ppermute x24, starting transfers between devices: 26.4 us -> 5.78 us  [ring(): return lax.ppermute(value, 'seq', pairs)]
    unnamed x194 -> x234, local copies, waits for them, and re-layouts: 23.5 us -> 35.1 us
    all_gather x2, waiting for transfers between devices: 30.5 us -> 21.6 us  [local(): lax.all_gather(n, 'seq', axis=0, tiled=True)]
    dot_general x24, matrix products: 168 us -> 159 us  [dot(): lax.dot_general(left, right, (dims, ((), ())), preferred_element_type=F32)]
  transfers between devices with their start and end apart: 62 -> 62, of which waited for: 25 -> 30; matrix products, arithmetic and copies ran while one was open for 59% -> 58% of each run, Pallas kernels for 0% -> 0%
where the time goes in v9:
time: 828 us; the launch traced here: 818 us
  waiting for transfers between devices  280 us (34%)
  matrix products  230 us (28%)
  local copies, waits for them, and re-layouts  143 us (17%)
  other arithmetic  121 us (15%)
  starting transfers between devices  28.1 us (3%)
  between operations  16.4 us (2%)
    ppermute x24, waiting for transfers between devices, ring(): return lax.ppermute(value, 'seq', pairs)  223 us
    dot_general x24, matrix products, dot(): lax.dot_general(left, right, (dims, ((), ())), preferred_element_type=F32)  159 us
    dot_general x6, matrix products, heads_dot(): return jnp.einsum(spec, left, right, preferred_element_type=F32)  46.6 us
    unnamed x234, local copies, waits for them, and re-layouts  35.1 us
    ppermute x18, waiting for transfers between devices, swap_row(): return lax.ppermute(value, 'rows', [(r, r ^ mask) for r in range(rows)])  26.9 us
    slice x1, local copies, waits for them, and re-layouts, local(): ffn_in_weight[:, 0]  24.7 us
    all_gather x2, waiting for transfers between devices, local(): lax.all_gather(n, 'seq', axis=0, tiled=True)  21.6 us
    ppermute x18, starting transfers between devices, swap_row(): return lax.ppermute(value, 'rows', [(r, r ^ mask) for r in range(rows)])  19.9 us
  transfers between devices with their start and end apart: 62, of which 30 were waited for; matrix products, arithmetic and copies ran while one was open for 58% of the time, Pallas kernels for 0%

profile of v9, /device:TPU:0, one launch (start us, length us, event | category | flops | bytes accessed | tf_op | source)
XLA Modules:
  0.0 818.3 jit_solution(7204895132111195887)
XLA Ops:
  121.1 10.1 %collective-permute-done.5 = bf16[2,3,256,256]{3,2,1,0:T(8,128)(2,1)S(1)} collective-permute-done((bf16[2,3,256,256]{3,2,1,0:T(8,128)(2,1)S(1)}, bf16[2,3,256,256]{3,2,1,0:T(8,128)(2,1)S(1)}, u32[]{:S(2)}, u32[]{:S(2)}) %collective-permute-start.5) | collective-permute-done | bytes 786464 | tf_op jit(solution)/shard_map/ppermute | solution.py:41
  224.9 24.7 %fusion.99 = (bf16[1024,1,2048]{2,1,0:T(2,128)(2,1)S(1)}, bf16[1024,1,2048]{2,1,0:T(2,128)(2,1)S(1)}) fusion(bf16[1024,2,2048]{2,1,0:T(2,128)(2,1)} %param.15), kind=kLoop, calls=%fused_computation.326 | loop fusion | bytes 16777216 | tf_op jit(solution)/shard_map/slice | solution.py:262
  257.4 12.3 %all-gather.9.cloned.1.call-done = bf16[1024,2048]{1,0:T(8,128)(2,1)} async-done(((bf16[128,2048]{1,0:T(8,128)(2,1)}), bf16[1024,2048]{1,0:T(8,128)(2,1)}) %all-gather.9.cloned.1.call-update) | async-done | bytes 4194320 | tf_op jit(solution)/shard_map/all_gather | solution.py:332
  269.7 15.3 %fusion.98 = f32[1024,2048]{0,1:T(8,128)} fusion(bf16[1024,2048]{1,0:T(8,128)(2,1)} %all-gather.9.cloned.1.call-done, bf16[1024,2048]{1,0:T(8,128)(2,1)} %get-tuple-element.181, bf16[1024,2048]{1,0:T(8,128)(2,1)} %get-tuple-element.182), kind=kOutput, calls=%fused_computation.325 | convolution fusion | flops 8606711808 | bytes 20971520 | tf_op jit(solution)/shard_map/dot_general | solution.py:17
  285.1 10.1 %multiply_convert_fusion.7 = (bf16[1024,1024]{0,1:T(8,128)(2,1)}, bf16[1024,1024]{0,1:T(8,128)(2,1)}, bf16[1024,1024]{0,1:T(8,128)(2,1)S(1)}) fusion(f32[1024,2048]{0,1:T(8,128)} %fusion.98, bf16[1024,2048]{1,0:T(8,128)(2,1)S(1)} %copy-done.90, bf16[1024,2048]{1,0:T(8,128)(2,1)S(1)} %copy-done.88), kind=kOutput, calls=%fused_computation.43 | convolution fusion | flops 4311744512 | bytes 23068672 | tf_op jit(solution)/shard_map/dot_general | solution.py:17
  295.1 13.2 %convolution_convert_fusion.5 = bf16[1024,2048]{1,0:T(8,128)(2,1)} fusion(bf16[1024,1024]{0,1:T(8,128)(2,1)} %get-tuple-element.109, bf16[1024,1024]{0,1:T(8,128)(2,1)} %get-tuple-element.108, bf16[1024,2048]{1,0:T(8,128)(2,1)S(1)} %copy-done.36, bf16[1024,2048]{1,0:T(8,128)(2,1)S(1)} %copy-done.38), kind=kOutput, calls=%fused_computation.50 | convolution fusion | flops 8617197568 | bytes 16777216 | tf_op jit(solution)/shard_map/dot_general | solution.py:17
  317.8 15.4 %fusion.97 = f32[1024,2048]{0,1:T(8,128)} fusion(bf16[1024,2048]{1,0:T(8,128)(2,1)} %all-gather.11.cloned.1.call-done, bf16[1024,2048]{1,0:T(8,128)(2,1)} %get-tuple-element.181, bf16[1024,2048]{1,0:T(8,128)(2,1)} %get-tuple-element.182), kind=kOutput, calls=%fused_computation.324 | convolution fusion | flops 8606711808 | bytes 20971520 | tf_op jit(solution)/shard_map/dot_general | solution.py:17
  333.2 10.7 %multiply_convert_fusion.5 = (bf16[1024,1024]{0,1:T(8,128)(2,1)S(1)}, bf16[1024,1024]{0,1:T(8,128)(2,1)S(1)}, bf16[1024,1024]{0,1:T(8,128)(2,1)}) fusion(f32[1024,2048]{0,1:T(8,128)} %fusion.97, bf16[1024,2048]{1,0:T(8,128)(2,1)} %all-gather.7.cloned.1.call-done, bf16[1024,2048]{1,0:T(8,128)(2,1)S(1)} %copy-done.89), kind=kOutput, calls=%fused_computation.40 | convolution fusion | flops 4311744512 | bytes 23068672 | tf_op jit(solution)/shard_map/dot_general | solution.py:17
  352.6 11.1 %convolution_convert_fusion.4 = bf16[1024,2048]{1,0:T(8,128)(2,1)} fusion(bf16[1024,2048]{1,0:T(8,128)(2,1)S(1)} %copy-done.37, bf16[1024,2048]{1,0:T(8,128)(2,1)S(1)} %copy-done.39, bf16[1024,1024]{0,1:T(8,128)(2,1)S(1)} %get-tuple-element.107, bf16[1024,1024]{0,1:T(8,128)(2,1)S(1)} %get-tuple-element.106), kind=kOutput, calls=%fused_computation.49 | convolution fusion | flops 8617197568 | bytes 16777216 | tf_op jit(solution)/shard_map/dot_general | solution.py:17
  365.3 15.1 %fusion.21 = f32[2048,2048]{1,0:T(8,128)} fusion(bf16[1024,2048]{1,0:T(8,128)(2,1)} %all-gather.9.cloned.1.call-done, bf16[1024,1024]{0,1:T(8,128)(2,1)} %get-tuple-element.109, bf16[1024,1024]{0,1:T(8,128)(2,1)S(1)} %copy-done.96), kind=kOutput, calls=%fused_computation.62 | convolution fusion | flops 8598323200 | bytes 25165824 | tf_op jit(solution)/shard_map/dot_general | solution.py:17
  380.4 16.9 %add_convert_fusion = bf16[2048,2048]{1,0:T(8,128)(2,1)} fusion(f32[2048,2048]{1,0:T(8,128)} %fusion.21, bf16[1024,2048]{0,1:T(8,128)(2,1)} %pad_maximum_fusion.2, bf16[1024,2048]{1,0:T(8,128)(2,1)} %all-gather.11.cloned.1.call-done), kind=kOutput, calls=%fused_computation.2 | convolution fusion | flops 8598323200 | bytes 33554432 | tf_op jit(solution)/shard_map/dot_general | solution.py:17
  415.2 14.0 %collective-permute-done.23 = bf16[128,2048]{1,0:T(8,128)(2,1)S(1)} collective-permute-done((bf16[128,2048]{1,0:T(8,128)(2,1)S(1)}, bf16[128,2048]{1,0:T(8,128)(2,1)S(1)}, u32[]{:S(2)}, u32[]{:S(2)}) %collective-permute-start.23) | collective-permute-done | bytes 524320 | tf_op jit(solution)/shard_map/ppermute | solution.py:37
  449.7 14.0 %collective-permute-done.25 = bf16[128,2048]{1,0:T(8,128)(2,1)S(1)} collective-permute-done((bf16[128,2048]{1,0:T(8,128)(2,1)S(1)}, bf16[128,2048]{1,0:T(8,128)(2,1)S(1)}, u32[]{:S(2)}, u32[]{:S(2)}) %collective-permute-start.25) | collective-permute-done | bytes 524320 | tf_op jit(solution)/shard_map/ppermute | solution.py:37
  477.5 11.7 %collective-permute-done.27 = bf16[128,2048]{1,0:T(8,128)(2,1)} collective-permute-done((bf16[128,2048]{1,0:T(8,128)(2,1)}, bf16[128,2048]{1,0:T(8,128)(2,1)}, u32[]{:S(2)}, u32[]{:S(2)}) %collective-permute-start.27) | collective-permute-done | bytes 524320 | tf_op jit(solution)/shard_map/ppermute | solution.py:37
  492.8 13.3 %collective-permute-done.28 = bf16[128,2048]{1,0:T(8,128)(2,1)S(1)} collective-permute-done((bf16[128,2048]{1,0:T(8,128)(2,1)S(1)}, bf16[128,2048]{1,0:T(8,128)(2,1)S(1)}, u32[]{:S(2)}, u32[]{:S(2)}) %collective-permute-start.28) | collective-permute-done | bytes 524320 | tf_op jit(solution)/shard_map/ppermute | solution.py:37
  541.3 12.4 %collective-permute-done.31 = bf16[256,2048]{1,0:T(8,128)(2,1)} collective-permute-done((bf16[256,2048]{1,0:T(8,128)(2,1)}, bf16[256,2048]{1,0:T(8,128)(2,1)}, u32[]{:S(2)}, u32[]{:S(2)}) %collective-permute-start.31) | collective-permute-done | bytes 1048608 | tf_op jit(solution)/shard_map/ppermute | solution.py:37
  556.8 12.7 %multiply_convert_fusion = bf16[2,4,512,1024]{3,2,1,0:T(8,128)(2,1)} fusion(f32[2,4,512,1024]{3,2,1,0:T(8,128)} %copy-done, f32[2,4,512]{2,1,0:T(4,128)S(1)} %multiply_reduce_fusion.2, f32[2,4,512]{2,1,0:T(4,128)S(1)} %fusion.83, pred[2,512,1024]{2,1,0:T(8,128)(4,1)S(1)} %copy-done.13, bf16[2,4,512,128]{3,2,1,0:T(8,128)(2,1)S(1)} %bitcast.380, ...), kind=kOutput, calls=%fused_computation | convolution fusion | flops 1098907648 | bytes 29392896 | tf_op jit(solution)/shard_map/rjqd,rjkd->rjqk/dot_general | solution.py:299
  569.5 10.5 %collective-permute-done.32 = bf16[256,2048]{1,0:T(8,128)(2,1)} collective-permute-done((bf16[256,2048]{1,0:T(8,128)(2,1)S(1)}, bf16[256,2048]{1,0:T(8,128)(2,1)}, u32[]{:S(2)}, u32[]{:S(2)}) %collective-permute-start.32) | collective-permute-done | bytes 1048608 | tf_op jit(solution)/shard_map/ppermute | solution.py:37
  598.4 10.6 %convert_bitcast_fusion = bf16[1,2,4,1024,128]{3,4,2,1,0:T(8,128)(2,1)} fusion(bf16[2,4,512,128]{3,2,1,0:T(8,128)(2,1)S(1)} %bitcast.381, f32[2,4,512,1024]{3,2,1,0:T(8,128)} %copy-done, f32[2,4,512]{2,1,0:T(4,128)S(1)} %fusion.83, pred[2,512,1024]{2,1,0:T(8,128)(4,1)S(1)} %copy-done.13), kind=kOutput, calls=%fused_computation.83 | convolution fusion | flops 1091567616 | bytes 20987904 | tf_op jit(solution)/shard_map/rjqk,rjqd->rjkd/dot_general | solution.py:299
  644.3 22.4 %collective-permute-done.39 = bf16[256,2048]{1,0:T(8,128)(2,1)S(1)} collective-permute-done((bf16[256,2048]{1,0:T(8,128)(2,1)S(1)}, bf16[256,2048]{1,0:T(8,128)(2,1)S(1)}, u32[]{:S(2)}, u32[]{:S(2)}) %collective-permute-start.39) | collective-permute-done | bytes 1048608 | tf_op jit(solution)/shard_map/ppermute | solution.py:37
  673.7 21.1 %collective-permute-done.40 = bf16[256,2048]{1,0:T(8,128)(2,1)S(1)} collective-permute-done((bf16[256,2048]{1,0:T(8,128)(2,1)S(1)}, bf16[256,2048]{1,0:T(8,128)(2,1)S(1)}, u32[]{:S(2)}, u32[]{:S(2)}) %collective-permute-start.40) | collective-permute-done | bytes 1048608 | tf_op jit(solution)/shard_map/ppermute | solution.py:37
  699.9 33.2 %collective-permute-done.34 = bf16[2,2,4,128,128]{3,4,2,1,0:T(8,128)(2,1)S(1)} collective-permute-done((bf16[2,2,4,128,128]{3,4,2,1,0:T(8,128)(2,1)S(1)}, bf16[2,2,4,128,128]{3,4,2,1,0:T(8,128)(2,1)S(1)}, u32[]{:S(2)}, u32[]{:S(2)}) %collective-permute-start.34) | collective-permute-done | bytes 524320 | tf_op jit(solution)/shard_map/ppermute | solution.py:37
  781.2 14.5 %copy.98 = bf16[2,1024,2048]{2,0,1:T(2,128)(2,1)S(1)} copy(bf16[2,1024,2048]{2,1,0:T(8,128)(2,1)} %bitcast.376) | data formatting | bytes 16777216 | tf_op jit(solution)/shard_map/reshape | solution.py:434
  795.7 10.8 %convert_element_type.692 = f32[1024,2,2048]{2,1,0:T(2,128)} convert(bf16[1024,2,2048]{2,1,0:T(2,128)(2,1)S(1)} %bitcast.351) | non-fusion elementwise | flops 4194304 | bytes 25165824 | tf_op jit(solution)/shard_map/convert_element_type | solution.py:443
  (530 shorter events, 445.8 us)
Async XLA Ops:
  7.2 201.9 %all-gather.5.cloned.1.call-start = ((), (), s32[]{:S(2)}) async-start(), calls=%async_computation.2 | async-start | bytes 4718592 | tf_op jit(solution)/shard_map/all_gather | solution.py:271
  7.2 105.6 %collective-permute-start.7 = (bf16[256,2048]{1,0:T(8,128)(2,1)}, bf16[256,2048]{1,0:T(8,128)(2,1)}, u32[]{:S(2)}, u32[]{:S(2)}) collective-permute-start(bf16[256,2048]{1,0:T(8,128)(2,1)} %param.13), channel_id=1, source_target_pairs={{0,1},{1,0},{2,3},{3,2},{4,5},{5,4},{6,7},{7,6},{8,9},{9,8},{10,11... | collective-permute-start | bytes 3145736 | tf_op jit(solution)/shard_map/ppermute | solution.py:32
  12.1 207.4 %collective-permute-start.20 = (bf16[256,2048]{1,0:T(8,128)(2,1)}, bf16[256,2048]{1,0:T(8,128)(2,1)}, u32[]{:S(2)}, u32[]{:S(2)}) collective-permute-start(bf16[256,2048]{1,0:T(8,128)(2,1)} %param.14), channel_id=1, source_target_pairs={{0,1},{1,0},{2,3},{3,2},{4,5},{5,4},{6,7},{7,6},{8,9},{9,8},{10,11... | collective-permute-start | bytes 3145736 | tf_op jit(solution)/shard_map/ppermute | solution.py:32
  106.7 116.4 %all-gather.7.cloned.1.call-start = ((), (), s32[]{:S(2)}) async-start(), calls=%async_computation.3 | async-start | bytes 4718592 | tf_op jit(solution)/shard_map/all_gather | solution.py:271
  135.7 31.1 %collective-permute-start.8 = (bf16[8,768,256]{2,1,0:T(8,128)(2,1)}, bf16[8,768,256]{2,1,0:T(8,128)(2,1)}, u32[]{:S(2)}, u32[]{:S(2)}) collective-permute-start(bf16[8,768,256]{2,1,0:T(8,128)(2,1)} %bitcast.22), channel_id=1, source_target_pairs={{0,1},{1,0},{2,3},{3,2},{4,5},{5,4},{6,7},{7,6},{8,9},{9,8},{10,11... | collective-permute-start | bytes 9437192 | tf_op jit(solution)/shard_map/ppermute | solution.py:32
  145.3 30.9 %collective-permute-start.17 = (bf16[2,2,4,512,128]{4,3,2,1,0:T(8,128)(2,1)}, bf16[2,2,4,512,128]{4,3,2,1,0:T(8,128)(2,1)}, u32[]{:S(2)}, u32[]{:S(2)}) collective-permute-start(bf16[2,2,4,512,128]{4,3,2,1,0:T(8,128)(2,1)} %pad_maximum_fusion.5), channel_id=1, source_target_pairs={{0,1},{1,0},{2,3},{3,2},{4,5},{5,4},{6,7},{7,6},{8,9},{9,8},{10,11... | collective-permute-start | bytes 6291464 | tf_op jit(solution)/shard_map/ppermute | solution.py:32
  166.5 42.7 %collective-permute-start.21 = (bf16[8,768,256]{1,2,0:T(8,128)(2,1)}, bf16[8,768,256]{1,2,0:T(8,128)(2,1)}, u32[]{:S(2)}, u32[]{:S(2)}) collective-permute-start(bf16[8,768,256]{1,2,0:T(8,128)(2,1)} %copy.57), channel_id=1, source_target_pairs={{0,1},{1,0},{2,3},{3,2},{4,5},{5,4},{6,7},{7,6},{8,9},{9,8},{10,11... | collective-permute-start | bytes 9437192 | tf_op jit(solution)/shard_map/ppermute | solution.py:32
  166.5 103.2 %all-gather.9.cloned.1.call-start = ((), (), s32[]{:S(2)}) async-start(), calls=%async_computation.4 | async-start | bytes 4718592 | tf_op jit(solution)/shard_map/all_gather | solution.py:332
  224.2 93.4 %all-gather.11.cloned.1.call-start = ((), (), s32[]{:S(2)}) async-start(), calls=%async_computation.5 | async-start | bytes 4718592 | tf_op jit(solution)/shard_map/all_gather | solution.py:332
  224.8 155.6 %reduce-scatter.3.cloned.1.call-start = ((), (), s32[]{:S(2)}) async-start(), calls=%async_computation.6 | async-start | bytes 4718592 | tf_op jit(solution)/shard_map/reduce_scatter | solution.py:349
  317.7 119.8 %reduce-scatter.5.cloned.1.call-start = ((), (), s32[]{:S(2)}) async-start(), calls=%async_computation.7 | async-start | bytes 4718592 | tf_op jit(solution)/shard_map/reduce_scatter | solution.py:349
  363.7 373.2 %all-reduce.3.cloned.1.call-start = ((), (), s32[]{:S(2)}) async-start(), calls=%async_computation.8 | async-start | bytes 25165824 | tf_op jit(solution)/shard_map/psum | solution.py:365
  471.3 54.6 %collective-permute-start.30 = (bf16[1024,2048]{1,0:T(8,128)(2,1)}, bf16[1024,2048]{1,0:T(8,128)(2,1)}, u32[]{:S(2)}, u32[]{:S(2)}) collective-permute-start(bf16[1024,2048]{1,0:T(8,128)(2,1)} %convolution_convert_fusion.3), channel_id=1, source_target_pairs={{0,1},{1,0},{2,3},{3,2},{4,5},{5,4},{6,7},{7,6},{8,9},{9,8},{10,11... | collective-permute-start | bytes 12582920 | tf_op jit(solution)/shard_map/ppermute | solution.py:32
  598.3 38.7 %collective-permute-start.38 = (bf16[1024,2048]{1,0:T(8,128)(2,1)}, bf16[1024,2048]{1,0:T(8,128)(2,1)}, u32[]{:S(2)}, u32[]{:S(2)}) collective-permute-start(bf16[1024,2048]{1,0:T(8,128)(2,1)} %convolution_convert_fusion), channel_id=1, source_target_pairs={{0,1},{1,0},{2,3},{3,2},{4,5},{5,4},{6,7},{7,6},{8,9},{9,8},{10,11... | collective-permute-start | bytes 12582920 | tf_op jit(solution)/shard_map/ppermute | solution.py:32
  608.9 88.3 %collective-permute-start.37 = (bf16[256,2048]{1,0:T(8,128)(2,1)}, bf16[256,2048]{1,0:T(8,128)(2,1)}, u32[]{:S(2)}, u32[]{:S(2)}) collective-permute-start(bf16[256,2048]{1,0:T(8,128)(2,1)} %add_convert_fusion.11), channel_id=1, source_target_pairs={{0,2},{1,3},{2,4},{3,5},{4,6},{5,7},{6,0},{7,1},{8,10},{9,11},{10,... | collective-permute-start | bytes 3145736 | tf_op jit(solution)/shard_map/ppermute | solution.py:37
  639.6 27.1 %collective-permute-start.39 = (bf16[256,2048]{1,0:T(8,128)(2,1)S(1)}, bf16[256,2048]{1,0:T(8,128)(2,1)S(1)}, u32[]{:S(2)}, u32[]{:S(2)}) collective-permute-start(bf16[256,2048]{1,0:T(8,128)(2,1)S(1)} %add_convert_fusion.8), channel_id=1, source_target_pairs={{0,2},{1,3},{2,4},{3,5},{4,6},{5,7},{6,0},{7,1},{8,10},{9,11},{10,... | collective-permute-start | bytes 3145736 | tf_op jit(solution)/shard_map/ppermute | solution.py:37
  641.5 55.2 %collective-permute-start.33 = (bf16[2,2,4,512,128]{3,4,2,1,0:T(8,128)(2,1)S(1)}, bf16[2,2,4,512,128]{3,4,2,1,0:T(8,128)(2,1)S(1)}, u32[]{:S(2)}, u32[]{:S(2)}) collective-permute-start(bf16[2,2,4,512,128]{3,4,2,1,0:T(8,128)(2,1)S(1)} %slice.493), channel_id=1, source_target_pairs={{0,1},{1,0},{2,3},{3,2},{4,5},{5,4},{6,7},{7,6},{8,9},{9,8},{10,11... | collective-permute-start | bytes 6291464 | tf_op jit(solution)/shard_map/ppermute | solution.py:32
  668.5 26.2 %collective-permute-start.40 = (bf16[256,2048]{1,0:T(8,128)(2,1)S(1)}, bf16[256,2048]{1,0:T(8,128)(2,1)S(1)}, u32[]{:S(2)}, u32[]{:S(2)}) collective-permute-start(bf16[256,2048]{1,0:T(8,128)(2,1)S(1)} %add_convert_fusion.6), channel_id=1, source_target_pairs={{0,2},{1,3},{2,4},{3,5},{4,6},{5,7},{6,0},{7,1},{8,10},{9,11},{10,... | collective-permute-start | bytes 3145736 | tf_op jit(solution)/shard_map/ppermute | solution.py:37
  696.6 37.5 %collective-permute-start.41 = (bf16[256,2048]{1,0:T(8,128)(2,1)S(1)}, bf16[256,2048]{1,0:T(8,128)(2,1)S(1)}, u32[]{:S(2)}, u32[]{:S(2)}) collective-permute-start(bf16[256,2048]{1,0:T(8,128)(2,1)S(1)} %add_convert_fusion.4), channel_id=1, source_target_pairs={{0,2},{1,3},{2,4},{3,5},{4,6},{5,7},{6,0},{7,1},{8,10},{9,11},{10,... | collective-permute-start | bytes 3145736 | tf_op jit(solution)/shard_map/ppermute | solution.py:37
  696.9 36.1 %collective-permute-start.34 = (bf16[2,2,4,128,128]{3,4,2,1,0:T(8,128)(2,1)S(1)}, bf16[2,2,4,128,128]{3,4,2,1,0:T(8,128)(2,1)S(1)}, u32[]{:S(2)}, u32[]{:S(2)}) collective-permute-start(bf16[2,2,4,128,128]{3,4,2,1,0:T(8,128)(2,1)S(1)} %add_convert_fusion.25), channel_id=1, source_target_pairs={{0,2},{1,3},{2,4},{3,5},{4,6},{5,7},{6,0},{7,1},{8,10},{9,11},{10,... | collective-permute-start | bytes 1572872 | tf_op jit(solution)/shard_map/ppermute | solution.py:37
  764.9 41.7 %collective-permute-start.52 = (bf16[128,2048]{1,0:T(8,128)(2,1)S(1)}, bf16[128,2048]{1,0:T(8,128)(2,1)}, u32[]{:S(2)}, u32[]{:S(2)}) collective-permute-start(bf16[128,2048]{1,0:T(8,128)(2,1)S(1)} %get-tuple-element.75), channel_id=1, source_target_pairs={{0,8},{8,0},{16,24},{24,16},{1,9},{9,1},{17,25},{25,17},{2,10},{10... | collective-permute-start | bytes 1572872 | tf_op jit(solution)/shard_map/ppermute | solution.py:41
  769.0 38.7 %collective-permute-start.51 = (bf16[128,2048]{1,0:T(8,128)(2,1)S(1)}, bf16[128,2048]{1,0:T(8,128)(2,1)S(1)}, u32[]{:S(2)}, u32[]{:S(2)}) collective-permute-start(bf16[128,2048]{1,0:T(8,128)(2,1)S(1)} %get-tuple-element.74), channel_id=1, source_target_pairs={{0,16},{8,24},{16,0},{24,8},{1,17},{9,25},{17,1},{25,9},{2,18},{10... | collective-permute-start | bytes 1572872 | tf_op jit(solution)/shard_map/ppermute | solution.py:41
  780.5 28.8 %collective-permute-start.54 = (bf16[128,2048]{1,0:T(8,128)(2,1)S(1)}, bf16[128,2048]{1,0:T(8,128)(2,1)S(1)}, u32[]{:S(2)}, u32[]{:S(2)}) collective-permute-start(bf16[128,2048]{1,0:T(8,128)(2,1)S(1)} %copy-done.51), channel_id=1, source_target_pairs={{0,8},{8,0},{16,24},{24,16},{1,9},{9,1},{17,25},{25,17},{2,10},{10... | collective-permute-start | bytes 1572872 | tf_op jit(solution)/shard_map/ppermute | solution.py:41
  780.8 28.6 %collective-permute-start.53 = (bf16[128,2048]{1,0:T(8,128)(2,1)S(1)}, bf16[128,2048]{1,0:T(8,128)(2,1)S(1)}, u32[]{:S(2)}, u32[]{:S(2)}) collective-permute-start(bf16[128,2048]{1,0:T(8,128)(2,1)S(1)} %copy-done.50), channel_id=1, source_target_pairs={{0,16},{8,24},{16,0},{24,8},{1,17},{9,25},{17,1},{25,9},{2,18},{10... | collective-permute-start | bytes 1572872 | tf_op jit(solution)/shard_map/ppermute | solution.py:41
  (135 other events, 1969.6 us)
Sparse Core Ops, SparseCore 0:
  106.9 45.2 all-gather.4
  166.6 45.1 all-gather.6
  224.4 45.2 all-gather.8
  271.7 45.8 all-gather.10
  319.8 48.7 reduce-scatter.2
  370.7 50.2 reduce-scatter.4
  474.3 241.6 all-reduce.2

commit v10 on v9

--- a/solution.py
+++ b/solution.py
@@ -143,7 +143,7 @@
         self.far = [parts, swap_core(parts, seq)]
         self.near = [shard, swap_core(shard, seq)]
 
-    def features(self, value, lane=None):
+    def features(self, value, lanes=()):
         if not self.split:
             out = own_order(dot(value, self.whole, ((1,), (1,))), *self.order)
             half = out.shape[1] // 2
@@ -151,8 +151,8 @@
         count = value.shape[0]
         out = []
         for near, far in zip(self.near, self.far, strict=True):
-            if out and lane is not None:
-                value = beside(value, lane)
+            if out:
+                value = beside(value, *lanes)
             blocks = value.reshape(count, 4, 2, -1).transpose(1, 2, 0, 3)
             blocks = xor_order(blocks, self.row_at).reshape(8, count, -1)
             term = jnp.einsum("ktc,kfc->ktf", blocks, far, preferred_element_type=F32)
@@ -200,22 +200,20 @@
     )
 
 
-def sum_rows(values, rows, other):
+def sum_rows(values, rows):
     if rows != 4:
-        return [lax.psum(v.astype(BF16), "rows").astype(F32) for v in values], other
+        return [lax.psum(v.astype(BF16), "rows").astype(F32) for v in values]
 
     def pair(item, mask):
         return item.astype(F32) + swap_row(item, rows, mask).astype(F32)
 
-    halves = []
+    out = []
     for value in values:
         half = value.shape[0] // 2
-        halves.append(pair(value[:half].astype(BF16), 1).astype(BF16))
-        halves.append(pair(value[half:].astype(BF16), 2).astype(BF16))
-    halves, other = lax.optimization_barrier((halves, other))
-    masks = [2, 1] * len(values)
-    sums = [pair(h, m) for h, m in zip(halves, masks, strict=True)]
-    return [jnp.concatenate(sums[2 * n : 2 * n + 2], axis=0) for n in range(len(values))], other
+        first, second = value[:half].astype(BF16), value[half:].astype(BF16)
+        first, second = pair(first, 1).astype(BF16), pair(second, 2).astype(BF16)
+        out.append(jnp.concatenate([pair(first, 2), pair(second, 1)], axis=0))
+    return out
 
 
 def sum_all(value, rows, seq):
@@ -359,8 +357,6 @@
         )
     in_part = over_tokens(grad_gate_up, normed_group)
     down_part = over_tokens(hidden, grad_group)
-    in_part, ffn_part[0] = lax.optimization_barrier((in_part, ffn_part[0]))
-    fill.add(("ffn", 0), scatter_tokens(ffn_part[0], chips, place, core))
     parts = (in_part, down_part)
     summed = lax.psum(parts, "rows")
 
@@ -374,9 +370,8 @@
         grad_middle.append(
             grad_out[r] + norm_back(grad_normed_two, scaled_two, inverse_two[r], gain_two)
         )
-    for r in range(1, rows_here):
-        part = tie(ffn_part[r], grad_middle[-1])
-        fill.add(("ffn", r), scatter_tokens(part, chips, place, core))
+    part = tie(ffn_part[0], grad_middle[-1])
+    fill.add(("ffn", 0), scatter_tokens(part, chips, place, core))
     grad_middle = jnp.concatenate(grad_middle, axis=0)
     grad_branch = grad_middle.astype(BF16)
     output_part = [dot(half, grad_branch, ((0,), (0,))).astype(BF16) for half in mixed]
@@ -388,13 +383,16 @@
         return scatter_halves(lambda j: take(parts[0], j), parts[1], take, chips)
 
     main.add("output", scatter_rows(output_part))
-    grad_heads = to_heads(output_proj.features(tie(grad_branch, output_part[1]), main))
+    grad_heads = to_heads(output_proj.features(tie(grad_branch, output_part[1]), (main, fill)))
     grad_heads = beside(grad_heads, main, fill)
     delta = jnp.sum(grad_heads.astype(F32) * mixed_heads, axis=-1, keepdims=True)
     scores = heads_dot("rjqd,rjkd->rjqk", query_heads, keys) * scale
     probs = jnp.where(valid, jnp.exp(scores - lse), 0.0)
     grad_probs = heads_dot("rjqd,rjkd->rjqk", grad_heads, values)
     grad_scores = beside((probs * (grad_probs - delta)).astype(BF16), main, fill)
+    for r in range(1, rows_here):
+        part, grad_scores = lax.optimization_barrier((ffn_part[r], grad_scores))
+        fill.add(("ffn", r), scatter_tokens(part, chips, place, core))
     query_term = from_heads(
         (heads_dot("rjqk,rjkd->rjqd", grad_scores, keys) * scale).astype(BF16)
     )
@@ -426,13 +424,16 @@
     ]
     cache_grad = fill.result("cache")
     cache_grad = cache_grad.transpose(1, 3, 0, 2, 4).reshape(rows_here, seg_len, 2, KV * HEAD)
-    sums = (main.result("output").astype(BF16), main.result("query").astype(BF16))
-    summed, sums, gain_grad = lax.optimization_barrier((summed, sums, gain_grad))
-    gain_grad = sum_all(gain_grad, rows, seq)
-    in_grad, down_grad = summed
-    (output_grad, query_grad), in_grad = sum_rows(sums, rows, in_grad)
+    output_sum = main.result("output")
+    for _ in range(chips - 1):
+        sent = main.step()
+    summed, output_sum = lax.optimization_barrier((summed, output_sum.astype(BF16)))
+    in_grad, down_grad = tie(summed, sent)
     in_grad = in_grad.reshape(2, units, width).transpose(1, 0, 2)
     in_grad = lax.optimization_barrier(in_grad)
+    query_sum, gain_grad = lax.optimization_barrier((main.result("query"), gain_grad))
+    gain_grad = sum_all(gain_grad, rows, seq)
+    output_grad, query_grad = sum_rows((output_sum, query_sum), rows)
     return (
         jnp.stack(layer_out),
         input_grad.reshape(rows_here, seg_len, width),

time: 828 us -> 830 us (level)
  matrix products: 230 us -> 220 us
    ppermute x24, waiting for transfers between devices: 223 us -> 207 us  [ring(): return lax.ppermute(value, 'seq', pairs)]
    unnamed x234 -> x230, local copies, waits for them, and re-layouts: 35.1 us -> 39.7 us
  transfers between devices with their start and end apart: 62 -> 62, of which waited for: 30 -> 34; matrix products, arithmetic and copies ran while one was open for 58% -> 57% of each run, Pallas kernels for 0% -> 0%
where the time goes in v10:
time: 830 us; the launch traced here: 819 us
  waiting for transfers between devices  278 us (33%)
  matrix products  220 us (27%)
  local copies, waits for them, and re-layouts  148 us (18%)
  other arithmetic  122 us (15%)
  starting transfers between devices  35.6 us (4%)
  between operations  16 us (2%)
    ppermute x24, waiting for transfers between devices, ring(): return lax.ppermute(value, 'seq', pairs)  207 us
    dot_general x24, matrix products, dot(): lax.dot_general(left, right, (dims, ((), ())), preferred_element_type=F32)  155 us
    dot_general x6, matrix products, heads_dot(): return jnp.einsum(spec, left, right, preferred_element_type=F32)  41.2 us
    unnamed x230, local copies, waits for them, and re-layouts  39.7 us
    ppermute x18, waiting for transfers between devices, swap_row(): return lax.ppermute(value, 'rows', [(r, r ^ mask) for r in range(rows)])  34.6 us
    all_gather x2, waiting for transfers between devices, local(): lax.all_gather(n, 'seq', axis=0, tiled=True)  29.5 us
    convert_element_type x10, other arithmetic, ring_scatter(): sent = total.astype(BF16)  21.1 us
    ppermute x18, starting transfers between devices, swap_row(): return lax.ppermute(value, 'rows', [(r, r ^ mask) for r in range(rows)])  18.9 us
  transfers between devices with their start and end apart: 62, of which 34 were waited for; matrix products, arithmetic and copies ran while one was open for 57% of the time, Pallas kernels for 0%

profile of v10, /device:TPU:0, one launch (start us, length us, event | category | flops | bytes accessed | tf_op | source)
XLA Modules:
  0.0 819.2 jit_solution(5031009152205713801)
XLA Ops:
  25.0 8.9 %collective-permute-done.1 = bf16[256,512]{1,0:T(8,128)(2,1)} collective-permute-done((bf16[256,512]{1,0:T(8,128)(2,1)S(1)}, bf16[256,512]{1,0:T(8,128)(2,1)}, u32[]{:S(2)}, u32[]{:S(2)}) %collective-permute-start.1) | collective-permute-done | bytes 262176 | tf_op jit(solution)/shard_map/ppermute | solution.py:37
  121.1 10.1 %collective-permute-done.5 = bf16[2,3,256,256]{3,2,1,0:T(8,128)(2,1)S(1)} collective-permute-done((bf16[2,3,256,256]{3,2,1,0:T(8,128)(2,1)S(1)}, bf16[2,3,256,256]{3,2,1,0:T(8,128)(2,1)S(1)}, u32[]{:S(2)}, u32[]{:S(2)}) %collective-permute-start.5) | collective-permute-done | bytes 786464 | tf_op jit(solution)/shard_map/ppermute | solution.py:41
  225.3 16.5 %fusion.99 = (bf16[1024,1,2048]{2,1,0:T(2,128)(2,1)S(1)}, bf16[1024,1,2048]{2,1,0:T(2,128)(2,1)S(1)}) fusion(bf16[1024,2,2048]{2,1,0:T(2,128)(2,1)} %param.15), kind=kLoop, calls=%fused_computation.326 | loop fusion | bytes 16777216 | tf_op jit(solution)/shard_map/slice | solution.py:260
  249.5 20.5 %all-gather.9.cloned.1.call-done = bf16[1024,2048]{1,0:T(8,128)(2,1)} async-done(((bf16[128,2048]{1,0:T(8,128)(2,1)}), bf16[1024,2048]{1,0:T(8,128)(2,1)}) %all-gather.9.cloned.1.call-update) | async-done | bytes 4194320 | tf_op jit(solution)/shard_map/all_gather | solution.py:330
  270.0 15.3 %fusion.98 = f32[1024,2048]{1,0:T(8,128)} fusion(bf16[1024,2048]{1,0:T(8,128)(2,1)} %all-gather.9.cloned.1.call-done, bf16[1024,2048]{1,0:T(8,128)(2,1)} %get-tuple-element.174, bf16[1024,2048]{1,0:T(8,128)(2,1)} %get-tuple-element.175), kind=kOutput, calls=%fused_computation.325 | convolution fusion | flops 8606711808 | bytes 20971520 | tf_op jit(solution)/shard_map/dot_general | solution.py:17
  285.3 10.2 %multiply_convert_fusion.6 = (bf16[1024,1024]{1,0:T(8,128)(2,1)S(1)}, bf16[1024,1024]{1,0:T(8,128)(2,1)}, bf16[1024,1024]{1,0:T(8,128)(2,1)}) fusion(f32[1024,2048]{1,0:T(8,128)} %fusion.98, bf16[1024,2048]{1,0:T(8,128)(2,1)S(1)} %copy-done.85, bf16[1024,2048]{1,0:T(8,128)(2,1)S(1)} %copy-done.81), kind=kOutput, calls=%fused_computation.42 | convolution fusion | flops 4311744512 | bytes 23068672 | tf_op jit(solution)/shard_map/dot_general | solution.py:17
  295.5 12.9 %convolution_convert_fusion.5 = bf16[1024,2048]{1,0:T(8,128)(2,1)} fusion(bf16[1024,1024]{1,0:T(8,128)(2,1)} %get-tuple-element.101, bf16[1024,1024]{1,0:T(8,128)(2,1)S(1)} %get-tuple-element.100, bf16[1024,2048]{1,0:T(8,128)(2,1)S(1)} %copy-done.40, bf16[1024,2048]{1,0:T(8,128)(2,1)S(1)} %copy-done.42), kind=kOutput, calls=%fused_computation.50 | convolution fusion | flops 8617197568 | bytes 16777216 | tf_op jit(solution)/shard_map/dot_general | solution.py:17
  308.4 9.0 %all-gather.11.cloned.1.call-done = bf16[1024,2048]{1,0:T(8,128)(2,1)} async-done(((bf16[128,2048]{1,0:T(8,128)(2,1)}), bf16[1024,2048]{1,0:T(8,128)(2,1)}) %all-gather.11.cloned.1.call-update) | async-done | bytes 4194320 | tf_op jit(solution)/shard_map/all_gather | solution.py:330
  317.4 15.3 %fusion.97 = f32[1024,2048]{1,0:T(8,128)} fusion(bf16[1024,2048]{1,0:T(8,128)(2,1)} %all-gather.11.cloned.1.call-done, bf16[1024,2048]{1,0:T(8,128)(2,1)} %get-tuple-element.174, bf16[1024,2048]{1,0:T(8,128)(2,1)} %get-tuple-element.175), kind=kOutput, calls=%fused_computation.324 | convolution fusion | flops 8606711808 | bytes 20971520 | tf_op jit(solution)/shard_map/dot_general | solution.py:17
  332.7 11.2 %multiply_convert_fusion.4 = (bf16[1024,1024]{1,0:T(8,128)(2,1)S(1)}, bf16[1024,1024]{1,0:T(8,128)(2,1)S(1)}, bf16[1024,1024]{1,0:T(8,128)(2,1)}) fusion(f32[1024,2048]{1,0:T(8,128)} %fusion.97, bf16[1024,2048]{1,0:T(8,128)(2,1)} %all-gather.7.cloned.1.call-done, bf16[1024,2048]{1,0:T(8,128)(2,1)S(1)} %copy-done.82), kind=kOutput, calls=%fused_computation.39 | convolution fusion | flops 4311744512 | bytes 23068672 | tf_op jit(solution)/shard_map/dot_general | solution.py:17
  345.3 10.5 %convolution_convert_fusion.4 = bf16[1024,2048]{1,0:T(8,128)(2,1)} fusion(bf16[1024,2048]{1,0:T(8,128)(2,1)S(1)} %copy-done.41, bf16[1024,2048]{1,0:T(8,128)(2,1)S(1)} %copy-done.43, bf16[1024,1024]{1,0:T(8,128)(2,1)S(1)} %get-tuple-element.99, bf16[1024,1024]{1,0:T(8,128)(2,1)S(1)} %get-tuple-element.98), kind=kOutput, calls=%fused_computation.49 | convolution fusion | flops 8617197568 | bytes 16777216 | tf_op jit(solution)/shard_map/dot_general | solution.py:17
  376.0 12.6 %fusion.21 = f32[2048,2048]{1,0:T(8,128)} fusion(bf16[1024,2048]{1,0:T(8,128)(2,1)S(1)} %copy-done.88, bf16[1024,1024]{1,0:T(8,128)(2,1)S(1)} %copy-done.94, bf16[1024,1024]{1,0:T(8,128)(2,1)S(1)} %copy-done.93), kind=kOutput, calls=%fused_computation.62 | convolution fusion | flops 8598323200 | bytes 25165824 | tf_op jit(solution)/shard_map/dot_general | solution.py:17
  388.7 9.8 %add_convert_fusion.1 = bf16[1024,2048]{1,0:T(8,128)(2,1)} fusion(f32[1024,2048]{1,0:T(8,128)} %fusion.109, bf16[1024,1024]{1,0:T(8,128)(2,1)S(1)} %copy-done.90, bf16[1024,2048]{1,0:T(8,128)(2,1)} %all-gather.7.cloned.1.call-done), kind=kOutput, calls=%fused_computation.21 | convolution fusion | flops 4299161600 | bytes 18874368 | tf_op jit(solution)/shard_map/dot_general | solution.py:17
  398.5 15.1 %add_convert_fusion = bf16[2048,2048]{1,0:T(8,128)(2,1)} fusion(f32[2048,2048]{1,0:T(8,128)} %fusion.21, bf16[1024,2048]{1,0:T(8,128)(2,1)S(1)} %copy-done.35, bf16[1024,2048]{1,0:T(8,128)(2,1)S(1)} %copy-done.87), kind=kOutput, calls=%fused_computation.2 | convolution fusion | flops 8598323200 | bytes 33554432 | tf_op jit(solution)/shard_map/dot_general | solution.py:17
  445.6 14.0 %collective-permute-done.23 = bf16[128,2048]{1,0:T(8,128)(2,1)S(1)} collective-permute-done((bf16[128,2048]{1,0:T(8,128)(2,1)S(1)}, bf16[128,2048]{1,0:T(8,128)(2,1)S(1)}, u32[]{:S(2)}, u32[]{:S(2)}) %collective-permute-start.23) | collective-permute-done | bytes 524320 | tf_op jit(solution)/shard_map/ppermute | solution.py:37
  501.0 16.9 %collective-permute-done.27 = bf16[256,2048]{1,0:T(8,128)(2,1)} collective-permute-done((bf16[256,2048]{1,0:T(8,128)(2,1)}, bf16[256,2048]{1,0:T(8,128)(2,1)}, u32[]{:S(2)}, u32[]{:S(2)}) %collective-permute-start.27) | collective-permute-done | bytes 1048608 | tf_op jit(solution)/shard_map/ppermute | solution.py:37
  522.4 11.8 %multiply_convert_fusion = bf16[2,4,512,1024]{3,2,1,0:T(8,128)(2,1)} fusion(f32[2,4,512,1024]{3,2,1,0:T(8,128)} %copy-done, f32[2,4,512]{2,1,0:T(4,128)S(1)} %multiply_reduce_fusion.2, f32[2,4,512]{2,1,0:T(4,128)S(1)} %fusion.83, pred[2,512,1024]{2,1,0:T(8,128)(4,1)S(1)} %copy-done.12, bf16[2,4,512,128]{3,2,1,0:T(8,128)(2,1)S(1)} %bitcast.380, ...), kind=kOutput, calls=%fused_computation | convolution fusion | flops 1098907648 | bytes 29392896 | tf_op jit(solution)/shard_map/rjqd,rjkd->rjqk/dot_general | solution.py:297
  534.2 9.4 %convert_bitcast_fusion = bf16[1,2,4,1024,128]{3,4,2,1,0:T(8,128)(2,1)} fusion(bf16[2,4,512,128]{3,2,1,0:T(8,128)(2,1)S(1)} %bitcast.381, f32[2,4,512,1024]{3,2,1,0:T(8,128)} %copy-done, f32[2,4,512]{2,1,0:T(4,128)S(1)} %fusion.83, pred[2,512,1024]{2,1,0:T(8,128)(4,1)S(1)} %copy-done.12), kind=kOutput, calls=%fused_computation.83 | convolution fusion | flops 1091567616 | bytes 20987904 | tf_op jit(solution)/shard_map/rjqk,rjqd->rjkd/dot_general | solution.py:297
  612.7 20.9 %collective-permute-done.34 = bf16[2,2,4,128,128]{3,4,2,1,0:T(8,128)(2,1)S(1)} collective-permute-done((bf16[2,2,4,128,128]{3,4,2,1,0:T(8,128)(2,1)S(1)}, bf16[2,2,4,128,128]{3,4,2,1,0:T(8,128)(2,1)S(1)}, u32[]{:S(2)}, u32[]{:S(2)}) %collective-permute-start.34) | collective-permute-done | bytes 524320 | tf_op jit(solution)/shard_map/ppermute | solution.py:37
  636.1 31.2 %collective-permute-done.35 = bf16[2,2,4,128,128]{3,4,2,1,0:T(8,128)(2,1)S(1)} collective-permute-done((bf16[2,2,4,128,128]{3,4,2,1,0:T(8,128)(2,1)S(1)}, bf16[2,2,4,128,128]{3,4,2,1,0:T(8,128)(2,1)S(1)}, u32[]{:S(2)}, u32[]{:S(2)}) %collective-permute-start.35) | collective-permute-done | bytes 524320 | tf_op jit(solution)/shard_map/ppermute | solution.py:37
  691.0 21.3 %collective-permute-done.39 = bf16[256,2048]{1,0:T(8,128)(2,1)S(1)} collective-permute-done((bf16[256,2048]{1,0:T(8,128)(2,1)S(1)}, bf16[256,2048]{1,0:T(8,128)(2,1)S(1)}, u32[]{:S(2)}, u32[]{:S(2)}) %collective-permute-start.39) | collective-permute-done | bytes 1048608 | tf_op jit(solution)/shard_map/ppermute | solution.py:37
  730.1 15.4 %collective-permute-done.40 = bf16[256,2048]{1,0:T(8,128)(2,1)} collective-permute-done((bf16[256,2048]{1,0:T(8,128)(2,1)}, bf16[256,2048]{1,0:T(8,128)(2,1)}, u32[]{:S(2)}, u32[]{:S(2)}) %collective-permute-start.40) | collective-permute-done | bytes 1048608 | tf_op jit(solution)/shard_map/ppermute | solution.py:37
  752.7 14.5 %copy.98 = bf16[2,1024,2048]{2,0,1:T(2,128)(2,1)S(1)} copy(bf16[2,1024,2048]{2,1,0:T(8,128)(2,1)} %bitcast.376) | data formatting | bytes 16777216 | tf_op jit(solution)/shard_map/reshape | solution.py:432
  767.2 10.8 %convert_element_type.690 = f32[1024,2,2048]{2,1,0:T(2,128)} convert(bf16[1024,2,2048]{2,1,0:T(2,128)(2,1)S(1)} %bitcast.351) | non-fusion elementwise | flops 4194304 | bytes 25165824 | tf_op jit(solution)/shard_map/convert_element_type | solution.py:444
  (526 shorter events, 459.4 us)
Async XLA Ops:
  7.2 202.1 %all-gather.5.cloned.1.call-start = ((), (), s32[]{:S(2)}) async-start(), calls=%async_computation.2 | async-start | bytes 4718592 | tf_op jit(solution)/shard_map/all_gather | solution.py:269
  7.2 105.6 %collective-permute-start.7 = (bf16[256,2048]{1,0:T(8,128)(2,1)}, bf16[256,2048]{1,0:T(8,128)(2,1)}, u32[]{:S(2)}, u32[]{:S(2)}) collective-permute-start(bf16[256,2048]{1,0:T(8,128)(2,1)} %param.13), channel_id=1, source_target_pairs={{0,1},{1,0},{2,3},{3,2},{4,5},{5,4},{6,7},{7,6},{8,9},{9,8},{10,11... | collective-permute-start | bytes 3145736 | tf_op jit(solution)/shard_map/ppermute | solution.py:32
  12.1 207.8 %collective-permute-start.20 = (bf16[256,2048]{1,0:T(8,128)(2,1)}, bf16[256,2048]{1,0:T(8,128)(2,1)}, u32[]{:S(2)}, u32[]{:S(2)}) collective-permute-start(bf16[256,2048]{1,0:T(8,128)(2,1)} %param.14), channel_id=1, source_target_pairs={{0,1},{1,0},{2,3},{3,2},{4,5},{5,4},{6,7},{7,6},{8,9},{9,8},{10,11... | collective-permute-start | bytes 3145736 | tf_op jit(solution)/shard_map/ppermute | solution.py:32
  106.7 116.8 %all-gather.7.cloned.1.call-start = ((), (), s32[]{:S(2)}) async-start(), calls=%async_computation.3 | async-start | bytes 4718592 | tf_op jit(solution)/shard_map/all_gather | solution.py:269
  166.4 42.9 %collective-permute-start.21 = (bf16[8,768,256]{1,2,0:T(8,128)(2,1)}, bf16[8,768,256]{1,2,0:T(8,128)(2,1)}, u32[]{:S(2)}, u32[]{:S(2)}) collective-permute-start(bf16[8,768,256]{1,2,0:T(8,128)(2,1)} %copy.57), channel_id=1, source_target_pairs={{0,1},{1,0},{2,3},{3,2},{4,5},{5,4},{6,7},{7,6},{8,9},{9,8},{10,11... | collective-permute-start | bytes 9437192 | tf_op jit(solution)/shard_map/ppermute | solution.py:32
  166.5 103.5 %all-gather.9.cloned.1.call-start = ((), (), s32[]{:S(2)}) async-start(), calls=%async_computation.4 | async-start | bytes 4718592 | tf_op jit(solution)/shard_map/all_gather | solution.py:330
  224.7 92.7 %all-gather.11.cloned.1.call-start = ((), (), s32[]{:S(2)}) async-start(), calls=%async_computation.5 | async-start | bytes 4718592 | tf_op jit(solution)/shard_map/all_gather | solution.py:330
  225.2 163.4 %reduce-scatter.5.cloned.1.call-start = ((), (), s32[]{:S(2)}) async-start(), calls=%async_computation.7 | async-start | bytes 4718592 | tf_op jit(solution)/shard_map/reduce_scatter | solution.py:347
  317.4 101.2 %reduce-scatter.3.cloned.1.call-start = ((), (), s32[]{:S(2)}) async-start(), calls=%async_computation.6 | async-start | bytes 4718592 | tf_op jit(solution)/shard_map/reduce_scatter | solution.py:347
  355.8 359.2 %all-reduce.3.cloned.1.call-start = ((), (), s32[]{:S(2)}) async-start(), calls=%async_computation.8 | async-start | bytes 25165824 | tf_op jit(solution)/shard_map/psum | solution.py:361
  430.0 50.6 %collective-permute-start.26 = (bf16[1024,2048]{1,0:T(8,128)(2,1)}, bf16[1024,2048]{1,0:T(8,128)(2,1)}, u32[]{:S(2)}, u32[]{:S(2)}) collective-permute-start(bf16[1024,2048]{1,0:T(8,128)(2,1)} %convolution_convert_fusion.3), channel_id=1, source_target_pairs={{0,1},{1,0},{2,3},{3,2},{4,5},{5,4},{6,7},{7,6},{8,9},{9,8},{10,11... | collective-permute-start | bytes 12582920 | tf_op jit(solution)/shard_map/ppermute | solution.py:32
  480.6 235.9 %collective-permute-start.25 = (bf16[128,2048]{1,0:T(8,128)(2,1)}, bf16[128,2048]{1,0:T(8,128)(2,1)}, u32[]{:S(2)}, u32[]{:S(2)}) collective-permute-start(bf16[128,2048]{1,0:T(8,128)(2,1)} %add_convert_fusion.32), channel_id=1, source_target_pairs={{0,2},{1,3},{2,4},{3,5},{4,6},{5,7},{6,0},{7,1},{8,10},{9,11},{10,... | collective-permute-start | bytes 1572872 | tf_op jit(solution)/shard_map/ppermute | solution.py:37
  483.2 34.6 %collective-permute-start.27 = (bf16[256,2048]{1,0:T(8,128)(2,1)}, bf16[256,2048]{1,0:T(8,128)(2,1)}, u32[]{:S(2)}, u32[]{:S(2)}) collective-permute-start(bf16[256,2048]{1,0:T(8,128)(2,1)} %add_convert_fusion.14), channel_id=1, source_target_pairs={{0,2},{1,3},{2,4},{3,5},{4,6},{5,7},{6,0},{7,1},{8,10},{9,11},{10,... | collective-permute-start | bytes 3145736 | tf_op jit(solution)/shard_map/ppermute | solution.py:37
  549.8 120.3 %collective-permute-start.50 = (bf16[256,2048]{1,0:T(8,128)(2,1)}, bf16[256,2048]{1,0:T(8,128)(2,1)}, u32[]{:S(2)}, u32[]{:S(2)}) collective-permute-start(bf16[256,2048]{1,0:T(8,128)(2,1)} %add_convert_fusion.10), channel_id=1, source_target_pairs={{0,2},{1,3},{2,4},{3,5},{4,6},{5,7},{6,0},{7,1},{8,10},{9,11},{10,... | collective-permute-start | bytes 3145736 | tf_op jit(solution)/shard_map/ppermute | solution.py:37
  551.6 52.5 %collective-permute-start.29 = (bf16[512,2048]{1,0:T(8,128)(2,1)}, bf16[512,2048]{1,0:T(8,128)(2,1)}, u32[]{:S(2)}, u32[]{:S(2)}) collective-permute-start(bf16[512,2048]{1,0:T(8,128)(2,1)} %pad_maximum_fusion.8), channel_id=1, source_target_pairs={{0,1},{1,0},{2,3},{3,2},{4,5},{5,4},{6,7},{7,6},{8,9},{9,8},{10,11... | collective-permute-start | bytes 6291464 | tf_op jit(solution)/shard_map/ppermute | solution.py:32
  609.9 57.7 %collective-permute-start.38 = (bf16[256,2048]{1,0:T(8,128)(2,1)S(1)}, bf16[256,2048]{1,0:T(8,128)(2,1)S(1)}, u32[]{:S(2)}, u32[]{:S(2)}) collective-permute-start(bf16[256,2048]{1,0:T(8,128)(2,1)S(1)} %add_convert_fusion.9), channel_id=1, source_target_pairs={{0,2},{1,3},{2,4},{3,5},{4,6},{5,7},{6,0},{7,1},{8,10},{9,11},{10,... | collective-permute-start | bytes 3145736 | tf_op jit(solution)/shard_map/ppermute | solution.py:37
  633.8 33.5 %collective-permute-start.35 = (bf16[2,2,4,128,128]{3,4,2,1,0:T(8,128)(2,1)S(1)}, bf16[2,2,4,128,128]{3,4,2,1,0:T(8,128)(2,1)S(1)}, u32[]{:S(2)}, u32[]{:S(2)}) collective-permute-start(bf16[2,2,4,128,128]{3,4,2,1,0:T(8,128)(2,1)S(1)} %add_convert_fusion.22), channel_id=1, source_target_pairs={{0,2},{1,3},{2,4},{3,5},{4,6},{5,7},{6,0},{7,1},{8,10},{9,11},{10,... | collective-permute-start | bytes 1572872 | tf_op jit(solution)/shard_map/ppermute | solution.py:37
  635.5 43.0 %collective-permute-start.31 = (bf16[128,2048]{1,0:T(8,128)(2,1)S(1)}, bf16[128,2048]{1,0:T(8,128)(2,1)S(1)}, u32[]{:S(2)}, u32[]{:S(2)}) collective-permute-start(bf16[128,2048]{1,0:T(8,128)(2,1)S(1)} %add_convert_fusion.28), channel_id=1, source_target_pairs={{0,2},{1,3},{2,4},{3,5},{4,6},{5,7},{6,0},{7,1},{8,10},{9,11},{10,... | collective-permute-start | bytes 1572872 | tf_op jit(solution)/shard_map/ppermute | solution.py:37
  669.4 42.9 %collective-permute-start.39 = (bf16[256,2048]{1,0:T(8,128)(2,1)S(1)}, bf16[256,2048]{1,0:T(8,128)(2,1)S(1)}, u32[]{:S(2)}, u32[]{:S(2)}) collective-permute-start(bf16[256,2048]{1,0:T(8,128)(2,1)S(1)} %add_convert_fusion.7), channel_id=1, source_target_pairs={{0,2},{1,3},{2,4},{3,5},{4,6},{5,7},{6,0},{7,1},{8,10},{9,11},{10,... | collective-permute-start | bytes 3145736 | tf_op jit(solution)/shard_map/ppermute | solution.py:37
  680.7 42.8 %collective-permute-start.32 = (bf16[128,2048]{1,0:T(8,128)(2,1)}, bf16[128,2048]{1,0:T(8,128)(2,1)}, u32[]{:S(2)}, u32[]{:S(2)}) collective-permute-start(bf16[128,2048]{1,0:T(8,128)(2,1)} %add_convert_fusion.26), channel_id=1, source_target_pairs={{0,2},{1,3},{2,4},{3,5},{4,6},{5,7},{6,0},{7,1},{8,10},{9,11},{10,... | collective-permute-start | bytes 1572872 | tf_op jit(solution)/shard_map/ppermute | solution.py:37
  728.4 57.3 %collective-permute-start.54 = (bf16[128,2048]{1,0:T(8,128)(2,1)S(1)}, bf16[128,2048]{1,0:T(8,128)(2,1)}, u32[]{:S(2)}, u32[]{:S(2)}) collective-permute-start(bf16[128,2048]{1,0:T(8,128)(2,1)S(1)} %get-tuple-element.119), channel_id=1, source_target_pairs={{0,8},{8,0},{16,24},{24,16},{1,9},{9,1},{17,25},{25,17},{2,10},{10... | collective-permute-start | bytes 1572872 | tf_op jit(solution)/shard_map/ppermute | solution.py:41
  749.0 41.1 %collective-permute-start.46 = (bf16[128,2048]{1,0:T(8,128)(2,1)}, bf16[128,2048]{1,0:T(8,128)(2,1)}, u32[]{:S(2)}, u32[]{:S(2)}) collective-permute-start(bf16[128,2048]{1,0:T(8,128)(2,1)} %get-tuple-element.124), channel_id=1, source_target_pairs={{0,8},{8,0},{16,24},{24,16},{1,9},{9,1},{17,25},{25,17},{2,10},{10... | collective-permute-start | bytes 1572872 | tf_op jit(solution)/shard_map/ppermute | solution.py:41
  749.0 41.1 %collective-permute-start.48 = (bf16[128,2048]{1,0:T(8,128)(2,1)}, bf16[128,2048]{1,0:T(8,128)(2,1)}, u32[]{:S(2)}, u32[]{:S(2)}) collective-permute-start(bf16[128,2048]{1,0:T(8,128)(2,1)} %get-tuple-element.125), channel_id=1, source_target_pairs={{0,16},{8,24},{16,0},{24,8},{1,17},{9,25},{17,1},{25,9},{2,18},{10... | collective-permute-start | bytes 1572872 | tf_op jit(solution)/shard_map/ppermute | solution.py:41
  750.3 33.0 %collective-permute-start.42 = (f32[2,2048]{1,0:T(2,128)S(1)}, f32[2,2048]{1,0:T(2,128)S(1)}, u32[]{:S(2)}, u32[]{:S(2)}) collective-permute-start(f32[2,2048]{1,0:T(2,128)S(1)} %add.555), channel_id=1, source_target_pairs={{0,2},{1,3},{2,0},{3,1},{4,6},{5,7},{6,4},{7,5},{8,10},{9,11},{10,... | collective-permute-start | bytes 49160 | tf_op jit(solution)/shard_map/ppermute | solution.py:222
  (133 other events, 1775.7 us)
Sparse Core Ops, SparseCore 0:
  106.9 45.2 all-gather.4
  166.6 45.1 all-gather.6
  224.8 45.1 all-gather.8
  271.4 45.8 all-gather.10
  319.5 48.7 reduce-scatter.4
  370.4 48.1 reduce-scatter.2
  437.5 238.5 all-reduce.2

commit v11 on v10

--- a/solution.py
+++ b/solution.py
@@ -51,30 +51,30 @@
 def ring_scatter(parts, chips):
     sent = parts[chips - 1]
     for j in range(chips - 2, -1, -1):
-        yield sent
-        total = ring(sent, chips).astype(F32) + parts[j].astype(F32)
+        after = yield sent
+        total = ring(sent, chips).astype(F32) + tie(parts[j], after).astype(F32)
         sent = total.astype(BF16)
     return total
 
 
 class Lane:
     def __init__(self):
-        self.waiting, self.results, self.sent = [], {}, None
+        self.waiting, self.results, self.begun, self.sent = [], {}, set(), None
 
     def add(self, name, steps):
         self.waiting.append((name, steps))
 
-    def step(self):
+    def step(self, after=None):
         if self.waiting:
             name, steps = self.waiting[0]
             try:
-                sent = next(steps)
-                self.sent = sent
-                return sent
+                self.sent = next(steps) if name not in self.begun else steps.send(after)
+                self.begun.add(name)
+                return self.sent
             except StopIteration as end:
                 self.results[name] = end.value
                 self.waiting.pop(0)
-                return self.step()
+                return self.step(after)
         return None
 
     def result(self, name):
@@ -85,7 +85,7 @@
 
 def beside(value, *lanes):
     for lane in lanes:
-        value = tie(value, lane.step())
+        value = tie(value, lane.step(value))
     return value
 
 
@@ -390,15 +390,19 @@
     probs = jnp.where(valid, jnp.exp(scores - lse), 0.0)
     grad_probs = heads_dot("rjqd,rjkd->rjqk", grad_heads, values)
     grad_scores = beside((probs * (grad_probs - delta)).astype(BF16), main, fill)
-    for r in range(1, rows_here):
-        part, grad_scores = lax.optimization_barrier((ffn_part[r], grad_scores))
-        fill.add(("ffn", r), scatter_tokens(part, chips, place, core))
     query_term = from_heads(
         (heads_dot("rjqk,rjkd->rjqd", grad_scores, keys) * scale).astype(BF16)
     )
+    query_part = [dot(half, normed_one, ((0,), (0,))).astype(BF16) for half in query_term]
+    query_part, grad_scores = lax.optimization_barrier((query_part, grad_scores))
+    output_sum = main.result("output")
+    main.add("query", scatter_rows(query_part))
+    main.step()
+    sent = main.step()
     grad_keys = heads_dot("rjqk,rjqd->rjkd", grad_scores, query_heads) * scale
     grad_values = heads_dot("rjqk,rjqd->rjkd", probs.astype(BF16), grad_heads)
     cache_part = from_slots(jnp.stack([grad_keys.astype(BF16), grad_values.astype(BF16)]))
+    cache_part = tie(cache_part, sent)
     half_len = cache_part.shape[3] // 2
 
     def positions_of(value, j):
@@ -410,8 +414,9 @@
             lambda j: positions_of(cache_part, j), cache_part[:, :, :, half_len:], positions_of, chips
         ),
     )
-    query_part = [dot(half, normed_one, ((0,), (0,))).astype(BF16) for half in query_term]
-    main.add("query", scatter_rows(query_part))
+    fill.result(("ffn", 0))
+    for r in range(1, rows_here):
+        fill.add(("ffn", r), scatter_tokens(tie(ffn_part[r], sent), chips, place, core))
 
     grad_normed_one = query_proj.back(query_term)
     scaled_one = inputs * inverse_one
@@ -424,14 +429,11 @@
     ]
     cache_grad = fill.result("cache")
     cache_grad = cache_grad.transpose(1, 3, 0, 2, 4).reshape(rows_here, seg_len, 2, KV * HEAD)
-    output_sum = main.result("output")
-    for _ in range(chips - 1):
-        sent = main.step()
-    summed, output_sum = lax.optimization_barrier((summed, output_sum.astype(BF16)))
-    in_grad, down_grad = tie(summed, sent)
+    summed, query_sum = lax.optimization_barrier((summed, main.result("query").astype(BF16)))
+    summed, gain_grad = lax.optimization_barrier((summed, gain_grad))
+    in_grad, down_grad = summed
     in_grad = in_grad.reshape(2, units, width).transpose(1, 0, 2)
     in_grad = lax.optimization_barrier(in_grad)
-    query_sum, gain_grad = lax.optimization_barrier((main.result("query"), gain_grad))
     gain_grad = sum_all(gain_grad, rows, seq)
     output_grad, query_grad = sum_rows((output_sum, query_sum), rows)
     return (

time: 830 us -> 828 us (level)
  waiting for transfers between devices: 278 us -> 255 us
  local copies, waits for them, and re-layouts: 148 us -> 157 us
    ppermute x24, waiting for transfers between devices: 207 us -> 172 us  [ring(): return lax.ppermute(value, 'seq', pairs)]
    psum x1, waiting for transfers between devices: 0.01 us -> 16.5 us  [local(): summed = lax.psum(parts, 'rows')]
    ppermute x18, waiting for transfers between devices: 34.6 us -> 23.5 us  [swap_row(): return lax.ppermute(value, 'rows', [(r, r ^ mask) for r in range(rows)])]
    another operation x2, local copies, waits for them, and re-layouts: 5.12 us -> 14.3 us  [xor_order(): value = value.reshape(2, 2, *shape[1:])]
    unnamed x230 -> x240, local copies, waits for them, and re-layouts: 39.7 us -> 37.3 us
  transfers between devices with their start and end apart: 62 -> 62, of which waited for: 34 -> 28; matrix products, arithmetic and copies ran while one was open for 57% -> 59% of each run, Pallas kernels for 0% -> 0%
where the time goes in v11:
time: 828 us; the launch traced here: 817 us
  waiting for transfers between devices  255 us (31%)
  matrix products  224 us (27%)
  local copies, waits for them, and re-layouts  157 us (19%)
  other arithmetic  127 us (15%)
  starting transfers between devices  38 us (5%)
  between operations  16.4 us (2%)
    ppermute x24, waiting for transfers between devices, ring(): return lax.ppermute(value, 'seq', pairs)  172 us
    dot_general x24, matrix products, dot(): lax.dot_general(left, right, (dims, ((), ())), preferred_element_type=F32)  158 us
    dot_general x6, matrix products, heads_dot(): return jnp.einsum(spec, left, right, preferred_element_type=F32)  42.8 us
    unnamed x240, local copies, waits for them, and re-layouts  37.3 us
    all_gather x2, waiting for transfers between devices, local(): lax.all_gather(n, 'seq', axis=0, tiled=True)  29.6 us
    ppermute x18, waiting for transfers between devices, swap_row(): return lax.ppermute(value, 'rows', [(r, r ^ mask) for r in range(rows)])  23.5 us
    ppermute x18, starting transfers between devices, swap_row(): return lax.ppermute(value, 'rows', [(r, r ^ mask) for r in range(rows)])  21.6 us
    convert_element_type x10, other arithmetic, ring_scatter(): sent = total.astype(BF16)  19.2 us
  transfers between devices with their start and end apart: 62, of which 28 were waited for; matrix products, arithmetic and copies ran while one was open for 59% of the time, Pallas kernels for 0%

profile of v11, /device:TPU:0, one launch (start us, length us, event | category | flops | bytes accessed | tf_op | source)
XLA Modules:
  0.0 817.3 jit_solution(3531696259101420688)
XLA Ops:
  121.2 10.1 %collective-permute-done.5 = bf16[2,3,256,256]{3,2,1,0:T(8,128)(2,1)S(1)} collective-permute-done((bf16[2,3,256,256]{3,2,1,0:T(8,128)(2,1)S(1)}, bf16[2,3,256,256]{3,2,1,0:T(8,128)(2,1)S(1)}, u32[]{:S(2)}, u32[]{:S(2)}) %collective-permute-start.5) | collective-permute-done | bytes 786464 | tf_op jit(solution)/shard_map/ppermute | solution.py:41
  214.7 11.1 %copy.57 = f32[2,2,2,256,256]{4,3,2,1,0:T(8,128)S(1)} copy(f32[2,2,2,256,256]{3,4,2,1,0:T(8,128)} %bitcast.378) | data formatting | bytes 4194304 | tf_op jit(solution)/shard_map/reshape;reshape | solution.py:94
  234.2 16.5 %fusion.99 = (bf16[1024,1,2048]{2,1,0:T(2,128)(2,1)S(1)}, bf16[1024,1,2048]{2,1,0:T(2,128)(2,1)S(1)}) fusion(bf16[1024,2,2048]{2,1,0:T(2,128)(2,1)} %param.15), kind=kLoop, calls=%fused_computation.326 | loop fusion | bytes 16777216 | tf_op jit(solution)/shard_map/slice | solution.py:260
  258.5 20.6 %all-gather.9.cloned.1.call-done = bf16[1024,2048]{1,0:T(8,128)(2,1)} async-done(((bf16[128,2048]{1,0:T(8,128)(2,1)}), bf16[1024,2048]{1,0:T(8,128)(2,1)}) %all-gather.9.cloned.1.call-update) | async-done | bytes 4194320 | tf_op jit(solution)/shard_map/all_gather | solution.py:330
  279.1 15.3 %fusion.98 = f32[1024,2048]{1,0:T(8,128)} fusion(bf16[1024,2048]{1,0:T(8,128)(2,1)} %all-gather.9.cloned.1.call-done, bf16[1024,2048]{1,0:T(8,128)(2,1)} %get-tuple-element.188, bf16[1024,2048]{1,0:T(8,128)(2,1)} %get-tuple-element.189), kind=kOutput, calls=%fused_computation.325 | convolution fusion | flops 8606711808 | bytes 20971520 | tf_op jit(solution)/shard_map/dot_general | solution.py:17
  294.4 10.2 %multiply_convert_fusion.6 = (bf16[1024,1024]{1,0:T(8,128)(2,1)S(1)}, bf16[1024,1024]{1,0:T(8,128)(2,1)}, bf16[1024,1024]{1,0:T(8,128)(2,1)}) fusion(f32[1024,2048]{1,0:T(8,128)} %fusion.98, bf16[1024,2048]{1,0:T(8,128)(2,1)S(1)} %copy-done.89, bf16[1024,2048]{1,0:T(8,128)(2,1)S(1)} %copy-done.86), kind=kOutput, calls=%fused_computation.42 | convolution fusion | flops 4311744512 | bytes 23068672 | tf_op jit(solution)/shard_map/dot_general | solution.py:17
  304.6 12.8 %convolution_convert_fusion.5 = bf16[1024,2048]{1,0:T(8,128)(2,1)} fusion(bf16[1024,1024]{1,0:T(8,128)(2,1)} %get-tuple-element.109, bf16[1024,1024]{1,0:T(8,128)(2,1)S(1)} %get-tuple-element.108, bf16[1024,2048]{1,0:T(8,128)(2,1)S(1)} %copy-done.41, bf16[1024,2048]{1,0:T(8,128)(2,1)S(1)} %copy-done.43), kind=kOutput, calls=%fused_computation.50 | convolution fusion | flops 8617197568 | bytes 16777216 | tf_op jit(solution)/shard_map/dot_general | solution.py:17
  326.5 15.3 %fusion.97 = f32[1024,2048]{1,0:T(8,128)} fusion(bf16[1024,2048]{1,0:T(8,128)(2,1)} %all-gather.11.cloned.1.call-done, bf16[1024,2048]{1,0:T(8,128)(2,1)} %get-tuple-element.188, bf16[1024,2048]{1,0:T(8,128)(2,1)} %get-tuple-element.189), kind=kOutput, calls=%fused_computation.324 | convolution fusion | flops 8606711808 | bytes 20971520 | tf_op jit(solution)/shard_map/dot_general | solution.py:17
  341.8 11.2 %multiply_convert_fusion.4 = (bf16[1024,1024]{1,0:T(8,128)(2,1)S(1)}, bf16[1024,1024]{1,0:T(8,128)(2,1)S(1)}, bf16[1024,1024]{1,0:T(8,128)(2,1)}) fusion(f32[1024,2048]{1,0:T(8,128)} %fusion.97, bf16[1024,2048]{1,0:T(8,128)(2,1)} %all-gather.7.cloned.1.call-done, bf16[1024,2048]{1,0:T(8,128)(2,1)S(1)} %copy-done.87), kind=kOutput, calls=%fused_computation.39 | convolution fusion | flops 4311744512 | bytes 23068672 | tf_op jit(solution)/shard_map/dot_general | solution.py:17
  354.3 10.5 %convolution_convert_fusion.4 = bf16[1024,2048]{1,0:T(8,128)(2,1)} fusion(bf16[1024,2048]{1,0:T(8,128)(2,1)S(1)} %copy-done.42, bf16[1024,2048]{1,0:T(8,128)(2,1)S(1)} %copy-done.44, bf16[1024,1024]{1,0:T(8,128)(2,1)S(1)} %get-tuple-element.107, bf16[1024,1024]{1,0:T(8,128)(2,1)S(1)} %get-tuple-element.106), kind=kOutput, calls=%fused_computation.49 | convolution fusion | flops 8617197568 | bytes 16777216 | tf_op jit(solution)/shard_map/dot_general | solution.py:17
  378.7 12.2 %fusion.21 = f32[2048,2048]{1,0:T(8,128)} fusion(bf16[1024,2048]{1,0:T(8,128)(2,1)S(1)} %copy-done.92, bf16[1024,1024]{1,0:T(8,128)(2,1)S(1)} %copy-done.99, bf16[1024,1024]{1,0:T(8,128)(2,1)S(1)} %copy-done.98), kind=kOutput, calls=%fused_computation.62 | convolution fusion | flops 8598323200 | bytes 25165824 | tf_op jit(solution)/shard_map/dot_general | solution.py:17
  391.0 9.9 %add_convert_fusion.1 = bf16[1024,2048]{1,0:T(8,128)(2,1)} fusion(f32[1024,2048]{1,0:T(8,128)} %fusion.109, bf16[1024,1024]{1,0:T(8,128)(2,1)S(1)} %copy-done.95, bf16[1024,2048]{1,0:T(8,128)(2,1)} %all-gather.7.cloned.1.call-done), kind=kOutput, calls=%fused_computation.21 | convolution fusion | flops 4299161600 | bytes 18874368 | tf_op jit(solution)/shard_map/dot_general | solution.py:17
  400.9 15.1 %add_convert_fusion = bf16[2048,2048]{1,0:T(8,128)(2,1)} fusion(f32[2048,2048]{1,0:T(8,128)} %fusion.21, bf16[1024,2048]{1,0:T(8,128)(2,1)S(1)} %copy-done.37, bf16[1024,2048]{1,0:T(8,128)(2,1)S(1)} %copy-done.91), kind=kOutput, calls=%fused_computation.2 | convolution fusion | flops 8598323200 | bytes 33554432 | tf_op jit(solution)/shard_map/dot_general | solution.py:17
  415.9 11.7 %reduce-scatter.3.cloned.1.call-done = bf16[128,2048]{1,0:T(8,128)(2,1)} async-done(((bf16[1024,2048]{1,0:T(8,128)(2,1)}), bf16[128,2048]{1,0:T(8,128)(2,1)}) %reduce-scatter.3.cloned.1.call-update) | async-done | bytes 524304 | tf_op jit(solution)/shard_map/reduce_scatter | solution.py:347
  499.1 14.9 %collective-permute-done.25 = bf16[256,2048]{1,0:T(8,128)(2,1)} collective-permute-done((bf16[256,2048]{1,0:T(8,128)(2,1)}, bf16[256,2048]{1,0:T(8,128)(2,1)}, u32[]{:S(2)}, u32[]{:S(2)}) %collective-permute-start.25) | collective-permute-done | bytes 1048608 | tf_op jit(solution)/shard_map/ppermute | solution.py:37
  519.6 11.2 %multiply_convert_fusion = bf16[2,4,512,1024]{3,2,1,0:T(8,128)(2,1)} fusion(f32[2,4,512,1024]{3,2,1,0:T(8,128)} %copy-done, f32[2,4,512]{2,1,0:T(4,128)S(1)} %multiply_reduce_fusion.2, f32[2,4,512]{2,1,0:T(4,128)S(1)} %fusion.83, pred[2,512,1024]{2,1,0:T(8,128)(4,1)S(1)} %copy-done.13, bf16[2,4,512,128]{3,2,1,0:T(8,128)(2,1)} %bitcast.380, ...), kind=kOutput, calls=%fused_computation | convolution fusion | flops 1098907648 | bytes 29392896 | tf_op jit(solution)/shard_map/rjqd,rjkd->rjqk/dot_general | solution.py:297
  530.7 11.4 %convert_bitcast_fusion = bf16[1,2,4,1024,128]{4,3,2,1,0:T(8,128)(2,1)} fusion(bf16[2,4,512,128]{3,2,1,0:T(8,128)(2,1)} %bitcast.381, f32[2,4,512,1024]{3,2,1,0:T(8,128)} %copy-done, f32[2,4,512]{2,1,0:T(4,128)S(1)} %fusion.83, pred[2,512,1024]{2,1,0:T(8,128)(4,1)S(1)} %copy-done.13), kind=kOutput, calls=%fused_computation.79 | convolution fusion | flops 1091567616 | bytes 20987904 | tf_op jit(solution)/shard_map/rjqk,rjqd->rjkd/dot_general | solution.py:297
  611.6 19.4 %collective-permute-done.30 = bf16[256,2048]{1,0:T(8,128)(2,1)S(1)} collective-permute-done((bf16[256,2048]{1,0:T(8,128)(2,1)S(1)}, bf16[256,2048]{1,0:T(8,128)(2,1)S(1)}, u32[]{:S(2)}, u32[]{:S(2)}) %collective-permute-start.30) | collective-permute-done | bytes 1048608 | tf_op jit(solution)/shard_map/ppermute | solution.py:37
  637.2 22.4 %collective-permute-done.39 = bf16[256,2048]{1,0:T(8,128)(2,1)S(1)} collective-permute-done((bf16[256,2048]{1,0:T(8,128)(2,1)S(1)}, bf16[256,2048]{1,0:T(8,128)(2,1)S(1)}, u32[]{:S(2)}, u32[]{:S(2)}) %collective-permute-start.39) | collective-permute-done | bytes 1048608 | tf_op jit(solution)/shard_map/ppermute | solution.py:37
  667.8 19.6 %collective-permute-done.40 = bf16[256,2048]{1,0:T(8,128)(2,1)S(1)} collective-permute-done((bf16[256,2048]{1,0:T(8,128)(2,1)S(1)}, bf16[256,2048]{1,0:T(8,128)(2,1)S(1)}, u32[]{:S(2)}, u32[]{:S(2)}) %collective-permute-start.40) | collective-permute-done | bytes 1048608 | tf_op jit(solution)/shard_map/ppermute | solution.py:37
  689.1 16.5 %all-reduce.3.cloned.1.call-done = (bf16[2048,2048]{1,0:T(8,128)(2,1)}, bf16[1024,2048]{1,0:T(8,128)(2,1)}) async-done(((bf16[2048,2048]{1,0:T(8,128)(2,1)}, bf16[1024,2048]{1,0:T(8,128)(2,1)}), (bf16[2048,2048]{1,0:T(8,128)(2,1)}, bf16[1024,2048]{1,0:T(8,128)(2,1)})) %all-reduce.3.cloned.1.call-update) | async-done | bytes 12582928 | tf_op jit(solution)/shard_map/psum | solution.py:361
  722.6 14.5 %copy.98 = bf16[2,1024,2048]{2,0,1:T(2,128)(2,1)S(1)} copy(bf16[2,1024,2048]{2,1,0:T(8,128)(2,1)} %bitcast.376) | data formatting | bytes 16777216 | tf_op jit(solution)/shard_map/reshape | solution.py:435
  737.1 10.8 %convert_element_type.690 = f32[1024,2,2048]{2,1,0:T(2,128)} convert(bf16[1024,2,2048]{2,1,0:T(2,128)(2,1)S(1)} %bitcast.351) | non-fusion elementwise | flops 4194304 | bytes 25165824 | tf_op jit(solution)/shard_map/convert_element_type | solution.py:446
  786.1 15.5 %collective-permute-done.38 = bf16[2,2,4,128,128]{4,3,2,1,0:T(8,128)(2,1)S(1)} collective-permute-done((bf16[2,2,4,128,128]{4,3,2,1,0:T(8,128)(2,1)S(1)}, bf16[2,2,4,128,128]{4,3,2,1,0:T(8,128)(2,1)S(1)}, u32[]{:S(2)}, u32[]{:S(2)}) %collective-permute-start.38) | collective-permute-done | bytes 524320 | tf_op jit(solution)/shard_map/ppermute | solution.py:37
  (537 shorter events, 462.5 us)
Async XLA Ops:
  7.2 202.0 %all-gather.5.cloned.1.call-start = ((), (), s32[]{:S(2)}) async-start(), calls=%async_computation.2 | async-start | bytes 4718592 | tf_op jit(solution)/shard_map/all_gather | solution.py:269
  7.2 105.6 %collective-permute-start.7 = (bf16[256,2048]{1,0:T(8,128)(2,1)}, bf16[256,2048]{1,0:T(8,128)(2,1)}, u32[]{:S(2)}, u32[]{:S(2)}) collective-permute-start(bf16[256,2048]{1,0:T(8,128)(2,1)} %param.13), channel_id=1, source_target_pairs={{0,1},{1,0},{2,3},{3,2},{4,5},{5,4},{6,7},{7,6},{8,9},{9,8},{10,11... | collective-permute-start | bytes 3145736 | tf_op jit(solution)/shard_map/ppermute | solution.py:32
  12.1 216.7 %collective-permute-start.20 = (bf16[256,2048]{1,0:T(8,128)(2,1)}, bf16[256,2048]{1,0:T(8,128)(2,1)}, u32[]{:S(2)}, u32[]{:S(2)}) collective-permute-start(bf16[256,2048]{1,0:T(8,128)(2,1)} %param.14), channel_id=1, source_target_pairs={{0,1},{1,0},{2,3},{3,2},{4,5},{5,4},{6,7},{7,6},{8,9},{9,8},{10,11... | collective-permute-start | bytes 3145736 | tf_op jit(solution)/shard_map/ppermute | solution.py:32
  106.7 125.8 %all-gather.7.cloned.1.call-start = ((), (), s32[]{:S(2)}) async-start(), calls=%async_computation.3 | async-start | bytes 4718592 | tf_op jit(solution)/shard_map/all_gather | solution.py:269
  166.6 42.7 %collective-permute-start.21 = (bf16[8,768,256]{1,2,0:T(8,128)(2,1)}, bf16[8,768,256]{1,2,0:T(8,128)(2,1)}, u32[]{:S(2)}, u32[]{:S(2)}) collective-permute-start(bf16[8,768,256]{1,2,0:T(8,128)(2,1)} %copy.56), channel_id=1, source_target_pairs={{0,1},{1,0},{2,3},{3,2},{4,5},{5,4},{6,7},{7,6},{8,9},{9,8},{10,11... | collective-permute-start | bytes 9437192 | tf_op jit(solution)/shard_map/ppermute | solution.py:32
  166.6 112.5 %all-gather.9.cloned.1.call-start = ((), (), s32[]{:S(2)}) async-start(), calls=%async_computation.4 | async-start | bytes 4718592 | tf_op jit(solution)/shard_map/all_gather | solution.py:330
  233.6 92.8 %all-gather.11.cloned.1.call-start = ((), (), s32[]{:S(2)}) async-start(), calls=%async_computation.5 | async-start | bytes 4718592 | tf_op jit(solution)/shard_map/all_gather | solution.py:330
  234.2 156.8 %reduce-scatter.5.cloned.1.call-start = ((), (), s32[]{:S(2)}) async-start(), calls=%async_computation.7 | async-start | bytes 4718592 | tf_op jit(solution)/shard_map/reduce_scatter | solution.py:347
  326.5 101.2 %reduce-scatter.3.cloned.1.call-start = ((), (), s32[]{:S(2)}) async-start(), calls=%async_computation.6 | async-start | bytes 4718592 | tf_op jit(solution)/shard_map/reduce_scatter | solution.py:347
  364.8 340.8 %all-reduce.3.cloned.1.call-start = ((), (), s32[]{:S(2)}) async-start(), calls=%async_computation.8 | async-start | bytes 25165824 | tf_op jit(solution)/shard_map/psum | solution.py:361
  436.4 39.6 %collective-permute-start.24 = (bf16[1024,2048]{1,0:T(8,128)(2,1)}, bf16[1024,2048]{1,0:T(8,128)(2,1)}, u32[]{:S(2)}, u32[]{:S(2)}) collective-permute-start(bf16[1024,2048]{1,0:T(8,128)(2,1)} %convolution_convert_fusion.3), channel_id=1, source_target_pairs={{0,1},{1,0},{2,3},{3,2},{4,5},{5,4},{6,7},{7,6},{8,9},{9,8},{10,11... | collective-permute-start | bytes 12582920 | tf_op jit(solution)/shard_map/ppermute | solution.py:32
  475.5 41.3 %collective-permute-start.23 = (bf16[128,2048]{1,0:T(8,128)(2,1)}, bf16[128,2048]{1,0:T(8,128)(2,1)}, u32[]{:S(2)}, u32[]{:S(2)}) collective-permute-start(bf16[128,2048]{1,0:T(8,128)(2,1)} %get-tuple-element.119), channel_id=1, source_target_pairs={{0,2},{1,3},{2,4},{3,5},{4,6},{5,7},{6,0},{7,1},{8,10},{9,11},{10,... | collective-permute-start | bytes 1572872 | tf_op jit(solution)/shard_map/ppermute | solution.py:37
  480.6 33.5 %collective-permute-start.25 = (bf16[256,2048]{1,0:T(8,128)(2,1)}, bf16[256,2048]{1,0:T(8,128)(2,1)}, u32[]{:S(2)}, u32[]{:S(2)}) collective-permute-start(bf16[256,2048]{1,0:T(8,128)(2,1)} %get-tuple-element.112), channel_id=1, source_target_pairs={{0,2},{1,3},{2,4},{3,5},{4,6},{5,7},{6,0},{7,1},{8,10},{9,11},{10,... | collective-permute-start | bytes 3145736 | tf_op jit(solution)/shard_map/ppermute | solution.py:37
  518.9 35.2 %collective-permute-start.26 = (bf16[128,2048]{1,0:T(8,128)(2,1)}, bf16[128,2048]{1,0:T(8,128)(2,1)}, u32[]{:S(2)}, u32[]{:S(2)}) collective-permute-start(bf16[128,2048]{1,0:T(8,128)(2,1)} %add_convert_fusion.35), channel_id=1, source_target_pairs={{0,2},{1,3},{2,4},{3,5},{4,6},{5,7},{6,0},{7,1},{8,10},{9,11},{10,... | collective-permute-start | bytes 1572872 | tf_op jit(solution)/shard_map/ppermute | solution.py:37
  556.1 250.3 %collective-permute-start.28 = (bf16[128,2048]{1,0:T(8,128)(2,1)}, bf16[128,2048]{1,0:T(8,128)(2,1)}, u32[]{:S(2)}, u32[]{:S(2)}) collective-permute-start(bf16[128,2048]{1,0:T(8,128)(2,1)} %add_convert_fusion.33), channel_id=1, source_target_pairs={{0,2},{1,3},{2,4},{3,5},{4,6},{5,7},{6,0},{7,1},{8,10},{9,11},{10,... | collective-permute-start | bytes 1572872 | tf_op jit(solution)/shard_map/ppermute | solution.py:37
  556.1 49.4 %collective-permute-start.50 = (bf16[256,2048]{1,0:T(8,128)(2,1)}, bf16[256,2048]{1,0:T(8,128)(2,1)}, u32[]{:S(2)}, u32[]{:S(2)}) collective-permute-start(bf16[256,2048]{1,0:T(8,128)(2,1)} %add_convert_fusion.11), channel_id=1, source_target_pairs={{0,2},{1,3},{2,4},{3,5},{4,6},{5,7},{6,0},{7,1},{8,10},{9,11},{10,... | collective-permute-start | bytes 3145736 | tf_op jit(solution)/shard_map/ppermute | solution.py:37
  634.0 32.6 %collective-permute-start.54 = (bf16[128,2048]{1,0:T(8,128)(2,1)S(1)}, bf16[128,2048]{1,0:T(8,128)(2,1)S(1)}, u32[]{:S(2)}, u32[]{:S(2)}) collective-permute-start(bf16[128,2048]{1,0:T(8,128)(2,1)S(1)} %get-tuple-element.133), channel_id=1, source_target_pairs={{0,8},{8,0},{16,24},{24,16},{1,9},{9,1},{17,25},{25,17},{2,10},{10... | collective-permute-start | bytes 1572872 | tf_op jit(solution)/shard_map/ppermute | solution.py:41
  637.2 76.5 %collective-permute-start.31 = (bf16[512,2048]{1,0:T(8,128)(2,1)}, bf16[512,2048]{1,0:T(8,128)(2,1)}, u32[]{:S(2)}, u32[]{:S(2)}) collective-permute-start(bf16[512,2048]{1,0:T(8,128)(2,1)} %pad_maximum_fusion.8), channel_id=1, source_target_pairs={{0,1},{1,0},{2,3},{3,2},{4,5},{5,4},{6,7},{7,6},{8,9},{9,8},{10,11... | collective-permute-start | bytes 6291464 | tf_op jit(solution)/shard_map/ppermute | solution.py:32
  663.7 41.9 %collective-permute-start.52 = (bf16[128,2048]{1,0:T(8,128)(2,1)}, bf16[128,2048]{1,0:T(8,128)(2,1)}, u32[]{:S(2)}, u32[]{:S(2)}) collective-permute-start(bf16[128,2048]{1,0:T(8,128)(2,1)} %get-tuple-element.132), channel_id=1, source_target_pairs={{0,16},{8,24},{16,0},{24,8},{1,17},{9,25},{17,1},{25,9},{2,18},{10... | collective-permute-start | bytes 1572872 | tf_op jit(solution)/shard_map/ppermute | solution.py:41
  666.6 50.6 %collective-permute-start.35 = (bf16[2,2,4,512,128]{4,3,2,1,0:T(8,128)(2,1)}, bf16[2,2,4,512,128]{4,3,2,1,0:T(8,128)(2,1)}, u32[]{:S(2)}, u32[]{:S(2)}) collective-permute-start(bf16[2,2,4,512,128]{4,3,2,1,0:T(8,128)(2,1)} %slice.410), channel_id=1, source_target_pairs={{0,1},{1,0},{2,3},{3,2},{4,5},{5,4},{6,7},{7,6},{8,9},{9,8},{10,11... | collective-permute-start | bytes 6291464 | tf_op jit(solution)/shard_map/ppermute | solution.py:32
  715.1 38.6 %collective-permute-start.32 = (bf16[128,2048]{1,0:T(8,128)(2,1)S(1)}, bf16[128,2048]{1,0:T(8,128)(2,1)S(1)}, u32[]{:S(2)}, u32[]{:S(2)}) collective-permute-start(bf16[128,2048]{1,0:T(8,128)(2,1)S(1)} %add_convert_fusion.31), channel_id=1, source_target_pairs={{0,2},{1,3},{2,4},{3,5},{4,6},{5,7},{6,0},{7,1},{8,10},{9,11},{10,... | collective-permute-start | bytes 1572872 | tf_op jit(solution)/shard_map/ppermute | solution.py:37
  718.4 38.1 %collective-permute-start.36 = (bf16[2,2,4,128,128]{4,3,2,1,0:T(8,128)(2,1)S(1)}, bf16[2,2,4,128,128]{4,3,2,1,0:T(8,128)(2,1)S(1)}, u32[]{:S(2)}, u32[]{:S(2)}) collective-permute-start(bf16[2,2,4,128,128]{4,3,2,1,0:T(8,128)(2,1)S(1)} %add_convert_fusion.25), channel_id=1, source_target_pairs={{0,2},{1,3},{2,4},{3,5},{4,6},{5,7},{6,0},{7,1},{8,10},{9,11},{10,... | collective-permute-start | bytes 1572872 | tf_op jit(solution)/shard_map/ppermute | solution.py:37
  721.3 37.9 %collective-permute-start.46 = (bf16[128,2048]{1,0:T(8,128)(2,1)S(1)}, bf16[128,2048]{1,0:T(8,128)(2,1)S(1)}, u32[]{:S(2)}, u32[]{:S(2)}) collective-permute-start(bf16[128,2048]{1,0:T(8,128)(2,1)S(1)} %get-tuple-element.138), channel_id=1, source_target_pairs={{0,8},{8,0},{16,24},{24,16},{1,9},{9,1},{17,25},{25,17},{2,10},{10... | collective-permute-start | bytes 1572872 | tf_op jit(solution)/shard_map/ppermute | solution.py:41
  774.0 32.4 %collective-permute-start.34 = (bf16[128,2048]{1,0:T(8,128)(2,1)}, bf16[128,2048]{1,0:T(8,128)(2,1)}, u32[]{:S(2)}, u32[]{:S(2)}) collective-permute-start(bf16[128,2048]{1,0:T(8,128)(2,1)} %add_convert_fusion.27), channel_id=1, source_target_pairs={{0,2},{1,3},{2,4},{3,5},{4,6},{5,7},{6,0},{7,1},{8,10},{9,11},{10,... | collective-permute-start | bytes 1572872 | tf_op jit(solution)/shard_map/ppermute | solution.py:37
  (138 other events, 1844.4 us)
Sparse Core Ops, SparseCore 0:
  106.8 45.1 all-gather.4
  166.7 45.1 all-gather.6
  233.7 45.3 all-gather.8
  280.5 45.8 all-gather.10
  328.6 48.7 reduce-scatter.4
  379.5 48.1 reduce-scatter.2
  451.9 253.5 all-reduce.2

commit v12 on v11

--- a/solution.py
+++ b/solution.py
@@ -397,7 +397,6 @@
     query_part, grad_scores = lax.optimization_barrier((query_part, grad_scores))
     output_sum = main.result("output")
     main.add("query", scatter_rows(query_part))
-    main.step()
     sent = main.step()
     grad_keys = heads_dot("rjqk,rjqd->rjkd", grad_scores, query_heads) * scale
     grad_values = heads_dot("rjqk,rjqd->rjkd", probs.astype(BF16), grad_heads)
@@ -408,7 +407,8 @@
     def positions_of(value, j):
         return value[:, :, :, j * seg_len : (j + 1) * seg_len]
 
-    fill.add(
+    cache_lane, last_lane = Lane(), Lane()
+    cache_lane.add(
         "cache",
         scatter_halves(
             lambda j: positions_of(cache_part, j), cache_part[:, :, :, half_len:], positions_of, chips
@@ -416,7 +416,8 @@
     )
     fill.result(("ffn", 0))
     for r in range(1, rows_here):
-        fill.add(("ffn", r), scatter_tokens(tie(ffn_part[r], sent), chips, place, core))
+        last_lane.add(("ffn", r), scatter_tokens(tie(ffn_part[r], sent), chips, place, core))
+    last_sent = [[lane.step() for _ in range(chips - 1)] for lane in (cache_lane, last_lane)]
 
     grad_normed_one = query_proj.back(query_term)
     scaled_one = inputs * inverse_one
@@ -424,18 +425,18 @@
     input_grad = grad_middle + norm_back(grad_normed_one, scaled_one, inverse_one, gain_one)
     gain_grad = jnp.stack([gain_one_grad, gain_two_grad])
 
-    layer_out = [
-        (live[r] * (middle[r] + fill.result(("ffn", r)))).astype(BF16) for r in range(rows_here)
-    ]
-    cache_grad = fill.result("cache")
+    ffn_out = [fill.result(("ffn", 0))]
+    ffn_out += [last_lane.result(("ffn", r)) for r in range(1, rows_here)]
+    layer_out = [(live[r] * (middle[r] + ffn_out[r])).astype(BF16) for r in range(rows_here)]
+    cache_grad = cache_lane.result("cache")
     cache_grad = cache_grad.transpose(1, 3, 0, 2, 4).reshape(rows_here, seg_len, 2, KV * HEAD)
-    summed, query_sum = lax.optimization_barrier((summed, main.result("query").astype(BF16)))
+    summed = tie(summed, [sent[-1] for sent in last_sent])
     summed, gain_grad = lax.optimization_barrier((summed, gain_grad))
     in_grad, down_grad = summed
     in_grad = in_grad.reshape(2, units, width).transpose(1, 0, 2)
     in_grad = lax.optimization_barrier(in_grad)
     gain_grad = sum_all(gain_grad, rows, seq)
-    output_grad, query_grad = sum_rows((output_sum, query_sum), rows)
+    output_grad, query_grad = sum_rows((output_sum, main.result("query")), rows)
     return (
         jnp.stack(layer_out),
         input_grad.reshape(rows_here, seg_len, width),

time: 828 us -> 829 us (level)
    ppermute x18, waiting for transfers between devices: 23.5 us -> 40.7 us  [swap_row(): return lax.ppermute(value, 'rows', [(r, r ^ mask) for r in range(rows)])]
    psum x1, waiting for transfers between devices: 16.5 us -> 0.01 us  [local(): summed = lax.psum(parts, 'rows')]
    unnamed x240 -> x246, local copies, waits for them, and re-layouts: 37.3 us -> 36.8 us
where the time goes in v12:
time: 829 us; the launch traced here: 818 us
  waiting for transfers between devices  259 us (31%)
  matrix products  224 us (27%)
  local copies, waits for them, and re-layouts  158 us (19%)
  other arithmetic  127 us (15%)
  starting transfers between devices  33.3 us (4%)
  between operations  16.5 us (2%)
    ppermute x24, waiting for transfers between devices, ring(): return lax.ppermute(value, 'seq', pairs)  174 us
    dot_general x24, matrix products, dot(): lax.dot_general(left, right, (dims, ((), ())), preferred_element_type=F32)  158 us
    dot_general x6, matrix products, heads_dot(): return jnp.einsum(spec, left, right, preferred_element_type=F32)  42.8 us
    ppermute x18, waiting for transfers between devices, swap_row(): return lax.ppermute(value, 'rows', [(r, r ^ mask) for r in range(rows)])  40.7 us
    unnamed x246, local copies, waits for them, and re-layouts  36.8 us
    all_gather x2, waiting for transfers between devices, local(): lax.all_gather(n, 'seq', axis=0, tiled=True)  29.7 us
    ppermute x18, starting transfers between devices, swap_row(): return lax.ppermute(value, 'rows', [(r, r ^ mask) for r in range(rows)])  21.1 us
    convert_element_type x10, other arithmetic, ring_scatter(): sent = total.astype(BF16)  18.6 us
  transfers between devices with their start and end apart: 62, of which 28 were waited for; matrix products, arithmetic and copies ran while one was open for 59% of the time, Pallas kernels for 0%

profile of v12, /device:TPU:0, one launch (start us, length us, event | category | flops | bytes accessed | tf_op | source)
XLA Modules:
  0.0 818.1 jit_solution(18142032527977736116)
XLA Ops:
  121.1 10.1 %collective-permute-done.5 = bf16[2,3,256,256]{3,2,1,0:T(8,128)(2,1)S(1)} collective-permute-done((bf16[2,3,256,256]{3,2,1,0:T(8,128)(2,1)S(1)}, bf16[2,3,256,256]{3,2,1,0:T(8,128)(2,1)S(1)}, u32[]{:S(2)}, u32[]{:S(2)}) %collective-permute-start.5) | collective-permute-done | bytes 786464 | tf_op jit(solution)/shard_map/ppermute | solution.py:41
  214.6 11.1 %copy.57 = f32[2,2,2,256,256]{4,3,2,1,0:T(8,128)S(1)} copy(f32[2,2,2,256,256]{3,4,2,1,0:T(8,128)} %bitcast.378) | data formatting | bytes 4194304 | tf_op jit(solution)/shard_map/reshape;reshape | solution.py:94
  234.1 16.5 %fusion.99 = (bf16[1024,1,2048]{2,1,0:T(2,128)(2,1)S(1)}, bf16[1024,1,2048]{2,1,0:T(2,128)(2,1)S(1)}) fusion(bf16[1024,2,2048]{2,1,0:T(2,128)(2,1)} %param.15), kind=kLoop, calls=%fused_computation.326 | loop fusion | bytes 16777216 | tf_op jit(solution)/shard_map/slice | solution.py:260
  258.4 20.6 %all-gather.9.cloned.1.call-done = bf16[1024,2048]{1,0:T(8,128)(2,1)} async-done(((bf16[128,2048]{1,0:T(8,128)(2,1)}), bf16[1024,2048]{1,0:T(8,128)(2,1)}) %all-gather.9.cloned.1.call-update) | async-done | bytes 4194320 | tf_op jit(solution)/shard_map/all_gather | solution.py:330
  279.0 15.3 %fusion.98 = f32[1024,2048]{1,0:T(8,128)} fusion(bf16[1024,2048]{1,0:T(8,128)(2,1)} %all-gather.9.cloned.1.call-done, bf16[1024,2048]{1,0:T(8,128)(2,1)} %get-tuple-element.186, bf16[1024,2048]{1,0:T(8,128)(2,1)} %get-tuple-element.187), kind=kOutput, calls=%fused_computation.325 | convolution fusion | flops 8606711808 | bytes 20971520 | tf_op jit(solution)/shard_map/dot_general | solution.py:17
  294.2 10.2 %multiply_convert_fusion.6 = (bf16[1024,1024]{1,0:T(8,128)(2,1)S(1)}, bf16[1024,1024]{1,0:T(8,128)(2,1)}, bf16[1024,1024]{1,0:T(8,128)(2,1)}) fusion(f32[1024,2048]{1,0:T(8,128)} %fusion.98, bf16[1024,2048]{1,0:T(8,128)(2,1)S(1)} %copy-done.92, bf16[1024,2048]{1,0:T(8,128)(2,1)S(1)} %copy-done.89), kind=kOutput, calls=%fused_computation.42 | convolution fusion | flops 4311744512 | bytes 23068672 | tf_op jit(solution)/shard_map/dot_general | solution.py:17
  304.5 12.7 %convolution_convert_fusion.5 = bf16[1024,2048]{1,0:T(8,128)(2,1)} fusion(bf16[1024,1024]{1,0:T(8,128)(2,1)} %get-tuple-element.107, bf16[1024,1024]{1,0:T(8,128)(2,1)S(1)} %get-tuple-element.106, bf16[1024,2048]{1,0:T(8,128)(2,1)S(1)} %copy-done.40, bf16[1024,2048]{1,0:T(8,128)(2,1)S(1)} %copy-done.42), kind=kOutput, calls=%fused_computation.50 | convolution fusion | flops 8617197568 | bytes 16777216 | tf_op jit(solution)/shard_map/dot_general | solution.py:17
  326.4 15.3 %fusion.97 = f32[1024,2048]{1,0:T(8,128)} fusion(bf16[1024,2048]{1,0:T(8,128)(2,1)} %all-gather.11.cloned.1.call-done, bf16[1024,2048]{1,0:T(8,128)(2,1)} %get-tuple-element.186, bf16[1024,2048]{1,0:T(8,128)(2,1)} %get-tuple-element.187), kind=kOutput, calls=%fused_computation.324 | convolution fusion | flops 8606711808 | bytes 20971520 | tf_op jit(solution)/shard_map/dot_general | solution.py:17
  341.7 11.1 %multiply_convert_fusion.4 = (bf16[1024,1024]{1,0:T(8,128)(2,1)S(1)}, bf16[1024,1024]{1,0:T(8,128)(2,1)S(1)}, bf16[1024,1024]{1,0:T(8,128)(2,1)}) fusion(f32[1024,2048]{1,0:T(8,128)} %fusion.97, bf16[1024,2048]{1,0:T(8,128)(2,1)} %all-gather.7.cloned.1.call-done, bf16[1024,2048]{1,0:T(8,128)(2,1)S(1)} %copy-done.90), kind=kOutput, calls=%fused_computation.39 | convolution fusion | flops 4311744512 | bytes 23068672 | tf_op jit(solution)/shard_map/dot_general | solution.py:17
  354.1 10.5 %convolution_convert_fusion.4 = bf16[1024,2048]{1,0:T(8,128)(2,1)} fusion(bf16[1024,2048]{1,0:T(8,128)(2,1)S(1)} %copy-done.41, bf16[1024,2048]{1,0:T(8,128)(2,1)S(1)} %copy-done.43, bf16[1024,1024]{1,0:T(8,128)(2,1)S(1)} %get-tuple-element.105, bf16[1024,1024]{1,0:T(8,128)(2,1)S(1)} %get-tuple-element.104), kind=kOutput, calls=%fused_computation.49 | convolution fusion | flops 8617197568 | bytes 16777216 | tf_op jit(solution)/shard_map/dot_general | solution.py:17
  378.7 12.2 %fusion.21 = f32[2048,2048]{1,0:T(8,128)} fusion(bf16[1024,2048]{1,0:T(8,128)(2,1)S(1)} %copy-done.95, bf16[1024,1024]{1,0:T(8,128)(2,1)S(1)} %copy-done.102, bf16[1024,1024]{1,0:T(8,128)(2,1)S(1)} %copy-done.101), kind=kOutput, calls=%fused_computation.62 | convolution fusion | flops 8598323200 | bytes 25165824 | tf_op jit(solution)/shard_map/dot_general | solution.py:17
  390.9 9.9 %add_convert_fusion.1 = bf16[1024,2048]{1,0:T(8,128)(2,1)} fusion(f32[1024,2048]{1,0:T(8,128)} %fusion.109, bf16[1024,1024]{1,0:T(8,128)(2,1)S(1)} %copy-done.98, bf16[1024,2048]{1,0:T(8,128)(2,1)} %all-gather.7.cloned.1.call-done), kind=kOutput, calls=%fused_computation.21 | convolution fusion | flops 4299161600 | bytes 18874368 | tf_op jit(solution)/shard_map/dot_general | solution.py:17
  400.8 15.1 %add_convert_fusion = bf16[2048,2048]{1,0:T(8,128)(2,1)} fusion(f32[2048,2048]{1,0:T(8,128)} %fusion.21, bf16[1024,2048]{1,0:T(8,128)(2,1)S(1)} %copy-done.37, bf16[1024,2048]{1,0:T(8,128)(2,1)S(1)} %copy-done.94), kind=kOutput, calls=%fused_computation.2 | convolution fusion | flops 8598323200 | bytes 33554432 | tf_op jit(solution)/shard_map/dot_general | solution.py:17
  415.9 11.6 %reduce-scatter.3.cloned.1.call-done = bf16[128,2048]{1,0:T(8,128)(2,1)} async-done(((bf16[1024,2048]{1,0:T(8,128)(2,1)}), bf16[128,2048]{1,0:T(8,128)(2,1)}) %reduce-scatter.3.cloned.1.call-update) | async-done | bytes 524304 | tf_op jit(solution)/shard_map/reduce_scatter | solution.py:347
  499.0 14.9 %collective-permute-done.25 = bf16[256,2048]{1,0:T(8,128)(2,1)} collective-permute-done((bf16[256,2048]{1,0:T(8,128)(2,1)}, bf16[256,2048]{1,0:T(8,128)(2,1)}, u32[]{:S(2)}, u32[]{:S(2)}) %collective-permute-start.25) | collective-permute-done | bytes 1048608 | tf_op jit(solution)/shard_map/ppermute | solution.py:37
  519.4 11.2 %multiply_convert_fusion = bf16[2,4,512,1024]{3,2,1,0:T(8,128)(2,1)} fusion(f32[2,4,512,1024]{3,2,1,0:T(8,128)} %copy-done, f32[2,4,512]{2,1,0:T(4,128)S(1)} %multiply_reduce_fusion.2, f32[2,4,512]{2,1,0:T(4,128)S(1)} %fusion.83, pred[2,512,1024]{2,1,0:T(8,128)(4,1)S(1)} %copy-done.12, bf16[2,4,512,128]{3,2,1,0:T(8,128)(2,1)} %bitcast.380, ...), kind=kOutput, calls=%fused_computation | convolution fusion | flops 1098907648 | bytes 29392896 | tf_op jit(solution)/shard_map/rjqd,rjkd->rjqk/dot_general | solution.py:297
  530.6 11.4 %convert_bitcast_fusion = bf16[1,2,4,1024,128]{4,3,2,1,0:T(8,128)(2,1)} fusion(bf16[2,4,512,128]{3,2,1,0:T(8,128)(2,1)} %bitcast.381, f32[2,4,512,1024]{3,2,1,0:T(8,128)} %copy-done, f32[2,4,512]{2,1,0:T(4,128)S(1)} %fusion.83, pred[2,512,1024]{2,1,0:T(8,128)(4,1)S(1)} %copy-done.12), kind=kOutput, calls=%fused_computation.81 | convolution fusion | flops 1091567616 | bytes 20987904 | tf_op jit(solution)/shard_map/rjqk,rjqd->rjkd/dot_general | solution.py:297
  616.1 21.9 %collective-permute-done.43 = bf16[256,2048]{1,0:T(8,128)(2,1)S(1)} collective-permute-done((bf16[256,2048]{1,0:T(8,128)(2,1)S(1)}, bf16[256,2048]{1,0:T(8,128)(2,1)S(1)}, u32[]{:S(2)}, u32[]{:S(2)}) %collective-permute-start.43) | collective-permute-done | bytes 1048608 | tf_op jit(solution)/shard_map/ppermute | solution.py:37
  646.1 17.5 %collective-permute-done.53 = bf16[128,2048]{1,0:T(8,128)(2,1)S(1)} collective-permute-done((bf16[128,2048]{1,0:T(8,128)(2,1)S(1)}, bf16[128,2048]{1,0:T(8,128)(2,1)S(1)}, u32[]{:S(2)}, u32[]{:S(2)}) %collective-permute-start.53) | collective-permute-done | bytes 524320 | tf_op jit(solution)/shard_map/ppermute | solution.py:41
  665.5 15.0 %collective-permute-done.31 = bf16[128,2048]{1,0:T(8,128)(2,1)S(1)} collective-permute-done((bf16[128,2048]{1,0:T(8,128)(2,1)S(1)}, bf16[128,2048]{1,0:T(8,128)(2,1)S(1)}, u32[]{:S(2)}, u32[]{:S(2)}) %collective-permute-start.31) | collective-permute-done | bytes 524320 | tf_op jit(solution)/shard_map/ppermute | solution.py:37
  693.8 21.7 %collective-permute-done.36 = bf16[2,2,4,128,128]{4,3,2,1,0:T(8,128)(2,1)S(1)} collective-permute-done((bf16[2,2,4,128,128]{4,3,2,1,0:T(8,128)(2,1)S(1)}, bf16[2,2,4,128,128]{4,3,2,1,0:T(8,128)(2,1)S(1)}, u32[]{:S(2)}, u32[]{:S(2)}) %collective-permute-start.36) | collective-permute-done | bytes 524320 | tf_op jit(solution)/shard_map/ppermute | solution.py:37
  720.3 20.6 %collective-permute-done.45 = bf16[256,2048]{1,0:T(8,128)(2,1)} collective-permute-done((bf16[256,2048]{1,0:T(8,128)(2,1)}, bf16[256,2048]{1,0:T(8,128)(2,1)}, u32[]{:S(2)}, u32[]{:S(2)}) %collective-permute-start.45) | collective-permute-done | bytes 1048608 | tf_op jit(solution)/shard_map/ppermute | solution.py:37
  758.0 17.2 %copy.98 = bf16[2,1024,2048]{2,0,1:T(2,128)(2,1)S(1)} copy(bf16[2,1024,2048]{2,1,0:T(8,128)(2,1)S(1)} %bitcast.376) | data formatting | bytes 16777216 | tf_op jit(solution)/shard_map/reshape | solution.py:436
  775.2 10.8 %convert_element_type.688 = f32[1024,2,2048]{2,1,0:T(2,128)} convert(bf16[1024,2,2048]{2,1,0:T(2,128)(2,1)S(1)} %bitcast.351) | non-fusion elementwise | flops 4194304 | bytes 25165824 | tf_op jit(solution)/shard_map/convert_element_type | solution.py:447
  (543 shorter events, 457.0 us)
Async XLA Ops:
  7.2 201.9 %all-gather.5.cloned.1.call-start = ((), (), s32[]{:S(2)}) async-start(), calls=%async_computation.2 | async-start | bytes 4718592 | tf_op jit(solution)/shard_map/all_gather | solution.py:269
  7.2 105.6 %collective-permute-start.7 = (bf16[256,2048]{1,0:T(8,128)(2,1)}, bf16[256,2048]{1,0:T(8,128)(2,1)}, u32[]{:S(2)}, u32[]{:S(2)}) collective-permute-start(bf16[256,2048]{1,0:T(8,128)(2,1)} %param.13), channel_id=1, source_target_pairs={{0,1},{1,0},{2,3},{3,2},{4,5},{5,4},{6,7},{7,6},{8,9},{9,8},{10,11... | collective-permute-start | bytes 3145736 | tf_op jit(solution)/shard_map/ppermute | solution.py:32
  12.1 216.6 %collective-permute-start.20 = (bf16[256,2048]{1,0:T(8,128)(2,1)}, bf16[256,2048]{1,0:T(8,128)(2,1)}, u32[]{:S(2)}, u32[]{:S(2)}) collective-permute-start(bf16[256,2048]{1,0:T(8,128)(2,1)} %param.14), channel_id=1, source_target_pairs={{0,1},{1,0},{2,3},{3,2},{4,5},{5,4},{6,7},{7,6},{8,9},{9,8},{10,11... | collective-permute-start | bytes 3145736 | tf_op jit(solution)/shard_map/ppermute | solution.py:32
  106.7 125.7 %all-gather.7.cloned.1.call-start = ((), (), s32[]{:S(2)}) async-start(), calls=%async_computation.3 | async-start | bytes 4718592 | tf_op jit(solution)/shard_map/all_gather | solution.py:269
  166.5 42.7 %collective-permute-start.21 = (bf16[8,768,256]{1,2,0:T(8,128)(2,1)}, bf16[8,768,256]{1,2,0:T(8,128)(2,1)}, u32[]{:S(2)}, u32[]{:S(2)}) collective-permute-start(bf16[8,768,256]{1,2,0:T(8,128)(2,1)} %copy.56), channel_id=1, source_target_pairs={{0,1},{1,0},{2,3},{3,2},{4,5},{5,4},{6,7},{7,6},{8,9},{9,8},{10,11... | collective-permute-start | bytes 9437192 | tf_op jit(solution)/shard_map/ppermute | solution.py:32
  166.5 112.5 %all-gather.9.cloned.1.call-start = ((), (), s32[]{:S(2)}) async-start(), calls=%async_computation.4 | async-start | bytes 4718592 | tf_op jit(solution)/shard_map/all_gather | solution.py:330
  233.5 92.8 %all-gather.11.cloned.1.call-start = ((), (), s32[]{:S(2)}) async-start(), calls=%async_computation.5 | async-start | bytes 4718592 | tf_op jit(solution)/shard_map/all_gather | solution.py:330
  234.1 156.8 %reduce-scatter.5.cloned.1.call-start = ((), (), s32[]{:S(2)}) async-start(), calls=%async_computation.7 | async-start | bytes 4718592 | tf_op jit(solution)/shard_map/reduce_scatter | solution.py:347
  326.3 101.2 %reduce-scatter.3.cloned.1.call-start = ((), (), s32[]{:S(2)}) async-start(), calls=%async_computation.6 | async-start | bytes 4718592 | tf_op jit(solution)/shard_map/reduce_scatter | solution.py:347
  364.7 354.3 %all-reduce.3.cloned.1.call-start = ((), (), s32[]{:S(2)}) async-start(), calls=%async_computation.8 | async-start | bytes 25165824 | tf_op jit(solution)/shard_map/psum | solution.py:361
  436.3 39.5 %collective-permute-start.24 = (bf16[1024,2048]{1,0:T(8,128)(2,1)}, bf16[1024,2048]{1,0:T(8,128)(2,1)}, u32[]{:S(2)}, u32[]{:S(2)}) collective-permute-start(bf16[1024,2048]{1,0:T(8,128)(2,1)} %convolution_convert_fusion.3), channel_id=1, source_target_pairs={{0,1},{1,0},{2,3},{3,2},{4,5},{5,4},{6,7},{7,6},{8,9},{9,8},{10,11... | collective-permute-start | bytes 12582920 | tf_op jit(solution)/shard_map/ppermute | solution.py:32
  475.4 41.3 %collective-permute-start.23 = (bf16[128,2048]{1,0:T(8,128)(2,1)}, bf16[128,2048]{1,0:T(8,128)(2,1)}, u32[]{:S(2)}, u32[]{:S(2)}) collective-permute-start(bf16[128,2048]{1,0:T(8,128)(2,1)} %get-tuple-element.117), channel_id=1, source_target_pairs={{0,2},{1,3},{2,4},{3,5},{4,6},{5,7},{6,0},{7,1},{8,10},{9,11},{10,... | collective-permute-start | bytes 1572872 | tf_op jit(solution)/shard_map/ppermute | solution.py:37
  518.8 35.2 %collective-permute-start.26 = (bf16[128,2048]{1,0:T(8,128)(2,1)}, bf16[128,2048]{1,0:T(8,128)(2,1)}, u32[]{:S(2)}, u32[]{:S(2)}) collective-permute-start(bf16[128,2048]{1,0:T(8,128)(2,1)} %add_convert_fusion.35), channel_id=1, source_target_pairs={{0,2},{1,3},{2,4},{3,5},{4,6},{5,7},{6,0},{7,1},{8,10},{9,11},{10,... | collective-permute-start | bytes 1572872 | tf_op jit(solution)/shard_map/ppermute | solution.py:37
  555.9 238.8 %collective-permute-start.28 = (bf16[128,2048]{1,0:T(8,128)(2,1)}, bf16[128,2048]{1,0:T(8,128)(2,1)}, u32[]{:S(2)}, u32[]{:S(2)}) collective-permute-start(bf16[128,2048]{1,0:T(8,128)(2,1)} %add_convert_fusion.33), channel_id=1, source_target_pairs={{0,2},{1,3},{2,4},{3,5},{4,6},{5,7},{6,0},{7,1},{8,10},{9,11},{10,... | collective-permute-start | bytes 1572872 | tf_op jit(solution)/shard_map/ppermute | solution.py:37
  555.9 55.5 %collective-permute-start.50 = (bf16[256,2048]{1,0:T(8,128)(2,1)}, bf16[256,2048]{1,0:T(8,128)(2,1)}, u32[]{:S(2)}, u32[]{:S(2)}) collective-permute-start(bf16[256,2048]{1,0:T(8,128)(2,1)} %add_convert_fusion.11), channel_id=1, source_target_pairs={{0,2},{1,3},{2,4},{3,5},{4,6},{5,7},{6,0},{7,1},{8,10},{9,11},{10,... | collective-permute-start | bytes 3145736 | tf_op jit(solution)/shard_map/ppermute | solution.py:37
  641.3 49.1 %collective-permute-start.44 = (bf16[256,2048]{1,0:T(8,128)(2,1)S(1)}, bf16[256,2048]{1,0:T(8,128)(2,1)S(1)}, u32[]{:S(2)}, u32[]{:S(2)}) collective-permute-start(bf16[256,2048]{1,0:T(8,128)(2,1)S(1)} %add_convert_fusion.8), channel_id=1, source_target_pairs={{0,2},{1,3},{2,4},{3,5},{4,6},{5,7},{6,0},{7,1},{8,10},{9,11},{10,... | collective-permute-start | bytes 3145736 | tf_op jit(solution)/shard_map/ppermute | solution.py:37
  643.0 37.5 %collective-permute-start.31 = (bf16[128,2048]{1,0:T(8,128)(2,1)S(1)}, bf16[128,2048]{1,0:T(8,128)(2,1)S(1)}, u32[]{:S(2)}, u32[]{:S(2)}) collective-permute-start(bf16[128,2048]{1,0:T(8,128)(2,1)S(1)} %add_convert_fusion.31), channel_id=1, source_target_pairs={{0,2},{1,3},{2,4},{3,5},{4,6},{5,7},{6,0},{7,1},{8,10},{9,11},{10,... | collective-permute-start | bytes 1572872 | tf_op jit(solution)/shard_map/ppermute | solution.py:37
  645.4 44.8 %collective-permute-start.35 = (bf16[2,2,4,128,128]{4,3,2,1,0:T(8,128)(2,1)S(1)}, bf16[2,2,4,128,128]{4,3,2,1,0:T(8,128)(2,1)S(1)}, u32[]{:S(2)}, u32[]{:S(2)}) collective-permute-start(bf16[2,2,4,128,128]{4,3,2,1,0:T(8,128)(2,1)S(1)} %add_convert_fusion.25), channel_id=1, source_target_pairs={{0,2},{1,3},{2,4},{3,5},{4,6},{5,7},{6,0},{7,1},{8,10},{9,11},{10,... | collective-permute-start | bytes 1572872 | tf_op jit(solution)/shard_map/ppermute | solution.py:37
  664.0 55.0 %collective-permute-start.54 = (bf16[128,2048]{1,0:T(8,128)(2,1)S(1)}, bf16[128,2048]{1,0:T(8,128)(2,1)}, u32[]{:S(2)}, u32[]{:S(2)}) collective-permute-start(bf16[128,2048]{1,0:T(8,128)(2,1)S(1)} %get-tuple-element.131), channel_id=1, source_target_pairs={{0,8},{8,0},{16,24},{24,16},{1,9},{9,1},{17,25},{25,17},{2,10},{10... | collective-permute-start | bytes 1572872 | tf_op jit(solution)/shard_map/ppermute | solution.py:41
  680.5 68.8 %collective-permute-start.52 = (bf16[128,2048]{1,0:T(8,128)(2,1)S(1)}, bf16[128,2048]{1,0:T(8,128)(2,1)}, u32[]{:S(2)}, u32[]{:S(2)}) collective-permute-start(bf16[128,2048]{1,0:T(8,128)(2,1)S(1)} %get-tuple-element.130), channel_id=1, source_target_pairs={{0,16},{8,24},{16,0},{24,8},{1,17},{9,25},{17,1},{25,9},{2,18},{10... | collective-permute-start | bytes 1572872 | tf_op jit(solution)/shard_map/ppermute | solution.py:41
  743.5 47.6 %collective-permute-start.46 = (bf16[128,2048]{1,0:T(8,128)(2,1)S(1)}, bf16[128,2048]{1,0:T(8,128)(2,1)S(1)}, u32[]{:S(2)}, u32[]{:S(2)}) collective-permute-start(bf16[128,2048]{1,0:T(8,128)(2,1)S(1)} %get-tuple-element.136), channel_id=1, source_target_pairs={{0,8},{8,0},{16,24},{24,16},{1,9},{9,1},{17,25},{25,17},{2,10},{10... | collective-permute-start | bytes 1572872 | tf_op jit(solution)/shard_map/ppermute | solution.py:41
  744.8 46.3 %collective-permute-start.48 = (bf16[128,2048]{1,0:T(8,128)(2,1)S(1)}, bf16[128,2048]{1,0:T(8,128)(2,1)S(1)}, u32[]{:S(2)}, u32[]{:S(2)}) collective-permute-start(bf16[128,2048]{1,0:T(8,128)(2,1)S(1)} %get-tuple-element.137), channel_id=1, source_target_pairs={{0,16},{8,24},{16,0},{24,8},{1,17},{9,25},{17,1},{25,9},{2,18},{10... | collective-permute-start | bytes 1572872 | tf_op jit(solution)/shard_map/ppermute | solution.py:41
  750.5 44.2 %collective-permute-start.33 = (bf16[128,2048]{1,0:T(8,128)(2,1)S(1)}, bf16[128,2048]{1,0:T(8,128)(2,1)S(1)}, u32[]{:S(2)}, u32[]{:S(2)}) collective-permute-start(bf16[128,2048]{1,0:T(8,128)(2,1)S(1)} %copy-done.68), channel_id=1, source_target_pairs={{0,2},{1,3},{2,4},{3,5},{4,6},{5,7},{6,0},{7,1},{8,10},{9,11},{10,... | collective-permute-start | bytes 1572872 | tf_op jit(solution)/shard_map/ppermute | solution.py:37
  755.4 35.1 %collective-permute-start.42 = (f32[2,2048]{1,0:T(2,128)S(1)}, f32[2,2048]{1,0:T(2,128)S(1)}, u32[]{:S(2)}, u32[]{:S(2)}) collective-permute-start(f32[2,2048]{1,0:T(2,128)S(1)} %add.552), channel_id=1, source_target_pairs={{0,16},{8,24},{16,0},{24,8},{1,17},{9,25},{17,1},{25,9},{2,18},{10... | collective-permute-start | bytes 49160 | tf_op jit(solution)/shard_map/ppermute | solution.py:41
  (141 other events, 2118.5 us)
Sparse Core Ops, SparseCore 0:
  106.9 45.2 all-gather.4
  166.6 45.1 all-gather.6
  233.6 45.3 all-gather.8
  280.4 45.8 all-gather.10
  328.4 48.7 reduce-scatter.4
  379.4 48.1 reduce-scatter.2
  451.8 260.8 all-reduce.2

commit v13 on v12

--- a/solution.py
+++ b/solution.py
@@ -430,7 +430,7 @@
     layer_out = [(live[r] * (middle[r] + ffn_out[r])).astype(BF16) for r in range(rows_here)]
     cache_grad = cache_lane.result("cache")
     cache_grad = cache_grad.transpose(1, 3, 0, 2, 4).reshape(rows_here, seg_len, 2, KV * HEAD)
-    summed = tie(summed, [sent[-1] for sent in last_sent])
+    summed = tie(summed, [sent[-2] for sent in last_sent])
     summed, gain_grad = lax.optimization_barrier((summed, gain_grad))
     in_grad, down_grad = summed
     in_grad = in_grad.reshape(2, units, width).transpose(1, 0, 2)

time: 829 us -> 832 us (level)
  starting transfers between devices: 33.3 us -> 44.8 us
  waiting for transfers between devices: 259 us -> 248 us
    ppermute x24, waiting for transfers between devices: 174 us -> 128 us  [ring(): return lax.ppermute(value, 'seq', pairs)]
    psum x1, waiting for transfers between devices: 0.01 us -> 32 us  [local(): summed = lax.psum(parts, 'rows')]
    ppermute x3, waiting for transfers between devices: 2.67 us -> 19.1 us  [sum_all(): lax.ppermute(value, 'seq', [(s, s ^ mask) for s in range(seq)])]
    ppermute x18, waiting for transfers between devices: 40.7 us -> 27.6 us  [swap_row(): return lax.ppermute(value, 'rows', [(r, r ^ mask) for r in range(rows)])]
    unnamed x246 -> x252, local copies, waits for them, and re-layouts: 36.8 us -> 38.8 us
  transfers between devices with their start and end apart: 62 -> 62, of which waited for: 28 -> 29; matrix products, arithmetic and copies ran while one was open for 59% -> 59% of each run, Pallas kernels for 0% -> 0%
where the time goes in v13:
time: 832 us; the launch traced here: 821 us
  waiting for transfers between devices  248 us (30%)
  matrix products  224 us (27%)
  local copies, waits for them, and re-layouts  161 us (19%)
  other arithmetic  126 us (15%)
  starting transfers between devices  44.8 us (5%)
  between operations  16.4 us (2%)
    dot_general x24, matrix products, dot(): lax.dot_general(left, right, (dims, ((), ())), preferred_element_type=F32)  158 us
    ppermute x24, waiting for transfers between devices, ring(): return lax.ppermute(value, 'seq', pairs)  128 us
    dot_general x6, matrix products, heads_dot(): return jnp.einsum(spec, left, right, preferred_element_type=F32)  42.8 us
    unnamed x252, local copies, waits for them, and re-layouts  38.8 us
    psum x1, waiting for transfers between devices, local(): summed = lax.psum(parts, 'rows')  32 us
    all_gather x2, waiting for transfers between devices, local(): lax.all_gather(n, 'seq', axis=0, tiled=True)  29.6 us
    ppermute x18, waiting for transfers between devices, swap_row(): return lax.ppermute(value, 'rows', [(r, r ^ mask) for r in range(rows)])  27.6 us
    ppermute x18, starting transfers between devices, swap_row(): return lax.ppermute(value, 'rows', [(r, r ^ mask) for r in range(rows)])  21.8 us
  transfers between devices with their start and end apart: 62, of which 29 were waited for; matrix products, arithmetic and copies ran while one was open for 59% of the time, Pallas kernels for 0%

profile of v13, /device:TPU:0, one launch (start us, length us, event | category | flops | bytes accessed | tf_op | source)
XLA Modules:
  0.0 821.1 jit_solution(15649757658341497864)
XLA Ops:
  121.1 10.1 %collective-permute-done.5 = bf16[2,3,256,256]{3,2,1,0:T(8,128)(2,1)S(1)} collective-permute-done((bf16[2,3,256,256]{3,2,1,0:T(8,128)(2,1)S(1)}, bf16[2,3,256,256]{3,2,1,0:T(8,128)(2,1)S(1)}, u32[]{:S(2)}, u32[]{:S(2)}) %collective-permute-start.5) | collective-permute-done | bytes 786464 | tf_op jit(solution)/shard_map/ppermute | solution.py:41
  214.5 11.1 %copy.57 = f32[2,2,2,256,256]{4,3,2,1,0:T(8,128)S(1)} copy(f32[2,2,2,256,256]{3,4,2,1,0:T(8,128)} %bitcast.380) | data formatting | bytes 4194304 | tf_op jit(solution)/shard_map/reshape;reshape | solution.py:94
  234.1 16.5 %fusion.99 = (bf16[1024,1,2048]{2,1,0:T(2,128)(2,1)S(1)}, bf16[1024,1,2048]{2,1,0:T(2,128)(2,1)S(1)}) fusion(bf16[1024,2,2048]{2,1,0:T(2,128)(2,1)} %param.15), kind=kLoop, calls=%fused_computation.326 | loop fusion | bytes 16777216 | tf_op jit(solution)/shard_map/slice | solution.py:260
  258.3 20.6 %all-gather.9.cloned.1.call-done = bf16[1024,2048]{1,0:T(8,128)(2,1)} async-done(((bf16[128,2048]{1,0:T(8,128)(2,1)}), bf16[1024,2048]{1,0:T(8,128)(2,1)}) %all-gather.9.cloned.1.call-update) | async-done | bytes 4194320 | tf_op jit(solution)/shard_map/all_gather | solution.py:330
  278.9 15.3 %fusion.98 = f32[1024,2048]{1,0:T(8,128)} fusion(bf16[1024,2048]{1,0:T(8,128)(2,1)} %all-gather.9.cloned.1.call-done, bf16[1024,2048]{1,0:T(8,128)(2,1)} %get-tuple-element.186, bf16[1024,2048]{1,0:T(8,128)(2,1)} %get-tuple-element.187), kind=kOutput, calls=%fused_computation.325 | convolution fusion | flops 8606711808 | bytes 20971520 | tf_op jit(solution)/shard_map/dot_general | solution.py:17
  294.2 10.2 %multiply_convert_fusion.6 = (bf16[1024,1024]{1,0:T(8,128)(2,1)S(1)}, bf16[1024,1024]{1,0:T(8,128)(2,1)}, bf16[1024,1024]{1,0:T(8,128)(2,1)}) fusion(f32[1024,2048]{1,0:T(8,128)} %fusion.98, bf16[1024,2048]{1,0:T(8,128)(2,1)S(1)} %copy-done.93, bf16[1024,2048]{1,0:T(8,128)(2,1)S(1)} %copy-done.90), kind=kOutput, calls=%fused_computation.42 | convolution fusion | flops 4311744512 | bytes 23068672 | tf_op jit(solution)/shard_map/dot_general | solution.py:17
  304.4 12.8 %convolution_convert_fusion.5 = bf16[1024,2048]{1,0:T(8,128)(2,1)} fusion(bf16[1024,1024]{1,0:T(8,128)(2,1)} %get-tuple-element.107, bf16[1024,1024]{1,0:T(8,128)(2,1)S(1)} %get-tuple-element.106, bf16[1024,2048]{1,0:T(8,128)(2,1)S(1)} %copy-done.39, bf16[1024,2048]{1,0:T(8,128)(2,1)S(1)} %copy-done.41), kind=kOutput, calls=%fused_computation.50 | convolution fusion | flops 8617197568 | bytes 16777216 | tf_op jit(solution)/shard_map/dot_general | solution.py:17
  317.2 9.1 %all-gather.11.cloned.1.call-done = bf16[1024,2048]{1,0:T(8,128)(2,1)} async-done(((bf16[128,2048]{1,0:T(8,128)(2,1)}), bf16[1024,2048]{1,0:T(8,128)(2,1)}) %all-gather.11.cloned.1.call-update) | async-done | bytes 4194320 | tf_op jit(solution)/shard_map/all_gather | solution.py:330
  326.3 15.3 %fusion.97 = f32[1024,2048]{1,0:T(8,128)} fusion(bf16[1024,2048]{1,0:T(8,128)(2,1)} %all-gather.11.cloned.1.call-done, bf16[1024,2048]{1,0:T(8,128)(2,1)} %get-tuple-element.186, bf16[1024,2048]{1,0:T(8,128)(2,1)} %get-tuple-element.187), kind=kOutput, calls=%fused_computation.324 | convolution fusion | flops 8606711808 | bytes 20971520 | tf_op jit(solution)/shard_map/dot_general | solution.py:17
  341.6 11.1 %multiply_convert_fusion.4 = (bf16[1024,1024]{1,0:T(8,128)(2,1)S(1)}, bf16[1024,1024]{1,0:T(8,128)(2,1)S(1)}, bf16[1024,1024]{1,0:T(8,128)(2,1)}) fusion(f32[1024,2048]{1,0:T(8,128)} %fusion.97, bf16[1024,2048]{1,0:T(8,128)(2,1)} %all-gather.7.cloned.1.call-done, bf16[1024,2048]{1,0:T(8,128)(2,1)S(1)} %copy-done.91), kind=kOutput, calls=%fused_computation.39 | convolution fusion | flops 4311744512 | bytes 23068672 | tf_op jit(solution)/shard_map/dot_general | solution.py:17
  354.1 10.5 %convolution_convert_fusion.4 = bf16[1024,2048]{1,0:T(8,128)(2,1)} fusion(bf16[1024,2048]{1,0:T(8,128)(2,1)S(1)} %copy-done.40, bf16[1024,2048]{1,0:T(8,128)(2,1)S(1)} %copy-done.42, bf16[1024,1024]{1,0:T(8,128)(2,1)S(1)} %get-tuple-element.105, bf16[1024,1024]{1,0:T(8,128)(2,1)S(1)} %get-tuple-element.104), kind=kOutput, calls=%fused_computation.49 | convolution fusion | flops 8617197568 | bytes 16777216 | tf_op jit(solution)/shard_map/dot_general | solution.py:17
  378.5 12.2 %fusion.21 = f32[2048,2048]{1,0:T(8,128)} fusion(bf16[1024,2048]{1,0:T(8,128)(2,1)S(1)} %copy-done.96, bf16[1024,1024]{1,0:T(8,128)(2,1)S(1)} %copy-done.103, bf16[1024,1024]{1,0:T(8,128)(2,1)S(1)} %copy-done.102), kind=kOutput, calls=%fused_computation.62 | convolution fusion | flops 8598323200 | bytes 25165824 | tf_op jit(solution)/shard_map/dot_general | solution.py:17
  390.8 9.8 %add_convert_fusion.1 = bf16[1024,2048]{1,0:T(8,128)(2,1)} fusion(f32[1024,2048]{1,0:T(8,128)} %fusion.109, bf16[1024,1024]{1,0:T(8,128)(2,1)S(1)} %copy-done.99, bf16[1024,2048]{1,0:T(8,128)(2,1)} %all-gather.7.cloned.1.call-done), kind=kOutput, calls=%fused_computation.21 | convolution fusion | flops 4299161600 | bytes 18874368 | tf_op jit(solution)/shard_map/dot_general | solution.py:17
  400.6 15.1 %add_convert_fusion = bf16[2048,2048]{1,0:T(8,128)(2,1)} fusion(f32[2048,2048]{1,0:T(8,128)} %fusion.21, bf16[1024,2048]{1,0:T(8,128)(2,1)S(1)} %copy-done.36, bf16[1024,2048]{1,0:T(8,128)(2,1)S(1)} %copy-done.95), kind=kOutput, calls=%fused_computation.2 | convolution fusion | flops 8598323200 | bytes 33554432 | tf_op jit(solution)/shard_map/dot_general | solution.py:17
  415.7 11.8 %reduce-scatter.3.cloned.1.call-done = bf16[128,2048]{1,0:T(8,128)(2,1)} async-done(((bf16[1024,2048]{1,0:T(8,128)(2,1)}), bf16[128,2048]{1,0:T(8,128)(2,1)}) %reduce-scatter.3.cloned.1.call-update) | async-done | bytes 524304 | tf_op jit(solution)/shard_map/reduce_scatter | solution.py:347
  499.0 14.9 %collective-permute-done.25 = bf16[256,2048]{1,0:T(8,128)(2,1)} collective-permute-done((bf16[256,2048]{1,0:T(8,128)(2,1)}, bf16[256,2048]{1,0:T(8,128)(2,1)}, u32[]{:S(2)}, u32[]{:S(2)}) %collective-permute-start.25) | collective-permute-done | bytes 1048608 | tf_op jit(solution)/shard_map/ppermute | solution.py:37
  519.4 11.2 %multiply_convert_fusion = bf16[2,4,512,1024]{3,2,1,0:T(8,128)(2,1)} fusion(f32[2,4,512,1024]{3,2,1,0:T(8,128)} %copy-done, f32[2,4,512]{2,1,0:T(4,128)S(1)} %multiply_reduce_fusion.2, f32[2,4,512]{2,1,0:T(4,128)S(1)} %fusion.83, pred[2,512,1024]{2,1,0:T(8,128)(4,1)S(1)} %copy-done.12, bf16[2,4,512,128]{3,2,1,0:T(8,128)(2,1)} %bitcast.382, ...), kind=kOutput, calls=%fused_computation | convolution fusion | flops 1098907648 | bytes 29392896 | tf_op jit(solution)/shard_map/rjqd,rjkd->rjqk/dot_general | solution.py:297
  530.6 11.3 %convert_bitcast_fusion = bf16[1,2,4,1024,128]{4,3,2,1,0:T(8,128)(2,1)} fusion(bf16[2,4,512,128]{3,2,1,0:T(8,128)(2,1)} %bitcast.383, f32[2,4,512,1024]{3,2,1,0:T(8,128)} %copy-done, f32[2,4,512]{2,1,0:T(4,128)S(1)} %fusion.83, pred[2,512,1024]{2,1,0:T(8,128)(4,1)S(1)} %copy-done.12), kind=kOutput, calls=%fused_computation.81 | convolution fusion | flops 1091567616 | bytes 20987904 | tf_op jit(solution)/shard_map/rjqk,rjqd->rjkd/dot_general | solution.py:297
  625.9 17.8 %collective-permute-done.43 = bf16[256,2048]{1,0:T(8,128)(2,1)S(1)} collective-permute-done((bf16[256,2048]{1,0:T(8,128)(2,1)S(1)}, bf16[256,2048]{1,0:T(8,128)(2,1)S(1)}, u32[]{:S(2)}, u32[]{:S(2)}) %collective-permute-start.43) | collective-permute-done | bytes 1048608 | tf_op jit(solution)/shard_map/ppermute | solution.py:37
  646.8 19.3 %collective-permute-done.35 = bf16[2,2,4,128,128]{4,3,2,1,0:T(8,128)(2,1)S(1)} collective-permute-done((bf16[2,2,4,128,128]{4,3,2,1,0:T(8,128)(2,1)S(1)}, bf16[2,2,4,128,128]{4,3,2,1,0:T(8,128)(2,1)S(1)}, u32[]{:S(2)}, u32[]{:S(2)}) %collective-permute-start.35) | collective-permute-done | bytes 524320 | tf_op jit(solution)/shard_map/ppermute | solution.py:37
  669.2 32.0 %all-reduce.3.cloned.1.call-done = (bf16[2048,2048]{1,0:T(8,128)(2,1)}, bf16[1024,2048]{1,0:T(8,128)(2,1)}) async-done(((bf16[2048,2048]{1,0:T(8,128)(2,1)}, bf16[1024,2048]{1,0:T(8,128)(2,1)}), (bf16[2048,2048]{1,0:T(8,128)(2,1)}, bf16[1024,2048]{1,0:T(8,128)(2,1)})) %all-reduce.3.cloned.1.call-update) | async-done | bytes 12582928 | tf_op jit(solution)/shard_map/psum | solution.py:361
  717.5 19.1 %collective-permute-done.40 = f32[2,2048]{1,0:T(2,128)S(1)} collective-permute-done((f32[2,2048]{1,0:T(2,128)S(1)}, f32[2,2048]{1,0:T(2,128)S(1)}, u32[]{:S(2)}, u32[]{:S(2)}) %collective-permute-start.40) | collective-permute-done | bytes 16416 | tf_op jit(solution)/shard_map/ppermute | solution.py:222
  743.9 17.3 %copy.98 = bf16[2,1024,2048]{2,0,1:T(2,128)(2,1)S(1)} copy(bf16[2,1024,2048]{2,1,0:T(8,128)(2,1)S(1)} %bitcast.378) | data formatting | bytes 16777216 | tf_op jit(solution)/shard_map/reshape | solution.py:436
  761.3 10.8 %convert_element_type.688 = f32[1024,2,2048]{2,1,0:T(2,128)} convert(bf16[1024,2,2048]{2,1,0:T(2,128)(2,1)S(1)} %bitcast.351) | non-fusion elementwise | flops 4194304 | bytes 25165824 | tf_op jit(solution)/shard_map/convert_element_type | solution.py:447
  (550 shorter events, 459.7 us)
Async XLA Ops:
  7.2 201.9 %all-gather.5.cloned.1.call-start = ((), (), s32[]{:S(2)}) async-start(), calls=%async_computation.2 | async-start | bytes 4718592 | tf_op jit(solution)/shard_map/all_gather | solution.py:269
  7.2 105.5 %collective-permute-start.7 = (bf16[256,2048]{1,0:T(8,128)(2,1)}, bf16[256,2048]{1,0:T(8,128)(2,1)}, u32[]{:S(2)}, u32[]{:S(2)}) collective-permute-start(bf16[256,2048]{1,0:T(8,128)(2,1)} %param.13), channel_id=1, source_target_pairs={{0,1},{1,0},{2,3},{3,2},{4,5},{5,4},{6,7},{7,6},{8,9},{9,8},{10,11... | collective-permute-start | bytes 3145736 | tf_op jit(solution)/shard_map/ppermute | solution.py:32
  12.1 216.6 %collective-permute-start.20 = (bf16[256,2048]{1,0:T(8,128)(2,1)}, bf16[256,2048]{1,0:T(8,128)(2,1)}, u32[]{:S(2)}, u32[]{:S(2)}) collective-permute-start(bf16[256,2048]{1,0:T(8,128)(2,1)} %param.14), channel_id=1, source_target_pairs={{0,1},{1,0},{2,3},{3,2},{4,5},{5,4},{6,7},{7,6},{8,9},{9,8},{10,11... | collective-permute-start | bytes 3145736 | tf_op jit(solution)/shard_map/ppermute | solution.py:32
  106.7 125.7 %all-gather.7.cloned.1.call-start = ((), (), s32[]{:S(2)}) async-start(), calls=%async_computation.3 | async-start | bytes 4718592 | tf_op jit(solution)/shard_map/all_gather | solution.py:269
  166.4 42.7 %collective-permute-start.21 = (bf16[8,768,256]{1,2,0:T(8,128)(2,1)}, bf16[8,768,256]{1,2,0:T(8,128)(2,1)}, u32[]{:S(2)}, u32[]{:S(2)}) collective-permute-start(bf16[8,768,256]{1,2,0:T(8,128)(2,1)} %copy.56), channel_id=1, source_target_pairs={{0,1},{1,0},{2,3},{3,2},{4,5},{5,4},{6,7},{7,6},{8,9},{9,8},{10,11... | collective-permute-start | bytes 9437192 | tf_op jit(solution)/shard_map/ppermute | solution.py:32
  166.4 112.5 %all-gather.9.cloned.1.call-start = ((), (), s32[]{:S(2)}) async-start(), calls=%async_computation.4 | async-start | bytes 4718592 | tf_op jit(solution)/shard_map/all_gather | solution.py:330
  233.5 92.8 %all-gather.11.cloned.1.call-start = ((), (), s32[]{:S(2)}) async-start(), calls=%async_computation.5 | async-start | bytes 4718592 | tf_op jit(solution)/shard_map/all_gather | solution.py:330
  234.0 156.7 %reduce-scatter.5.cloned.1.call-start = ((), (), s32[]{:S(2)}) async-start(), calls=%async_computation.7 | async-start | bytes 4718592 | tf_op jit(solution)/shard_map/reduce_scatter | solution.py:347
  326.3 101.2 %reduce-scatter.3.cloned.1.call-start = ((), (), s32[]{:S(2)}) async-start(), calls=%async_computation.6 | async-start | bytes 4718592 | tf_op jit(solution)/shard_map/reduce_scatter | solution.py:347
  364.6 336.6 %all-reduce.3.cloned.1.call-start = ((), (), s32[]{:S(2)}) async-start(), calls=%async_computation.8 | async-start | bytes 25165824 | tf_op jit(solution)/shard_map/psum | solution.py:361
  436.2 39.6 %collective-permute-start.24 = (bf16[1024,2048]{1,0:T(8,128)(2,1)}, bf16[1024,2048]{1,0:T(8,128)(2,1)}, u32[]{:S(2)}, u32[]{:S(2)}) collective-permute-start(bf16[1024,2048]{1,0:T(8,128)(2,1)} %convolution_convert_fusion.3), channel_id=1, source_target_pairs={{0,1},{1,0},{2,3},{3,2},{4,5},{5,4},{6,7},{7,6},{8,9},{9,8},{10,11... | collective-permute-start | bytes 12582920 | tf_op jit(solution)/shard_map/ppermute | solution.py:32
  475.4 41.3 %collective-permute-start.23 = (bf16[128,2048]{1,0:T(8,128)(2,1)}, bf16[128,2048]{1,0:T(8,128)(2,1)}, u32[]{:S(2)}, u32[]{:S(2)}) collective-permute-start(bf16[128,2048]{1,0:T(8,128)(2,1)} %get-tuple-element.117), channel_id=1, source_target_pairs={{0,2},{1,3},{2,4},{3,5},{4,6},{5,7},{6,0},{7,1},{8,10},{9,11},{10,... | collective-permute-start | bytes 1572872 | tf_op jit(solution)/shard_map/ppermute | solution.py:37
  518.7 35.2 %collective-permute-start.26 = (bf16[128,2048]{1,0:T(8,128)(2,1)}, bf16[128,2048]{1,0:T(8,128)(2,1)}, u32[]{:S(2)}, u32[]{:S(2)}) collective-permute-start(bf16[128,2048]{1,0:T(8,128)(2,1)} %add_convert_fusion.35), channel_id=1, source_target_pairs={{0,2},{1,3},{2,4},{3,5},{4,6},{5,7},{6,0},{7,1},{8,10},{9,11},{10,... | collective-permute-start | bytes 1572872 | tf_op jit(solution)/shard_map/ppermute | solution.py:37
  555.9 237.9 %collective-permute-start.28 = (bf16[128,2048]{1,0:T(8,128)(2,1)}, bf16[128,2048]{1,0:T(8,128)(2,1)}, u32[]{:S(2)}, u32[]{:S(2)}) collective-permute-start(bf16[128,2048]{1,0:T(8,128)(2,1)} %add_convert_fusion.33), channel_id=1, source_target_pairs={{0,2},{1,3},{2,4},{3,5},{4,6},{5,7},{6,0},{7,1},{8,10},{9,11},{10,... | collective-permute-start | bytes 1572872 | tf_op jit(solution)/shard_map/ppermute | solution.py:37
  555.9 57.4 %collective-permute-start.50 = (bf16[256,2048]{1,0:T(8,128)(2,1)}, bf16[256,2048]{1,0:T(8,128)(2,1)}, u32[]{:S(2)}, u32[]{:S(2)}) collective-permute-start(bf16[256,2048]{1,0:T(8,128)(2,1)} %add_convert_fusion.11), channel_id=1, source_target_pairs={{0,2},{1,3},{2,4},{3,5},{4,6},{5,7},{6,0},{7,1},{8,10},{9,11},{10,... | collective-permute-start | bytes 3145736 | tf_op jit(solution)/shard_map/ppermute | solution.py:37
  617.1 84.1 %collective-permute-start.51 = (bf16[128,2048]{1,0:T(8,128)(2,1)}, bf16[128,2048]{1,0:T(8,128)(2,1)}, u32[]{:S(2)}, u32[]{:S(2)}) collective-permute-start(bf16[128,2048]{1,0:T(8,128)(2,1)} %get-tuple-element.132), channel_id=1, source_target_pairs={{0,8},{8,0},{16,24},{24,16},{1,9},{9,1},{17,25},{25,17},{2,10},{10... | collective-permute-start | bytes 1572872 | tf_op jit(solution)/shard_map/ppermute | solution.py:41
  618.7 82.5 %collective-permute-start.53 = (bf16[128,2048]{1,0:T(8,128)(2,1)}, bf16[128,2048]{1,0:T(8,128)(2,1)}, u32[]{:S(2)}, u32[]{:S(2)}) collective-permute-start(bf16[128,2048]{1,0:T(8,128)(2,1)} %get-tuple-element.133), channel_id=1, source_target_pairs={{0,16},{8,24},{16,0},{24,8},{1,17},{9,25},{17,1},{25,9},{2,18},{10... | collective-permute-start | bytes 1572872 | tf_op jit(solution)/shard_map/ppermute | solution.py:41
  621.9 45.1 %collective-permute-start.31 = (bf16[128,2048]{1,0:T(8,128)(2,1)S(1)}, bf16[128,2048]{1,0:T(8,128)(2,1)S(1)}, u32[]{:S(2)}, u32[]{:S(2)}) collective-permute-start(bf16[128,2048]{1,0:T(8,128)(2,1)S(1)} %add_convert_fusion.31), channel_id=1, source_target_pairs={{0,2},{1,3},{2,4},{3,5},{4,6},{5,7},{6,0},{7,1},{8,10},{9,11},{10,... | collective-permute-start | bytes 1572872 | tf_op jit(solution)/shard_map/ppermute | solution.py:37
  666.0 40.8 %collective-permute-start.44 = (bf16[256,2048]{1,0:T(8,128)(2,1)}, bf16[256,2048]{1,0:T(8,128)(2,1)}, u32[]{:S(2)}, u32[]{:S(2)}) collective-permute-start(bf16[256,2048]{1,0:T(8,128)(2,1)} %add_convert_fusion.8), channel_id=1, source_target_pairs={{0,2},{1,3},{2,4},{3,5},{4,6},{5,7},{6,0},{7,1},{8,10},{9,11},{10,... | collective-permute-start | bytes 3145736 | tf_op jit(solution)/shard_map/ppermute | solution.py:37
  703.4 34.5 %collective-permute-start.52 = (bf16[128,2048]{1,0:T(8,128)(2,1)S(1)}, bf16[128,2048]{1,0:T(8,128)(2,1)S(1)}, u32[]{:S(2)}, u32[]{:S(2)}) collective-permute-start(bf16[128,2048]{1,0:T(8,128)(2,1)S(1)} %get-tuple-element.130), channel_id=1, source_target_pairs={{0,16},{8,24},{16,0},{24,8},{1,17},{9,25},{17,1},{25,9},{2,18},{10... | collective-permute-start | bytes 1572872 | tf_op jit(solution)/shard_map/ppermute | solution.py:41
  709.2 67.9 %collective-permute-start.45 = (bf16[256,2048]{1,0:T(8,128)(2,1)S(1)}, bf16[256,2048]{1,0:T(8,128)(2,1)S(1)}, u32[]{:S(2)}, u32[]{:S(2)}) collective-permute-start(bf16[256,2048]{1,0:T(8,128)(2,1)S(1)} %add_convert_fusion.6), channel_id=1, source_target_pairs={{0,2},{1,3},{2,4},{3,5},{4,6},{5,7},{6,0},{7,1},{8,10},{9,11},{10,... | collective-permute-start | bytes 3145736 | tf_op jit(solution)/shard_map/ppermute | solution.py:37
  740.4 36.1 %collective-permute-start.42 = (f32[2,2048]{1,0:T(2,128)S(1)}, f32[2,2048]{1,0:T(2,128)S(1)}, u32[]{:S(2)}, u32[]{:S(2)}) collective-permute-start(f32[2,2048]{1,0:T(2,128)S(1)} %add.552), channel_id=1, source_target_pairs={{0,16},{8,24},{16,0},{24,8},{1,17},{9,25},{17,1},{25,9},{2,18},{10... | collective-permute-start | bytes 49160 | tf_op jit(solution)/shard_map/ppermute | solution.py:41
  743.4 37.9 %collective-permute-start.32 = (bf16[128,2048]{1,0:T(8,128)(2,1)S(1)}, bf16[128,2048]{1,0:T(8,128)(2,1)S(1)}, u32[]{:S(2)}, u32[]{:S(2)}) collective-permute-start(bf16[128,2048]{1,0:T(8,128)(2,1)S(1)} %copy-done.69), channel_id=1, source_target_pairs={{0,2},{1,3},{2,4},{3,5},{4,6},{5,7},{6,0},{7,1},{8,10},{9,11},{10,... | collective-permute-start | bytes 1572872 | tf_op jit(solution)/shard_map/ppermute | solution.py:37
  743.9 40.3 %collective-permute-start.36 = (bf16[2,2,4,128,128]{4,3,2,1,0:T(8,128)(2,1)S(1)}, bf16[2,2,4,128,128]{4,3,2,1,0:T(8,128)(2,1)S(1)}, u32[]{:S(2)}, u32[]{:S(2)}) collective-permute-start(bf16[2,2,4,128,128]{4,3,2,1,0:T(8,128)(2,1)S(1)} %copy-done.70), channel_id=1, source_target_pairs={{0,2},{1,3},{2,4},{3,5},{4,6},{5,7},{6,0},{7,1},{8,10},{9,11},{10,... | collective-permute-start | bytes 1572872 | tf_op jit(solution)/shard_map/ppermute | solution.py:37
  (144 other events, 2005.6 us)
Sparse Core Ops, SparseCore 0:
  106.8 45.2 all-gather.4
  166.5 45.1 all-gather.6
  233.6 45.2 all-gather.8
  280.3 45.8 all-gather.10
  328.4 48.7 reduce-scatter.4
  379.3 48.1 reduce-scatter.2
  451.7 249.3 all-reduce.2

commit v14 on v12

--- a/solution.py
+++ b/solution.py
@@ -435,6 +435,9 @@
     in_grad, down_grad = summed
     in_grad = in_grad.reshape(2, units, width).transpose(1, 0, 2)
     in_grad = lax.optimization_barrier(in_grad)
+    for _ in range(chips - 2):
+        main.step()
+    main.step(in_grad)
     gain_grad = sum_all(gain_grad, rows, seq)
     output_grad, query_grad = sum_rows((output_sum, main.result("query")), rows)
     return (

time: 829 us -> 812 us (0.979)
  waiting for transfers between devices: 259 us -> 241 us
    ppermute x24, waiting for transfers between devices: 174 us -> 156 us  [ring(): return lax.ppermute(value, 'seq', pairs)]
    unnamed x246 -> x244, local copies, waits for them, and re-layouts: 36.8 us -> 37 us
  transfers between devices with their start and end apart: 62 -> 62, of which waited for: 28 -> 28; matrix products, arithmetic and copies ran while one was open for 59% -> 60% of each run, Pallas kernels for 0% -> 0%
where the time goes in v14:
time: 812 us; the launch traced here: 801 us
  waiting for transfers between devices  241 us (30%)
  matrix products  224 us (28%)
  local copies, waits for them, and re-layouts  156 us (19%)
  other arithmetic  128 us (16%)
  starting transfers between devices  35.2 us (4%)
  between operations  16.5 us (2%)
    dot_general x24, matrix products, dot(): lax.dot_general(left, right, (dims, ((), ())), preferred_element_type=F32)  158 us
    ppermute x24, waiting for transfers between devices, ring(): return lax.ppermute(value, 'seq', pairs)  156 us
    dot_general x6, matrix products, heads_dot(): return jnp.einsum(spec, left, right, preferred_element_type=F32)  42.8 us
    ppermute x18, waiting for transfers between devices, swap_row(): return lax.ppermute(value, 'rows', [(r, r ^ mask) for r in range(rows)])  41.1 us
    unnamed x244, local copies, waits for them, and re-layouts  37 us
    all_gather x2, waiting for transfers between devices, local(): lax.all_gather(n, 'seq', axis=0, tiled=True)  29.6 us
    ppermute x18, starting transfers between devices, swap_row(): return lax.ppermute(value, 'rows', [(r, r ^ mask) for r in range(rows)])  21.7 us
    convert_element_type x10, other arithmetic, ring_scatter(): sent = total.astype(BF16)  19.4 us
  transfers between devices with their start and end apart: 62, of which 28 were waited for; matrix products, arithmetic and copies ran while one was open for 60% of the time, Pallas kernels for 0%

profile of v14, /device:TPU:0, one launch (start us, length us, event | category | flops | bytes accessed | tf_op | source)
XLA Modules:
  0.0 801.3 jit_solution(12841987233906983133)
XLA Ops:
  121.1 10.1 %collective-permute-done.5 = bf16[2,3,256,256]{3,2,1,0:T(8,128)(2,1)S(1)} collective-permute-done((bf16[2,3,256,256]{3,2,1,0:T(8,128)(2,1)S(1)}, bf16[2,3,256,256]{3,2,1,0:T(8,128)(2,1)S(1)}, u32[]{:S(2)}, u32[]{:S(2)}) %collective-permute-start.5) | collective-permute-done | bytes 786464 | tf_op jit(solution)/shard_map/ppermute | solution.py:41
  214.7 11.1 %copy.57 = f32[2,2,2,256,256]{4,3,2,1,0:T(8,128)S(1)} copy(f32[2,2,2,256,256]{3,4,2,1,0:T(8,128)} %bitcast.378) | data formatting | bytes 4194304 | tf_op jit(solution)/shard_map/reshape;reshape | solution.py:94
  234.2 16.5 %fusion.99 = (bf16[1024,1,2048]{2,1,0:T(2,128)(2,1)S(1)}, bf16[1024,1,2048]{2,1,0:T(2,128)(2,1)S(1)}) fusion(bf16[1024,2,2048]{2,1,0:T(2,128)(2,1)} %param.15), kind=kLoop, calls=%fused_computation.326 | loop fusion | bytes 16777216 | tf_op jit(solution)/shard_map/slice | solution.py:260
  258.4 20.6 %all-gather.9.cloned.1.call-done = bf16[1024,2048]{1,0:T(8,128)(2,1)} async-done(((bf16[128,2048]{1,0:T(8,128)(2,1)}), bf16[1024,2048]{1,0:T(8,128)(2,1)}) %all-gather.9.cloned.1.call-update) | async-done | bytes 4194320 | tf_op jit(solution)/shard_map/all_gather | solution.py:330
  279.0 15.3 %fusion.98 = f32[1024,2048]{1,0:T(8,128)} fusion(bf16[1024,2048]{1,0:T(8,128)(2,1)} %all-gather.9.cloned.1.call-done, bf16[1024,2048]{1,0:T(8,128)(2,1)} %get-tuple-element.190, bf16[1024,2048]{1,0:T(8,128)(2,1)} %get-tuple-element.191), kind=kOutput, calls=%fused_computation.325 | convolution fusion | flops 8606711808 | bytes 20971520 | tf_op jit(solution)/shard_map/dot_general | solution.py:17
  294.3 10.2 %multiply_convert_fusion.6 = (bf16[1024,1024]{1,0:T(8,128)(2,1)S(1)}, bf16[1024,1024]{1,0:T(8,128)(2,1)}, bf16[1024,1024]{1,0:T(8,128)(2,1)}) fusion(f32[1024,2048]{1,0:T(8,128)} %fusion.98, bf16[1024,2048]{1,0:T(8,128)(2,1)S(1)} %copy-done.91, bf16[1024,2048]{1,0:T(8,128)(2,1)S(1)} %copy-done.88), kind=kOutput, calls=%fused_computation.42 | convolution fusion | flops 4311744512 | bytes 23068672 | tf_op jit(solution)/shard_map/dot_general | solution.py:17
  304.5 12.8 %convolution_convert_fusion.5 = bf16[1024,2048]{1,0:T(8,128)(2,1)} fusion(bf16[1024,1024]{1,0:T(8,128)(2,1)} %get-tuple-element.109, bf16[1024,1024]{1,0:T(8,128)(2,1)S(1)} %get-tuple-element.108, bf16[1024,2048]{1,0:T(8,128)(2,1)S(1)} %copy-done.39, bf16[1024,2048]{1,0:T(8,128)(2,1)S(1)} %copy-done.41), kind=kOutput, calls=%fused_computation.50 | convolution fusion | flops 8617197568 | bytes 16777216 | tf_op jit(solution)/shard_map/dot_general | solution.py:17
  317.3 9.0 %all-gather.11.cloned.1.call-done = bf16[1024,2048]{1,0:T(8,128)(2,1)} async-done(((bf16[128,2048]{1,0:T(8,128)(2,1)}), bf16[1024,2048]{1,0:T(8,128)(2,1)}) %all-gather.11.cloned.1.call-update) | async-done | bytes 4194320 | tf_op jit(solution)/shard_map/all_gather | solution.py:330
  326.4 15.3 %fusion.97 = f32[1024,2048]{1,0:T(8,128)} fusion(bf16[1024,2048]{1,0:T(8,128)(2,1)} %all-gather.11.cloned.1.call-done, bf16[1024,2048]{1,0:T(8,128)(2,1)} %get-tuple-element.190, bf16[1024,2048]{1,0:T(8,128)(2,1)} %get-tuple-element.191), kind=kOutput, calls=%fused_computation.324 | convolution fusion | flops 8606711808 | bytes 20971520 | tf_op jit(solution)/shard_map/dot_general | solution.py:17
  341.7 11.2 %multiply_convert_fusion.4 = (bf16[1024,1024]{1,0:T(8,128)(2,1)S(1)}, bf16[1024,1024]{1,0:T(8,128)(2,1)S(1)}, bf16[1024,1024]{1,0:T(8,128)(2,1)}) fusion(f32[1024,2048]{1,0:T(8,128)} %fusion.97, bf16[1024,2048]{1,0:T(8,128)(2,1)} %all-gather.7.cloned.1.call-done, bf16[1024,2048]{1,0:T(8,128)(2,1)S(1)} %copy-done.89), kind=kOutput, calls=%fused_computation.39 | convolution fusion | flops 4311744512 | bytes 23068672 | tf_op jit(solution)/shard_map/dot_general | solution.py:17
  354.1 10.5 %convolution_convert_fusion.4 = bf16[1024,2048]{1,0:T(8,128)(2,1)} fusion(bf16[1024,2048]{1,0:T(8,128)(2,1)S(1)} %copy-done.40, bf16[1024,2048]{1,0:T(8,128)(2,1)S(1)} %copy-done.42, bf16[1024,1024]{1,0:T(8,128)(2,1)S(1)} %get-tuple-element.107, bf16[1024,1024]{1,0:T(8,128)(2,1)S(1)} %get-tuple-element.106), kind=kOutput, calls=%fused_computation.49 | convolution fusion | flops 8617197568 | bytes 16777216 | tf_op jit(solution)/shard_map/dot_general | solution.py:17
  378.7 12.2 %fusion.21 = f32[2048,2048]{1,0:T(8,128)} fusion(bf16[1024,2048]{1,0:T(8,128)(2,1)S(1)} %copy-done.94, bf16[1024,1024]{1,0:T(8,128)(2,1)S(1)} %copy-done.101, bf16[1024,1024]{1,0:T(8,128)(2,1)S(1)} %copy-done.100), kind=kOutput, calls=%fused_computation.62 | convolution fusion | flops 8598323200 | bytes 25165824 | tf_op jit(solution)/shard_map/dot_general | solution.py:17
  390.9 9.8 %add_convert_fusion.1 = bf16[1024,2048]{1,0:T(8,128)(2,1)} fusion(f32[1024,2048]{1,0:T(8,128)} %fusion.109, bf16[1024,1024]{1,0:T(8,128)(2,1)S(1)} %copy-done.97, bf16[1024,2048]{1,0:T(8,128)(2,1)} %all-gather.7.cloned.1.call-done), kind=kOutput, calls=%fused_computation.21 | convolution fusion | flops 4299161600 | bytes 18874368 | tf_op jit(solution)/shard_map/dot_general | solution.py:17
  400.7 15.1 %add_convert_fusion = bf16[2048,2048]{1,0:T(8,128)(2,1)} fusion(f32[2048,2048]{1,0:T(8,128)} %fusion.21, bf16[1024,2048]{1,0:T(8,128)(2,1)S(1)} %copy-done.36, bf16[1024,2048]{1,0:T(8,128)(2,1)S(1)} %copy-done.93), kind=kOutput, calls=%fused_computation.2 | convolution fusion | flops 8598323200 | bytes 33554432 | tf_op jit(solution)/shard_map/dot_general | solution.py:17
  415.8 11.7 %reduce-scatter.3.cloned.1.call-done = bf16[128,2048]{1,0:T(8,128)(2,1)} async-done(((bf16[1024,2048]{1,0:T(8,128)(2,1)}), bf16[128,2048]{1,0:T(8,128)(2,1)}) %reduce-scatter.3.cloned.1.call-update) | async-done | bytes 524304 | tf_op jit(solution)/shard_map/reduce_scatter | solution.py:347
  499.2 14.7 %collective-permute-done.25 = bf16[256,2048]{1,0:T(8,128)(2,1)} collective-permute-done((bf16[256,2048]{1,0:T(8,128)(2,1)}, bf16[256,2048]{1,0:T(8,128)(2,1)}, u32[]{:S(2)}, u32[]{:S(2)}) %collective-permute-start.25) | collective-permute-done | bytes 1048608 | tf_op jit(solution)/shard_map/ppermute | solution.py:37
  519.5 11.2 %multiply_convert_fusion = bf16[2,4,512,1024]{3,2,1,0:T(8,128)(2,1)} fusion(f32[2,4,512,1024]{3,2,1,0:T(8,128)} %copy-done, f32[2,4,512]{2,1,0:T(4,128)S(1)} %multiply_reduce_fusion.2, f32[2,4,512]{2,1,0:T(4,128)S(1)} %fusion.83, pred[2,512,1024]{2,1,0:T(8,128)(4,1)S(1)} %copy-done.12, bf16[2,4,512,128]{3,2,1,0:T(8,128)(2,1)} %bitcast.380, ...), kind=kOutput, calls=%fused_computation | convolution fusion | flops 1098907648 | bytes 29392896 | tf_op jit(solution)/shard_map/rjqd,rjkd->rjqk/dot_general | solution.py:297
  530.6 11.3 %convert_bitcast_fusion = bf16[1,2,4,1024,128]{4,3,2,1,0:T(8,128)(2,1)} fusion(bf16[2,4,512,128]{3,2,1,0:T(8,128)(2,1)} %bitcast.381, f32[2,4,512,1024]{3,2,1,0:T(8,128)} %copy-done, f32[2,4,512]{2,1,0:T(4,128)S(1)} %fusion.83, pred[2,512,1024]{2,1,0:T(8,128)(4,1)S(1)} %copy-done.12), kind=kOutput, calls=%fused_computation.81 | convolution fusion | flops 1091567616 | bytes 20987904 | tf_op jit(solution)/shard_map/rjqk,rjqd->rjkd/dot_general | solution.py:297
  616.1 21.9 %collective-permute-done.43 = bf16[256,2048]{1,0:T(8,128)(2,1)S(1)} collective-permute-done((bf16[256,2048]{1,0:T(8,128)(2,1)S(1)}, bf16[256,2048]{1,0:T(8,128)(2,1)S(1)}, u32[]{:S(2)}, u32[]{:S(2)}) %collective-permute-start.43) | collective-permute-done | bytes 1048608 | tf_op jit(solution)/shard_map/ppermute | solution.py:37
  646.2 17.4 %collective-permute-done.53 = bf16[128,2048]{1,0:T(8,128)(2,1)S(1)} collective-permute-done((bf16[128,2048]{1,0:T(8,128)(2,1)S(1)}, bf16[128,2048]{1,0:T(8,128)(2,1)S(1)}, u32[]{:S(2)}, u32[]{:S(2)}) %collective-permute-start.53) | collective-permute-done | bytes 524320 | tf_op jit(solution)/shard_map/ppermute | solution.py:41
  666.4 14.2 %collective-permute-done.31 = bf16[128,2048]{1,0:T(8,128)(2,1)S(1)} collective-permute-done((bf16[128,2048]{1,0:T(8,128)(2,1)S(1)}, bf16[128,2048]{1,0:T(8,128)(2,1)S(1)}, u32[]{:S(2)}, u32[]{:S(2)}) %collective-permute-start.31) | collective-permute-done | bytes 524320 | tf_op jit(solution)/shard_map/ppermute | solution.py:37
  695.0 20.5 %collective-permute-done.36 = bf16[2,2,4,128,128]{4,3,2,1,0:T(8,128)(2,1)S(1)} collective-permute-done((bf16[2,2,4,128,128]{4,3,2,1,0:T(8,128)(2,1)S(1)}, bf16[2,2,4,128,128]{4,3,2,1,0:T(8,128)(2,1)S(1)}, u32[]{:S(2)}, u32[]{:S(2)}) %collective-permute-start.36) | collective-permute-done | bytes 524320 | tf_op jit(solution)/shard_map/ppermute | solution.py:37
  720.0 14.5 %copy.98 = bf16[2,1024,2048]{2,0,1:T(2,128)(2,1)S(1)} copy(bf16[2,1024,2048]{2,1,0:T(8,128)(2,1)} %bitcast.376) | data formatting | bytes 16777216 | tf_op jit(solution)/shard_map/reshape | solution.py:436
  757.7 10.7 %convert_element_type.688 = f32[1024,2,2048]{2,1,0:T(2,128)} convert(bf16[1024,2,2048]{2,1,0:T(2,128)(2,1)S(1)} %bitcast.351) | non-fusion elementwise | flops 4194304 | bytes 25165824 | tf_op jit(solution)/shard_map/convert_element_type | solution.py:450
  (541 shorter events, 456.9 us)
Async XLA Ops:
  7.2 202.0 %all-gather.5.cloned.1.call-start = ((), (), s32[]{:S(2)}) async-start(), calls=%async_computation.2 | async-start | bytes 4718592 | tf_op jit(solution)/shard_map/all_gather | solution.py:269
  7.2 105.5 %collective-permute-start.7 = (bf16[256,2048]{1,0:T(8,128)(2,1)}, bf16[256,2048]{1,0:T(8,128)(2,1)}, u32[]{:S(2)}, u32[]{:S(2)}) collective-permute-start(bf16[256,2048]{1,0:T(8,128)(2,1)} %param.13), channel_id=1, source_target_pairs={{0,1},{1,0},{2,3},{3,2},{4,5},{5,4},{6,7},{7,6},{8,9},{9,8},{10,11... | collective-permute-start | bytes 3145736 | tf_op jit(solution)/shard_map/ppermute | solution.py:32
  12.1 216.7 %collective-permute-start.20 = (bf16[256,2048]{1,0:T(8,128)(2,1)}, bf16[256,2048]{1,0:T(8,128)(2,1)}, u32[]{:S(2)}, u32[]{:S(2)}) collective-permute-start(bf16[256,2048]{1,0:T(8,128)(2,1)} %param.14), channel_id=1, source_target_pairs={{0,1},{1,0},{2,3},{3,2},{4,5},{5,4},{6,7},{7,6},{8,9},{9,8},{10,11... | collective-permute-start | bytes 3145736 | tf_op jit(solution)/shard_map/ppermute | solution.py:32
  106.7 125.8 %all-gather.7.cloned.1.call-start = ((), (), s32[]{:S(2)}) async-start(), calls=%async_computation.3 | async-start | bytes 4718592 | tf_op jit(solution)/shard_map/all_gather | solution.py:269
  166.5 42.8 %collective-permute-start.21 = (bf16[8,768,256]{1,2,0:T(8,128)(2,1)}, bf16[8,768,256]{1,2,0:T(8,128)(2,1)}, u32[]{:S(2)}, u32[]{:S(2)}) collective-permute-start(bf16[8,768,256]{1,2,0:T(8,128)(2,1)} %copy.56), channel_id=1, source_target_pairs={{0,1},{1,0},{2,3},{3,2},{4,5},{5,4},{6,7},{7,6},{8,9},{9,8},{10,11... | collective-permute-start | bytes 9437192 | tf_op jit(solution)/shard_map/ppermute | solution.py:32
  166.5 112.5 %all-gather.9.cloned.1.call-start = ((), (), s32[]{:S(2)}) async-start(), calls=%async_computation.4 | async-start | bytes 4718592 | tf_op jit(solution)/shard_map/all_gather | solution.py:330
  233.6 92.7 %all-gather.11.cloned.1.call-start = ((), (), s32[]{:S(2)}) async-start(), calls=%async_computation.5 | async-start | bytes 4718592 | tf_op jit(solution)/shard_map/all_gather | solution.py:330
  234.2 156.7 %reduce-scatter.5.cloned.1.call-start = ((), (), s32[]{:S(2)}) async-start(), calls=%async_computation.7 | async-start | bytes 4718592 | tf_op jit(solution)/shard_map/reduce_scatter | solution.py:347
  326.3 101.2 %reduce-scatter.3.cloned.1.call-start = ((), (), s32[]{:S(2)}) async-start(), calls=%async_computation.6 | async-start | bytes 4718592 | tf_op jit(solution)/shard_map/reduce_scatter | solution.py:347
  364.7 353.9 %all-reduce.3.cloned.1.call-start = ((), (), s32[]{:S(2)}) async-start(), calls=%async_computation.8 | async-start | bytes 25165824 | tf_op jit(solution)/shard_map/psum | solution.py:361
  436.3 39.5 %collective-permute-start.24 = (bf16[1024,2048]{1,0:T(8,128)(2,1)}, bf16[1024,2048]{1,0:T(8,128)(2,1)}, u32[]{:S(2)}, u32[]{:S(2)}) collective-permute-start(bf16[1024,2048]{1,0:T(8,128)(2,1)} %convolution_convert_fusion.3), channel_id=1, source_target_pairs={{0,1},{1,0},{2,3},{3,2},{4,5},{5,4},{6,7},{7,6},{8,9},{9,8},{10,11... | collective-permute-start | bytes 12582920 | tf_op jit(solution)/shard_map/ppermute | solution.py:32
  475.4 41.3 %collective-permute-start.23 = (bf16[128,2048]{1,0:T(8,128)(2,1)}, bf16[128,2048]{1,0:T(8,128)(2,1)}, u32[]{:S(2)}, u32[]{:S(2)}) collective-permute-start(bf16[128,2048]{1,0:T(8,128)(2,1)} %get-tuple-element.121), channel_id=1, source_target_pairs={{0,2},{1,3},{2,4},{3,5},{4,6},{5,7},{6,0},{7,1},{8,10},{9,11},{10,... | collective-permute-start | bytes 1572872 | tf_op jit(solution)/shard_map/ppermute | solution.py:37
  480.5 33.4 %collective-permute-start.25 = (bf16[256,2048]{1,0:T(8,128)(2,1)}, bf16[256,2048]{1,0:T(8,128)(2,1)}, u32[]{:S(2)}, u32[]{:S(2)}) collective-permute-start(bf16[256,2048]{1,0:T(8,128)(2,1)} %get-tuple-element.114), channel_id=1, source_target_pairs={{0,2},{1,3},{2,4},{3,5},{4,6},{5,7},{6,0},{7,1},{8,10},{9,11},{10,... | collective-permute-start | bytes 3145736 | tf_op jit(solution)/shard_map/ppermute | solution.py:37
  518.8 35.2 %collective-permute-start.26 = (bf16[128,2048]{1,0:T(8,128)(2,1)}, bf16[128,2048]{1,0:T(8,128)(2,1)}, u32[]{:S(2)}, u32[]{:S(2)}) collective-permute-start(bf16[128,2048]{1,0:T(8,128)(2,1)} %add_convert_fusion.35), channel_id=1, source_target_pairs={{0,2},{1,3},{2,4},{3,5},{4,6},{5,7},{6,0},{7,1},{8,10},{9,11},{10,... | collective-permute-start | bytes 1572872 | tf_op jit(solution)/shard_map/ppermute | solution.py:37
  555.9 222.5 %collective-permute-start.28 = (bf16[128,2048]{1,0:T(8,128)(2,1)}, bf16[128,2048]{1,0:T(8,128)(2,1)}, u32[]{:S(2)}, u32[]{:S(2)}) collective-permute-start(bf16[128,2048]{1,0:T(8,128)(2,1)} %add_convert_fusion.33), channel_id=1, source_target_pairs={{0,2},{1,3},{2,4},{3,5},{4,6},{5,7},{6,0},{7,1},{8,10},{9,11},{10,... | collective-permute-start | bytes 1572872 | tf_op jit(solution)/shard_map/ppermute | solution.py:37
  555.9 55.5 %collective-permute-start.50 = (bf16[256,2048]{1,0:T(8,128)(2,1)}, bf16[256,2048]{1,0:T(8,128)(2,1)}, u32[]{:S(2)}, u32[]{:S(2)}) collective-permute-start(bf16[256,2048]{1,0:T(8,128)(2,1)} %add_convert_fusion.11), channel_id=1, source_target_pairs={{0,2},{1,3},{2,4},{3,5},{4,6},{5,7},{6,0},{7,1},{8,10},{9,11},{10,... | collective-permute-start | bytes 3145736 | tf_op jit(solution)/shard_map/ppermute | solution.py:37
  606.8 34.6 %collective-permute-start.30 = (bf16[512,2048]{1,0:T(8,128)(2,1)S(1)}, bf16[512,2048]{1,0:T(8,128)(2,1)S(1)}, u32[]{:S(2)}, u32[]{:S(2)}) collective-permute-start(bf16[512,2048]{1,0:T(8,128)(2,1)S(1)} %pad_maximum_fusion.8), channel_id=1, source_target_pairs={{0,1},{1,0},{2,3},{3,2},{4,5},{5,4},{6,7},{7,6},{8,9},{9,8},{10,11... | collective-permute-start | bytes 6291464 | tf_op jit(solution)/shard_map/ppermute | solution.py:32
  611.2 31.9 %collective-permute-start.34 = (bf16[2,2,4,512,128]{4,3,2,1,0:T(8,128)(2,1)S(1)}, bf16[2,2,4,512,128]{4,3,2,1,0:T(8,128)(2,1)S(1)}, u32[]{:S(2)}, u32[]{:S(2)}) collective-permute-start(bf16[2,2,4,512,128]{4,3,2,1,0:T(8,128)(2,1)S(1)} %slice.410), channel_id=1, source_target_pairs={{0,1},{1,0},{2,3},{3,2},{4,5},{5,4},{6,7},{7,6},{8,9},{9,8},{10,11... | collective-permute-start | bytes 6291464 | tf_op jit(solution)/shard_map/ppermute | solution.py:32
  641.4 49.0 %collective-permute-start.44 = (bf16[256,2048]{1,0:T(8,128)(2,1)S(1)}, bf16[256,2048]{1,0:T(8,128)(2,1)S(1)}, u32[]{:S(2)}, u32[]{:S(2)}) collective-permute-start(bf16[256,2048]{1,0:T(8,128)(2,1)S(1)} %add_convert_fusion.8), channel_id=1, source_target_pairs={{0,2},{1,3},{2,4},{3,5},{4,6},{5,7},{6,0},{7,1},{8,10},{9,11},{10,... | collective-permute-start | bytes 3145736 | tf_op jit(solution)/shard_map/ppermute | solution.py:37
  643.1 37.5 %collective-permute-start.31 = (bf16[128,2048]{1,0:T(8,128)(2,1)S(1)}, bf16[128,2048]{1,0:T(8,128)(2,1)S(1)}, u32[]{:S(2)}, u32[]{:S(2)}) collective-permute-start(bf16[128,2048]{1,0:T(8,128)(2,1)S(1)} %add_convert_fusion.31), channel_id=1, source_target_pairs={{0,2},{1,3},{2,4},{3,5},{4,6},{5,7},{6,0},{7,1},{8,10},{9,11},{10,... | collective-permute-start | bytes 1572872 | tf_op jit(solution)/shard_map/ppermute | solution.py:37
  645.5 44.7 %collective-permute-start.35 = (bf16[2,2,4,128,128]{4,3,2,1,0:T(8,128)(2,1)S(1)}, bf16[2,2,4,128,128]{4,3,2,1,0:T(8,128)(2,1)S(1)}, u32[]{:S(2)}, u32[]{:S(2)}) collective-permute-start(bf16[2,2,4,128,128]{4,3,2,1,0:T(8,128)(2,1)S(1)} %add_convert_fusion.25), channel_id=1, source_target_pairs={{0,2},{1,3},{2,4},{3,5},{4,6},{5,7},{6,0},{7,1},{8,10},{9,11},{10,... | collective-permute-start | bytes 1572872 | tf_op jit(solution)/shard_map/ppermute | solution.py:37
  665.0 53.7 %collective-permute-start.54 = (bf16[128,2048]{1,0:T(8,128)(2,1)}, bf16[128,2048]{1,0:T(8,128)(2,1)}, u32[]{:S(2)}, u32[]{:S(2)}) collective-permute-start(bf16[128,2048]{1,0:T(8,128)(2,1)} %get-tuple-element.135), channel_id=1, source_target_pairs={{0,8},{8,0},{16,24},{24,16},{1,9},{9,1},{17,25},{25,17},{2,10},{10... | collective-permute-start | bytes 1572872 | tf_op jit(solution)/shard_map/ppermute | solution.py:41
  680.6 67.7 %collective-permute-start.52 = (bf16[128,2048]{1,0:T(8,128)(2,1)}, bf16[128,2048]{1,0:T(8,128)(2,1)}, u32[]{:S(2)}, u32[]{:S(2)}) collective-permute-start(bf16[128,2048]{1,0:T(8,128)(2,1)} %get-tuple-element.134), channel_id=1, source_target_pairs={{0,16},{8,24},{16,0},{24,8},{1,17},{9,25},{17,1},{25,9},{2,18},{10... | collective-permute-start | bytes 1572872 | tf_op jit(solution)/shard_map/ppermute | solution.py:41
  742.3 32.2 %collective-permute-start.46 = (bf16[128,2048]{1,0:T(8,128)(2,1)S(1)}, bf16[128,2048]{1,0:T(8,128)(2,1)S(1)}, u32[]{:S(2)}, u32[]{:S(2)}) collective-permute-start(bf16[128,2048]{1,0:T(8,128)(2,1)S(1)} %get-tuple-element.140), channel_id=1, source_target_pairs={{0,8},{8,0},{16,24},{24,16},{1,9},{9,1},{17,25},{25,17},{2,10},{10... | collective-permute-start | bytes 1572872 | tf_op jit(solution)/shard_map/ppermute | solution.py:41
  (140 other events, 2084.9 us)
Sparse Core Ops, SparseCore 0:
  106.9 45.2 all-gather.4
  166.6 45.1 all-gather.6
  233.7 45.2 all-gather.8
  280.4 45.7 all-gather.10
  328.4 48.7 reduce-scatter.4
  379.4 48.1 reduce-scatter.2
  451.8 260.8 all-reduce.2
